TPU v7x, 32 devices: a whole 2x2x4 slice. The times are simulated.
32 devices in a mesh: bin: 16 (over z, y, x), wave: 2 (over core).
Axes of the slice: x: 2, y: 2, z: 4, core: 2. Of those that a mesh axis runs over, the one named last changes fastest.
Arguments:
- sources: bfloat16 [16384, 256], P(('bin', 'wave')), may hold values from -6 to 6
- density: bfloat16 [16384], P(('bin', 'wave')), may hold values from 0.5 to 1.5
- temp_bins: int32 [16384, 1], P(('bin', 'wave')), may hold values from 0 to 15; in each aligned block of 512 rows (0 to 511, 512 to 1023, ...) at most 64 rows name the same one
- ray_index: int32 [16384], P(('bin', 'wave')), may hold values from 0 to 255
- rate_tables: bfloat16 [16, 256, 256], P('bin'), as said below
- line_table: bfloat16 [256, 8192], P(None, 'wave'), may hold values from -0.046875 to 0.046875
Outputs:
- intensity: float32 [256, 8192], P('bin', 'wave')
Inputs may be any that keep to these rules, and one draw needn't show every extreme that they name: `temp_bins`: among the 512 cells of one device (aligned blocks of 512 rows) no bin is named more than 64 times; some bin is named exactly 64 times. `rate_tables`: each bin's matrix has a diagonal between 0.25 and 0.55 and independent off-diagonal entries.
All inputs are finite; a program needn't handle non-finite values.
Results may differ from a plain program's by a relative error of at most 0.005.
Values may be sent and summed in bfloat16 or wider, within the bound.
No kernel may reach another device: no remote copies, remote signals or barrier semaphores. Data moves between devices by JAX's collectives and lax.ppermute only.
A program may use at most 64 MiB of HBM per device.

v0:
```python
import jax
import jax.numpy as jnp
from jax import lax
from jax.sharding import PartitionSpec as P

RAY_DEV = 16


def iterate_levels(src_rows, den_rows, table):
    den_col = den_rows[:, None].astype(jnp.float32)
    src_wide = src_rows.astype(jnp.float32)
    first = (
        den_col * jnp.dot(src_rows, table, preferred_element_type=jnp.float32) + src_wide
    ).astype(jnp.bfloat16)
    second = (
        den_col * jnp.dot(first, table, preferred_element_type=jnp.float32) + src_wide
    ).astype(jnp.bfloat16)
    return second


def line_product(whole_rays, line_table):
    return jnp.dot(
        whole_rays,
        line_table.astype(jnp.float32),
        precision=lax.Precision.HIGHEST,
        preferred_element_type=jnp.float32,
    )


def per_device(sources, density, temp_bins, ray_index, rate_tables, line_table):
    cell_count, level_count = sources.shape
    bin_total = lax.axis_size("bin")
    capacity = max(2, 2 * cell_count // bin_total)
    ray_total = RAY_DEV * bin_total
    bin_of = temp_bins[:, 0]
    member = (bin_of[:, None] == jnp.arange(bin_total, dtype=jnp.int32)[None, :]).astype(jnp.int32)
    position = jnp.sum(jnp.cumsum(member, axis=0) * member, axis=1) - 1
    slot_index = bin_of * capacity + position
    outgoing = (
        jnp.zeros((bin_total * capacity, level_count), sources.dtype).at[slot_index].set(sources)
    )
    outgoing = outgoing.reshape(bin_total, capacity, level_count)
    out_density = jnp.zeros((bin_total * capacity,), density.dtype).at[slot_index].set(density)
    out_density = out_density.reshape(bin_total, capacity)
    table = rate_tables[0]
    out_rays = jnp.zeros((bin_total * capacity,), jnp.int32).at[slot_index].set(ray_index)
    held_rays = lax.all_to_all(
        out_rays.reshape(bin_total, capacity), "bin", split_axis=0, concat_axis=0, tiled=True
    )
    src_rows = lax.all_to_all(outgoing, "bin", split_axis=0, concat_axis=0, tiled=True)
    den_rows = lax.all_to_all(out_density, "bin", split_axis=0, concat_axis=0, tiled=True)
    shape_rows = src_rows.shape
    populated = iterate_levels(src_rows.reshape(-1, level_count), den_rows.reshape(-1), table)
    held_pops = populated.reshape(shape_rows)
    held_sums = jax.ops.segment_sum(
        held_pops.reshape(-1, level_count).astype(jnp.float32),
        held_rays.reshape(-1),
        num_segments=ray_total,
    )
    owner_rays = lax.psum_scatter(held_sums, "bin", scatter_dimension=0, tiled=True)
    owner_whole = lax.psum(owner_rays, "wave")
    return line_product(owner_whole, line_table)


def solution(mesh):
    in_specs = (
        P(("bin", "wave"), None),
        P(("bin", "wave")),
        P(("bin", "wave"), None),
        P(("bin", "wave")),
        P("bin", None, None),
        P(None, "wave"),
    )
    out_specs = P("bin", "wave")
    return jax.shard_map(
        per_device, mesh=mesh, in_specs=in_specs, out_specs=out_specs, check_vma=False
    )
```

profile of v0, /device:TPU:0, one launch (start us, length us, event | category | flops | bytes accessed | tf_op | source)
XLA Modules:
  0.0 155.4 jit_solution(8804827635843308499)
XLA Ops:
  6.5 0.0 copy-start
  6.5 0.8 fusion.14
  7.4 1.1 reduce-window.6
  8.5 0.2 slice_reduce_fusion
  8.8 0.8 fusion.13
  9.6 0.7 compare_select_fusion
  10.2 3.9 %scatter_custom_fusion.1 = bf16[1024]{0:T(1024)(128)(2,1)S(1)} fusion(s32[512]{0:T(512)S(1)} %bitcast.32, bf16[512]{0:T(512)(128)(2,1)} %param.7, bf16[]{:T(256)} %constant.5.clone.1), kind=kCustom, calls=%fused_computation.29 | custom fusion | bytes 2560 | tf_op jit(solution)/shard_map/scatter | solution.py:43
  14.2 0.7 all_to_all.20
  14.8 8.3 %all-to-all-start.1 = ((bf16[16,1,64]{2,1,0:T(2,128)(2,1)}), bf16[16,1,64]{2,1,0:T(2,128)(2,1)S(1)}, u32[]{:S(2)}, u32[]{:S(2)}) async-start(bf16[16,1,64]{2,1,0:T(2,128)(2,1)} %all_to_all.20), calls=%async_computation.1 | async-start | bytes 16384 | tf_op jit(solution)/shard_map/all_to_all | solution.py:51
  23.2 2.6 %scatter_custom_fusion = s32[1024]{0:T(1024)S(1)} fusion(s32[512]{0:T(512)S(1)} %bitcast.33, s32[512]{0:T(512)} %param.9, s32[]{:T(128)} %constant.7.clone.1), kind=kCustom, calls=%fused_computation.27 | custom fusion | bytes 4608 | tf_op jit(solution)/shard_map/scatter | solution.py:46
  25.8 0.7 all_to_all.15
  26.5 4.0 %all-to-all-done.1 = bf16[16,1,64]{2,1,0:T(2,128)(2,1)S(1)} async-done(((bf16[16,1,64]{2,1,0:T(2,128)(2,1)}), bf16[16,1,64]{2,1,0:T(2,128)(2,1)S(1)}, u32[]{:S(2)}, u32[]{:S(2)}) %all-to-all-start.1) | async-done | bytes 2080 | tf_op jit(solution)/shard_map/all_to_all | solution.py:51
  30.4 3.5 %all-to-all-start = ((s32[16,1,64]{2,1,0:T(1,128)}), s32[16,1,64]{2,1,0:T(1,128)S(1)}, u32[]{:S(2)}, u32[]{:S(2)}) async-start(s32[16,1,64]{2,1,0:T(1,128)} %all_to_all.15), calls=%async_computation | async-start | bytes 16384 | tf_op jit(solution)/shard_map/all_to_all | solution.py:47
  33.9 3.5 %scatter_custom_fusion.2 = bf16[1024,256]{1,0:T(8,128)(2,1)} fusion(s32[512]{0:T(512)S(1)} %bitcast.34, bf16[512,256]{1,0:T(8,128)(2,1)} %param.6, bf16[]{:T(256)} %constant.5.clone.1), kind=kCustom, calls=%fused_computation.12 | custom fusion | bytes 524800 | tf_op jit(solution)/shard_map/scatter | solution.py:40
  37.4 3.6 %all-to-all-done = s32[16,1,64]{2,1,0:T(1,128)S(1)} async-done(((s32[16,1,64]{2,1,0:T(1,128)}), s32[16,1,64]{2,1,0:T(1,128)S(1)}, u32[]{:S(2)}, u32[]{:S(2)}) %all-to-all-start) | async-done | bytes 4128 | tf_op jit(solution)/shard_map/all_to_all | solution.py:47
  41.1 3.6 %all-to-all-start.2 = ((bf16[16,64,256]{2,1,0:T(8,128)(2,1)}), bf16[16,64,256]{2,1,0:T(8,128)(2,1)S(1)}, u32[]{:S(2)}, u32[]{:S(2)}) async-start(bf16[16,64,256]{2,1,0:T(8,128)(2,1)} %bitcast.5), calls=%async_computation.2 | async-start | bytes 1048576 | tf_op jit(solution)/shard_map/all_to_all | solution.py:50
  44.7 0.0 reduce-scatter.2.cloned.1.call-start
  44.7 0.1 reshape.53
  44.8 0.5 broadcast.52
  45.3 0.7 reduce.9
  46.0 0.1 reshape.80
  46.1 11.8 %all-to-all-done.2 = bf16[16,64,256]{2,1,0:T(8,128)(2,1)S(1)} async-done(((bf16[16,64,256]{2,1,0:T(8,128)(2,1)}), bf16[16,64,256]{2,1,0:T(8,128)(2,1)S(1)}, u32[]{:S(2)}, u32[]{:S(2)}) %all-to-all-start.2) | async-done | bytes 524320 | tf_op jit(solution)/shard_map/all_to_all | solution.py:50
  57.9 2.5 %fusion.4 = f32[1024,256]{1,0:T(8,128)} fusion(bf16[1024,256]{1,0:T(8,128)(2,1)S(1)} %bitcast.28, f32[1024]{0:T(1024)S(1)} %reshape.53, bf16[1,256,256]{2,1,0:T(8,128)(2,1)} %param.10), kind=kOutput, calls=%fused_computation.10 | convolution fusion | flops 270794752 | bytes 1708032 | tf_op jit(solution)/shard_map/dot_general | solution.py:16
  60.4 7.6 %scatter_custom_fusion.3 = f32[256,256]{1,0:T(8,128)} fusion(s32[1024]{0:T(1024)S(1)} %reshape.80, f32[1024,256]{1,0:T(8,128)} %fusion.4, f32[]{:T(128)} %constant.6.clone.1), kind=kCustom, calls=%fused_computation.15 | custom fusion | flops 262144 | bytes 262656 | tf_op jit(solution)/shard_map/scatter-add | solution.py:55
  68.0 0.0 reduce-scatter.2.cloned.1.call-update
  68.0 74.9 %reduce-scatter.2.cloned.1.call-done = f32[16,256]{1,0:T(8,128)} async-done(((f32[256,256]{1,0:T(8,128)}), f32[16,256]{1,0:T(8,128)}) %reduce-scatter.2.cloned.1.call-update) | async-done | bytes 16400 | tf_op jit(solution)/shard_map/reduce_scatter | solution.py:60
  142.9 4.0 %psum.7 = f32[16,256]{1,0:T(8,128)S(1)} all-reduce(f32[16,256]{1,0:T(8,128)} %reduce-scatter.2.cloned.1.call-done), channel_id=1, replica_groups=mesh['bin'=16,'wave'=2] {'wave'}, use_global_device_ids=true, to_apply=%region_8.9 | all-reduce | flops 4096 | bytes 32768 | tf_op jit(solution)/shard_map/psum | solution.py:61
  146.9 0.0 copy-done
  146.9 1.6 %fusion.19 = f32[16,4096]{1,0:T(8,128)} fusion(f32[16,256]{1,0:T(8,128)S(1)} %psum.7, bf16[256,4096]{1,0:T(8,128)(2,1)S(1)} %copy-done), kind=kOutput, calls=%fused_computation.32 | convolution fusion | flops 201326592 | bytes 2375680 | tf_op jit(solution)/shard_map/dot_general | solution.py:22
  (4 shorter events, 0.1 us)
Async XLA Ops:
  6.5 140.4 %copy-start = (bf16[256,4096]{1,0:T(8,128)(2,1)S(1)}, bf16[256,4096]{1,0:T(8,128)(2,1)}, u32[]{:S(2)}) copy-start(bf16[256,4096]{1,0:T(8,128)(2,1)} %param.11) | copy-start | bytes 6291460
  14.8 15.6 %all-to-all-start.1 = ((bf16[16,1,64]{2,1,0:T(2,128)(2,1)}), bf16[16,1,64]{2,1,0:T(2,128)(2,1)S(1)}, u32[]{:S(2)}, u32[]{:S(2)}) async-start(bf16[16,1,64]{2,1,0:T(2,128)(2,1)} %all_to_all.20), calls=%async_computation.1 | async-start | bytes 16384 | tf_op jit(solution)/shard_map/all_to_all | solution.py:51
  30.4 10.6 %all-to-all-start = ((s32[16,1,64]{2,1,0:T(1,128)}), s32[16,1,64]{2,1,0:T(1,128)S(1)}, u32[]{:S(2)}, u32[]{:S(2)}) async-start(s32[16,1,64]{2,1,0:T(1,128)} %all_to_all.15), calls=%async_computation | async-start | bytes 16384 | tf_op jit(solution)/shard_map/all_to_all | solution.py:47
  41.1 16.8 %all-to-all-start.2 = ((bf16[16,64,256]{2,1,0:T(8,128)(2,1)}), bf16[16,64,256]{2,1,0:T(8,128)(2,1)S(1)}, u32[]{:S(2)}, u32[]{:S(2)}) async-start(bf16[16,64,256]{2,1,0:T(8,128)(2,1)} %bitcast.5), calls=%async_computation.2 | async-start | bytes 1048576 | tf_op jit(solution)/shard_map/all_to_all | solution.py:50
  44.7 98.3 %reduce-scatter.2.cloned.1.call-start = ((), (), s32[]{:S(2)}) async-start(), calls=%async_computation.4 | async-start | bytes 278528 | tf_op jit(solution)/shard_map/reduce_scatter | solution.py:60
Sparse Core Ops, SparseCore 0:
  68.1 74.7 reduce-scatter.1
where the time goes:
time: 156 us; the launch traced here: 155 us
  waiting for transfers between devices  94.4 us (61%)
  starting transfers between devices  15.4 us (10%)
  between operations  13.5 us (9%)
  local copies, waits for them, and re-layouts  12.3 us (8%)
  other arithmetic  11.7 us (8%)
  matrix products  4.16 us (3%)
  blocking collectives  3.99 us (3%)
    reduce_scatter x1, waiting for transfers between devices, per_device(): lax.psum_scatter(held_sums, 'bin', scatter_dimension=0, tiled=True)  74.9 us
    all_to_all x1, waiting for transfers between devices, per_device(): lax.all_to_all(outgoing, 'bin', split_axis=0, concat_axis=0, tiled=True)  11.8 us
    all_to_all x1, starting transfers between devices, per_device(): lax.all_to_all(out_density, 'bin', split_axis=0, concat_axis=0, tiled=True)  8.31 us
    scatter-add x1, other arithmetic, per_device(): jax.ops.segment_sum(held_pops.reshape(-1, level_count).astype(jnp.float32...  7.56 us
    psum x1, blocking collectives, per_device(): owner_whole = lax.psum(owner_rays, 'wave')  3.99 us
    all_to_all x1, waiting for transfers between devices, per_device(): lax.all_to_all(out_density, 'bin', split_axis=0, concat_axis=0, tiled=True)  3.98 us
    scatter x1, local copies, waits for them, and re-layouts, per_device(): jnp.zeros((bin_total * capacity,), density.dtype).at[slot_index]  3.92 us
    all_to_all x1, waiting for transfers between devices, per_device(): lax.all_to_all(out_rays.reshape(bin_total, capacity), 'bin', split_axis=0...  3.64 us
  transfers between devices with their start and end apart: 4, of which 4 were waited for; matrix products, arithmetic and copies ran while one was open for 5% of the time, Pallas kernels for 0%

commit v1 on v0

v1 whole, which is shorter than its diff:
```python
import functools

import jax
import jax.numpy as jnp
from jax import lax
from jax.experimental import pallas as pl
from jax.experimental.pallas import tpu as pltpu
from jax.sharding import PartitionSpec as P

META_ROWS = 16
RAY_BASE = 32
VMEM_LIMIT = 32 * 1024 * 1024
F32 = jnp.float32
BF16 = jnp.bfloat16


def nt_dot(a, b):
    return lax.dot_general(a, b, (((1,), (1,)), ((), ())), preferred_element_type=F32)


def pack_kernel(bin_total, capacity, half_ref, src_ref, den_ref, bin_ref, ray_ref, out_ref):
    cells, levels = src_ref.shape
    half = bin_total // 2
    block = 2 * capacity
    bins = bin_ref[...]
    hot = (lax.broadcasted_iota(jnp.int32, (bin_total, cells), 0) == bins).astype(F32)
    earlier = (
        lax.broadcasted_iota(jnp.int32, (cells, cells), 0)
        < lax.broadcasted_iota(jnp.int32, (cells, cells), 1)
    ).astype(F32).astype(BF16)
    before = jnp.dot(hot.astype(BF16), earlier, preferred_element_type=F32)
    position = jnp.sum(hot * before, axis=0, keepdims=True).astype(jnp.int32)
    upper = (bins >= half).astype(jnp.int32)
    other = jnp.where(upper == half_ref[0], 0, 1)
    slot = (bins - upper * half) * block + other * capacity + position
    rays = ray_ref[...]
    ray_high = rays // RAY_BASE
    ray_low = rays - ray_high * RAY_BASE
    meta = jnp.concatenate(
        [
            den_ref[...].astype(F32),
            ray_high.astype(F32),
            ray_low.astype(F32),
            jnp.zeros((META_ROWS - 3, cells), F32),
        ],
        axis=0,
    ).astype(BF16)
    place = (
        lax.broadcasted_iota(jnp.int32, (half * block, cells), 0) == slot
    ).astype(F32).astype(BF16)
    rows = jnp.dot(place, src_ref[...], preferred_element_type=F32).astype(BF16)
    moved = nt_dot(meta, place).astype(BF16)
    out_ref[:, :block, :] = rows.reshape(half, block, levels)
    out_ref[:, block:, :] = jnp.zeros((half, META_ROWS, levels), BF16)
    for target in range(half):
        out_ref[target, block:, :block] = moved[:, target * block : (target + 1) * block]


def level_kernel(capacity, rays, got_ref, own_ref, other_ref, out_ref):
    sources, _, levels = got_ref.shape
    block = 2 * capacity
    total = jnp.zeros((rays, levels), F32)
    meta = [got_ref[s, block:, :block].astype(F32) for s in range(sources)]
    columns = [jnp.transpose(m[:8]) for m in meta]
    for part, table_ref in ((0, own_ref), (1, other_ref)):
        low, high = part * capacity, (part + 1) * capacity
        src = got_ref[:, low:high, :].reshape(sources * capacity, levels)
        den = jnp.concatenate([c[low:high, 0:1] for c in columns], axis=0)
        ray = jnp.concatenate(
            [m[1:2, low:high] * RAY_BASE + m[2:3, low:high] for m in meta], axis=1
        ).astype(jnp.int32)
        wide = src.astype(F32)
        table = table_ref[...]
        first = (den * jnp.dot(src, table, preferred_element_type=F32) + wide).astype(BF16)
        pops = (den * jnp.dot(first, table, preferred_element_type=F32) + wide).astype(BF16)
        pick = (
            lax.broadcasted_iota(jnp.int32, (rays, sources * capacity), 0) == ray
        ).astype(F32).astype(BF16)
        total = total + jnp.dot(pick, pops, preferred_element_type=F32)
    out_ref[...] = total.astype(BF16)


def line_kernel(mine_ref, theirs_ref, line_ref, out_ref):
    sums = mine_ref[...] + theirs_ref[...]
    rows = sums.shape[0]
    high = sums.astype(BF16)
    low = (sums - high.astype(F32)).astype(BF16)
    both = jnp.concatenate([high, low], axis=0)
    got = jnp.dot(both, line_ref[...], preferred_element_type=F32)
    out_ref[...] = got[:rows] + got[rows:]


def whole(shape):
    return pl.BlockSpec(memory_space=pltpu.VMEM)


def per_device(ray_total, sources, density, temp_bins, ray_index, rate_tables, line_table):
    cells, levels = sources.shape
    bin_total = lax.axis_size("bin")
    wave_total = lax.axis_size("wave")
    half = bin_total // 2
    capacity = max(2, 2 * cells // bin_total)
    block = 2 * capacity
    params = pltpu.CompilerParams(vmem_limit_bytes=VMEM_LIMIT)
    vmem = pl.BlockSpec(memory_space=pltpu.VMEM)
    smem = pl.BlockSpec(memory_space=pltpu.SMEM)

    own = rate_tables[0]
    other = lax.ppermute(own, "bin", [(i, (i + half) % bin_total) for i in range(bin_total)])

    my_half = (lax.axis_index("bin") // half).astype(jnp.int32).reshape(1)
    outgoing = pl.pallas_call(
        functools.partial(pack_kernel, bin_total, capacity),
        out_shape=jax.ShapeDtypeStruct((half, block + META_ROWS, levels), BF16),
        in_specs=[smem, vmem, vmem, vmem, vmem],
        out_specs=vmem,
        compiler_params=params,
    )(
        my_half,
        sources,
        density.reshape(1, cells),
        temp_bins.reshape(1, cells),
        ray_index.reshape(1, cells),
    )
    groups = [list(range(half)), list(range(half, bin_total))]
    got = lax.all_to_all(
        outgoing, "bin", split_axis=0, concat_axis=0, tiled=True, axis_index_groups=groups
    )
    partial_sums = pl.pallas_call(
        functools.partial(level_kernel, capacity, ray_total),
        out_shape=jax.ShapeDtypeStruct((ray_total, levels), BF16),
        in_specs=[vmem, vmem, vmem],
        out_specs=vmem,
        compiler_params=params,
    )(got, own, other)
    ray_rows = ray_total // bin_total
    held = lax.all_to_all(
        partial_sums.reshape(bin_total, ray_rows, levels), "bin", split_axis=0, concat_axis=0, tiled=True
    )
    sums = jnp.sum(held.astype(F32), axis=0)
    step = 1
    theirs = jnp.zeros_like(sums)
    while step < wave_total:
        sums = sums + theirs
        theirs = lax.ppermute(sums, "wave", [(i, i ^ step) for i in range(wave_total)])
        step *= 2
    return pl.pallas_call(
        line_kernel,
        out_shape=jax.ShapeDtypeStruct((ray_rows, line_table.shape[1]), F32),
        in_specs=[vmem, vmem, vmem],
        out_specs=vmem,
        compiler_params=params,
    )(sums, theirs, line_table)


def solution(mesh):
    in_specs = (
        P(("bin", "wave"), None),
        P(("bin", "wave")),
        P(("bin", "wave"), None),
        P(("bin", "wave")),
        P("bin", None, None),
        P(None, "wave"),
    )
    ray_total = RAY_DEV * mesh.shape["bin"]
    return jax.shard_map(
        functools.partial(per_device, ray_total),
        mesh=mesh,
        in_specs=in_specs,
        out_specs=P("bin", "wave"),
        check_vma=False,
    )


RAY_DEV = 16
```

time: 156 us -> 40.7 us (0.26)
  waiting for transfers between devices: 94.4 us -> 11.1 us
  between operations: 13.5 us -> 0.03 us
  other arithmetic: 11.7 us -> 0.02 us
  blocking collectives: 3.99 us -> 12.4 us
  local copies, waits for them, and re-layouts: 12.3 us -> 4.05 us
  starting transfers between devices: 15.4 us -> 8.84 us
  matrix products: 4.16 us -> 0 us
  Pallas kernels: 0 us -> 3.95 us
    reduce_scatter x1 -> x0, waiting for transfers between devices: 74.9 us -> none  [per_device(): lax.psum_scatter(held_sums, 'bin', scatter_dimension=0, tiled=True)]
    all_to_all x3 -> x1, waiting for transfers between devices: 19.4 us -> 3.1 us  [per_device(): lax.all_to_all(outgoing, 'bin', split_axis=0, concat_axis=0, tiled=True,...]
    all_to_all x0 -> x1, blocking collectives: none -> 12.4 us  [per_device(): lax.all_to_all(partial_sums.reshape(bin_total, ray_rows, levels), 'bin',...]
    scatter x3 -> x0, local copies, waits for them, and re-layouts: 10.1 us -> none  [the longest x1 3.92 us: per_device(): jnp.zeros((bin_total * capacity,), density.dtype).at[slot_index]]
    all_to_all x3 -> x1, starting transfers between devices: 15.4 us -> 6.18 us  [per_device(): lax.all_to_all(outgoing, 'bin', split_axis=0, concat_axis=0, tiled=True,...]
    ppermute x0 -> x2, waiting for transfers between devices: none -> 7.97 us  [the longest x1 6.8 us: per_device(): lax.ppermute(own, 'bin', [(i, (i + half) % bin_total) for i in range(bin_...]
    scatter-add x1 -> x0, other arithmetic: 7.56 us -> none  [per_device(): jax.ops.segment_sum(held_pops.reshape(-1, level_count).astype(jnp.float32...]
    dot_general x2 -> x0, matrix products: 4.16 us -> none  [the longest x1 2.52 us: iterate_levels(): jnp.dot(first, table, preferred_element_type=jnp.float32)]
  transfers between devices with their start and end apart: 4 -> 3, of which waited for: 4 -> 3; matrix products, arithmetic and copies ran while one was open for 5% -> 0% of each run, Pallas kernels for 0% -> 0%
where the time goes in v1:
time: 40.7 us; the launch traced here: 40.4 us
  blocking collectives  12.4 us (30%)
  waiting for transfers between devices  11.1 us (27%)
  starting transfers between devices  8.84 us (22%)
  local copies, waits for them, and re-layouts  4.05 us (10%)
  Pallas kernels  3.95 us (10%)
    all_to_all x1, blocking collectives, per_device(): lax.all_to_all(partial_sums.reshape(bin_total, ray_rows, levels), 'bin',...  12.4 us
    ppermute x1, waiting for transfers between devices, per_device(): lax.ppermute(own, 'bin', [(i, (i + half) % bin_total) for i in range(bin_...  6.8 us
    all_to_all x1, starting transfers between devices, per_device(): lax.all_to_all(outgoing, 'bin', split_axis=0, concat_axis=0, tiled=True,...  6.18 us
    unnamed x10, local copies, waits for them, and re-layouts  3.22 us
    all_to_all x1, waiting for transfers between devices, per_device(): lax.all_to_all(outgoing, 'bin', split_axis=0, concat_axis=0, tiled=True,...  3.1 us
    ppermute x1, starting transfers between devices, per_device(): lax.ppermute(own, 'bin', [(i, (i + half) % bin_total) for i in range(bin_...  2.59 us
    pallas_call x1, Pallas kernels, per_device(): pl.pallas_call(functools.partial(pack_kernel, bin_total, capacity), out_s...  1.75 us
    ppermute x1, waiting for transfers between devices, per_device(): lax.ppermute(sums, 'wave', [(i, i ^ step) for i in range(wave_total)])  1.17 us
  transfers between devices with their start and end apart: 3, of which 3 were waited for; matrix products, arithmetic and copies ran while one was open for 0% of the time, Pallas kernels for 0%

profile of v1, /device:TPU:0, one launch (start us, length us, event | category | flops | bytes accessed | tf_op | source)
XLA Modules:
  0.0 40.4 jit_solution(9316494928072767772)
XLA Ops:
  0.0 0.0 copy-start
  0.0 0.8 %reshape.16.den_ref = bf16[1,512]{1,0:T(2,128)(2,1)S(1)} reshape(bf16[512]{0:T(512)(128)(2,1)} %param.7) | data formatting | bytes 2048 | tf_op jit(solution)/shard_map/reshape | solution.py:121
  0.8 0.0 copy-start.1
  0.8 0.9 %copy-done.1 = bf16[512,256]{1,0:T(8,128)(2,1)S(1)} copy-done((bf16[512,256]{1,0:T(8,128)(2,1)S(1)}, bf16[512,256]{1,0:T(8,128)(2,1)}, u32[]{:S(2)}) %copy-start.1) | copy-done | bytes 262168
  1.8 0.0 copy-start.3
  1.8 0.7 %copy-done.3 = s32[512,1]{0,1:T(1,128)S(1)} copy-done((s32[512,1]{0,1:T(1,128)S(1)}, s32[512,1]{0,1:T(1,128)}, u32[]{:S(2)}) %copy-start.3) | copy-done | bytes 2072
  2.5 0.0 copy-start.4
  2.5 0.7 %copy-done.4 = s32[512]{0:T(512)S(1)} copy-done((s32[512]{0:T(512)S(1)}, s32[512]{0:T(512)}, u32[]{:S(2)}) %copy-start.4) | copy-done | bytes 2072
  3.1 1.8 %shard_map.64 = bf16[8,144,256]{2,1,0:T(8,128)(2,1)} custom-call(s32[1]{0:T(128)} %bitcast.half_ref, bf16[512,256]{1,0:T(8,128)(2,1)S(1)} %copy-done.1, bf16[1,512]{1,0:T(2,128)(2,1)S(1)} %reshape.16.den_ref, s32[1,512]{1,0:T(1,128)S(1)} %bitcast.8, s32[1,512]{1,0:T(1,128)S(1)} %bitcast.9), custom_call_target="tpu_custom_call" | custom-call | tf_op jit(solution)/shard_map/pallas_call | solution.py:112
  4.9 6.2 %all-to-all-start = ((bf16[8,144,256]{2,1,0:T(8,128)(2,1)}), bf16[8,144,256]{2,1,0:T(8,128)(2,1)S(1)}, u32[]{:S(2)}, u32[]{:S(2)}) async-start(bf16[8,144,256]{2,1,0:T(8,128)(2,1)} %shard_map.64), calls=%async_computation | async-start | bytes 1179648 | tf_op jit(solution)/shard_map/all_to_all | solution.py:126
  11.1 2.6 %collective-permute-start = (bf16[256,256]{1,0:T(8,128)(2,1)}, bf16[256,256]{1,0:T(8,128)(2,1)S(1)}, u32[]{:S(2)}, u32[]{:S(2)}) collective-permute-start(bf16[256,256]{1,0:T(8,128)(2,1)} %bitcast.6), channel_id=1, source_target_pairs={{0,16},{2,18},{4,20},{6,22},{8,24},{10,26},{12,28},{14,30},{16,0},... | collective-permute-start | bytes 393224 | tf_op jit(solution)/shard_map/ppermute | solution.py:109
  13.7 6.8 %collective-permute-done.other_ref = bf16[256,256]{1,0:T(8,128)(2,1)S(1)} collective-permute-done((bf16[256,256]{1,0:T(8,128)(2,1)}, bf16[256,256]{1,0:T(8,128)(2,1)S(1)}, u32[]{:S(2)}, u32[]{:S(2)}) %collective-permute-start) | collective-permute-done | bytes 131104 | tf_op jit(solution)/shard_map/ppermute | solution.py:109
  20.5 3.1 %all-to-all-done.got_ref = bf16[8,144,256]{2,1,0:T(8,128)(2,1)S(1)} async-done(((bf16[8,144,256]{2,1,0:T(8,128)(2,1)}), bf16[8,144,256]{2,1,0:T(8,128)(2,1)S(1)}, u32[]{:S(2)}, u32[]{:S(2)}) %all-to-all-start) | async-done | bytes 589856 | tf_op jit(solution)/shard_map/all_to_all | solution.py:126
  23.6 0.0 copy-start.2
  23.6 0.9 %copy-done.2 = bf16[1,256,256]{2,1,0:T(8,128)(2,1)S(1)} copy-done((bf16[1,256,256]{2,1,0:T(8,128)(2,1)S(1)}, bf16[1,256,256]{2,1,0:T(8,128)(2,1)}, u32[]{:S(2)}) %copy-start.2) | copy-done | bytes 131096
  24.5 1.0 %shard_map.65 = bf16[256,256]{1,0:T(8,128)(2,1)S(1)} custom-call(bf16[8,144,256]{2,1,0:T(8,128)(2,1)S(1)} %all-to-all-done.got_ref, bf16[256,256]{1,0:T(8,128)(2,1)S(1)} %bitcast.7, bf16[256,256]{1,0:T(8,128)(2,1)S(1)} %collective-permute-done.other_ref), custom_call_target="tpu_custom_call" | custom-call | tf_op jit(solution)/shard_map/pallas_call | solution.py:129
  25.5 12.4 %all_to_all.10 = bf16[16,16,256]{2,1,0:T(8,128)(2,1)S(1)} all-to-all(bf16[16,16,256]{2,1,0:T(8,128)(2,1)S(1)} %bitcast.5), channel_id=1, replica_groups=mesh['bin'=16,'wave'=2] {'bin'}, dimensions={0} | all-to-all | bytes 262144 | tf_op jit(solution)/shard_map/all_to_all | solution.py:137
  38.0 0.1 collective-permute-start.1
  38.0 1.2 %collective-permute-done.1.theirs_ref = f32[16,256]{1,0:T(8,128)S(1)} collective-permute-done((f32[16,256]{1,0:T(8,128)S(1)}, f32[16,256]{1,0:T(8,128)S(1)}, u32[]{:S(2)}, u32[]{:S(2)}) %collective-permute-start.1) | collective-permute-done | bytes 16416 | tf_op jit(solution)/shard_map/ppermute | solution.py:145
  39.2 0.0 copy-done
  39.2 1.2 %shard_map.66 = f32[16,4096]{1,0:T(8,128)} custom-call(f32[16,256]{1,0:T(8,128)S(1)} %convert_reduce_fusion.mine_ref, f32[16,256]{1,0:T(8,128)S(1)} %collective-permute-done.1.theirs_ref, bf16[256,4096]{1,0:T(8,128)(2,1)S(1)} %copy-done), custom_call_target="tpu_custom_call" | custom-call | tf_op jit(solution)/shard_map/pallas_call | solution.py:147
  (1 shorter events, 0.0 us)
Async XLA Ops:
  0.0 39.2 %copy-start = (bf16[256,4096]{1,0:T(8,128)(2,1)S(1)}, bf16[256,4096]{1,0:T(8,128)(2,1)}, u32[]{:S(2)}) copy-start(bf16[256,4096]{1,0:T(8,128)(2,1)} %line_ref.1) | copy-start | bytes 6291460
  0.8 0.9 %copy-start.1 = (bf16[512,256]{1,0:T(8,128)(2,1)S(1)}, bf16[512,256]{1,0:T(8,128)(2,1)}, u32[]{:S(2)}) copy-start(bf16[512,256]{1,0:T(8,128)(2,1)} %src_ref.1) | copy-start | bytes 786436
  1.8 0.7 %copy-start.3 = (s32[512,1]{0,1:T(1,128)S(1)}, s32[512,1]{0,1:T(1,128)}, u32[]{:S(2)}) copy-start(s32[512,1]{0,1:T(1,128)} %param.8) | copy-start | bytes 6148
  2.5 0.7 %copy-start.4 = (s32[512]{0:T(512)S(1)}, s32[512]{0:T(512)}, u32[]{:S(2)}) copy-start(s32[512]{0:T(512)} %param.9) | copy-start | bytes 6148
  4.9 18.7 %all-to-all-start = ((bf16[8,144,256]{2,1,0:T(8,128)(2,1)}), bf16[8,144,256]{2,1,0:T(8,128)(2,1)S(1)}, u32[]{:S(2)}, u32[]{:S(2)}) async-start(bf16[8,144,256]{2,1,0:T(8,128)(2,1)} %shard_map.64), calls=%async_computation | async-start | bytes 1179648 | tf_op jit(solution)/shard_map/all_to_all | solution.py:126
  11.1 9.4 %collective-permute-start = (bf16[256,256]{1,0:T(8,128)(2,1)}, bf16[256,256]{1,0:T(8,128)(2,1)S(1)}, u32[]{:S(2)}, u32[]{:S(2)}) collective-permute-start(bf16[256,256]{1,0:T(8,128)(2,1)} %bitcast.6), channel_id=1, source_target_pairs={{0,16},{2,18},{4,20},{6,22},{8,24},{10,26},{12,28},{14,30},{16,0},... | collective-permute-start | bytes 393224 | tf_op jit(solution)/shard_map/ppermute | solution.py:109
  23.6 0.9 %copy-start.2 = (bf16[1,256,256]{2,1,0:T(8,128)(2,1)S(1)}, bf16[1,256,256]{2,1,0:T(8,128)(2,1)}, u32[]{:S(2)}) copy-start(bf16[1,256,256]{2,1,0:T(8,128)(2,1)} %param.10) | copy-start | bytes 393220
  38.0 1.2 %collective-permute-start.1 = (f32[16,256]{1,0:T(8,128)S(1)}, f32[16,256]{1,0:T(8,128)S(1)}, u32[]{:S(2)}, u32[]{:S(2)}) collective-permute-start(f32[16,256]{1,0:T(8,128)S(1)} %convert_reduce_fusion.mine_ref), channel_id=1, source_target_pairs={{0,1},{1,0},{2,3},{3,2},{4,5},{5,4},{6,7},{7,6},{8,9},{9,8},{10,11... | collective-permute-start | bytes 49160 | tf_op jit(solution)/shard_map/ppermute | solution.py:145

commit v2 on v1

v2 whole, which is shorter than its diff:
```python
import functools

import jax
import jax.numpy as jnp
from jax import lax
from jax.experimental import pallas as pl
from jax.experimental.pallas import tpu as pltpu
from jax.sharding import PartitionSpec as P

RAY_DEV = 16
META_ROWS = 16
RAY_BASE = 32
LANES = 128
VMEM_LIMIT = 32 * 1024 * 1024
PACK_VMEM = 60 * 1024 * 1024
F32 = jnp.float32
BF16 = jnp.bfloat16
I32 = jnp.int32


def nt_dot(a, b):
    return lax.dot_general(a, b, (((1,), (1,)), ((), ())), preferred_element_type=F32)


def iota(shape, dim):
    return lax.broadcasted_iota(I32, shape, dim)


def pack_kernel(bin_total, capacity, me_ref, src_hbm, den_hbm, bin_hbm, ray_hbm, *rest):
    half = bin_total // 2
    outs = rest[:half]
    src_ref, den_ref, bin_ref, ray_ref, held, in_sems, out_sems = rest[half:]
    copies = [
        pltpu.make_async_copy(a, b, in_sems.at[i])
        for i, (a, b) in enumerate(
            ((bin_hbm, bin_ref), (ray_hbm, ray_ref), (den_hbm, den_ref), (src_hbm, src_ref))
        )
    ]
    for copy in copies:
        copy.start()
    cells, levels = src_ref.shape
    block = 2 * capacity
    earlier = (iota((cells, cells), 0) < iota((cells, cells), 1)).astype(F32).astype(BF16)
    me = me_ref[0]
    held[:, block:, :] = jnp.zeros((half, META_ROWS, levels), BF16)
    for copy in copies[:3]:
        copy.wait()
    bins = bin_ref[...]
    hot = (iota((bin_total, cells), 0) == bins).astype(F32)
    before = jnp.dot(hot.astype(BF16), earlier, preferred_element_type=F32)
    position = jnp.sum(hot * before, axis=0, keepdims=True).astype(I32)
    relative = bins ^ me
    upper = (relative >= half).astype(I32)
    slot = (relative - upper * half) * block + upper * capacity + position
    rays = ray_ref[...]
    ray_high = rays // RAY_BASE
    ray_low = rays - ray_high * RAY_BASE
    den = den_ref[...].astype(F32)
    den_row = jnp.concatenate([den[i : i + 1] for i in range(den.shape[0])], axis=1)
    meta = jnp.concatenate(
        [den_row, ray_high.astype(F32), ray_low.astype(F32), jnp.zeros((META_ROWS - 3, cells), F32)],
        axis=0,
    ).astype(BF16)
    place = (iota((half * block, cells), 0) == slot).astype(F32).astype(BF16)
    moved = nt_dot(meta, place).astype(BF16)
    copies[3].wait()
    src = src_ref[...]
    leaving = [
        pltpu.make_async_copy(held.at[t], outs[t], out_sems.at[t]) for t in range(half)
    ]
    for target in list(range(1, half)) + [0]:
        low, high = target * block, (target + 1) * block
        rows = jnp.dot(place[low:high], src, preferred_element_type=F32)
        held[target, :block, :] = rows.astype(BF16)
        held[target, block:, :block] = moved[:, low:high]
        leaving[target].start()
    for copy in leaving:
        copy.wait()


def level_kernel(capacity, low_total, high_total, ray_rows, me_ref, *refs):
    got = refs[: -(low_total + 2)]
    own_ref, other_ref = refs[len(got) : len(got) + 2]
    outs = refs[len(got) + 2 :]
    block = 2 * capacity
    rays = low_total * high_total * ray_rows
    me = me_ref[0]
    meta = [g[block:, :block].astype(F32) for g in got]
    columns = [jnp.transpose(m[:8]) for m in meta]
    total = jnp.zeros((rays, own_ref.shape[1]), F32)
    for part, table_ref in ((0, own_ref), (1, other_ref)):
        low, high = part * capacity, (part + 1) * capacity
        src = jnp.concatenate([g[low:high, :] for g in got], axis=0)
        den = jnp.concatenate([c[low:high, 0:1] for c in columns], axis=0)
        ray = jnp.concatenate(
            [m[1:2, low:high] * RAY_BASE + m[2:3, low:high] for m in meta], axis=1
        ).astype(I32)
        owner = ray // ray_rows
        relative = owner ^ me
        row = (
            (relative % low_total) * (high_total * ray_rows)
            + (relative // low_total) * ray_rows
            + (ray - owner * ray_rows)
        )
        wide = src.astype(F32)
        table = table_ref[...]
        first = (den * jnp.dot(src, table, preferred_element_type=F32) + wide).astype(BF16)
        pops = (den * jnp.dot(first, table, preferred_element_type=F32) + wide).astype(BF16)
        pick = (iota((rays, src.shape[0]), 0) == row).astype(F32).astype(BF16)
        total = total + jnp.dot(pick, pops, preferred_element_type=F32)
    size = high_total * ray_rows
    for d in range(low_total):
        outs[d][...] = total[d * size : (d + 1) * size].astype(outs[d].dtype)


def line_kernel(mine_ref, theirs_ref, line_ref, out_ref):
    sums = mine_ref[...] + theirs_ref[...]
    rows = sums.shape[0]
    high = sums.astype(BF16)
    low = (sums - high.astype(F32)).astype(BF16)
    both = jnp.concatenate([high, low], axis=0)
    got = jnp.dot(both, line_ref[...], preferred_element_type=F32)
    out_ref[...] = got[:rows] + got[rows:]


def swap(value, axis, mask):
    total = lax.axis_size(axis)
    return lax.ppermute(value, axis, [(i, i ^ mask) for i in range(total)])


def per_device(sources, density, temp_bins, ray_index, rate_tables, line_table):
    cells, levels = sources.shape
    bin_total = lax.axis_size("bin")
    wave_total = lax.axis_size("wave")
    half = bin_total // 2
    capacity = max(2, 2 * cells // bin_total)
    block = 2 * capacity
    low_total = 1 << (bin_total.bit_length() // 2)
    high_total = bin_total // low_total
    params = pltpu.CompilerParams(vmem_limit_bytes=VMEM_LIMIT)
    vmem = pl.BlockSpec(memory_space=pltpu.VMEM)
    smem = pl.BlockSpec(memory_space=pltpu.SMEM)
    hbm = pl.BlockSpec(memory_space=pl.ANY)

    other = swap(rate_tables[0], "bin", half)
    me = lax.axis_index("bin").astype(I32).reshape(1)
    den_rows = cells // min(cells, LANES)
    outgoing = pl.pallas_call(
        functools.partial(pack_kernel, bin_total, capacity),
        out_shape=[jax.ShapeDtypeStruct((block + META_ROWS, levels), BF16)] * half,
        in_specs=[smem] + [hbm] * 4,
        out_specs=[hbm] * half,
        scratch_shapes=[
            pltpu.VMEM((cells, levels), BF16),
            pltpu.VMEM((den_rows, cells // den_rows), BF16),
            pltpu.VMEM((1, cells), I32),
            pltpu.VMEM((1, cells), I32),
            pltpu.VMEM((half, block + META_ROWS, levels), BF16),
            pltpu.SemaphoreType.DMA((4,)),
            pltpu.SemaphoreType.DMA((half,)),
        ],
        compiler_params=pltpu.CompilerParams(vmem_limit_bytes=PACK_VMEM),
    )(
        me,
        sources,
        density.reshape(den_rows, cells // den_rows),
        temp_bins.reshape(1, cells),
        ray_index.reshape(1, cells),
    )
    got = [outgoing[0]] + [swap(outgoing[d], "bin", d) for d in range(1, half)]
    ray_rows = RAY_DEV
    size = high_total * ray_rows
    partial_sums = pl.pallas_call(
        functools.partial(level_kernel, capacity, low_total, high_total, ray_rows),
        out_shape=[
            jax.ShapeDtypeStruct((size, levels), F32 if d == 0 else BF16) for d in range(low_total)
        ],
        in_specs=[smem] + [vmem] * (half + 2),
        out_specs=[vmem] * low_total,
        compiler_params=params,
    )(me, *got, rate_tables[0], other)
    sums = partial_sums[0]
    for d in range(1, low_total):
        sums = sums + swap(partial_sums[d], "bin", d).astype(F32)
    total = sums[:ray_rows]
    for h in range(1, high_total):
        leaving = sums[h * ray_rows : (h + 1) * ray_rows].astype(BF16)
        total = total + swap(leaving, "bin", h * low_total).astype(F32)
    step = 1
    theirs = jnp.zeros_like(total)
    while step < wave_total:
        total = total + theirs if step > 1 else total
        theirs = swap(total, "wave", step)
        step *= 2
    return pl.pallas_call(
        line_kernel,
        out_shape=jax.ShapeDtypeStruct((ray_rows, line_table.shape[1]), F32),
        in_specs=[vmem, vmem, vmem],
        out_specs=vmem,
        compiler_params=params,
    )(total, theirs, line_table)


def solution(mesh):
    in_specs = (
        P(("bin", "wave"), None),
        P(("bin", "wave")),
        P(("bin", "wave"), None),
        P(("bin", "wave")),
        P("bin", None, None),
        P(None, "wave"),
    )
    return jax.shard_map(
        per_device, mesh=mesh, in_specs=in_specs, out_specs=P("bin", "wave"), check_vma=False
    )
```

time: 40.7 us -> 42.6 us (1.047)
  blocking collectives: 12.4 us -> 0 us
  starting transfers between devices: 8.84 us -> 20.6 us
  waiting for transfers between devices: 11.1 us -> 13.5 us
  Pallas kernels: 3.95 us -> 4.81 us
  local copies, waits for them, and re-layouts: 4.05 us -> 3.38 us
    ppermute x2 -> x15, starting transfers between devices: 2.66 us -> 20.6 us  [swap(): return lax.ppermute(value, axis, [(i, i ^ mask) for i in range(total)])]
    all_to_all x1 -> x0, blocking collectives: 12.4 us -> none  [per_device(): lax.all_to_all(partial_sums.reshape(bin_total, ray_rows, levels), 'bin',...]
    all_to_all x1 -> x0, starting transfers between devices: 6.18 us -> none  [per_device(): lax.all_to_all(outgoing, 'bin', split_axis=0, concat_axis=0, tiled=True,...]
    ppermute x2 -> x15, waiting for transfers between devices: 7.97 us -> 13.5 us  [swap(): return lax.ppermute(value, axis, [(i, i ^ mask) for i in range(total)])]
    all_to_all x1 -> x0, waiting for transfers between devices: 3.1 us -> none  [per_device(): lax.all_to_all(outgoing, 'bin', split_axis=0, concat_axis=0, tiled=True,...]
    pallas_call x1, Pallas kernels: 1.75 us -> 2.6 us  [per_device(): pl.pallas_call(functools.partial(pack_kernel, bin_total, capacity), out_s...]
    reshape x1 -> x0, local copies, waits for them, and re-layouts: 0.83 us -> none  [per_device(): density.reshape(1, cells)]
    unnamed x10 -> x6, local copies, waits for them, and re-layouts: 3.22 us -> 3.38 us
  transfers between devices with their start and end apart: 3 -> 15, of which waited for: 3 -> 11; matrix products, arithmetic and copies ran while one was open for 0% -> 0% of each run, Pallas kernels for 0% -> 0%
where the time goes in v2:
time: 42.6 us; the launch traced here: 42.4 us
  starting transfers between devices  20.6 us (48%)
  waiting for transfers between devices  13.5 us (32%)
  Pallas kernels  4.81 us (11%)
  local copies, waits for them, and re-layouts  3.38 us (8%)
    ppermute x15, starting transfers between devices, swap(): return lax.ppermute(value, axis, [(i, i ^ mask) for i in range(total)])  20.6 us
    ppermute x15, waiting for transfers between devices, swap(): return lax.ppermute(value, axis, [(i, i ^ mask) for i in range(total)])  13.5 us
    unnamed x6, local copies, waits for them, and re-layouts  3.38 us
    pallas_call x1, Pallas kernels, per_device(): pl.pallas_call(functools.partial(pack_kernel, bin_total, capacity), out_s...  2.6 us
    pallas_call x1, Pallas kernels, per_device(): pl.pallas_call(line_kernel, out_shape=jax.ShapeDtypeStruct((ray_rows, lin...  1.17 us
    pallas_call x1, Pallas kernels, per_device(): pl.pallas_call(functools.partial(level_kernel, capacity, low_total, high_...  1.04 us
  transfers between devices with their start and end apart: 15, of which 11 were waited for; matrix products, arithmetic and copies ran while one was open for 0% of the time, Pallas kernels for 0%

profile of v2, /device:TPU:0, one launch (start us, length us, event | category | flops | bytes accessed | tf_op | source)
XLA Modules:
  0.0 42.4 jit_solution(11699918966515404005)
XLA Ops:
  0.0 2.6 %shard_map.64 = (bf16[144,256]{1,0:T(8,128)(2,1)}, bf16[144,256]{1,0:T(8,128)(2,1)}, bf16[144,256]{1,0:T(8,128)(2,1)}, bf16[144,256]{1,0:T(8,128)(2,1)}, bf16[14...) custom-call(s32[1]{0:T(128)} %bitcast.me_ref, ...), custom_call_target="tpu_custom_call" | custom-call | tf_op jit(solution)/shard_map/pallas_call | solution.py:148
  2.6 3.0 %collective-permute-start = (bf16[144,256]{1,0:T(8,128)(2,1)}, bf16[144,256]{1,0:T(8,128)(2,1)S(1)}, u32[]{:S(2)}, u32[]{:S(2)}) collective-permute-start(bf16[144,256]{1,0:T(8,128)(2,1)} %get-tuple-element.18), channel_id=1, source_target_pairs={{0,2},{2,0},{4,6},{6,4},{8,10},{10,8},{12,14},{14,12},{16,18},{18,... | collective-permute-start | bytes 221192 | tf_op jit(solution)/shard_map/ppermute | solution.py:128
  5.6 1.5 %collective-permute-start.1 = (bf16[144,256]{1,0:T(8,128)(2,1)}, bf16[144,256]{1,0:T(8,128)(2,1)S(1)}, u32[]{:S(2)}, u32[]{:S(2)}) collective-permute-start(bf16[144,256]{1,0:T(8,128)(2,1)} %get-tuple-element.19), channel_id=1, source_target_pairs={{0,4},{2,6},{4,0},{6,2},{8,12},{10,14},{12,8},{14,10},{16,20},{18,... | collective-permute-start | bytes 221192 | tf_op jit(solution)/shard_map/ppermute | solution.py:128
  7.1 0.0 collective-permute-start.2
  7.2 3.1 %collective-permute-start.7 = (bf16[256,256]{1,0:T(8,128)(2,1)}, bf16[256,256]{1,0:T(8,128)(2,1)S(1)}, u32[]{:S(2)}, u32[]{:S(2)}) collective-permute-start(bf16[256,256]{1,0:T(8,128)(2,1)} %bitcast.5), channel_id=1, source_target_pairs={{0,16},{2,18},{4,20},{6,22},{8,24},{10,26},{12,28},{14,30},{16,0},... | collective-permute-start | bytes 393224 | tf_op jit(solution)/shard_map/ppermute | solution.py:128
  10.2 1.6 %collective-permute-start.3 = (bf16[144,256]{1,0:T(8,128)(2,1)}, bf16[144,256]{1,0:T(8,128)(2,1)S(1)}, u32[]{:S(2)}, u32[]{:S(2)}) collective-permute-start(bf16[144,256]{1,0:T(8,128)(2,1)} %get-tuple-element.21), channel_id=1, source_target_pairs={{0,8},{2,10},{4,12},{6,14},{8,0},{10,2},{12,4},{14,6},{16,24},{18,... | collective-permute-start | bytes 221192 | tf_op jit(solution)/shard_map/ppermute | solution.py:128
  11.8 0.0 collective-permute-done.refs_1_
  11.8 1.4 %collective-permute-start.4 = (bf16[144,256]{1,0:T(8,128)(2,1)}, bf16[144,256]{1,0:T(8,128)(2,1)S(1)}, u32[]{:S(2)}, u32[]{:S(2)}) collective-permute-start(bf16[144,256]{1,0:T(8,128)(2,1)} %get-tuple-element.22), channel_id=1, source_target_pairs={{0,10},{2,8},{4,14},{6,12},{8,2},{10,0},{12,6},{14,4},{16,26},{18,... | collective-permute-start | bytes 221192 | tf_op jit(solution)/shard_map/ppermute | solution.py:128
  13.2 0.0 collective-permute-done.1.refs_2_
  13.2 2.5 %collective-permute-start.5 = (bf16[144,256]{1,0:T(8,128)(2,1)}, bf16[144,256]{1,0:T(8,128)(2,1)S(1)}, u32[]{:S(2)}, u32[]{:S(2)}) collective-permute-start(bf16[144,256]{1,0:T(8,128)(2,1)} %get-tuple-element.23), channel_id=1, source_target_pairs={{0,12},{2,14},{4,8},{6,10},{8,4},{10,6},{12,0},{14,2},{16,28},{18,... | collective-permute-start | bytes 221192 | tf_op jit(solution)/shard_map/ppermute | solution.py:128
  15.7 0.0 collective-permute-done.2.refs_3_
  15.7 0.4 collective-permute-start.6
  16.1 0.3 collective-permute-done.3.refs_4_
  16.4 2.6 %collective-permute-done.4.refs_5_ = bf16[144,256]{1,0:T(8,128)(2,1)S(1)} collective-permute-done((bf16[144,256]{1,0:T(8,128)(2,1)}, bf16[144,256]{1,0:T(8,128)(2,1)S(1)}, u32[]{:S(2)}, u32[]{:S(2)}) %collective-permute-start.4) | collective-permute-done | bytes 73760 | tf_op jit(solution)/shard_map/ppermute | solution.py:128
  18.9 1.7 %collective-permute-done.5.refs_6_ = bf16[144,256]{1,0:T(8,128)(2,1)S(1)} collective-permute-done((bf16[144,256]{1,0:T(8,128)(2,1)}, bf16[144,256]{1,0:T(8,128)(2,1)S(1)}, u32[]{:S(2)}, u32[]{:S(2)}) %collective-permute-start.5) | collective-permute-done | bytes 73760 | tf_op jit(solution)/shard_map/ppermute | solution.py:128
  20.6 1.5 %collective-permute-done.6.refs_7_ = bf16[144,256]{1,0:T(8,128)(2,1)S(1)} collective-permute-done((bf16[144,256]{1,0:T(8,128)(2,1)}, bf16[144,256]{1,0:T(8,128)(2,1)S(1)}, u32[]{:S(2)}, u32[]{:S(2)}) %collective-permute-start.6) | collective-permute-done | bytes 73760 | tf_op jit(solution)/shard_map/ppermute | solution.py:128
  22.1 0.0 collective-permute-done.7.refs_9_
  22.1 0.0 copy-start.1
  22.1 0.9 %copy-done.1 = bf16[1,256,256]{2,1,0:T(8,128)(2,1)S(1)} copy-done((bf16[1,256,256]{2,1,0:T(8,128)(2,1)S(1)}, bf16[1,256,256]{2,1,0:T(8,128)(2,1)}, u32[]{:S(2)}) %copy-start.1) | copy-done | bytes 131096
  23.0 0.0 copy-start.2
  23.0 0.9 %copy-done.2 = bf16[144,256]{1,0:T(8,128)(2,1)S(1)} copy-done((bf16[144,256]{1,0:T(8,128)(2,1)S(1)}, bf16[144,256]{1,0:T(8,128)(2,1)}, u32[]{:S(2)}) %copy-start.2) | copy-done | bytes 73752
  23.9 1.0 %shard_map.65 = (f32[64,256]{1,0:T(8,128)S(1)}, bf16[64,256]{1,0:T(8,128)(2,1)S(1)}, bf16[64,256]{1,0:T(8,128)(2,1)S(1)}, bf16[64,256]{1,0:T(8,128)(2,1)S(1)}) custom-call(s32[1]{0:T(128)} %bitcast.me_ref, bf16[144,256]{1,0:T(8,128)(2,1)S(1)} %copy-done.2, bf16[144,256]{1,0:T(8,128)(2,1)S(1)} %collective-permute-done.refs_1_, ...), custom_call_target="tpu_custom_call" | custom-call | tf_op jit(solution)/shard_map/pallas_call | solution.py:173
  24.9 0.8 %collective-permute-start.8 = (bf16[64,256]{1,0:T(8,128)(2,1)S(1)}, bf16[64,256]{1,0:T(8,128)(2,1)S(1)}, u32[]{:S(2)}, u32[]{:S(2)}) collective-permute-start(bf16[64,256]{1,0:T(8,128)(2,1)S(1)} %get-tuple-element.26), channel_id=1, source_target_pairs={{0,2},{2,0},{4,6},{6,4},{8,10},{10,8},{12,14},{14,12},{16,18},{18,... | collective-permute-start | bytes 98312 | tf_op jit(solution)/shard_map/ppermute | solution.py:128
  25.7 0.5 %collective-permute-start.9 = (bf16[64,256]{1,0:T(8,128)(2,1)S(1)}, bf16[64,256]{1,0:T(8,128)(2,1)S(1)}, u32[]{:S(2)}, u32[]{:S(2)}) collective-permute-start(bf16[64,256]{1,0:T(8,128)(2,1)S(1)} %get-tuple-element.27), channel_id=1, source_target_pairs={{0,4},{2,6},{4,0},{6,2},{8,12},{10,14},{12,8},{14,10},{16,20},{18,... | collective-permute-start | bytes 98312 | tf_op jit(solution)/shard_map/ppermute | solution.py:128
  26.1 2.3 %collective-permute-start.10 = (bf16[64,256]{1,0:T(8,128)(2,1)S(1)}, bf16[64,256]{1,0:T(8,128)(2,1)S(1)}, u32[]{:S(2)}, u32[]{:S(2)}) collective-permute-start(bf16[64,256]{1,0:T(8,128)(2,1)S(1)} %get-tuple-element.28), channel_id=1, source_target_pairs={{0,6},{2,4},{4,2},{6,0},{8,14},{10,12},{12,10},{14,8},{16,22},{18,... | collective-permute-start | bytes 98312 | tf_op jit(solution)/shard_map/ppermute | solution.py:128
  28.5 0.4 %collective-permute-done.8 = bf16[64,256]{1,0:T(8,128)(2,1)S(1)} collective-permute-done((bf16[64,256]{1,0:T(8,128)(2,1)S(1)}, bf16[64,256]{1,0:T(8,128)(2,1)S(1)}, u32[]{:S(2)}, u32[]{:S(2)}) %collective-permute-start.8) | collective-permute-done | bytes 32800 | tf_op jit(solution)/shard_map/ppermute | solution.py:128
  28.9 0.7 %collective-permute-done.9 = bf16[64,256]{1,0:T(8,128)(2,1)S(1)} collective-permute-done((bf16[64,256]{1,0:T(8,128)(2,1)S(1)}, bf16[64,256]{1,0:T(8,128)(2,1)S(1)}, u32[]{:S(2)}, u32[]{:S(2)}) %collective-permute-start.9) | collective-permute-done | bytes 32800 | tf_op jit(solution)/shard_map/ppermute | solution.py:128
  29.6 1.4 %collective-permute-done.10 = bf16[64,256]{1,0:T(8,128)(2,1)S(1)} collective-permute-done((bf16[64,256]{1,0:T(8,128)(2,1)S(1)}, bf16[64,256]{1,0:T(8,128)(2,1)S(1)}, u32[]{:S(2)}, u32[]{:S(2)}) %collective-permute-start.10) | collective-permute-done | bytes 32800 | tf_op jit(solution)/shard_map/ppermute | solution.py:128
  31.0 0.9 %collective-permute-start.11 = (bf16[16,256]{1,0:T(8,128)(2,1)S(1)}, bf16[16,256]{1,0:T(8,128)(2,1)S(1)}, u32[]{:S(2)}, u32[]{:S(2)}) collective-permute-start(bf16[16,256]{1,0:T(8,128)(2,1)S(1)} %get-tuple-element.31), channel_id=1, source_target_pairs={{0,8},{2,10},{4,12},{6,14},{8,0},{10,2},{12,4},{14,6},{16,24},{18,... | collective-permute-start | bytes 24584 | tf_op jit(solution)/shard_map/ppermute | solution.py:128
  31.9 1.9 %collective-permute-start.13 = (bf16[16,256]{1,0:T(8,128)(2,1)S(1)}, bf16[16,256]{1,0:T(8,128)(2,1)S(1)}, u32[]{:S(2)}, u32[]{:S(2)}) collective-permute-start(bf16[16,256]{1,0:T(8,128)(2,1)S(1)} %get-tuple-element.32), channel_id=1, source_target_pairs={{0,24},{2,26},{4,28},{6,30},{8,16},{10,18},{12,20},{14,22},{16,8},... | collective-permute-start | bytes 24584 | tf_op jit(solution)/shard_map/ppermute | solution.py:128
  33.8 0.7 %collective-permute-start.12 = (bf16[16,256]{1,0:T(8,128)(2,1)S(1)}, bf16[16,256]{1,0:T(8,128)(2,1)S(1)}, u32[]{:S(2)}, u32[]{:S(2)}) collective-permute-start(bf16[16,256]{1,0:T(8,128)(2,1)S(1)} %get-tuple-element.33), channel_id=1, source_target_pairs={{0,16},{2,18},{4,20},{6,22},{8,24},{10,26},{12,28},{14,30},{16,0},... | collective-permute-start | bytes 24584 | tf_op jit(solution)/shard_map/ppermute | solution.py:128
  34.5 0.2 collective-permute-done.11
  34.7 2.7 %collective-permute-done.13 = bf16[16,256]{1,0:T(8,128)(2,1)S(1)} collective-permute-done((bf16[16,256]{1,0:T(8,128)(2,1)S(1)}, bf16[16,256]{1,0:T(8,128)(2,1)S(1)}, u32[]{:S(2)}, u32[]{:S(2)}) %collective-permute-start.13) | collective-permute-done | bytes 8224 | tf_op jit(solution)/shard_map/ppermute | solution.py:128
  37.4 1.0 %collective-permute-done.12 = bf16[16,256]{1,0:T(8,128)(2,1)S(1)} collective-permute-done((bf16[16,256]{1,0:T(8,128)(2,1)S(1)}, bf16[16,256]{1,0:T(8,128)(2,1)S(1)}, u32[]{:S(2)}, u32[]{:S(2)}) %collective-permute-start.12) | collective-permute-done | bytes 8224 | tf_op jit(solution)/shard_map/ppermute | solution.py:128
  38.4 0.1 collective-permute-start.14
  38.5 1.2 %collective-permute-done.14.theirs_ref = f32[16,256]{1,0:T(8,128)S(1)} collective-permute-done((f32[16,256]{1,0:T(8,128)S(1)}, f32[16,256]{1,0:T(8,128)S(1)}, u32[]{:S(2)}, u32[]{:S(2)}) %collective-permute-start.14) | collective-permute-done | bytes 16416 | tf_op jit(solution)/shard_map/ppermute | solution.py:128
  39.6 0.0 copy-start
  39.6 1.6 %copy-done = bf16[256,4096]{1,0:T(8,128)(2,1)S(1)} copy-done((bf16[256,4096]{1,0:T(8,128)(2,1)S(1)}, bf16[256,4096]{1,0:T(8,128)(2,1)}, u32[]{:S(2)}) %copy-start) | copy-done | bytes 2097176
  41.2 1.2 %shard_map.66 = f32[16,4096]{1,0:T(8,128)} custom-call(f32[16,256]{1,0:T(8,128)S(1)} %fusion.1.mine_ref, f32[16,256]{1,0:T(8,128)S(1)} %collective-permute-done.14.theirs_ref, bf16[256,4096]{1,0:T(8,128)(2,1)S(1)} %copy-done), custom_call_target="tpu_custom_call" | custom-call | tf_op jit(solution)/shard_map/pallas_call | solution.py:195
  (3 shorter events, 0.0 us)
Async XLA Ops:
  2.6 9.2 %collective-permute-start = (bf16[144,256]{1,0:T(8,128)(2,1)}, bf16[144,256]{1,0:T(8,128)(2,1)S(1)}, u32[]{:S(2)}, u32[]{:S(2)}) collective-permute-start(bf16[144,256]{1,0:T(8,128)(2,1)} %get-tuple-element.18), channel_id=1, source_target_pairs={{0,2},{2,0},{4,6},{6,4},{8,10},{10,8},{12,14},{14,12},{16,18},{18,... | collective-permute-start | bytes 221192 | tf_op jit(solution)/shard_map/ppermute | solution.py:128
  5.6 7.6 %collective-permute-start.1 = (bf16[144,256]{1,0:T(8,128)(2,1)}, bf16[144,256]{1,0:T(8,128)(2,1)S(1)}, u32[]{:S(2)}, u32[]{:S(2)}) collective-permute-start(bf16[144,256]{1,0:T(8,128)(2,1)} %get-tuple-element.19), channel_id=1, source_target_pairs={{0,4},{2,6},{4,0},{6,2},{8,12},{10,14},{12,8},{14,10},{16,20},{18,... | collective-permute-start | bytes 221192 | tf_op jit(solution)/shard_map/ppermute | solution.py:128
  7.1 8.6 %collective-permute-start.2 = (bf16[144,256]{1,0:T(8,128)(2,1)}, bf16[144,256]{1,0:T(8,128)(2,1)S(1)}, u32[]{:S(2)}, u32[]{:S(2)}) collective-permute-start(bf16[144,256]{1,0:T(8,128)(2,1)} %get-tuple-element.20), channel_id=1, source_target_pairs={{0,6},{2,4},{4,2},{6,0},{8,14},{10,12},{12,10},{14,8},{16,22},{18,... | collective-permute-start | bytes 221192 | tf_op jit(solution)/shard_map/ppermute | solution.py:128
  7.2 14.9 %collective-permute-start.7 = (bf16[256,256]{1,0:T(8,128)(2,1)}, bf16[256,256]{1,0:T(8,128)(2,1)S(1)}, u32[]{:S(2)}, u32[]{:S(2)}) collective-permute-start(bf16[256,256]{1,0:T(8,128)(2,1)} %bitcast.5), channel_id=1, source_target_pairs={{0,16},{2,18},{4,20},{6,22},{8,24},{10,26},{12,28},{14,30},{16,0},... | collective-permute-start | bytes 393224 | tf_op jit(solution)/shard_map/ppermute | solution.py:128
  10.2 6.1 %collective-permute-start.3 = (bf16[144,256]{1,0:T(8,128)(2,1)}, bf16[144,256]{1,0:T(8,128)(2,1)S(1)}, u32[]{:S(2)}, u32[]{:S(2)}) collective-permute-start(bf16[144,256]{1,0:T(8,128)(2,1)} %get-tuple-element.21), channel_id=1, source_target_pairs={{0,8},{2,10},{4,12},{6,14},{8,0},{10,2},{12,4},{14,6},{16,24},{18,... | collective-permute-start | bytes 221192 | tf_op jit(solution)/shard_map/ppermute | solution.py:128
  11.8 7.1 %collective-permute-start.4 = (bf16[144,256]{1,0:T(8,128)(2,1)}, bf16[144,256]{1,0:T(8,128)(2,1)S(1)}, u32[]{:S(2)}, u32[]{:S(2)}) collective-permute-start(bf16[144,256]{1,0:T(8,128)(2,1)} %get-tuple-element.22), channel_id=1, source_target_pairs={{0,10},{2,8},{4,14},{6,12},{8,2},{10,0},{12,6},{14,4},{16,26},{18,... | collective-permute-start | bytes 221192 | tf_op jit(solution)/shard_map/ppermute | solution.py:128
  13.2 7.4 %collective-permute-start.5 = (bf16[144,256]{1,0:T(8,128)(2,1)}, bf16[144,256]{1,0:T(8,128)(2,1)S(1)}, u32[]{:S(2)}, u32[]{:S(2)}) collective-permute-start(bf16[144,256]{1,0:T(8,128)(2,1)} %get-tuple-element.23), channel_id=1, source_target_pairs={{0,12},{2,14},{4,8},{6,10},{8,4},{10,6},{12,0},{14,2},{16,28},{18,... | collective-permute-start | bytes 221192 | tf_op jit(solution)/shard_map/ppermute | solution.py:128
  15.7 6.4 %collective-permute-start.6 = (bf16[144,256]{1,0:T(8,128)(2,1)}, bf16[144,256]{1,0:T(8,128)(2,1)S(1)}, u32[]{:S(2)}, u32[]{:S(2)}) collective-permute-start(bf16[144,256]{1,0:T(8,128)(2,1)} %get-tuple-element.24), channel_id=1, source_target_pairs={{0,14},{2,12},{4,10},{6,8},{8,6},{10,4},{12,2},{14,0},{16,30},{18,... | collective-permute-start | bytes 221192 | tf_op jit(solution)/shard_map/ppermute | solution.py:128
  22.1 0.9 %copy-start.1 = (bf16[1,256,256]{2,1,0:T(8,128)(2,1)S(1)}, bf16[1,256,256]{2,1,0:T(8,128)(2,1)}, u32[]{:S(2)}) copy-start(bf16[1,256,256]{2,1,0:T(8,128)(2,1)} %param.10) | copy-start | bytes 393220
  23.0 0.9 %copy-start.2 = (bf16[144,256]{1,0:T(8,128)(2,1)S(1)}, bf16[144,256]{1,0:T(8,128)(2,1)}, u32[]{:S(2)}) copy-start(bf16[144,256]{1,0:T(8,128)(2,1)} %get-tuple-element.17.refs_0_) | copy-start | bytes 221188
  24.9 4.0 %collective-permute-start.8 = (bf16[64,256]{1,0:T(8,128)(2,1)S(1)}, bf16[64,256]{1,0:T(8,128)(2,1)S(1)}, u32[]{:S(2)}, u32[]{:S(2)}) collective-permute-start(bf16[64,256]{1,0:T(8,128)(2,1)S(1)} %get-tuple-element.26), channel_id=1, source_target_pairs={{0,2},{2,0},{4,6},{6,4},{8,10},{10,8},{12,14},{14,12},{16,18},{18,... | collective-permute-start | bytes 98312 | tf_op jit(solution)/shard_map/ppermute | solution.py:128
  25.7 3.9 %collective-permute-start.9 = (bf16[64,256]{1,0:T(8,128)(2,1)S(1)}, bf16[64,256]{1,0:T(8,128)(2,1)S(1)}, u32[]{:S(2)}, u32[]{:S(2)}) collective-permute-start(bf16[64,256]{1,0:T(8,128)(2,1)S(1)} %get-tuple-element.27), channel_id=1, source_target_pairs={{0,4},{2,6},{4,0},{6,2},{8,12},{10,14},{12,8},{14,10},{16,20},{18,... | collective-permute-start | bytes 98312 | tf_op jit(solution)/shard_map/ppermute | solution.py:128
  26.1 4.8 %collective-permute-start.10 = (bf16[64,256]{1,0:T(8,128)(2,1)S(1)}, bf16[64,256]{1,0:T(8,128)(2,1)S(1)}, u32[]{:S(2)}, u32[]{:S(2)}) collective-permute-start(bf16[64,256]{1,0:T(8,128)(2,1)S(1)} %get-tuple-element.28), channel_id=1, source_target_pairs={{0,6},{2,4},{4,2},{6,0},{8,14},{10,12},{12,10},{14,8},{16,22},{18,... | collective-permute-start | bytes 98312 | tf_op jit(solution)/shard_map/ppermute | solution.py:128
  31.0 3.7 %collective-permute-start.11 = (bf16[16,256]{1,0:T(8,128)(2,1)S(1)}, bf16[16,256]{1,0:T(8,128)(2,1)S(1)}, u32[]{:S(2)}, u32[]{:S(2)}) collective-permute-start(bf16[16,256]{1,0:T(8,128)(2,1)S(1)} %get-tuple-element.31), channel_id=1, source_target_pairs={{0,8},{2,10},{4,12},{6,14},{8,0},{10,2},{12,4},{14,6},{16,24},{18,... | collective-permute-start | bytes 24584 | tf_op jit(solution)/shard_map/ppermute | solution.py:128
  31.9 5.4 %collective-permute-start.13 = (bf16[16,256]{1,0:T(8,128)(2,1)S(1)}, bf16[16,256]{1,0:T(8,128)(2,1)S(1)}, u32[]{:S(2)}, u32[]{:S(2)}) collective-permute-start(bf16[16,256]{1,0:T(8,128)(2,1)S(1)} %get-tuple-element.32), channel_id=1, source_target_pairs={{0,24},{2,26},{4,28},{6,30},{8,16},{10,18},{12,20},{14,22},{16,8},... | collective-permute-start | bytes 24584 | tf_op jit(solution)/shard_map/ppermute | solution.py:128
  33.8 4.5 %collective-permute-start.12 = (bf16[16,256]{1,0:T(8,128)(2,1)S(1)}, bf16[16,256]{1,0:T(8,128)(2,1)S(1)}, u32[]{:S(2)}, u32[]{:S(2)}) collective-permute-start(bf16[16,256]{1,0:T(8,128)(2,1)S(1)} %get-tuple-element.33), channel_id=1, source_target_pairs={{0,16},{2,18},{4,20},{6,22},{8,24},{10,26},{12,28},{14,30},{16,0},... | collective-permute-start | bytes 24584 | tf_op jit(solution)/shard_map/ppermute | solution.py:128
  38.4 1.2 %collective-permute-start.14 = (f32[16,256]{1,0:T(8,128)S(1)}, f32[16,256]{1,0:T(8,128)S(1)}, u32[]{:S(2)}, u32[]{:S(2)}) collective-permute-start(f32[16,256]{1,0:T(8,128)S(1)} %fusion.1.mine_ref), channel_id=1, source_target_pairs={{0,1},{1,0},{2,3},{3,2},{4,5},{5,4},{6,7},{7,6},{8,9},{9,8},{10,11... | collective-permute-start | bytes 49160 | tf_op jit(solution)/shard_map/ppermute | solution.py:128
  39.6 1.6 %copy-start = (bf16[256,4096]{1,0:T(8,128)(2,1)S(1)}, bf16[256,4096]{1,0:T(8,128)(2,1)}, u32[]{:S(2)}) copy-start(bf16[256,4096]{1,0:T(8,128)(2,1)} %line_ref.1) | copy-start | bytes 6291460

commit v3 on v2

v3 whole, which is shorter than its diff:
```python
import functools

import jax
import jax.numpy as jnp
from jax import lax
from jax.experimental import pallas as pl
from jax.experimental.pallas import tpu as pltpu
from jax.sharding import PartitionSpec as P

RAY_DEV = 16
META_ROWS = 16
RAY_BASE = 32
LANES = 128
VMEM_LIMIT = 32 * 1024 * 1024
F32 = jnp.float32
BF16 = jnp.bfloat16
I32 = jnp.int32


def nt_dot(a, b):
    return lax.dot_general(a, b, (((1,), (1,)), ((), ())), preferred_element_type=F32)


def iota(shape, dim):
    return lax.broadcasted_iota(I32, shape, dim)


def pack_kernel(plan, me_ref, src_hbm, den_hbm, bin_hbm, ray_hbm, out_hbm, *scratch):
    src_ref, den_ref, bin_ref, ray_ref, held, in_sems, out_sems = scratch
    copies = [
        pltpu.make_async_copy(a, b, in_sems.at[i])
        for i, (a, b) in enumerate(
            ((bin_hbm, bin_ref), (ray_hbm, ray_ref), (den_hbm, den_ref), (src_hbm, src_ref))
        )
    ]
    for copy in copies:
        copy.start()
    cells, levels = src_ref.shape
    targets, block = plan.targets, plan.block
    earlier = (iota((cells, cells), 0) < iota((cells, cells), 1)).astype(F32).astype(BF16)
    held[:, block:, :] = jnp.zeros((targets, META_ROWS, levels), BF16)
    my_part = me_ref[0] // plan.wave
    for copy in copies[:3]:
        copy.wait()
    bins = bin_ref[...]
    hot = (iota((plan.low * plan.high, cells), 0) == bins).astype(F32)
    before = jnp.dot(hot.astype(BF16), earlier, preferred_element_type=F32)
    position = jnp.sum(hot * before, axis=0, keepdims=True).astype(I32)
    high = bins // plan.low
    target = (bins - high * plan.low) * plan.wave + high % plan.wave
    slot = target * block + ((high // plan.wave) ^ my_part) * plan.capacity + position
    rays = ray_ref[...]
    ray_high = rays // RAY_BASE
    ray_low = rays - ray_high * RAY_BASE
    den = den_ref[...].astype(F32)
    den_row = jnp.concatenate([den[i : i + 1] for i in range(den.shape[0])], axis=1)
    meta = jnp.concatenate(
        [den_row, ray_high.astype(F32), ray_low.astype(F32), jnp.zeros((META_ROWS - 3, cells), F32)],
        axis=0,
    ).astype(BF16)
    place = (iota((targets * block, cells), 0) == slot).astype(F32).astype(BF16)
    moved = nt_dot(meta, place).astype(BF16)
    copies[3].wait()
    src = src_ref[...]
    leaving = [
        pltpu.make_async_copy(held.at[t], out_hbm.at[t], out_sems.at[t]) for t in range(targets)
    ]
    for t in range(targets):
        first, last = t * block, (t + 1) * block
        rows = jnp.dot(place[first:last], src, preferred_element_type=F32)
        held[t, :block, :] = rows.astype(BF16)
        held[t, block:, :block] = moved[:, first:last]
        leaving[t].start()
    for copy in leaving:
        copy.wait()


def level_kernel(plan, rays, got_ref, *refs):
    table_refs, out_ref = refs[:-1], refs[-1]
    targets, block = plan.targets, plan.block
    meta = [got_ref[s, block:, :block].astype(F32) for s in range(targets)]
    columns = [jnp.transpose(m[:8]) for m in meta]
    total = jnp.zeros(out_ref.shape, F32)
    for part, table_ref in enumerate(table_refs):
        low, high = part * plan.capacity, (part + 1) * plan.capacity
        src = got_ref[:, low:high, :].reshape(targets * plan.capacity, got_ref.shape[2])
        den = jnp.concatenate([c[low:high, 0:1] for c in columns], axis=0)
        ray = jnp.concatenate(
            [m[1:2, low:high] * RAY_BASE + m[2:3, low:high] for m in meta], axis=1
        ).astype(I32)
        wide = src.astype(F32)
        table = table_ref[...]
        first = (den * jnp.dot(src, table, preferred_element_type=F32) + wide).astype(BF16)
        pops = (den * jnp.dot(first, table, preferred_element_type=F32) + wide).astype(BF16)
        pick = (iota((rays, src.shape[0]), 0) == ray).astype(F32).astype(BF16)
        total = total + jnp.dot(pick, pops, preferred_element_type=F32)
    out_ref[...] = total.astype(BF16)


def line_kernel(mine_ref, theirs_ref, line_ref, out_ref):
    sums = mine_ref[...] + theirs_ref[...]
    rows = sums.shape[0]
    high = sums.astype(BF16)
    low = (sums - high.astype(F32)).astype(BF16)
    both = jnp.concatenate([high, low], axis=0)
    got = jnp.dot(both, line_ref[...], preferred_element_type=F32)
    out_ref[...] = got[:rows] + got[rows:]


class Plan:
    def __init__(self, bin_total, wave_total, cells):
        self.wave = wave_total
        self.high = max(wave_total, 1 << (bin_total.bit_length() // 2))
        self.low = bin_total // self.high
        self.parts = self.high // wave_total
        self.targets = self.low * wave_total
        self.capacity = max(2, 2 * cells // bin_total)
        self.block = self.parts * self.capacity

    def device(self, high, low, wave):
        return (high * self.low + low) * self.wave + wave

    def table_moves(self, k):
        moves = []
        for high in range(self.high):
            for low in range(self.low):
                for core in range(self.wave):
                    to = self.wave * ((high // self.wave) ^ k) + core
                    moves.append(
                        (self.device(high, low, core), self.device(to, low, high % self.wave))
                    )
        return moves

    def planes(self):
        size = self.low * self.wave
        return [list(range(h * size, (h + 1) * size)) for h in range(self.high)]


def per_device(sources, density, temp_bins, ray_index, rate_tables, line_table):
    cells, levels = sources.shape
    bin_total = lax.axis_size("bin")
    wave_total = lax.axis_size("wave")
    plan = Plan(bin_total, wave_total, cells)
    rows = plan.block + META_ROWS
    params = pltpu.CompilerParams(vmem_limit_bytes=VMEM_LIMIT)
    vmem = pl.BlockSpec(memory_space=pltpu.VMEM)
    smem = pl.BlockSpec(memory_space=pltpu.SMEM)
    hbm = pl.BlockSpec(memory_space=pltpu.HBM)

    def in_hbm(x):
        return pltpu.with_memory_space_constraint(x, pltpu.HBM)

    tables = [
        lax.ppermute(rate_tables[0], ("bin", "wave"), plan.table_moves(k)) for k in range(plan.parts)
    ]
    me = (lax.axis_index("bin") // plan.low).astype(I32).reshape(1)
    den_rows = cells // min(cells, LANES)
    outgoing = pl.pallas_call(
        functools.partial(pack_kernel, plan),
        out_shape=jax.ShapeDtypeStruct((plan.targets, rows, levels), BF16),
        in_specs=[smem] + [hbm] * 4,
        out_specs=hbm,
        scratch_shapes=[
            pltpu.VMEM((cells, levels), BF16),
            pltpu.VMEM((den_rows, cells // den_rows), BF16),
            pltpu.VMEM((1, cells), I32),
            pltpu.VMEM((1, cells), I32),
            pltpu.VMEM((plan.targets, rows, levels), BF16),
            pltpu.SemaphoreType.DMA((4,)),
            pltpu.SemaphoreType.DMA((plan.targets,)),
        ],
        compiler_params=params,
    )(
        me,
        in_hbm(sources),
        in_hbm(density.reshape(den_rows, cells // den_rows)),
        in_hbm(temp_bins.reshape(1, cells)),
        in_hbm(ray_index.reshape(1, cells)),
    )
    got = lax.all_to_all(
        outgoing,
        ("bin", "wave"),
        split_axis=0,
        concat_axis=0,
        tiled=True,
        axis_index_groups=plan.planes(),
    )
    ray_rows = RAY_DEV
    rays = ray_rows * bin_total
    partial_sums = pl.pallas_call(
        functools.partial(level_kernel, plan, rays),
        out_shape=jax.ShapeDtypeStruct((rays, levels), BF16),
        in_specs=[vmem] * (1 + plan.parts),
        out_specs=vmem,
        compiler_params=params,
    )(got, *tables)
    held = lax.all_to_all(
        partial_sums.reshape(bin_total, ray_rows, levels),
        "bin",
        split_axis=0,
        concat_axis=0,
        tiled=True,
    )
    total = jnp.sum(held.astype(F32), axis=0)
    theirs = jnp.zeros_like(total)
    step = 1
    while step < wave_total:
        total = total + theirs if step > 1 else total
        theirs = lax.ppermute(total, "wave", [(i, i ^ step) for i in range(wave_total)])
        step *= 2
    return pl.pallas_call(
        line_kernel,
        out_shape=jax.ShapeDtypeStruct((ray_rows, line_table.shape[1]), F32),
        in_specs=[vmem, vmem, vmem],
        out_specs=vmem,
        compiler_params=params,
    )(total, theirs, line_table)


def solution(mesh):
    in_specs = (
        P(("bin", "wave"), None),
        P(("bin", "wave")),
        P(("bin", "wave"), None),
        P(("bin", "wave")),
        P("bin", None, None),
        P(None, "wave"),
    )
    return jax.shard_map(
        per_device, mesh=mesh, in_specs=in_specs, out_specs=P("bin", "wave"), check_vma=False
    )
```

time: 42.6 us -> 36.2 us (0.85)
  blocking collectives: 0 us -> 13.4 us
  starting transfers between devices: 20.6 us -> 9.39 us
  waiting for transfers between devices: 13.5 us -> 8.22 us
  local copies, waits for them, and re-layouts: 3.38 us -> 0.01 us
    ppermute x15 -> x3, starting transfers between devices: 20.6 us -> 4.21 us  [the longest x2 4.14 us: per_device(): lax.ppermute(rate_tables[0], ('bin', 'wave'), plan.table_moves(k))]
    all_to_all x0 -> x1, blocking collectives: none -> 13.4 us  [per_device(): lax.all_to_all(partial_sums.reshape(bin_total, ray_rows, levels), 'bin',...]
    ppermute x15 -> x3, waiting for transfers between devices: 13.5 us -> 8.21 us  [the longest x2 7.04 us: per_device(): lax.ppermute(rate_tables[0], ('bin', 'wave'), plan.table_moves(k))]
    all_to_all x0 -> x1, starting transfers between devices: none -> 5.18 us  [per_device(): lax.all_to_all(outgoing, ('bin', 'wave'), split_axis=0, concat_axis=0, ti...]
    unnamed x6 -> x2, local copies, waits for them, and re-layouts: 3.38 us -> 0.01 us
  transfers between devices with their start and end apart: 15 -> 4, of which waited for: 11 -> 2; matrix products, arithmetic and copies ran while one was open for 0% -> 0% of each run, Pallas kernels for 0% -> 0%
where the time goes in v3:
time: 36.2 us; the launch traced here: 36 us
  blocking collectives  13.4 us (37%)
  starting transfers between devices  9.39 us (26%)
  waiting for transfers between devices  8.22 us (23%)
  Pallas kernels  4.93 us (14%)
    all_to_all x1, blocking collectives, per_device(): lax.all_to_all(partial_sums.reshape(bin_total, ray_rows, levels), 'bin',...  13.4 us
    ppermute x2, waiting for transfers between devices, per_device(): lax.ppermute(rate_tables[0], ('bin', 'wave'), plan.table_moves(k))  7.04 us
    all_to_all x1, starting transfers between devices, per_device(): lax.all_to_all(outgoing, ('bin', 'wave'), split_axis=0, concat_axis=0, ti...  5.18 us
    ppermute x2, starting transfers between devices, per_device(): lax.ppermute(rate_tables[0], ('bin', 'wave'), plan.table_moves(k))  4.14 us
    pallas_call x1, Pallas kernels, per_device(): pl.pallas_call(functools.partial(pack_kernel, plan), out_shape=jax.ShapeD...  2.73 us
    ppermute x1, waiting for transfers between devices, per_device(): lax.ppermute(total, 'wave', [(i, i ^ step) for i in range(wave_total)])  1.17 us
    pallas_call x1, Pallas kernels, per_device(): pl.pallas_call(line_kernel, out_shape=jax.ShapeDtypeStruct((ray_rows, lin...  1.17 us
    pallas_call x1, Pallas kernels, per_device(): pl.pallas_call(functools.partial(level_kernel, plan, rays), out_shape=jax...  1.04 us
  transfers between devices with their start and end apart: 4, of which 2 were waited for; matrix products, arithmetic and copies ran while one was open for 0% of the time, Pallas kernels for 0%

profile of v3, /device:TPU:0, one launch (start us, length us, event | category | flops | bytes accessed | tf_op | source)
XLA Modules:
  0.0 36.0 jit_solution(8509602063567333436)
XLA Ops:
  0.0 0.0 copy-start
  0.0 2.7 %shard_map.64 = bf16[8,144,256]{2,1,0:T(8,128)(2,1)} custom-call(s32[1]{0:T(128)} %bitcast.me_ref, bf16[512,256]{1,0:T(8,128)(2,1)} %src_hbm.1, bf16[4,128]{1,0:T(4,128)(2,1)} %bitcast.9, s32[1,512]{1,0:T(1,128)} %bitcast.7, s32[1,512]{1,0:T(1,128)} %bitcast.8), custom_call_target="tpu_custom_call" | custom-call | tf_op jit(solution)/shard_map/pallas_call | solution.py:158
  2.7 5.2 %all-to-all-start = ((bf16[8,144,256]{2,1,0:T(8,128)(2,1)}), bf16[8,144,256]{2,1,0:T(8,128)(2,1)S(1)}, u32[]{:S(2)}, u32[]{:S(2)}) async-start(bf16[8,144,256]{2,1,0:T(8,128)(2,1)} %shard_map.64), calls=%async_computation | async-start | bytes 1179648 | tf_op jit(solution)/shard_map/all_to_all | solution.py:180
  7.9 1.6 %collective-permute-start = (bf16[256,256]{1,0:T(8,128)(2,1)}, bf16[256,256]{1,0:T(8,128)(2,1)S(1)}, u32[]{:S(2)}, u32[]{:S(2)}) collective-permute-start(bf16[256,256]{1,0:T(8,128)(2,1)} %bitcast.10), channel_id=1, source_target_pairs={{0,0},{1,8},{2,2},{3,10},{4,4},{5,12},{6,6},{7,14},{8,1},{9,9},{10... | collective-permute-start | bytes 393224 | tf_op jit(solution)/shard_map/ppermute | solution.py:154
  9.5 2.6 %collective-permute-start.1 = (bf16[256,256]{1,0:T(8,128)(2,1)}, bf16[256,256]{1,0:T(8,128)(2,1)S(1)}, u32[]{:S(2)}, u32[]{:S(2)}) collective-permute-start(bf16[256,256]{1,0:T(8,128)(2,1)} %bitcast.11), channel_id=1, source_target_pairs={{0,16},{1,24},{2,18},{3,26},{4,20},{5,28},{6,22},{7,30},{8,17},{9,... | collective-permute-start | bytes 393224 | tf_op jit(solution)/shard_map/ppermute | solution.py:154
  12.1 0.0 collective-permute-done.refs_0_
  12.1 7.0 %collective-permute-done.1.refs_1_ = bf16[256,256]{1,0:T(8,128)(2,1)S(1)} collective-permute-done((bf16[256,256]{1,0:T(8,128)(2,1)}, bf16[256,256]{1,0:T(8,128)(2,1)S(1)}, u32[]{:S(2)}, u32[]{:S(2)}) %collective-permute-start.1) | collective-permute-done | bytes 131104 | tf_op jit(solution)/shard_map/ppermute | solution.py:154
  19.1 0.0 all-to-all-done.got_ref
  19.1 1.0 %shard_map.65 = bf16[256,256]{1,0:T(8,128)(2,1)S(1)} custom-call(bf16[8,144,256]{2,1,0:T(8,128)(2,1)S(1)} %all-to-all-done.got_ref, bf16[256,256]{1,0:T(8,128)(2,1)S(1)} %collective-permute-done.refs_0_, bf16[256,256]{1,0:T(8,128)(2,1)S(1)} %collective-permute-done.1.refs_1_), custom_call_target="tpu_custom_call" | custom-call | tf_op jit(solution)/shard_map/pallas_call | solution.py:190
  20.2 13.4 %all_to_all.10 = bf16[16,16,256]{2,1,0:T(8,128)(2,1)S(1)} all-to-all(bf16[16,16,256]{2,1,0:T(8,128)(2,1)S(1)} %bitcast.6), channel_id=1, replica_groups=mesh['bin'=16,'wave'=2] {'bin'}, dimensions={0} | all-to-all | bytes 262144 | tf_op jit(solution)/shard_map/all_to_all | solution.py:197
  33.6 0.1 collective-permute-start.2
  33.6 1.2 %collective-permute-done.2.theirs_ref = f32[16,256]{1,0:T(8,128)S(1)} collective-permute-done((f32[16,256]{1,0:T(8,128)S(1)}, f32[16,256]{1,0:T(8,128)S(1)}, u32[]{:S(2)}, u32[]{:S(2)}) %collective-permute-start.2) | collective-permute-done | bytes 16416 | tf_op jit(solution)/shard_map/ppermute | solution.py:209
  34.8 0.0 copy-done
  34.8 1.2 %shard_map.66 = f32[16,4096]{1,0:T(8,128)} custom-call(f32[16,256]{1,0:T(8,128)S(1)} %convert_reduce_fusion.mine_ref, f32[16,256]{1,0:T(8,128)S(1)} %collective-permute-done.2.theirs_ref, bf16[256,4096]{1,0:T(8,128)(2,1)S(1)} %copy-done), custom_call_target="tpu_custom_call" | custom-call | tf_op jit(solution)/shard_map/pallas_call | solution.py:211
  (1 shorter events, 0.0 us)
Async XLA Ops:
  0.0 34.8 %copy-start = (bf16[256,4096]{1,0:T(8,128)(2,1)S(1)}, bf16[256,4096]{1,0:T(8,128)(2,1)}, u32[]{:S(2)}) copy-start(bf16[256,4096]{1,0:T(8,128)(2,1)} %line_ref.1) | copy-start | bytes 6291460
  2.7 16.4 %all-to-all-start = ((bf16[8,144,256]{2,1,0:T(8,128)(2,1)}), bf16[8,144,256]{2,1,0:T(8,128)(2,1)S(1)}, u32[]{:S(2)}, u32[]{:S(2)}) async-start(bf16[8,144,256]{2,1,0:T(8,128)(2,1)} %shard_map.64), calls=%async_computation | async-start | bytes 1179648 | tf_op jit(solution)/shard_map/all_to_all | solution.py:180
  7.9 4.1 %collective-permute-start = (bf16[256,256]{1,0:T(8,128)(2,1)}, bf16[256,256]{1,0:T(8,128)(2,1)S(1)}, u32[]{:S(2)}, u32[]{:S(2)}) collective-permute-start(bf16[256,256]{1,0:T(8,128)(2,1)} %bitcast.10), channel_id=1, source_target_pairs={{0,0},{1,8},{2,2},{3,10},{4,4},{5,12},{6,6},{7,14},{8,1},{9,9},{10... | collective-permute-start | bytes 393224 | tf_op jit(solution)/shard_map/ppermute | solution.py:154
  9.5 9.6 %collective-permute-start.1 = (bf16[256,256]{1,0:T(8,128)(2,1)}, bf16[256,256]{1,0:T(8,128)(2,1)S(1)}, u32[]{:S(2)}, u32[]{:S(2)}) collective-permute-start(bf16[256,256]{1,0:T(8,128)(2,1)} %bitcast.11), channel_id=1, source_target_pairs={{0,16},{1,24},{2,18},{3,26},{4,20},{5,28},{6,22},{7,30},{8,17},{9,... | collective-permute-start | bytes 393224 | tf_op jit(solution)/shard_map/ppermute | solution.py:154
  33.6 1.2 %collective-permute-start.2 = (f32[16,256]{1,0:T(8,128)S(1)}, f32[16,256]{1,0:T(8,128)S(1)}, u32[]{:S(2)}, u32[]{:S(2)}) collective-permute-start(f32[16,256]{1,0:T(8,128)S(1)} %convert_reduce_fusion.mine_ref), channel_id=1, source_target_pairs={{0,1},{1,0},{2,3},{3,2},{4,5},{5,4},{6,7},{7,6},{8,9},{9,8},{10,11... | collective-permute-start | bytes 49160 | tf_op jit(solution)/shard_map/ppermute | solution.py:209

commit v4 on v3

--- a/solution.py
+++ b/solution.py
@@ -25,21 +25,29 @@
     return lax.broadcasted_iota(I32, shape, dim)
 
 
-def pack_kernel(plan, me_ref, src_hbm, den_hbm, bin_hbm, ray_hbm, out_hbm, *scratch):
-    src_ref, den_ref, bin_ref, ray_ref, held, in_sems, out_sems = scratch
+def pack_kernel(plan, me_ref, src_hbm, den_hbm, bin_hbm, ray_hbm, table_hbm, line_hbm, *rest):
+    targets, block = plan.targets, plan.block
+    outs, table_out, line_out = rest[:targets], rest[targets], rest[targets + 1]
+    src_ref, den_ref, bin_ref, ray_ref, sems = rest[targets + 2 :]
     copies = [
-        pltpu.make_async_copy(a, b, in_sems.at[i])
+        pltpu.make_async_copy(a, b, sems.at[i])
         for i, (a, b) in enumerate(
-            ((bin_hbm, bin_ref), (ray_hbm, ray_ref), (den_hbm, den_ref), (src_hbm, src_ref))
+            (
+                (bin_hbm, bin_ref),
+                (ray_hbm, ray_ref),
+                (den_hbm, den_ref),
+                (src_hbm, src_ref),
+                (table_hbm, table_out),
+                (line_hbm, line_out),
+            )
         )
     ]
     for copy in copies:
         copy.start()
     cells, levels = src_ref.shape
-    targets, block = plan.targets, plan.block
     earlier = (iota((cells, cells), 0) < iota((cells, cells), 1)).astype(F32).astype(BF16)
-    held[:, block:, :] = jnp.zeros((targets, META_ROWS, levels), BF16)
-    my_part = me_ref[0] // plan.wave
+    my_high = me_ref[0] // targets
+    my_place = me_ref[0] - my_high * targets
     for copy in copies[:3]:
         copy.wait()
     bins = bin_ref[...]
@@ -47,8 +55,10 @@
     before = jnp.dot(hot.astype(BF16), earlier, preferred_element_type=F32)
     position = jnp.sum(hot * before, axis=0, keepdims=True).astype(I32)
     high = bins // plan.low
-    target = (bins - high * plan.low) * plan.wave + high % plan.wave
-    slot = target * block + ((high // plan.wave) ^ my_part) * plan.capacity + position
+    turn = high ^ my_high
+    core = turn // plan.parts
+    target = ((bins - high * plan.low) * plan.wave + core) ^ my_place
+    slot = target * block + (turn - core * plan.parts) * plan.capacity + position
     rays = ray_ref[...]
     ray_high = rays // RAY_BASE
     ray_low = rays - ray_high * RAY_BASE
@@ -61,35 +71,34 @@
     place = (iota((targets * block, cells), 0) == slot).astype(F32).astype(BF16)
     moved = nt_dot(meta, place).astype(BF16)
     copies[3].wait()
-    src = src_ref[...]
-    leaving = [
-        pltpu.make_async_copy(held.at[t], out_hbm.at[t], out_sems.at[t]) for t in range(targets)
-    ]
+    rows = jnp.dot(place, src_ref[...], preferred_element_type=F32).astype(BF16)
     for t in range(targets):
         first, last = t * block, (t + 1) * block
-        rows = jnp.dot(place[first:last], src, preferred_element_type=F32)
-        held[t, :block, :] = rows.astype(BF16)
-        held[t, block:, :block] = moved[:, first:last]
-        leaving[t].start()
-    for copy in leaving:
+        outs[t][:block, :] = rows[first:last]
+        outs[t][block:, :] = jnp.zeros((META_ROWS, levels), BF16)
+        outs[t][block:, :block] = moved[:, first:last]
+    for copy in copies[4:]:
         copy.wait()
 
 
-def level_kernel(plan, rays, got_ref, *refs):
-    table_refs, out_ref = refs[:-1], refs[-1]
-    targets, block = plan.targets, plan.block
-    meta = [got_ref[s, block:, :block].astype(F32) for s in range(targets)]
+def level_kernel(plan, rays, me_ref, own_ref, *refs):
+    got, table_refs, out_ref = refs[: plan.targets], refs[plan.targets : -1], refs[-1]
+    block = plan.block
+    first_core = me_ref[0] % plan.wave == 0
+    meta = [g[block:, :block].astype(F32) for g in got]
     columns = [jnp.transpose(m[:8]) for m in meta]
     total = jnp.zeros(out_ref.shape, F32)
     for part, table_ref in enumerate(table_refs):
         low, high = part * plan.capacity, (part + 1) * plan.capacity
-        src = got_ref[:, low:high, :].reshape(targets * plan.capacity, got_ref.shape[2])
+        src = jnp.concatenate([g[low:high, :] for g in got], axis=0)
         den = jnp.concatenate([c[low:high, 0:1] for c in columns], axis=0)
         ray = jnp.concatenate(
             [m[1:2, low:high] * RAY_BASE + m[2:3, low:high] for m in meta], axis=1
         ).astype(I32)
         wide = src.astype(F32)
         table = table_ref[...]
+        if part == 0:
+            table = jnp.where(first_core, own_ref[...], table)
         first = (den * jnp.dot(src, table, preferred_element_type=F32) + wide).astype(BF16)
         pops = (den * jnp.dot(first, table, preferred_element_type=F32) + wide).astype(BF16)
         pick = (iota((rays, src.shape[0]), 0) == ray).astype(F32).astype(BF16)
@@ -125,15 +134,15 @@
         for high in range(self.high):
             for low in range(self.low):
                 for core in range(self.wave):
-                    to = self.wave * ((high // self.wave) ^ k) + core
-                    moves.append(
-                        (self.device(high, low, core), self.device(to, low, high % self.wave))
-                    )
+                    turn = core * self.parts + k
+                    if turn:
+                        moves.append(
+                            (self.device(high, low, core), self.device(high ^ turn, low, core))
+                        )
         return moves
 
-    def planes(self):
-        size = self.low * self.wave
-        return [list(range(h * size, (h + 1) * size)) for h in range(self.high)]
+    def plane_moves(self, k):
+        return [(i, i ^ k) for i in range(self.high * self.targets)]
 
 
 def per_device(sources, density, temp_bins, ray_index, rate_tables, line_table):
@@ -146,28 +155,28 @@
     vmem = pl.BlockSpec(memory_space=pltpu.VMEM)
     smem = pl.BlockSpec(memory_space=pltpu.SMEM)
     hbm = pl.BlockSpec(memory_space=pltpu.HBM)
+    both = ("bin", "wave")
 
     def in_hbm(x):
         return pltpu.with_memory_space_constraint(x, pltpu.HBM)
 
     tables = [
-        lax.ppermute(rate_tables[0], ("bin", "wave"), plan.table_moves(k)) for k in range(plan.parts)
-    ]
-    me = (lax.axis_index("bin") // plan.low).astype(I32).reshape(1)
+        lax.ppermute(rate_tables[0], both, plan.table_moves(k)) for k in reversed(range(plan.parts))
+    ][::-1]
+    me = lax.axis_index(both).astype(I32).reshape(1)
     den_rows = cells // min(cells, LANES)
-    outgoing = pl.pallas_call(
+    *outgoing, own, held_line = pl.pallas_call(
         functools.partial(pack_kernel, plan),
-        out_shape=jax.ShapeDtypeStruct((plan.targets, rows, levels), BF16),
-        in_specs=[smem] + [hbm] * 4,
-        out_specs=hbm,
+        out_shape=[jax.ShapeDtypeStruct((rows, levels), BF16)] * plan.targets
+        + [jax.ShapeDtypeStruct(a, BF16) for a in (rate_tables.shape[1:], line_table.shape)],
+        in_specs=[smem] + [hbm] * 6,
+        out_specs=[vmem] * (plan.targets + 2),
         scratch_shapes=[
             pltpu.VMEM((cells, levels), BF16),
             pltpu.VMEM((den_rows, cells // den_rows), BF16),
             pltpu.VMEM((1, cells), I32),
             pltpu.VMEM((1, cells), I32),
-            pltpu.VMEM((plan.targets, rows, levels), BF16),
-            pltpu.SemaphoreType.DMA((4,)),
-            pltpu.SemaphoreType.DMA((plan.targets,)),
+            pltpu.SemaphoreType.DMA((6,)),
         ],
         compiler_params=params,
     )(
@@ -176,24 +185,21 @@
         in_hbm(density.reshape(den_rows, cells // den_rows)),
         in_hbm(temp_bins.reshape(1, cells)),
         in_hbm(ray_index.reshape(1, cells)),
-    )
-    got = lax.all_to_all(
-        outgoing,
-        ("bin", "wave"),
-        split_axis=0,
-        concat_axis=0,
-        tiled=True,
-        axis_index_groups=plan.planes(),
-    )
+        in_hbm(rate_tables[0]),
+        in_hbm(line_table),
+    )
+    got = [outgoing[0]] + [
+        lax.ppermute(outgoing[k], both, plan.plane_moves(k)) for k in range(1, plan.targets)
+    ]
     ray_rows = RAY_DEV
     rays = ray_rows * bin_total
     partial_sums = pl.pallas_call(
         functools.partial(level_kernel, plan, rays),
         out_shape=jax.ShapeDtypeStruct((rays, levels), BF16),
-        in_specs=[vmem] * (1 + plan.parts),
+        in_specs=[smem] + [vmem] * (1 + plan.targets + plan.parts),
         out_specs=vmem,
         compiler_params=params,
-    )(got, *tables)
+    )(me, own, *got, *tables)
     held = lax.all_to_all(
         partial_sums.reshape(bin_total, ray_rows, levels),
         "bin",
@@ -214,7 +220,7 @@
         in_specs=[vmem, vmem, vmem],
         out_specs=vmem,
         compiler_params=params,
-    )(total, theirs, line_table)
+    )(total, theirs, held_line)
 
 
 def solution(mesh):

time: 36.2 us -> 35.9 us (level)
  starting transfers between devices: 9.39 us -> 12.9 us
  waiting for transfers between devices: 8.22 us -> 5.86 us
  Pallas kernels: 4.93 us -> 4.14 us
  blocking collectives: 13.4 us -> 12.7 us
    ppermute x2 -> x9, starting transfers between devices: 4.14 us -> 12.8 us  [the longest x7 10.6 us: per_device(): lax.ppermute(outgoing[k], both, plan.plane_moves(k))]
    all_to_all x1 -> x0, starting transfers between devices: 5.18 us -> none  [per_device(): lax.all_to_all(outgoing, ('bin', 'wave'), split_axis=0, concat_axis=0, ti...]
    ppermute x2 -> x9, waiting for transfers between devices: 7.04 us -> 4.69 us  [the longest x7 4.68 us: per_device(): lax.ppermute(outgoing[k], both, plan.plane_moves(k))]
    pallas_call x1, Pallas kernels: 2.73 us -> 1.94 us  [per_device(): pl.pallas_call(functools.partial(pack_kernel, plan), out_shape=[jax.Shape...]
    all_to_all x1, blocking collectives: 13.4 us -> 12.7 us  [per_device(): lax.all_to_all(partial_sums.reshape(bin_total, ray_rows, levels), 'bin',...]
  transfers between devices with their start and end apart: 4 -> 10, of which waited for: 2 -> 4; matrix products, arithmetic and copies ran while one was open for 0% -> 0% of each run, Pallas kernels for 0% -> 0%
where the time goes in v4:
time: 35.9 us; the launch traced here: 35.7 us
  starting transfers between devices  12.9 us (36%)
  blocking collectives  12.7 us (35%)
  waiting for transfers between devices  5.86 us (16%)
  Pallas kernels  4.14 us (12%)
    all_to_all x1, blocking collectives, per_device(): lax.all_to_all(partial_sums.reshape(bin_total, ray_rows, levels), 'bin',...  12.7 us
    ppermute x7, starting transfers between devices, per_device(): lax.ppermute(outgoing[k], both, plan.plane_moves(k))  10.6 us
    ppermute x7, waiting for transfers between devices, per_device(): lax.ppermute(outgoing[k], both, plan.plane_moves(k))  4.68 us
    ppermute x2, starting transfers between devices, per_device(): lax.ppermute(rate_tables[0], both, plan.table_moves(k))  2.23 us
    pallas_call x1, Pallas kernels, per_device(): pl.pallas_call(functools.partial(pack_kernel, plan), out_shape=[jax.Shape...  1.94 us
    ppermute x1, waiting for transfers between devices, per_device(): lax.ppermute(total, 'wave', [(i, i ^ step) for i in range(wave_total)])  1.17 us
    pallas_call x1, Pallas kernels, per_device(): pl.pallas_call(line_kernel, out_shape=jax.ShapeDtypeStruct((ray_rows, lin...  1.17 us
    pallas_call x1, Pallas kernels, per_device(): pl.pallas_call(functools.partial(level_kernel, plan, rays), out_shape=jax...  1.04 us
  transfers between devices with their start and end apart: 10, of which 4 were waited for; matrix products, arithmetic and copies ran while one was open for 0% of the time, Pallas kernels for 0%

profile of v4, /device:TPU:0, one launch (start us, length us, event | category | flops | bytes accessed | tf_op | source)
XLA Modules:
  0.0 35.7 jit_solution(376767907633062264)
XLA Ops:
  0.0 0.0 copy-start
  0.0 1.9 %shard_map.64 = (bf16[144,256]{1,0:T(8,128)(2,1)S(1)}, bf16[144,256]{1,0:T(8,128)(2,1)S(1)}, bf16[144,256]{1,0:T(8,128)(2,1)S(1)}, bf16[144,256]{1,0:T(8,128)(2,...) custom-call(s32[1]{0:T(128)} %bitcast.me_ref, ...), custom_call_target="tpu_custom_call" | custom-call | tf_op jit(solution)/shard_map/pallas_call | solution.py:168
  1.9 0.5 %collective-permute-start = (bf16[144,256]{1,0:T(8,128)(2,1)S(1)}, bf16[144,256]{1,0:T(8,128)(2,1)S(1)}, u32[]{:S(2)}, u32[]{:S(2)}) collective-permute-start(bf16[144,256]{1,0:T(8,128)(2,1)S(1)} %get-tuple-element.17), channel_id=1, source_target_pairs={{0,1},{1,0},{2,3},{3,2},{4,5},{5,4},{6,7},{7,6},{8,9},{9,8},{10,11... | collective-permute-start | bytes 221192 | tf_op jit(solution)/shard_map/ppermute | solution.py:192
  2.5 2.6 %collective-permute-start.1 = (bf16[144,256]{1,0:T(8,128)(2,1)S(1)}, bf16[144,256]{1,0:T(8,128)(2,1)S(1)}, u32[]{:S(2)}, u32[]{:S(2)}) collective-permute-start(bf16[144,256]{1,0:T(8,128)(2,1)S(1)} %get-tuple-element.18), channel_id=1, source_target_pairs={{0,2},{1,3},{2,0},{3,1},{4,6},{5,7},{6,4},{7,5},{8,10},{9,11},{10,... | collective-permute-start | bytes 221192 | tf_op jit(solution)/shard_map/ppermute | solution.py:192
  5.0 0.1 collective-permute-start.2
  5.1 1.8 %collective-permute-start.3 = (bf16[144,256]{1,0:T(8,128)(2,1)S(1)}, bf16[144,256]{1,0:T(8,128)(2,1)S(1)}, u32[]{:S(2)}, u32[]{:S(2)}) collective-permute-start(bf16[144,256]{1,0:T(8,128)(2,1)S(1)} %get-tuple-element.20), channel_id=1, source_target_pairs={{0,4},{1,5},{2,6},{3,7},{4,0},{5,1},{6,2},{7,3},{8,12},{9,13},{10,... | collective-permute-start | bytes 221192 | tf_op jit(solution)/shard_map/ppermute | solution.py:192
  6.9 0.0 copy-done
  6.9 1.6 %collective-permute-start.8 = (bf16[256,256]{1,0:T(8,128)(2,1)S(1)}, bf16[256,256]{1,0:T(8,128)(2,1)S(1)}, u32[]{:S(2)}, u32[]{:S(2)}) collective-permute-start(bf16[256,256]{1,0:T(8,128)(2,1)S(1)} %bitcast.8), channel_id=1, source_target_pairs={{0,8},{1,25},{2,10},{3,27},{4,12},{5,29},{6,14},{7,31},{8,0},{9,17... | collective-permute-start | bytes 393224 | tf_op jit(solution)/shard_map/ppermute | solution.py:164
  8.4 0.0 collective-permute-done.refs_1_
  8.4 0.7 %collective-permute-start.7 = (bf16[256,256]{1,0:T(8,128)(2,1)S(1)}, bf16[256,256]{1,0:T(8,128)(2,1)S(1)}, u32[]{:S(2)}, u32[]{:S(2)}) collective-permute-start(bf16[256,256]{1,0:T(8,128)(2,1)S(1)} %bitcast.9), channel_id=1, source_target_pairs={{1,17},{3,19},{5,21},{7,23},{9,25},{11,27},{13,29},{15,31},{17,1},... | collective-permute-start | bytes 393224 | tf_op jit(solution)/shard_map/ppermute | solution.py:164
  9.1 0.0 collective-permute-done.1.refs_2_
  9.1 3.2 %collective-permute-start.4 = (bf16[144,256]{1,0:T(8,128)(2,1)S(1)}, bf16[144,256]{1,0:T(8,128)(2,1)S(1)}, u32[]{:S(2)}, u32[]{:S(2)}) collective-permute-start(bf16[144,256]{1,0:T(8,128)(2,1)S(1)} %get-tuple-element.21), channel_id=1, source_target_pairs={{0,5},{1,4},{2,7},{3,6},{4,1},{5,0},{6,3},{7,2},{8,13},{9,12},{10,... | collective-permute-start | bytes 221192 | tf_op jit(solution)/shard_map/ppermute | solution.py:192
  12.4 0.0 collective-permute-done.2.refs_3_
  12.4 2.4 %collective-permute-start.5 = (bf16[144,256]{1,0:T(8,128)(2,1)S(1)}, bf16[144,256]{1,0:T(8,128)(2,1)S(1)}, u32[]{:S(2)}, u32[]{:S(2)}) collective-permute-start(bf16[144,256]{1,0:T(8,128)(2,1)S(1)} %get-tuple-element.22), channel_id=1, source_target_pairs={{0,6},{1,7},{2,4},{3,5},{4,2},{5,3},{6,0},{7,1},{8,14},{9,15},{10,... | collective-permute-start | bytes 221192 | tf_op jit(solution)/shard_map/ppermute | solution.py:192
  14.8 0.0 collective-permute-done.3.refs_4_
  14.8 0.0 collective-permute-start.6
  14.8 0.2 collective-permute-done.4.refs_5_
  15.0 2.6 %collective-permute-done.5.refs_6_ = bf16[144,256]{1,0:T(8,128)(2,1)S(1)} collective-permute-done((bf16[144,256]{1,0:T(8,128)(2,1)S(1)}, bf16[144,256]{1,0:T(8,128)(2,1)S(1)}, u32[]{:S(2)}, u32[]{:S(2)}) %collective-permute-start.5) | collective-permute-done | bytes 73760 | tf_op jit(solution)/shard_map/ppermute | solution.py:192
  17.7 1.8 %collective-permute-done.6.refs_7_ = bf16[144,256]{1,0:T(8,128)(2,1)S(1)} collective-permute-done((bf16[144,256]{1,0:T(8,128)(2,1)S(1)}, bf16[144,256]{1,0:T(8,128)(2,1)S(1)}, u32[]{:S(2)}, u32[]{:S(2)}) %collective-permute-start.6) | collective-permute-done | bytes 73760 | tf_op jit(solution)/shard_map/ppermute | solution.py:192
  19.5 0.0 collective-permute-done.8.refs_9_
  19.5 0.0 collective-permute-done.7.refs_8_
  19.5 1.0 %shard_map.65 = bf16[256,256]{1,0:T(8,128)(2,1)S(1)} custom-call(s32[1]{0:T(128)} %bitcast.me_ref, bf16[256,256]{1,0:T(8,128)(2,1)S(1)} %get-tuple-element.15.own_ref, bf16[144,256]{1,0:T(8,128)(2,1)S(1)} %get-tuple-element.16.refs_0_, bf16[144,256]{1,0:T(8,128)(2,1)S(1)} %collective-permute-done.refs_1_, ...), custom_call_target="tpu_custom_call" | custom-call | tf_op jit(solution)/shard_map/pallas_call | solution.py:196
  20.5 12.7 %all_to_all.5 = bf16[16,16,256]{2,1,0:T(8,128)(2,1)S(1)} all-to-all(bf16[16,16,256]{2,1,0:T(8,128)(2,1)S(1)} %bitcast.6), channel_id=1, replica_groups=mesh['bin'=16,'wave'=2] {'bin'}, dimensions={0} | all-to-all | bytes 262144 | tf_op jit(solution)/shard_map/all_to_all | solution.py:203
  33.3 0.1 collective-permute-start.9
  33.4 1.2 %collective-permute-done.9.theirs_ref = f32[16,256]{1,0:T(8,128)S(1)} collective-permute-done((f32[16,256]{1,0:T(8,128)S(1)}, f32[16,256]{1,0:T(8,128)S(1)}, u32[]{:S(2)}, u32[]{:S(2)}) %collective-permute-start.9) | collective-permute-done | bytes 16416 | tf_op jit(solution)/shard_map/ppermute | solution.py:215
  34.5 1.2 %shard_map.66 = f32[16,4096]{1,0:T(8,128)} custom-call(f32[16,256]{1,0:T(8,128)S(1)} %convert_reduce_fusion.mine_ref, f32[16,256]{1,0:T(8,128)S(1)} %collective-permute-done.9.theirs_ref, bf16[256,4096]{1,0:T(8,128)(2,1)S(1)} %get-tuple-element.24.line_ref), custom_call_target="tpu_custom_call" | custom-call | tf_op jit(solution)/shard_map/pallas_call | solution.py:217
  (1 shorter events, 0.0 us)
Async XLA Ops:
  0.0 6.9 %copy-start = (bf16[1,256,256]{2,1,0:T(8,128)(2,1)S(1)}, bf16[1,256,256]{2,1,0:T(8,128)(2,1)}, u32[]{:S(2)}) copy-start(bf16[1,256,256]{2,1,0:T(8,128)(2,1)} %param.10) | copy-start | bytes 393220
  1.9 6.5 %collective-permute-start = (bf16[144,256]{1,0:T(8,128)(2,1)S(1)}, bf16[144,256]{1,0:T(8,128)(2,1)S(1)}, u32[]{:S(2)}, u32[]{:S(2)}) collective-permute-start(bf16[144,256]{1,0:T(8,128)(2,1)S(1)} %get-tuple-element.17), channel_id=1, source_target_pairs={{0,1},{1,0},{2,3},{3,2},{4,5},{5,4},{6,7},{7,6},{8,9},{9,8},{10,11... | collective-permute-start | bytes 221192 | tf_op jit(solution)/shard_map/ppermute | solution.py:192
  2.5 6.6 %collective-permute-start.1 = (bf16[144,256]{1,0:T(8,128)(2,1)S(1)}, bf16[144,256]{1,0:T(8,128)(2,1)S(1)}, u32[]{:S(2)}, u32[]{:S(2)}) collective-permute-start(bf16[144,256]{1,0:T(8,128)(2,1)S(1)} %get-tuple-element.18), channel_id=1, source_target_pairs={{0,2},{1,3},{2,0},{3,1},{4,6},{5,7},{6,4},{7,5},{8,10},{9,11},{10,... | collective-permute-start | bytes 221192 | tf_op jit(solution)/shard_map/ppermute | solution.py:192
  5.0 7.3 %collective-permute-start.2 = (bf16[144,256]{1,0:T(8,128)(2,1)S(1)}, bf16[144,256]{1,0:T(8,128)(2,1)S(1)}, u32[]{:S(2)}, u32[]{:S(2)}) collective-permute-start(bf16[144,256]{1,0:T(8,128)(2,1)S(1)} %get-tuple-element.19), channel_id=1, source_target_pairs={{0,3},{1,2},{2,1},{3,0},{4,7},{5,6},{6,5},{7,4},{8,11},{9,10},{10,... | collective-permute-start | bytes 221192 | tf_op jit(solution)/shard_map/ppermute | solution.py:192
  5.1 9.7 %collective-permute-start.3 = (bf16[144,256]{1,0:T(8,128)(2,1)S(1)}, bf16[144,256]{1,0:T(8,128)(2,1)S(1)}, u32[]{:S(2)}, u32[]{:S(2)}) collective-permute-start(bf16[144,256]{1,0:T(8,128)(2,1)S(1)} %get-tuple-element.20), channel_id=1, source_target_pairs={{0,4},{1,5},{2,6},{3,7},{4,0},{5,1},{6,2},{7,3},{8,12},{9,13},{10,... | collective-permute-start | bytes 221192 | tf_op jit(solution)/shard_map/ppermute | solution.py:192
  6.9 12.6 %collective-permute-start.8 = (bf16[256,256]{1,0:T(8,128)(2,1)S(1)}, bf16[256,256]{1,0:T(8,128)(2,1)S(1)}, u32[]{:S(2)}, u32[]{:S(2)}) collective-permute-start(bf16[256,256]{1,0:T(8,128)(2,1)S(1)} %bitcast.8), channel_id=1, source_target_pairs={{0,8},{1,25},{2,10},{3,27},{4,12},{5,29},{6,14},{7,31},{8,0},{9,17... | collective-permute-start | bytes 393224 | tf_op jit(solution)/shard_map/ppermute | solution.py:164
  8.4 11.1 %collective-permute-start.7 = (bf16[256,256]{1,0:T(8,128)(2,1)S(1)}, bf16[256,256]{1,0:T(8,128)(2,1)S(1)}, u32[]{:S(2)}, u32[]{:S(2)}) collective-permute-start(bf16[256,256]{1,0:T(8,128)(2,1)S(1)} %bitcast.9), channel_id=1, source_target_pairs={{1,17},{3,19},{5,21},{7,23},{9,25},{11,27},{13,29},{15,31},{17,1},... | collective-permute-start | bytes 393224 | tf_op jit(solution)/shard_map/ppermute | solution.py:164
  9.1 5.9 %collective-permute-start.4 = (bf16[144,256]{1,0:T(8,128)(2,1)S(1)}, bf16[144,256]{1,0:T(8,128)(2,1)S(1)}, u32[]{:S(2)}, u32[]{:S(2)}) collective-permute-start(bf16[144,256]{1,0:T(8,128)(2,1)S(1)} %get-tuple-element.21), channel_id=1, source_target_pairs={{0,5},{1,4},{2,7},{3,6},{4,1},{5,0},{6,3},{7,2},{8,13},{9,12},{10,... | collective-permute-start | bytes 221192 | tf_op jit(solution)/shard_map/ppermute | solution.py:192
  12.4 5.3 %collective-permute-start.5 = (bf16[144,256]{1,0:T(8,128)(2,1)S(1)}, bf16[144,256]{1,0:T(8,128)(2,1)S(1)}, u32[]{:S(2)}, u32[]{:S(2)}) collective-permute-start(bf16[144,256]{1,0:T(8,128)(2,1)S(1)} %get-tuple-element.22), channel_id=1, source_target_pairs={{0,6},{1,7},{2,4},{3,5},{4,2},{5,3},{6,0},{7,1},{8,14},{9,15},{10,... | collective-permute-start | bytes 221192 | tf_op jit(solution)/shard_map/ppermute | solution.py:192
  14.8 4.7 %collective-permute-start.6 = (bf16[144,256]{1,0:T(8,128)(2,1)S(1)}, bf16[144,256]{1,0:T(8,128)(2,1)S(1)}, u32[]{:S(2)}, u32[]{:S(2)}) collective-permute-start(bf16[144,256]{1,0:T(8,128)(2,1)S(1)} %get-tuple-element.23), channel_id=1, source_target_pairs={{0,7},{1,6},{2,5},{3,4},{4,3},{5,2},{6,1},{7,0},{8,15},{9,14},{10,... | collective-permute-start | bytes 221192 | tf_op jit(solution)/shard_map/ppermute | solution.py:192
  33.3 1.2 %collective-permute-start.9 = (f32[16,256]{1,0:T(8,128)S(1)}, f32[16,256]{1,0:T(8,128)S(1)}, u32[]{:S(2)}, u32[]{:S(2)}) collective-permute-start(f32[16,256]{1,0:T(8,128)S(1)} %convert_reduce_fusion.mine_ref), channel_id=1, source_target_pairs={{0,1},{1,0},{2,3},{3,2},{4,5},{5,4},{6,7},{7,6},{8,9},{9,8},{10,11... | collective-permute-start | bytes 49160 | tf_op jit(solution)/shard_map/ppermute | solution.py:215

commit v5 on v4

--- a/solution.py
+++ b/solution.py
@@ -11,6 +11,7 @@
 META_ROWS = 16
 RAY_BASE = 32
 LANES = 128
+OVERLAP_FLOPS = 10**10
 VMEM_LIMIT = 32 * 1024 * 1024
 F32 = jnp.float32
 BF16 = jnp.bfloat16
@@ -81,10 +82,16 @@
         copy.wait()
 
 
-def level_kernel(plan, rays, me_ref, own_ref, *refs):
+def choose_kernel(plan, me_ref, own_ref, *refs):
+    tables, outs = refs[: plan.parts], refs[plan.parts :]
+    outs[0][...] = jnp.where(me_ref[0] % plan.wave == 0, own_ref[...], tables[0][...])
+    for table, out in zip(tables[1:], outs[1:]):
+        out[...] = table[...]
+
+
+def level_kernel(plan, rays, *refs):
     got, table_refs, out_ref = refs[: plan.targets], refs[plan.targets : -1], refs[-1]
     block = plan.block
-    first_core = me_ref[0] % plan.wave == 0
     meta = [g[block:, :block].astype(F32) for g in got]
     columns = [jnp.transpose(m[:8]) for m in meta]
     total = jnp.zeros(out_ref.shape, F32)
@@ -97,8 +104,6 @@
         ).astype(I32)
         wide = src.astype(F32)
         table = table_ref[...]
-        if part == 0:
-            table = jnp.where(first_core, own_ref[...], table)
         first = (den * jnp.dot(src, table, preferred_element_type=F32) + wide).astype(BF16)
         pops = (den * jnp.dot(first, table, preferred_element_type=F32) + wide).astype(BF16)
         pick = (iota((rays, src.shape[0]), 0) == ray).astype(F32).astype(BF16)
@@ -140,6 +145,10 @@
                             (self.device(high, low, core), self.device(high ^ turn, low, core))
                         )
         return moves
+
+    def order(self):
+        across = range(self.wave, self.targets)
+        return sorted(across, key=lambda k: (k % self.wave, k)) + list(range(1, self.wave))
 
     def plane_moves(self, k):
         return [(i, i ^ k) for i in range(self.high * self.targets)]
@@ -188,18 +197,28 @@
         in_hbm(rate_tables[0]),
         in_hbm(line_table),
     )
-    got = [outgoing[0]] + [
-        lax.ppermute(outgoing[k], both, plan.plane_moves(k)) for k in range(1, plan.targets)
-    ]
+    got = list(outgoing)
+    for k in plan.order():
+        got[k] = lax.ppermute(outgoing[k], both, plan.plane_moves(k))
+    tables = pl.pallas_call(
+        functools.partial(choose_kernel, plan),
+        out_shape=[jax.ShapeDtypeStruct(rate_tables.shape[1:], BF16)] * plan.parts,
+        in_specs=[smem] + [vmem] * (1 + plan.parts),
+        out_specs=[vmem] * plan.parts,
+        compiler_params=params,
+        cost_estimate=pl.CostEstimate(
+            flops=OVERLAP_FLOPS, bytes_accessed=2 * own.size * 2 * plan.parts, transcendentals=0
+        ),
+    )(me, own, *tables)
     ray_rows = RAY_DEV
     rays = ray_rows * bin_total
     partial_sums = pl.pallas_call(
         functools.partial(level_kernel, plan, rays),
         out_shape=jax.ShapeDtypeStruct((rays, levels), BF16),
-        in_specs=[smem] + [vmem] * (1 + plan.targets + plan.parts),
+        in_specs=[vmem] * (plan.targets + plan.parts),
         out_specs=vmem,
         compiler_params=params,
-    )(me, own, *got, *tables)
+    )(*got, *tables)
     held = lax.all_to_all(
         partial_sums.reshape(bin_total, ray_rows, levels),
         "bin",

time: 35.9 us -> 37.8 us (1.053)
  waiting for transfers between devices: 5.86 us -> 6.8 us
  starting transfers between devices: 12.9 us -> 13.5 us
    ppermute x2, starting transfers between devices: 2.23 us -> 3.68 us  [per_device(): lax.ppermute(rate_tables[0], both, plan.table_moves(k))]
    ppermute x7, waiting for transfers between devices: 4.68 us -> 5.62 us  [per_device(): got[k] = lax.ppermute(outgoing[k], both, plan.plane_moves(k))]
    ppermute x7, starting transfers between devices: 10.6 us -> 9.8 us  [per_device(): got[k] = lax.ppermute(outgoing[k], both, plan.plane_moves(k))]
  transfers between devices with their start and end apart: 10 -> 10, of which waited for: 4 -> 5; matrix products, arithmetic and copies ran while one was open for 0% -> 0% of each run, Pallas kernels for 0% -> 5%
where the time goes in v5:
time: 37.8 us; the launch traced here: 37.6 us
  starting transfers between devices  13.5 us (36%)
  blocking collectives  13 us (34%)
  waiting for transfers between devices  6.8 us (18%)
  Pallas kernels  4.14 us (11%)
    all_to_all x1, blocking collectives, per_device(): lax.all_to_all(partial_sums.reshape(bin_total, ray_rows, levels), 'bin',...  13 us
    ppermute x7, starting transfers between devices, per_device(): got[k] = lax.ppermute(outgoing[k], both, plan.plane_moves(k))  9.8 us
    ppermute x7, waiting for transfers between devices, per_device(): got[k] = lax.ppermute(outgoing[k], both, plan.plane_moves(k))  5.62 us
    ppermute x2, starting transfers between devices, per_device(): lax.ppermute(rate_tables[0], both, plan.table_moves(k))  3.68 us
    pallas_call x1, Pallas kernels, per_device(): pl.pallas_call(functools.partial(pack_kernel, plan), out_shape=[jax.Shape...  1.9 us
    ppermute x1, waiting for transfers between devices, per_device(): lax.ppermute(total, 'wave', [(i, i ^ step) for i in range(wave_total)])  1.17 us
    pallas_call x1, Pallas kernels, per_device(): pl.pallas_call(line_kernel, out_shape=jax.ShapeDtypeStruct((ray_rows, lin...  1.17 us
    pallas_call x1, Pallas kernels, per_device(): pl.pallas_call(functools.partial(level_kernel, plan, rays), out_shape=jax...  1.04 us
  transfers between devices with their start and end apart: 10, of which 5 were waited for; matrix products, arithmetic and copies ran while one was open for 0% of the time, Pallas kernels for 5%

profile of v5, /device:TPU:0, one launch (start us, length us, event | category | flops | bytes accessed | tf_op | source)
XLA Modules:
  0.0 37.6 jit_solution(4778213376557282695)
XLA Ops:
  0.0 3.0 %collective-permute-start.8 = (bf16[256,256]{1,0:T(8,128)(2,1)}, bf16[256,256]{1,0:T(8,128)(2,1)S(1)}, u32[]{:S(2)}, u32[]{:S(2)}) collective-permute-start(bf16[256,256]{1,0:T(8,128)(2,1)} %bitcast.7), channel_id=1, source_target_pairs={{0,8},{1,25},{2,10},{3,27},{4,12},{5,29},{6,14},{7,31},{8,0},{9,17... | collective-permute-start | bytes 393224 | tf_op jit(solution)/shard_map/ppermute | solution.py:173
  3.0 0.7 %collective-permute-start.7 = (bf16[256,256]{1,0:T(8,128)(2,1)}, bf16[256,256]{1,0:T(8,128)(2,1)S(1)}, u32[]{:S(2)}, u32[]{:S(2)}) collective-permute-start(bf16[256,256]{1,0:T(8,128)(2,1)} %bitcast.8), channel_id=1, source_target_pairs={{1,17},{3,19},{5,21},{7,23},{9,25},{11,27},{13,29},{15,31},{17,1},... | collective-permute-start | bytes 393224 | tf_op jit(solution)/shard_map/ppermute | solution.py:173
  3.7 1.9 %shard_map.64 = (bf16[144,256]{1,0:T(8,128)(2,1)S(1)}, bf16[144,256]{1,0:T(8,128)(2,1)S(1)}, bf16[144,256]{1,0:T(8,128)(2,1)S(1)}, bf16[144,256]{1,0:T(8,128)(2,...) custom-call(s32[1]{0:T(128)} %bitcast.me_ref, ...), custom_call_target="tpu_custom_call" | custom-call | tf_op jit(solution)/shard_map/pallas_call | solution.py:177
  5.6 2.9 %collective-permute-start = (bf16[144,256]{1,0:T(8,128)(2,1)S(1)}, bf16[144,256]{1,0:T(8,128)(2,1)S(1)}, u32[]{:S(2)}, u32[]{:S(2)}) collective-permute-start(bf16[144,256]{1,0:T(8,128)(2,1)S(1)} %get-tuple-element.18), channel_id=1, source_target_pairs={{0,1},{1,0},{2,3},{3,2},{4,5},{5,4},{6,7},{7,6},{8,9},{9,8},{10,11... | collective-permute-start | bytes 221192 | tf_op jit(solution)/shard_map/ppermute | solution.py:202
  8.5 1.5 %collective-permute-start.1 = (bf16[144,256]{1,0:T(8,128)(2,1)S(1)}, bf16[144,256]{1,0:T(8,128)(2,1)S(1)}, u32[]{:S(2)}, u32[]{:S(2)}) collective-permute-start(bf16[144,256]{1,0:T(8,128)(2,1)S(1)} %get-tuple-element.19), channel_id=1, source_target_pairs={{0,2},{1,3},{2,0},{3,1},{4,6},{5,7},{6,4},{7,5},{8,10},{9,11},{10,... | collective-permute-start | bytes 221192 | tf_op jit(solution)/shard_map/ppermute | solution.py:202
  10.0 0.0 collective-permute-start.2
  10.0 0.0 collective-permute-done.refs_1_
  10.0 1.5 %collective-permute-start.3 = (bf16[144,256]{1,0:T(8,128)(2,1)S(1)}, bf16[144,256]{1,0:T(8,128)(2,1)S(1)}, u32[]{:S(2)}, u32[]{:S(2)}) collective-permute-start(bf16[144,256]{1,0:T(8,128)(2,1)S(1)} %get-tuple-element.21), channel_id=1, source_target_pairs={{0,4},{1,5},{2,6},{3,7},{4,0},{5,1},{6,2},{7,3},{8,12},{9,13},{10,... | collective-permute-start | bytes 221192 | tf_op jit(solution)/shard_map/ppermute | solution.py:202
  11.5 1.3 %collective-permute-done.1.refs_2_ = bf16[144,256]{1,0:T(8,128)(2,1)S(1)} collective-permute-done((bf16[144,256]{1,0:T(8,128)(2,1)S(1)}, bf16[144,256]{1,0:T(8,128)(2,1)S(1)}, u32[]{:S(2)}, u32[]{:S(2)}) %collective-permute-start.1) | collective-permute-done | bytes 73760 | tf_op jit(solution)/shard_map/ppermute | solution.py:202
  12.9 0.1 collective-permute-start.4
  12.9 0.0 collective-permute-done.8.refs_1_
  12.9 3.1 %collective-permute-start.5 = (bf16[144,256]{1,0:T(8,128)(2,1)S(1)}, bf16[144,256]{1,0:T(8,128)(2,1)S(1)}, u32[]{:S(2)}, u32[]{:S(2)}) collective-permute-start(bf16[144,256]{1,0:T(8,128)(2,1)S(1)} %get-tuple-element.23), channel_id=1, source_target_pairs={{0,6},{1,7},{2,4},{3,5},{4,2},{5,3},{6,0},{7,1},{8,14},{9,15},{10,... | collective-permute-start | bytes 221192 | tf_op jit(solution)/shard_map/ppermute | solution.py:202
  16.1 0.0 collective-permute-done.7.refs_0_
  16.1 0.7 %collective-permute-start.6 = (bf16[144,256]{1,0:T(8,128)(2,1)S(1)}, bf16[144,256]{1,0:T(8,128)(2,1)S(1)}, u32[]{:S(2)}, u32[]{:S(2)}) collective-permute-start(bf16[144,256]{1,0:T(8,128)(2,1)S(1)} %get-tuple-element.24), channel_id=1, source_target_pairs={{0,7},{1,6},{2,5},{3,4},{4,3},{5,2},{6,1},{7,0},{8,15},{9,14},{10,... | collective-permute-start | bytes 221192 | tf_op jit(solution)/shard_map/ppermute | solution.py:202
  16.8 0.0 collective-permute-done.2.refs_3_
  16.8 0.0 collective-permute-done.3.refs_4_
  16.8 0.5 %collective-permute-done.4.refs_5_ = bf16[144,256]{1,0:T(8,128)(2,1)S(1)} collective-permute-done((bf16[144,256]{1,0:T(8,128)(2,1)S(1)}, bf16[144,256]{1,0:T(8,128)(2,1)S(1)}, u32[]{:S(2)}, u32[]{:S(2)}) %collective-permute-start.4) | collective-permute-done | bytes 73760 | tf_op jit(solution)/shard_map/ppermute | solution.py:202
  17.3 1.5 %collective-permute-done.5.refs_6_ = bf16[144,256]{1,0:T(8,128)(2,1)S(1)} collective-permute-done((bf16[144,256]{1,0:T(8,128)(2,1)S(1)}, bf16[144,256]{1,0:T(8,128)(2,1)S(1)}, u32[]{:S(2)}, u32[]{:S(2)}) %collective-permute-start.5) | collective-permute-done | bytes 73760 | tf_op jit(solution)/shard_map/ppermute | solution.py:202
  18.9 2.2 %collective-permute-done.6.refs_7_ = bf16[144,256]{1,0:T(8,128)(2,1)S(1)} collective-permute-done((bf16[144,256]{1,0:T(8,128)(2,1)S(1)}, bf16[144,256]{1,0:T(8,128)(2,1)S(1)}, u32[]{:S(2)}, u32[]{:S(2)}) %collective-permute-start.6) | collective-permute-done | bytes 73760 | tf_op jit(solution)/shard_map/ppermute | solution.py:202
  21.1 1.0 %shard_map.66 = bf16[256,256]{1,0:T(8,128)(2,1)S(1)} custom-call(bf16[144,256]{1,0:T(8,128)(2,1)S(1)} %get-tuple-element.17.refs_0_, bf16[144,256]{1,0:T(8,128)(2,1)S(1)} %collective-permute-done.refs_1_, bf16[144,256]{1,0:T(8,128)(2,1)S(1)} %collective-permute-done.1.refs_2_, bf16[144,256]{1,0:T(8,128)(2,1)S(1)} %collective-permute-done.2.refs_3_, ...), custom_call_target="tpu_custom_call" | custom-call | tf_op jit(solution)/shard_map/pallas_call | solution.py:215
  22.1 13.0 %all_to_all.5 = bf16[16,16,256]{2,1,0:T(8,128)(2,1)S(1)} all-to-all(bf16[16,16,256]{2,1,0:T(8,128)(2,1)S(1)} %bitcast.6), channel_id=1, replica_groups=mesh['bin'=16,'wave'=2] {'bin'}, dimensions={0} | all-to-all | bytes 262144 | tf_op jit(solution)/shard_map/all_to_all | solution.py:222
  35.2 0.1 collective-permute-start.9
  35.3 1.2 %collective-permute-done.9.theirs_ref = f32[16,256]{1,0:T(8,128)S(1)} collective-permute-done((f32[16,256]{1,0:T(8,128)S(1)}, f32[16,256]{1,0:T(8,128)S(1)}, u32[]{:S(2)}, u32[]{:S(2)}) %collective-permute-start.9) | collective-permute-done | bytes 16416 | tf_op jit(solution)/shard_map/ppermute | solution.py:234
  36.4 1.2 %shard_map.67 = f32[16,4096]{1,0:T(8,128)} custom-call(f32[16,256]{1,0:T(8,128)S(1)} %convert_reduce_fusion.mine_ref, f32[16,256]{1,0:T(8,128)S(1)} %collective-permute-done.9.theirs_ref, bf16[256,4096]{1,0:T(8,128)(2,1)S(1)} %get-tuple-element.28.line_ref), custom_call_target="tpu_custom_call" | custom-call | tf_op jit(solution)/shard_map/pallas_call | solution.py:236
  (2 shorter events, 0.1 us)
Async XLA Ops:
  0.0 12.9 %collective-permute-start.8 = (bf16[256,256]{1,0:T(8,128)(2,1)}, bf16[256,256]{1,0:T(8,128)(2,1)S(1)}, u32[]{:S(2)}, u32[]{:S(2)}) collective-permute-start(bf16[256,256]{1,0:T(8,128)(2,1)} %bitcast.7), channel_id=1, source_target_pairs={{0,8},{1,25},{2,10},{3,27},{4,12},{5,29},{6,14},{7,31},{8,0},{9,17... | collective-permute-start | bytes 393224 | tf_op jit(solution)/shard_map/ppermute | solution.py:173
  3.0 13.0 %collective-permute-start.7 = (bf16[256,256]{1,0:T(8,128)(2,1)}, bf16[256,256]{1,0:T(8,128)(2,1)S(1)}, u32[]{:S(2)}, u32[]{:S(2)}) collective-permute-start(bf16[256,256]{1,0:T(8,128)(2,1)} %bitcast.8), channel_id=1, source_target_pairs={{1,17},{3,19},{5,21},{7,23},{9,25},{11,27},{13,29},{15,31},{17,1},... | collective-permute-start | bytes 393224 | tf_op jit(solution)/shard_map/ppermute | solution.py:173
  5.6 4.4 %collective-permute-start = (bf16[144,256]{1,0:T(8,128)(2,1)S(1)}, bf16[144,256]{1,0:T(8,128)(2,1)S(1)}, u32[]{:S(2)}, u32[]{:S(2)}) collective-permute-start(bf16[144,256]{1,0:T(8,128)(2,1)S(1)} %get-tuple-element.18), channel_id=1, source_target_pairs={{0,1},{1,0},{2,3},{3,2},{4,5},{5,4},{6,7},{7,6},{8,9},{9,8},{10,11... | collective-permute-start | bytes 221192 | tf_op jit(solution)/shard_map/ppermute | solution.py:202
  8.5 4.4 %collective-permute-start.1 = (bf16[144,256]{1,0:T(8,128)(2,1)S(1)}, bf16[144,256]{1,0:T(8,128)(2,1)S(1)}, u32[]{:S(2)}, u32[]{:S(2)}) collective-permute-start(bf16[144,256]{1,0:T(8,128)(2,1)S(1)} %get-tuple-element.19), channel_id=1, source_target_pairs={{0,2},{1,3},{2,0},{3,1},{4,6},{5,7},{6,4},{7,5},{8,10},{9,11},{10,... | collective-permute-start | bytes 221192 | tf_op jit(solution)/shard_map/ppermute | solution.py:202
  10.0 6.8 %collective-permute-start.2 = (bf16[144,256]{1,0:T(8,128)(2,1)S(1)}, bf16[144,256]{1,0:T(8,128)(2,1)S(1)}, u32[]{:S(2)}, u32[]{:S(2)}) collective-permute-start(bf16[144,256]{1,0:T(8,128)(2,1)S(1)} %get-tuple-element.20), channel_id=1, source_target_pairs={{0,3},{1,2},{2,1},{3,0},{4,7},{5,6},{6,5},{7,4},{8,11},{9,10},{10,... | collective-permute-start | bytes 221192 | tf_op jit(solution)/shard_map/ppermute | solution.py:202
  10.0 6.8 %collective-permute-start.3 = (bf16[144,256]{1,0:T(8,128)(2,1)S(1)}, bf16[144,256]{1,0:T(8,128)(2,1)S(1)}, u32[]{:S(2)}, u32[]{:S(2)}) collective-permute-start(bf16[144,256]{1,0:T(8,128)(2,1)S(1)} %get-tuple-element.21), channel_id=1, source_target_pairs={{0,4},{1,5},{2,6},{3,7},{4,0},{5,1},{6,2},{7,3},{8,12},{9,13},{10,... | collective-permute-start | bytes 221192 | tf_op jit(solution)/shard_map/ppermute | solution.py:202
  12.9 4.5 %collective-permute-start.4 = (bf16[144,256]{1,0:T(8,128)(2,1)S(1)}, bf16[144,256]{1,0:T(8,128)(2,1)S(1)}, u32[]{:S(2)}, u32[]{:S(2)}) collective-permute-start(bf16[144,256]{1,0:T(8,128)(2,1)S(1)} %get-tuple-element.22), channel_id=1, source_target_pairs={{0,5},{1,4},{2,7},{3,6},{4,1},{5,0},{6,3},{7,2},{8,13},{9,12},{10,... | collective-permute-start | bytes 221192 | tf_op jit(solution)/shard_map/ppermute | solution.py:202
  12.9 6.0 %collective-permute-start.5 = (bf16[144,256]{1,0:T(8,128)(2,1)S(1)}, bf16[144,256]{1,0:T(8,128)(2,1)S(1)}, u32[]{:S(2)}, u32[]{:S(2)}) collective-permute-start(bf16[144,256]{1,0:T(8,128)(2,1)S(1)} %get-tuple-element.23), channel_id=1, source_target_pairs={{0,6},{1,7},{2,4},{3,5},{4,2},{5,3},{6,0},{7,1},{8,14},{9,15},{10,... | collective-permute-start | bytes 221192 | tf_op jit(solution)/shard_map/ppermute | solution.py:202
  16.1 5.0 %collective-permute-start.6 = (bf16[144,256]{1,0:T(8,128)(2,1)S(1)}, bf16[144,256]{1,0:T(8,128)(2,1)S(1)}, u32[]{:S(2)}, u32[]{:S(2)}) collective-permute-start(bf16[144,256]{1,0:T(8,128)(2,1)S(1)} %get-tuple-element.24), channel_id=1, source_target_pairs={{0,7},{1,6},{2,5},{3,4},{4,3},{5,2},{6,1},{7,0},{8,15},{9,14},{10,... | collective-permute-start | bytes 221192 | tf_op jit(solution)/shard_map/ppermute | solution.py:202
  35.2 1.2 %collective-permute-start.9 = (f32[16,256]{1,0:T(8,128)S(1)}, f32[16,256]{1,0:T(8,128)S(1)}, u32[]{:S(2)}, u32[]{:S(2)}) collective-permute-start(f32[16,256]{1,0:T(8,128)S(1)} %convert_reduce_fusion.mine_ref), channel_id=1, source_target_pairs={{0,1},{1,0},{2,3},{3,2},{4,5},{5,4},{6,7},{7,6},{8,9},{9,8},{10,11... | collective-permute-start | bytes 49160 | tf_op jit(solution)/shard_map/ppermute | solution.py:234

commit v6 on v4

v6 whole, which is shorter than its diff:
```python
import functools

import jax
import jax.numpy as jnp
from jax import lax
from jax.experimental import pallas as pl
from jax.experimental.pallas import tpu as pltpu
from jax.sharding import PartitionSpec as P

RAY_DEV = 16
META_ROWS = 16
RAY_BASE = 32
LANES = 128
OVERLAP_FLOPS = 10**10
VMEM_LIMIT = 32 * 1024 * 1024
F32 = jnp.float32
BF16 = jnp.bfloat16
I32 = jnp.int32


def nt_dot(a, b):
    return lax.dot_general(a, b, (((1,), (1,)), ((), ())), preferred_element_type=F32)


def iota(shape, dim):
    return lax.broadcasted_iota(I32, shape, dim)


def pack_kernel(plan, me_ref, src_hbm, den_hbm, bin_hbm, ray_hbm, table_hbm, line_hbm, *rest):
    targets, block = plan.targets, plan.block
    out, table_out, line_out, src_ref, den_ref, bin_ref, ray_ref, sems = rest
    copies = [
        pltpu.make_async_copy(a, b, sems.at[i])
        for i, (a, b) in enumerate(
            (
                (bin_hbm, bin_ref),
                (ray_hbm, ray_ref),
                (den_hbm, den_ref),
                (src_hbm, src_ref),
                (table_hbm, table_out),
                (line_hbm, line_out),
            )
        )
    ]
    for copy in copies:
        copy.start()
    cells, levels = src_ref.shape
    earlier = (iota((cells, cells), 0) < iota((cells, cells), 1)).astype(F32).astype(BF16)
    my_half = me_ref[0] // targets
    for copy in copies[:3]:
        copy.wait()
    bins = bin_ref[...]
    hot = (iota((plan.bins, cells), 0) == bins).astype(F32)
    before = jnp.dot(hot.astype(BF16), earlier, preferred_element_type=F32)
    position = jnp.sum(hot * before, axis=0, keepdims=True).astype(I32)
    half = bins // targets
    slot = (bins - half * targets) * block + (half ^ my_half) * plan.capacity + position
    rays = ray_ref[...]
    ray_high = rays // RAY_BASE
    ray_low = rays - ray_high * RAY_BASE
    den = den_ref[...].astype(F32)
    den_row = jnp.concatenate([den[i : i + 1] for i in range(den.shape[0])], axis=1)
    meta = jnp.concatenate(
        [den_row, ray_high.astype(F32), ray_low.astype(F32), jnp.zeros((META_ROWS - 3, cells), F32)],
        axis=0,
    ).astype(BF16)
    place = (iota((targets * block, cells), 0) == slot).astype(F32).astype(BF16)
    moved = nt_dot(meta, place).astype(BF16)
    copies[3].wait()
    rows = jnp.dot(place, src_ref[...], preferred_element_type=F32).astype(BF16)
    out[:, :block, :] = rows.reshape(targets, block, levels)
    out[:, block:, :] = jnp.zeros((targets, META_ROWS, levels), BF16)
    for t in range(targets):
        out[t, block:, :block] = moved[:, t * block : (t + 1) * block]
    for copy in copies[4:]:
        copy.wait()


def keep_kernel(table_ref, out_ref):
    out_ref[...] = table_ref[...]


def level_kernel(plan, rays, got_ref, *refs):
    table_refs, out_ref = refs[:-1], refs[-1]
    targets, block = plan.targets, plan.block
    meta = [got_ref[s, block:, :block].astype(F32) for s in range(targets)]
    columns = [jnp.transpose(m[:8]) for m in meta]
    total = jnp.zeros(out_ref.shape, F32)
    for part, table_ref in enumerate(table_refs):
        low, high = part * plan.capacity, (part + 1) * plan.capacity
        src = got_ref[:, low:high, :].reshape(targets * plan.capacity, got_ref.shape[2])
        den = jnp.concatenate([c[low:high, 0:1] for c in columns], axis=0)
        ray = jnp.concatenate(
            [m[1:2, low:high] * RAY_BASE + m[2:3, low:high] for m in meta], axis=1
        ).astype(I32)
        wide = src.astype(F32)
        table = table_ref[...]
        first = (den * jnp.dot(src, table, preferred_element_type=F32) + wide).astype(BF16)
        pops = (den * jnp.dot(first, table, preferred_element_type=F32) + wide).astype(BF16)
        pick = (iota((rays, src.shape[0]), 0) == ray).astype(F32).astype(BF16)
        total = total + jnp.dot(pick, pops, preferred_element_type=F32)
    out_ref[...] = total.astype(BF16)


def line_kernel(mine_ref, theirs_ref, line_ref, out_ref):
    sums = mine_ref[...] + theirs_ref[...]
    rows = sums.shape[0]
    high = sums.astype(BF16)
    low = (sums - high.astype(F32)).astype(BF16)
    both = jnp.concatenate([high, low], axis=0)
    got = jnp.dot(both, line_ref[...], preferred_element_type=F32)
    out_ref[...] = got[:rows] + got[rows:]


class Plan:
    def __init__(self, bin_total, cells):
        self.bins = bin_total
        self.targets = bin_total // 2
        self.capacity = max(2, 2 * cells // bin_total)
        self.block = 2 * self.capacity

    def table_moves(self):
        return [(i, (i + self.targets) % self.bins) for i in range(self.bins)]

    def halves(self):
        return [list(range(self.targets)), list(range(self.targets, self.bins))]


def per_device(sources, density, temp_bins, ray_index, rate_tables, line_table):
    cells, levels = sources.shape
    bin_total = lax.axis_size("bin")
    wave_total = lax.axis_size("wave")
    plan = Plan(bin_total, cells)
    rows = plan.block + META_ROWS
    params = pltpu.CompilerParams(vmem_limit_bytes=VMEM_LIMIT)
    vmem = pl.BlockSpec(memory_space=pltpu.VMEM)
    smem = pl.BlockSpec(memory_space=pltpu.SMEM)
    hbm = pl.BlockSpec(memory_space=pltpu.HBM)

    def in_hbm(x):
        return pltpu.with_memory_space_constraint(x, pltpu.HBM)

    arrived = lax.ppermute(rate_tables[0], "bin", plan.table_moves())
    me = lax.axis_index("bin").astype(I32).reshape(1)
    den_rows = cells // min(cells, LANES)
    outgoing, own, held_line = pl.pallas_call(
        functools.partial(pack_kernel, plan),
        out_shape=[
            jax.ShapeDtypeStruct(a, BF16)
            for a in ((plan.targets, rows, levels), rate_tables.shape[1:], line_table.shape)
        ],
        in_specs=[smem] + [hbm] * 6,
        out_specs=[vmem] * 3,
        scratch_shapes=[
            pltpu.VMEM((cells, levels), BF16),
            pltpu.VMEM((den_rows, cells // den_rows), BF16),
            pltpu.VMEM((1, cells), I32),
            pltpu.VMEM((1, cells), I32),
            pltpu.SemaphoreType.DMA((6,)),
        ],
        compiler_params=params,
    )(
        me,
        in_hbm(sources),
        in_hbm(density.reshape(den_rows, cells // den_rows)),
        in_hbm(temp_bins.reshape(1, cells)),
        in_hbm(ray_index.reshape(1, cells)),
        in_hbm(rate_tables[0]),
        in_hbm(line_table),
    )
    got = lax.all_to_all(
        outgoing, "bin", split_axis=0, concat_axis=0, tiled=True, axis_index_groups=plan.halves()
    )
    other = pl.pallas_call(
        keep_kernel,
        out_shape=jax.ShapeDtypeStruct(arrived.shape, BF16),
        in_specs=[vmem],
        out_specs=vmem,
        compiler_params=params,
        cost_estimate=pl.CostEstimate(
            flops=OVERLAP_FLOPS, bytes_accessed=4 * arrived.size, transcendentals=0
        ),
    )(arrived)
    ray_rows = RAY_DEV
    rays = ray_rows * bin_total
    partial_sums = pl.pallas_call(
        functools.partial(level_kernel, plan, rays),
        out_shape=jax.ShapeDtypeStruct((rays, levels), BF16),
        in_specs=[vmem] * 3,
        out_specs=vmem,
        compiler_params=params,
    )(got, own, other)
    held = lax.all_to_all(
        partial_sums.reshape(bin_total, ray_rows, levels),
        "bin",
        split_axis=0,
        concat_axis=0,
        tiled=True,
    )
    total = jnp.sum(held.astype(F32), axis=0)
    theirs = jnp.zeros_like(total)
    step = 1
    while step < wave_total:
        total = total + theirs if step > 1 else total
        theirs = lax.ppermute(total, "wave", [(i, i ^ step) for i in range(wave_total)])
        step *= 2
    return pl.pallas_call(
        line_kernel,
        out_shape=jax.ShapeDtypeStruct((ray_rows, line_table.shape[1]), F32),
        in_specs=[vmem, vmem, vmem],
        out_specs=vmem,
        compiler_params=params,
    )(total, theirs, held_line)


def solution(mesh):
    in_specs = (
        P(("bin", "wave"), None),
        P(("bin", "wave")),
        P(("bin", "wave"), None),
        P(("bin", "wave")),
        P("bin", None, None),
        P(None, "wave"),
    )
    return jax.shard_map(
        per_device, mesh=mesh, in_specs=in_specs, out_specs=P("bin", "wave"), check_vma=False
    )
```

time: 35.9 us -> 35.1 us (0.978)
  waiting for transfers between devices: 5.86 us -> 10.6 us
  starting transfers between devices: 12.9 us -> 8.85 us
  blocking collectives: 12.7 us -> 10.4 us
  Pallas kernels: 4.14 us -> 4.92 us
    all_to_all x0 -> x1, waiting for transfers between devices: none -> 9.42 us  [per_device(): lax.all_to_all(outgoing, 'bin', split_axis=0, concat_axis=0, tiled=True,...]
    ppermute x9 -> x1, starting transfers between devices: 12.8 us -> 4.04 us  [per_device(): arrived = lax.ppermute(rate_tables[0], 'bin', plan.table_moves())]
    all_to_all x0 -> x1, starting transfers between devices: none -> 4.75 us  [per_device(): lax.all_to_all(outgoing, 'bin', split_axis=0, concat_axis=0, tiled=True,...]
    ppermute x9 -> x1, waiting for transfers between devices: 4.69 us -> 0.01 us  [per_device(): arrived = lax.ppermute(rate_tables[0], 'bin', plan.table_moves())]
    all_to_all x1, blocking collectives: 12.7 us -> 10.4 us  [per_device(): lax.all_to_all(partial_sums.reshape(bin_total, ray_rows, levels), 'bin',...]
    pallas_call x1, Pallas kernels: 1.94 us -> 2.71 us  [per_device(): pl.pallas_call(functools.partial(pack_kernel, plan), out_shape=[jax.Shape...]
  transfers between devices with their start and end apart: 10 -> 3, of which waited for: 4 -> 2; matrix products, arithmetic and copies ran while one was open for 0% -> 0% of each run, Pallas kernels for 0% -> 8%
where the time goes in v6:
time: 35.1 us; the launch traced here: 34.8 us
  waiting for transfers between devices  10.6 us (30%)
  blocking collectives  10.4 us (30%)
  starting transfers between devices  8.85 us (25%)
  Pallas kernels  4.92 us (14%)
    all_to_all x1, blocking collectives, per_device(): lax.all_to_all(partial_sums.reshape(bin_total, ray_rows, levels), 'bin',...  10.4 us
    all_to_all x1, waiting for transfers between devices, per_device(): lax.all_to_all(outgoing, 'bin', split_axis=0, concat_axis=0, tiled=True,...  9.42 us
    all_to_all x1, starting transfers between devices, per_device(): lax.all_to_all(outgoing, 'bin', split_axis=0, concat_axis=0, tiled=True,...  4.75 us
    ppermute x1, starting transfers between devices, per_device(): arrived = lax.ppermute(rate_tables[0], 'bin', plan.table_moves())  4.04 us
    pallas_call x1, Pallas kernels, per_device(): pl.pallas_call(functools.partial(pack_kernel, plan), out_shape=[jax.Shape...  2.71 us
    ppermute x1, waiting for transfers between devices, per_device(): lax.ppermute(total, 'wave', [(i, i ^ step) for i in range(wave_total)])  1.17 us
    pallas_call x1, Pallas kernels, per_device(): pl.pallas_call(line_kernel, out_shape=jax.ShapeDtypeStruct((ray_rows, lin...  1.17 us
    pallas_call x1, Pallas kernels, per_device(): pl.pallas_call(functools.partial(level_kernel, plan, rays), out_shape=jax...  1.04 us
  transfers between devices with their start and end apart: 3, of which 2 were waited for; matrix products, arithmetic and copies ran while one was open for 0% of the time, Pallas kernels for 8%

profile of v6, /device:TPU:0, one launch (start us, length us, event | category | flops | bytes accessed | tf_op | source)
XLA Modules:
  0.0 34.8 jit_solution(8221530839177995843)
XLA Ops:
  0.0 4.0 %collective-permute-start = (bf16[256,256]{1,0:T(8,128)(2,1)}, bf16[256,256]{1,0:T(8,128)(2,1)S(1)}, u32[]{:S(2)}, u32[]{:S(2)}) collective-permute-start(bf16[256,256]{1,0:T(8,128)(2,1)} %bitcast.7), channel_id=1, source_target_pairs={{0,16},{2,18},{4,20},{6,22},{8,24},{10,26},{12,28},{14,30},{16,0},... | collective-permute-start | bytes 393224 | tf_op jit(solution)/shard_map/ppermute | solution.py:143
  4.0 2.7 %shard_map.64 = (bf16[8,144,256]{2,1,0:T(8,128)(2,1)}, bf16[256,256]{1,0:T(8,128)(2,1)S(1)}, bf16[256,4096]{1,0:T(8,128)(2,1)S(1)}) custom-call(s32[1]{0:T(128)} %bitcast.me_ref, bf16[512,256]{1,0:T(8,128)(2,1)} %src_hbm.1, bf16[4,128]{1,0:T(4,128)(2,1)} %bitcast.11, s32[1,512]{1,0:T(1,128)} %bitcast.9, s32[1,512]{1,0:T(1,128)} %bitcast.10, ...), custom_call_target="tpu_custom_call" | custom-call | tf_op jit(solution)/shard_map/pallas_call | solution.py:146
  6.8 4.7 %all-to-all-start = ((bf16[8,144,256]{2,1,0:T(8,128)(2,1)}), bf16[8,144,256]{2,1,0:T(8,128)(2,1)S(1)}, u32[]{:S(2)}, u32[]{:S(2)}) async-start(bf16[8,144,256]{2,1,0:T(8,128)(2,1)} %get-tuple-element.8), calls=%async_computation | async-start | bytes 1179648 | tf_op jit(solution)/shard_map/all_to_all | solution.py:171
  11.5 0.0 collective-permute-done.table_ref
  11.5 9.4 %all-to-all-done.got_ref = bf16[8,144,256]{2,1,0:T(8,128)(2,1)S(1)} async-done(((bf16[8,144,256]{2,1,0:T(8,128)(2,1)}), bf16[8,144,256]{2,1,0:T(8,128)(2,1)S(1)}, u32[]{:S(2)}, u32[]{:S(2)}) %all-to-all-start) | async-done | bytes 589856 | tf_op jit(solution)/shard_map/all_to_all | solution.py:171
  20.9 1.0 %shard_map.66 = bf16[256,256]{1,0:T(8,128)(2,1)S(1)} custom-call(bf16[8,144,256]{2,1,0:T(8,128)(2,1)S(1)} %all-to-all-done.got_ref, bf16[256,256]{1,0:T(8,128)(2,1)S(1)} %get-tuple-element.9.refs_0_, bf16[256,256]{1,0:T(8,128)(2,1)S(1)} %shard_map.65.refs_1_), custom_call_target="tpu_custom_call" | custom-call | tf_op jit(solution)/shard_map/pallas_call | solution.py:186
  22.0 10.4 %all_to_all.10 = bf16[16,16,256]{2,1,0:T(8,128)(2,1)S(1)} all-to-all(bf16[16,16,256]{2,1,0:T(8,128)(2,1)S(1)} %bitcast.6), channel_id=1, replica_groups=mesh['bin'=16,'wave'=2] {'bin'}, dimensions={0} | all-to-all | bytes 262144 | tf_op jit(solution)/shard_map/all_to_all | solution.py:193
  32.4 0.1 collective-permute-start.1
  32.5 1.2 %collective-permute-done.1.theirs_ref = f32[16,256]{1,0:T(8,128)S(1)} collective-permute-done((f32[16,256]{1,0:T(8,128)S(1)}, f32[16,256]{1,0:T(8,128)S(1)}, u32[]{:S(2)}, u32[]{:S(2)}) %collective-permute-start.1) | collective-permute-done | bytes 16416 | tf_op jit(solution)/shard_map/ppermute | solution.py:205
  33.7 1.2 %shard_map.67 = f32[16,4096]{1,0:T(8,128)} custom-call(f32[16,256]{1,0:T(8,128)S(1)} %convert_reduce_fusion.mine_ref, f32[16,256]{1,0:T(8,128)S(1)} %collective-permute-done.1.theirs_ref, bf16[256,4096]{1,0:T(8,128)(2,1)S(1)} %get-tuple-element.10.line_ref), custom_call_target="tpu_custom_call" | custom-call | tf_op jit(solution)/shard_map/pallas_call | solution.py:207
  (2 shorter events, 0.0 us)
Async XLA Ops:
  0.0 11.5 %collective-permute-start = (bf16[256,256]{1,0:T(8,128)(2,1)}, bf16[256,256]{1,0:T(8,128)(2,1)S(1)}, u32[]{:S(2)}, u32[]{:S(2)}) collective-permute-start(bf16[256,256]{1,0:T(8,128)(2,1)} %bitcast.7), channel_id=1, source_target_pairs={{0,16},{2,18},{4,20},{6,22},{8,24},{10,26},{12,28},{14,30},{16,0},... | collective-permute-start | bytes 393224 | tf_op jit(solution)/shard_map/ppermute | solution.py:143
  6.8 14.2 %all-to-all-start = ((bf16[8,144,256]{2,1,0:T(8,128)(2,1)}), bf16[8,144,256]{2,1,0:T(8,128)(2,1)S(1)}, u32[]{:S(2)}, u32[]{:S(2)}) async-start(bf16[8,144,256]{2,1,0:T(8,128)(2,1)} %get-tuple-element.8), calls=%async_computation | async-start | bytes 1179648 | tf_op jit(solution)/shard_map/all_to_all | solution.py:171
  32.4 1.2 %collective-permute-start.1 = (f32[16,256]{1,0:T(8,128)S(1)}, f32[16,256]{1,0:T(8,128)S(1)}, u32[]{:S(2)}, u32[]{:S(2)}) collective-permute-start(f32[16,256]{1,0:T(8,128)S(1)} %convert_reduce_fusion.mine_ref), channel_id=1, source_target_pairs={{0,1},{1,0},{2,3},{3,2},{4,5},{5,4},{6,7},{7,6},{8,9},{9,8},{10,11... | collective-permute-start | bytes 49160 | tf_op jit(solution)/shard_map/ppermute | solution.py:205

commit v7 on v6

--- a/solution.py
+++ b/solution.py
@@ -85,7 +85,7 @@
     targets, block = plan.targets, plan.block
     meta = [got_ref[s, block:, :block].astype(F32) for s in range(targets)]
     columns = [jnp.transpose(m[:8]) for m in meta]
-    total = jnp.zeros(out_ref.shape, F32)
+    total = jnp.zeros((rays, got_ref.shape[2]), F32)
     for part, table_ref in enumerate(table_refs):
         low, high = part * plan.capacity, (part + 1) * plan.capacity
         src = got_ref[:, low:high, :].reshape(targets * plan.capacity, got_ref.shape[2])
@@ -99,11 +99,13 @@
         pops = (den * jnp.dot(first, table, preferred_element_type=F32) + wide).astype(BF16)
         pick = (iota((rays, src.shape[0]), 0) == ray).astype(F32).astype(BF16)
         total = total + jnp.dot(pick, pops, preferred_element_type=F32)
-    out_ref[...] = total.astype(BF16)
-
-
-def line_kernel(mine_ref, theirs_ref, line_ref, out_ref):
-    sums = mine_ref[...] + theirs_ref[...]
+    blocks = total.astype(BF16).reshape(out_ref.shape[0], *out_ref.shape[2:])
+    for core in range(out_ref.shape[1]):
+        out_ref[:, core] = blocks
+
+
+def line_kernel(sums_ref, line_ref, out_ref):
+    sums = sums_ref[...]
     rows = sums.shape[0]
     high = sums.astype(BF16)
     low = (sums - high.astype(F32)).astype(BF16)
@@ -185,32 +187,26 @@
     rays = ray_rows * bin_total
     partial_sums = pl.pallas_call(
         functools.partial(level_kernel, plan, rays),
-        out_shape=jax.ShapeDtypeStruct((rays, levels), BF16),
+        out_shape=jax.ShapeDtypeStruct((bin_total, wave_total, ray_rows, levels), BF16),
         in_specs=[vmem] * 3,
         out_specs=vmem,
         compiler_params=params,
     )(got, own, other)
     held = lax.all_to_all(
-        partial_sums.reshape(bin_total, ray_rows, levels),
-        "bin",
+        partial_sums.reshape(bin_total * wave_total, ray_rows, levels),
+        ("bin", "wave"),
         split_axis=0,
         concat_axis=0,
         tiled=True,
     )
     total = jnp.sum(held.astype(F32), axis=0)
-    theirs = jnp.zeros_like(total)
-    step = 1
-    while step < wave_total:
-        total = total + theirs if step > 1 else total
-        theirs = lax.ppermute(total, "wave", [(i, i ^ step) for i in range(wave_total)])
-        step *= 2
     return pl.pallas_call(
         line_kernel,
         out_shape=jax.ShapeDtypeStruct((ray_rows, line_table.shape[1]), F32),
-        in_specs=[vmem, vmem, vmem],
+        in_specs=[vmem, vmem],
         out_specs=vmem,
         compiler_params=params,
-    )(total, theirs, held_line)
+    )(total, held_line)
 
 
 def solution(mesh):

time: 35.1 us -> 35.7 us (1.017)
  blocking collectives: 10.4 us -> 12.3 us
  waiting for transfers between devices: 10.6 us -> 9.43 us
    all_to_all x1, blocking collectives: 10.4 us -> 12.3 us  [per_device(): lax.all_to_all(partial_sums.reshape(bin_total * wave_total, ray_rows, lev...]
    ppermute x1 -> x0, waiting for transfers between devices: 1.17 us -> none  [per_device(): lax.ppermute(total, 'wave', [(i, i ^ step) for i in range(wave_total)])]
  transfers between devices with their start and end apart: 3 -> 2, of which waited for: 2 -> 1; matrix products, arithmetic and copies ran while one was open for 0% -> 0% of each run, Pallas kernels for 8% -> 8%
where the time goes in v7:
time: 35.7 us; the launch traced here: 35.5 us
  blocking collectives  12.3 us (34%)
  waiting for transfers between devices  9.43 us (26%)
  starting transfers between devices  8.78 us (25%)
  Pallas kernels  4.92 us (14%)
    all_to_all x1, blocking collectives, per_device(): lax.all_to_all(partial_sums.reshape(bin_total * wave_total, ray_rows, lev...  12.3 us
    all_to_all x1, waiting for transfers between devices, per_device(): lax.all_to_all(outgoing, 'bin', split_axis=0, concat_axis=0, tiled=True,...  9.42 us
    all_to_all x1, starting transfers between devices, per_device(): lax.all_to_all(outgoing, 'bin', split_axis=0, concat_axis=0, tiled=True,...  4.75 us
    ppermute x1, starting transfers between devices, per_device(): arrived = lax.ppermute(rate_tables[0], 'bin', plan.table_moves())  4.04 us
    pallas_call x1, Pallas kernels, per_device(): pl.pallas_call(functools.partial(pack_kernel, plan), out_shape=[jax.Shape...  2.7 us
    pallas_call x1, Pallas kernels, per_device(): pl.pallas_call(line_kernel, out_shape=jax.ShapeDtypeStruct((ray_rows, lin...  1.17 us
    pallas_call x1, Pallas kernels, per_device(): pl.pallas_call(functools.partial(level_kernel, plan, rays), out_shape=jax...  1.04 us
  transfers between devices with their start and end apart: 2, of which 1 were waited for; matrix products, arithmetic and copies ran while one was open for 0% of the time, Pallas kernels for 8%

profile of v7, /device:TPU:0, one launch (start us, length us, event | category | flops | bytes accessed | tf_op | source)
XLA Modules:
  0.0 35.5 jit_solution(5501401079023649486)
XLA Ops:
  0.0 4.0 %collective-permute-start = (bf16[256,256]{1,0:T(8,128)(2,1)}, bf16[256,256]{1,0:T(8,128)(2,1)S(1)}, u32[]{:S(2)}, u32[]{:S(2)}) collective-permute-start(bf16[256,256]{1,0:T(8,128)(2,1)} %bitcast.7), channel_id=1, source_target_pairs={{0,16},{2,18},{4,20},{6,22},{8,24},{10,26},{12,28},{14,30},{16,0},... | collective-permute-start | bytes 393224 | tf_op jit(solution)/shard_map/ppermute | solution.py:145
  4.0 2.7 %shard_map.64 = (bf16[8,144,256]{2,1,0:T(8,128)(2,1)}, bf16[256,256]{1,0:T(8,128)(2,1)S(1)}, bf16[256,4096]{1,0:T(8,128)(2,1)S(1)}) custom-call(s32[1]{0:T(128)} %bitcast.me_ref, bf16[512,256]{1,0:T(8,128)(2,1)} %src_hbm.1, bf16[4,128]{1,0:T(4,128)(2,1)} %bitcast.11, s32[1,512]{1,0:T(1,128)} %bitcast.9, s32[1,512]{1,0:T(1,128)} %bitcast.10, ...), custom_call_target="tpu_custom_call" | custom-call | tf_op jit(solution)/shard_map/pallas_call | solution.py:148
  6.7 4.7 %all-to-all-start = ((bf16[8,144,256]{2,1,0:T(8,128)(2,1)}), bf16[8,144,256]{2,1,0:T(8,128)(2,1)S(1)}, u32[]{:S(2)}, u32[]{:S(2)}) async-start(bf16[8,144,256]{2,1,0:T(8,128)(2,1)} %get-tuple-element.8), calls=%async_computation | async-start | bytes 1179648 | tf_op jit(solution)/shard_map/all_to_all | solution.py:173
  11.5 0.0 collective-permute-done.table_ref
  11.5 9.4 %all-to-all-done.got_ref = bf16[8,144,256]{2,1,0:T(8,128)(2,1)S(1)} async-done(((bf16[8,144,256]{2,1,0:T(8,128)(2,1)}), bf16[8,144,256]{2,1,0:T(8,128)(2,1)S(1)}, u32[]{:S(2)}, u32[]{:S(2)}) %all-to-all-start) | async-done | bytes 589856 | tf_op jit(solution)/shard_map/all_to_all | solution.py:173
  20.9 1.0 %shard_map.66 = bf16[16,2,16,256]{3,2,1,0:T(8,128)(2,1)S(1)} custom-call(bf16[8,144,256]{2,1,0:T(8,128)(2,1)S(1)} %all-to-all-done.got_ref, bf16[256,256]{1,0:T(8,128)(2,1)S(1)} %get-tuple-element.9.refs_0_, bf16[256,256]{1,0:T(8,128)(2,1)S(1)} %shard_map.65.refs_1_), custom_call_target="tpu_custom_call" | custom-call | tf_op jit(solution)/shard_map/pallas_call | solution.py:188
  22.0 12.3 %all_to_all.10 = bf16[32,16,256]{2,1,0:T(8,128)(2,1)S(1)} all-to-all(bf16[32,16,256]{2,1,0:T(8,128)(2,1)S(1)} %bitcast.6), channel_id=1, replica_groups=mesh['bin'=16,'wave'=2] {'bin','wave'}, dimensions={0} | all-to-all | bytes 524288 | tf_op jit(solution)/shard_map/all_to_all | solution.py:195
  34.3 1.2 %shard_map.67 = f32[16,4096]{1,0:T(8,128)} custom-call(f32[16,256]{1,0:T(8,128)S(1)} %convert_reduce_fusion.sums_ref, bf16[256,4096]{1,0:T(8,128)(2,1)S(1)} %get-tuple-element.10.line_ref), custom_call_target="tpu_custom_call" | custom-call | tf_op jit(solution)/shard_map/pallas_call | solution.py:203
  (2 shorter events, 0.1 us)
Async XLA Ops:
  0.0 11.5 %collective-permute-start = (bf16[256,256]{1,0:T(8,128)(2,1)}, bf16[256,256]{1,0:T(8,128)(2,1)S(1)}, u32[]{:S(2)}, u32[]{:S(2)}) collective-permute-start(bf16[256,256]{1,0:T(8,128)(2,1)} %bitcast.7), channel_id=1, source_target_pairs={{0,16},{2,18},{4,20},{6,22},{8,24},{10,26},{12,28},{14,30},{16,0},... | collective-permute-start | bytes 393224 | tf_op jit(solution)/shard_map/ppermute | solution.py:145
  6.7 14.2 %all-to-all-start = ((bf16[8,144,256]{2,1,0:T(8,128)(2,1)}), bf16[8,144,256]{2,1,0:T(8,128)(2,1)S(1)}, u32[]{:S(2)}, u32[]{:S(2)}) async-start(bf16[8,144,256]{2,1,0:T(8,128)(2,1)} %get-tuple-element.8), calls=%async_computation | async-start | bytes 1179648 | tf_op jit(solution)/shard_map/all_to_all | solution.py:173

commit v8 on v6

--- a/solution.py
+++ b/solution.py
@@ -26,9 +26,9 @@
     return lax.broadcasted_iota(I32, shape, dim)
 
 
-def pack_kernel(plan, me_ref, src_hbm, den_hbm, bin_hbm, ray_hbm, table_hbm, line_hbm, *rest):
+def pack_kernel(plan, src_hbm, den_hbm, bin_hbm, ray_hbm, line_hbm, *rest):
     targets, block = plan.targets, plan.block
-    out, table_out, line_out, src_ref, den_ref, bin_ref, ray_ref, sems = rest
+    out, line_out, src_ref, den_ref, bin_ref, ray_ref, sems = rest
     copies = [
         pltpu.make_async_copy(a, b, sems.at[i])
         for i, (a, b) in enumerate(
@@ -37,7 +37,6 @@
                 (ray_hbm, ray_ref),
                 (den_hbm, den_ref),
                 (src_hbm, src_ref),
-                (table_hbm, table_out),
                 (line_hbm, line_out),
             )
         )
@@ -46,7 +45,6 @@
         copy.start()
     cells, levels = src_ref.shape
     earlier = (iota((cells, cells), 0) < iota((cells, cells), 1)).astype(F32).astype(BF16)
-    my_half = me_ref[0] // targets
     for copy in copies[:3]:
         copy.wait()
     bins = bin_ref[...]
@@ -54,7 +52,7 @@
     before = jnp.dot(hot.astype(BF16), earlier, preferred_element_type=F32)
     position = jnp.sum(hot * before, axis=0, keepdims=True).astype(I32)
     half = bins // targets
-    slot = (bins - half * targets) * block + (half ^ my_half) * plan.capacity + position
+    slot = (bins - half * targets) * block + half * plan.capacity + position
     rays = ray_ref[...]
     ray_high = rays // RAY_BASE
     ray_low = rays - ray_high * RAY_BASE
@@ -76,17 +74,16 @@
         copy.wait()
 
 
-def keep_kernel(table_ref, out_ref):
-    out_ref[...] = table_ref[...]
-
-
-def level_kernel(plan, rays, got_ref, *refs):
-    table_refs, out_ref = refs[:-1], refs[-1]
+def keep_kernel(tables_ref, out_ref):
+    out_ref[...] = tables_ref[...]
+
+
+def level_kernel(plan, rays, got_ref, tables_ref, out_ref):
     targets, block = plan.targets, plan.block
     meta = [got_ref[s, block:, :block].astype(F32) for s in range(targets)]
     columns = [jnp.transpose(m[:8]) for m in meta]
     total = jnp.zeros(out_ref.shape, F32)
-    for part, table_ref in enumerate(table_refs):
+    for part in range(2):
         low, high = part * plan.capacity, (part + 1) * plan.capacity
         src = got_ref[:, low:high, :].reshape(targets * plan.capacity, got_ref.shape[2])
         den = jnp.concatenate([c[low:high, 0:1] for c in columns], axis=0)
@@ -94,7 +91,7 @@
             [m[1:2, low:high] * RAY_BASE + m[2:3, low:high] for m in meta], axis=1
         ).astype(I32)
         wide = src.astype(F32)
-        table = table_ref[...]
+        table = tables_ref[part]
         first = (den * jnp.dot(src, table, preferred_element_type=F32) + wide).astype(BF16)
         pops = (den * jnp.dot(first, table, preferred_element_type=F32) + wide).astype(BF16)
         pick = (iota((rays, src.shape[0]), 0) == ray).astype(F32).astype(BF16)
@@ -119,8 +116,8 @@
         self.capacity = max(2, 2 * cells // bin_total)
         self.block = 2 * self.capacity
 
-    def table_moves(self):
-        return [(i, (i + self.targets) % self.bins) for i in range(self.bins)]
+    def pairs(self):
+        return [[i, i + self.targets] for i in range(self.targets)]
 
     def halves(self):
         return [list(range(self.targets)), list(range(self.targets, self.bins))]
@@ -134,44 +131,40 @@
     rows = plan.block + META_ROWS
     params = pltpu.CompilerParams(vmem_limit_bytes=VMEM_LIMIT)
     vmem = pl.BlockSpec(memory_space=pltpu.VMEM)
-    smem = pl.BlockSpec(memory_space=pltpu.SMEM)
     hbm = pl.BlockSpec(memory_space=pltpu.HBM)
 
     def in_hbm(x):
         return pltpu.with_memory_space_constraint(x, pltpu.HBM)
 
-    arrived = lax.ppermute(rate_tables[0], "bin", plan.table_moves())
-    me = lax.axis_index("bin").astype(I32).reshape(1)
+    arrived = lax.all_gather(rate_tables[0], "bin", axis_index_groups=plan.pairs())
     den_rows = cells // min(cells, LANES)
-    outgoing, own, held_line = pl.pallas_call(
+    outgoing, held_line = pl.pallas_call(
         functools.partial(pack_kernel, plan),
         out_shape=[
             jax.ShapeDtypeStruct(a, BF16)
-            for a in ((plan.targets, rows, levels), rate_tables.shape[1:], line_table.shape)
+            for a in ((plan.targets, rows, levels), line_table.shape)
         ],
-        in_specs=[smem] + [hbm] * 6,
-        out_specs=[vmem] * 3,
+        in_specs=[hbm] * 5,
+        out_specs=[vmem] * 2,
         scratch_shapes=[
             pltpu.VMEM((cells, levels), BF16),
             pltpu.VMEM((den_rows, cells // den_rows), BF16),
             pltpu.VMEM((1, cells), I32),
             pltpu.VMEM((1, cells), I32),
-            pltpu.SemaphoreType.DMA((6,)),
+            pltpu.SemaphoreType.DMA((5,)),
         ],
         compiler_params=params,
     )(
-        me,
         in_hbm(sources),
         in_hbm(density.reshape(den_rows, cells // den_rows)),
         in_hbm(temp_bins.reshape(1, cells)),
         in_hbm(ray_index.reshape(1, cells)),
-        in_hbm(rate_tables[0]),
         in_hbm(line_table),
     )
     got = lax.all_to_all(
         outgoing, "bin", split_axis=0, concat_axis=0, tiled=True, axis_index_groups=plan.halves()
     )
-    other = pl.pallas_call(
+    tables = pl.pallas_call(
         keep_kernel,
         out_shape=jax.ShapeDtypeStruct(arrived.shape, BF16),
         in_specs=[vmem],
@@ -186,10 +179,10 @@
     partial_sums = pl.pallas_call(
         functools.partial(level_kernel, plan, rays),
         out_shape=jax.ShapeDtypeStruct((rays, levels), BF16),
-        in_specs=[vmem] * 3,
+        in_specs=[vmem] * 2,
         out_specs=vmem,
         compiler_params=params,
-    )(got, own, other)
+    )(got, tables)
     held = lax.all_to_all(
         partial_sums.reshape(bin_total, ray_rows, levels),
         "bin",

time: 35.1 us -> 37.6 us (1.071)
  blocking collectives: 10.4 us -> 21.7 us
  waiting for transfers between devices: 10.6 us -> 4.36 us
  starting transfers between devices: 8.85 us -> 6.27 us
    all_gather x0 -> x1, blocking collectives: none -> 9.28 us  [per_device(): lax.all_gather(rate_tables[0], 'bin', axis_index_groups=plan.pairs())]
    all_to_all x1, waiting for transfers between devices: 9.42 us -> 3.19 us  [per_device(): lax.all_to_all(outgoing, 'bin', split_axis=0, concat_axis=0, tiled=True,...]
    ppermute x1 -> x0, starting transfers between devices: 4.04 us -> none  [per_device(): arrived = lax.ppermute(rate_tables[0], 'bin', plan.table_moves())]
    all_to_all x1, blocking collectives: 10.4 us -> 12.4 us  [per_device(): lax.all_to_all(partial_sums.reshape(bin_total, ray_rows, levels), 'bin',...]
    all_to_all x1, starting transfers between devices: 4.75 us -> 6.2 us  [per_device(): lax.all_to_all(outgoing, 'bin', split_axis=0, concat_axis=0, tiled=True,...]
  transfers between devices with their start and end apart: 3 -> 2, of which waited for: 2 -> 2; matrix products, arithmetic and copies ran while one was open for 0% -> 0% of each run, Pallas kernels for 8% -> 0%
where the time goes in v8:
time: 37.6 us; the launch traced here: 37.3 us
  blocking collectives  21.7 us (58%)
  starting transfers between devices  6.27 us (17%)
  Pallas kernels  4.95 us (13%)
  waiting for transfers between devices  4.36 us (12%)
    all_to_all x1, blocking collectives, per_device(): lax.all_to_all(partial_sums.reshape(bin_total, ray_rows, levels), 'bin',...  12.4 us
    all_gather x1, blocking collectives, per_device(): lax.all_gather(rate_tables[0], 'bin', axis_index_groups=plan.pairs())  9.28 us
    all_to_all x1, starting transfers between devices, per_device(): lax.all_to_all(outgoing, 'bin', split_axis=0, concat_axis=0, tiled=True,...  6.2 us
    all_to_all x1, waiting for transfers between devices, per_device(): lax.all_to_all(outgoing, 'bin', split_axis=0, concat_axis=0, tiled=True,...  3.19 us
    pallas_call x1, Pallas kernels, per_device(): pl.pallas_call(functools.partial(pack_kernel, plan), out_shape=[jax.Shape...  2.73 us
    ppermute x1, waiting for transfers between devices, per_device(): lax.ppermute(total, 'wave', [(i, i ^ step) for i in range(wave_total)])  1.17 us
    pallas_call x1, Pallas kernels, per_device(): pl.pallas_call(line_kernel, out_shape=jax.ShapeDtypeStruct((ray_rows, lin...  1.17 us
    pallas_call x1, Pallas kernels, per_device(): pl.pallas_call(functools.partial(level_kernel, plan, rays), out_shape=jax...  1.04 us
  transfers between devices with their start and end apart: 2, of which 2 were waited for; matrix products, arithmetic and copies ran while one was open for 0% of the time, Pallas kernels for 0%

profile of v8, /device:TPU:0, one launch (start us, length us, event | category | flops | bytes accessed | tf_op | source)
XLA Modules:
  0.0 37.3 jit_solution(14304401939948747880)
XLA Ops:
  0.0 0.0 copy-start
  0.0 2.7 %shard_map.64 = (bf16[8,144,256]{2,1,0:T(8,128)(2,1)}, bf16[256,4096]{1,0:T(8,128)(2,1)S(1)}) custom-call(bf16[512,256]{1,0:T(8,128)(2,1)} %src_hbm.1, bf16[4,128]{1,0:T(4,128)(2,1)} %bitcast.7, s32[1,512]{1,0:T(1,128)} %bitcast.5, s32[1,512]{1,0:T(1,128)} %bitcast.6, bf16[256,4096]{1,0:T(8,128)(2,1)} %line_hbm.1), custom_call_target="tpu_custom_call" | custom-call | tf_op jit(solution)/shard_map/pallas_call | solution.py:141
  2.7 6.2 %all-to-all-start = ((bf16[8,144,256]{2,1,0:T(8,128)(2,1)}), bf16[8,144,256]{2,1,0:T(8,128)(2,1)S(1)}, u32[]{:S(2)}, u32[]{:S(2)}) async-start(bf16[8,144,256]{2,1,0:T(8,128)(2,1)} %get-tuple-element.7), calls=%async_computation | async-start | bytes 1179648 | tf_op jit(solution)/shard_map/all_to_all | solution.py:164
  8.9 0.0 copy-done
  8.9 9.3 %all_gather.3.tables_ref = bf16[2,256,256]{2,1,0:T(8,128)(2,1)S(1)} all-gather(bf16[1,256,256]{2,1,0:T(8,128)(2,1)S(1)} %copy-done), channel_id=1, replica_groups={{0,16},{2,18},{4,20},{6,22},{8,24},{10,26},{12,28},{14,30},{1,17},{3,19..., dimensions={0}, use_global_device_ids=true | all-gather | bytes 393216 | tf_op jit(solution)/shard_map/all_gather | solution.py:139
  18.2 3.2 %all-to-all-done.got_ref = bf16[8,144,256]{2,1,0:T(8,128)(2,1)S(1)} async-done(((bf16[8,144,256]{2,1,0:T(8,128)(2,1)}), bf16[8,144,256]{2,1,0:T(8,128)(2,1)S(1)}, u32[]{:S(2)}, u32[]{:S(2)}) %all-to-all-start) | async-done | bytes 589856 | tf_op jit(solution)/shard_map/all_to_all | solution.py:164
  21.4 1.0 %shard_map.66 = bf16[256,256]{1,0:T(8,128)(2,1)S(1)} custom-call(bf16[8,144,256]{2,1,0:T(8,128)(2,1)S(1)} %all-to-all-done.got_ref, bf16[2,256,256]{2,1,0:T(8,128)(2,1)S(1)} %shard_map.65.tables_ref), custom_call_target="tpu_custom_call" | custom-call | tf_op jit(solution)/shard_map/pallas_call | solution.py:179
  22.5 12.4 %all_to_all.10 = bf16[16,16,256]{2,1,0:T(8,128)(2,1)S(1)} all-to-all(bf16[16,16,256]{2,1,0:T(8,128)(2,1)S(1)} %bitcast.4), channel_id=1, replica_groups=mesh['bin'=16,'wave'=2] {'bin'}, dimensions={0} | all-to-all | bytes 262144 | tf_op jit(solution)/shard_map/all_to_all | solution.py:186
  34.9 0.1 collective-permute-start
  35.0 1.2 %collective-permute-done.theirs_ref = f32[16,256]{1,0:T(8,128)S(1)} collective-permute-done((f32[16,256]{1,0:T(8,128)S(1)}, f32[16,256]{1,0:T(8,128)S(1)}, u32[]{:S(2)}, u32[]{:S(2)}) %collective-permute-start) | collective-permute-done | bytes 16416 | tf_op jit(solution)/shard_map/ppermute | solution.py:198
  36.2 1.2 %shard_map.67 = f32[16,4096]{1,0:T(8,128)} custom-call(f32[16,256]{1,0:T(8,128)S(1)} %convert_reduce_fusion.mine_ref, f32[16,256]{1,0:T(8,128)S(1)} %collective-permute-done.theirs_ref, bf16[256,4096]{1,0:T(8,128)(2,1)S(1)} %get-tuple-element.8.line_ref), custom_call_target="tpu_custom_call" | custom-call | tf_op jit(solution)/shard_map/pallas_call | solution.py:200
  (2 shorter events, 0.0 us)
Async XLA Ops:
  0.0 8.9 %copy-start = (bf16[1,256,256]{2,1,0:T(8,128)(2,1)S(1)}, bf16[1,256,256]{2,1,0:T(8,128)(2,1)}, u32[]{:S(2)}) copy-start(bf16[1,256,256]{2,1,0:T(8,128)(2,1)} %param.10) | copy-start | bytes 393220
  2.7 18.7 %all-to-all-start = ((bf16[8,144,256]{2,1,0:T(8,128)(2,1)}), bf16[8,144,256]{2,1,0:T(8,128)(2,1)S(1)}, u32[]{:S(2)}, u32[]{:S(2)}) async-start(bf16[8,144,256]{2,1,0:T(8,128)(2,1)} %get-tuple-element.7), calls=%async_computation | async-start | bytes 1179648 | tf_op jit(solution)/shard_map/all_to_all | solution.py:164
  34.9 1.2 %collective-permute-start = (f32[16,256]{1,0:T(8,128)S(1)}, f32[16,256]{1,0:T(8,128)S(1)}, u32[]{:S(2)}, u32[]{:S(2)}) collective-permute-start(f32[16,256]{1,0:T(8,128)S(1)} %convert_reduce_fusion.mine_ref), channel_id=1, source_target_pairs={{0,1},{1,0},{2,3},{3,2},{4,5},{5,4},{6,7},{7,6},{8,9},{9,8},{10,11... | collective-permute-start | bytes 49160 | tf_op jit(solution)/shard_map/ppermute | solution.py:198

commit v9 on v7

--- a/solution.py
+++ b/solution.py
@@ -80,9 +80,11 @@
     out_ref[...] = table_ref[...]
 
 
-def level_kernel(plan, rays, got_ref, *refs):
+def level_kernel(plan, ray_rows, me_ref, got_ref, *refs):
     table_refs, out_ref = refs[:-1], refs[-1]
     targets, block = plan.targets, plan.block
+    rays = plan.bins * ray_rows
+    my_half = me_ref[0] // targets
     meta = [got_ref[s, block:, :block].astype(F32) for s in range(targets)]
     columns = [jnp.transpose(m[:8]) for m in meta]
     total = jnp.zeros((rays, got_ref.shape[2]), F32)
@@ -93,19 +95,24 @@
         ray = jnp.concatenate(
             [m[1:2, low:high] * RAY_BASE + m[2:3, low:high] for m in meta], axis=1
         ).astype(I32)
+        owner = ray // ray_rows
+        half = owner // targets
+        place = (owner - half * targets) * 2 + (half ^ my_half)
+        row = place * ray_rows + (ray - owner * ray_rows)
         wide = src.astype(F32)
         table = table_ref[...]
         first = (den * jnp.dot(src, table, preferred_element_type=F32) + wide).astype(BF16)
         pops = (den * jnp.dot(first, table, preferred_element_type=F32) + wide).astype(BF16)
-        pick = (iota((rays, src.shape[0]), 0) == ray).astype(F32).astype(BF16)
+        pick = (iota((rays, src.shape[0]), 0) == row).astype(F32).astype(BF16)
         total = total + jnp.dot(pick, pops, preferred_element_type=F32)
-    blocks = total.astype(BF16).reshape(out_ref.shape[0], *out_ref.shape[2:])
-    for core in range(out_ref.shape[1]):
-        out_ref[:, core] = blocks
-
-
-def line_kernel(sums_ref, line_ref, out_ref):
-    sums = sums_ref[...]
+    out_ref[...] = total.astype(BF16).reshape(out_ref.shape)
+
+
+def line_kernel(mine_ref, *refs):
+    theirs, line_ref, out_ref = refs[:-2], refs[-2], refs[-1]
+    sums = mine_ref[...]
+    for their in theirs:
+        sums = sums + their[...].astype(F32)
     rows = sums.shape[0]
     high = sums.astype(BF16)
     low = (sums - high.astype(F32)).astype(BF16)
@@ -123,6 +130,13 @@
 
     def table_moves(self):
         return [(i, (i + self.targets) % self.bins) for i in range(self.bins)]
+
+    def sum_moves(self, wave_total, flip, turn):
+        return [
+            (b * wave_total + w, (b + flip * self.targets) % self.bins * wave_total + (w ^ turn))
+            for b in range(self.bins)
+            for w in range(wave_total)
+        ]
 
     def halves(self):
         return [list(range(self.targets)), list(range(self.targets, self.bins))]
@@ -184,29 +198,31 @@
         ),
     )(arrived)
     ray_rows = RAY_DEV
-    rays = ray_rows * bin_total
     partial_sums = pl.pallas_call(
-        functools.partial(level_kernel, plan, rays),
-        out_shape=jax.ShapeDtypeStruct((bin_total, wave_total, ray_rows, levels), BF16),
-        in_specs=[vmem] * 3,
+        functools.partial(level_kernel, plan, ray_rows),
+        out_shape=jax.ShapeDtypeStruct((plan.targets, 2 * ray_rows, levels), BF16),
+        in_specs=[smem] + [vmem] * 3,
         out_specs=vmem,
         compiler_params=params,
-    )(got, own, other)
+    )(me, got, own, other)
     held = lax.all_to_all(
-        partial_sums.reshape(bin_total * wave_total, ray_rows, levels),
-        ("bin", "wave"),
-        split_axis=0,
-        concat_axis=0,
-        tiled=True,
-    )
-    total = jnp.sum(held.astype(F32), axis=0)
+        partial_sums, "bin", split_axis=0, concat_axis=0, tiled=True, axis_index_groups=plan.halves()
+    )
+    sums = jnp.sum(held.astype(F32), axis=0)
+    mine, opposite = sums[:ray_rows], sums[ray_rows:].astype(BF16)
+    near = sums[:ray_rows].astype(BF16)
+    theirs = [
+        lax.ppermute(value, ("bin", "wave"), plan.sum_moves(wave_total, flip, turn))
+        for value, flip, turn in [(opposite, 1, w) for w in range(wave_total)]
+        + [(near, 0, w) for w in range(1, wave_total)]
+    ]
     return pl.pallas_call(
         line_kernel,
         out_shape=jax.ShapeDtypeStruct((ray_rows, line_table.shape[1]), F32),
-        in_specs=[vmem, vmem],
+        in_specs=[vmem] * (2 + len(theirs)),
         out_specs=vmem,
         compiler_params=params,
-    )(total, held_line)
+    )(mine, *theirs, held_line)
 
 
 def solution(mesh):

time: 35.7 us -> 36.7 us (1.028)
  blocking collectives: 12.3 us -> 8.52 us
  starting transfers between devices: 8.78 us -> 11.9 us
  waiting for transfers between devices: 9.43 us -> 11 us
    all_to_all x1, blocking collectives: 12.3 us -> 8.52 us  [per_device(): lax.all_to_all(partial_sums, 'bin', split_axis=0, concat_axis=0, tiled=Tr...]
    ppermute x0 -> x3, starting transfers between devices: none -> 3.11 us  [per_device(): lax.ppermute(value, ('bin', 'wave'), plan.sum_moves(wave_total, flip, turn))]
    ppermute x0 -> x3, waiting for transfers between devices: none -> 1.62 us  [per_device(): lax.ppermute(value, ('bin', 'wave'), plan.sum_moves(wave_total, flip, turn))]
  transfers between devices with their start and end apart: 2 -> 5, of which waited for: 1 -> 2; matrix products, arithmetic and copies ran while one was open for 0% -> 0% of each run, Pallas kernels for 8% -> 7%
where the time goes in v9:
time: 36.7 us; the launch traced here: 36.5 us
  starting transfers between devices  11.9 us (32%)
  waiting for transfers between devices  11 us (30%)
  blocking collectives  8.52 us (23%)
  Pallas kernels  4.93 us (13%)
    all_to_all x1, waiting for transfers between devices, per_device(): lax.all_to_all(outgoing, 'bin', split_axis=0, concat_axis=0, tiled=True,...  9.42 us
    all_to_all x1, blocking collectives, per_device(): lax.all_to_all(partial_sums, 'bin', split_axis=0, concat_axis=0, tiled=Tr...  8.52 us
    all_to_all x1, starting transfers between devices, per_device(): lax.all_to_all(outgoing, 'bin', split_axis=0, concat_axis=0, tiled=True,...  4.75 us
    ppermute x1, starting transfers between devices, per_device(): arrived = lax.ppermute(rate_tables[0], 'bin', plan.table_moves())  4.04 us
    ppermute x3, starting transfers between devices, per_device(): lax.ppermute(value, ('bin', 'wave'), plan.sum_moves(wave_total, flip, turn))  3.11 us
    pallas_call x1, Pallas kernels, per_device(): pl.pallas_call(functools.partial(pack_kernel, plan), out_shape=[jax.Shape...  2.72 us
    ppermute x3, waiting for transfers between devices, per_device(): lax.ppermute(value, ('bin', 'wave'), plan.sum_moves(wave_total, flip, turn))  1.62 us
    pallas_call x1, Pallas kernels, per_device(): pl.pallas_call(line_kernel, out_shape=jax.ShapeDtypeStruct((ray_rows, lin...  1.17 us
  transfers between devices with their start and end apart: 5, of which 2 were waited for; matrix products, arithmetic and copies ran while one was open for 0% of the time, Pallas kernels for 7%

profile of v9, /device:TPU:0, one launch (start us, length us, event | category | flops | bytes accessed | tf_op | source)
XLA Modules:
  0.0 36.5 jit_solution(13287727321349738912)
XLA Ops:
  0.0 4.0 %collective-permute-start = (bf16[256,256]{1,0:T(8,128)(2,1)}, bf16[256,256]{1,0:T(8,128)(2,1)S(1)}, u32[]{:S(2)}, u32[]{:S(2)}) collective-permute-start(bf16[256,256]{1,0:T(8,128)(2,1)} %bitcast.5), channel_id=1, source_target_pairs={{0,16},{2,18},{4,20},{6,22},{8,24},{10,26},{12,28},{14,30},{16,0},... | collective-permute-start | bytes 393224 | tf_op jit(solution)/shard_map/ppermute | solution.py:159
  4.0 2.7 %shard_map.64 = (bf16[8,144,256]{2,1,0:T(8,128)(2,1)}, bf16[256,256]{1,0:T(8,128)(2,1)S(1)}, bf16[256,4096]{1,0:T(8,128)(2,1)S(1)}) custom-call(s32[1]{0:T(128)} %bitcast.me_ref, bf16[512,256]{1,0:T(8,128)(2,1)} %src_hbm.1, bf16[4,128]{1,0:T(4,128)(2,1)} %bitcast.9, s32[1,512]{1,0:T(1,128)} %bitcast.7, s32[1,512]{1,0:T(1,128)} %bitcast.8, ...), custom_call_target="tpu_custom_call" | custom-call | tf_op jit(solution)/shard_map/pallas_call | solution.py:162
  6.8 4.7 %all-to-all-start = ((bf16[8,144,256]{2,1,0:T(8,128)(2,1)}), bf16[8,144,256]{2,1,0:T(8,128)(2,1)S(1)}, u32[]{:S(2)}, u32[]{:S(2)}) async-start(bf16[8,144,256]{2,1,0:T(8,128)(2,1)} %get-tuple-element.8), calls=%async_computation | async-start | bytes 1179648 | tf_op jit(solution)/shard_map/all_to_all | solution.py:187
  11.5 0.0 collective-permute-done.table_ref
  11.5 9.4 %all-to-all-done.got_ref = bf16[8,144,256]{2,1,0:T(8,128)(2,1)S(1)} async-done(((bf16[8,144,256]{2,1,0:T(8,128)(2,1)}), bf16[8,144,256]{2,1,0:T(8,128)(2,1)S(1)}, u32[]{:S(2)}, u32[]{:S(2)}) %all-to-all-start) | async-done | bytes 589856 | tf_op jit(solution)/shard_map/all_to_all | solution.py:187
  21.0 1.0 %shard_map.66 = bf16[8,32,256]{2,1,0:T(8,128)(2,1)S(1)} custom-call(s32[1]{0:T(128)} %bitcast.me_ref, bf16[8,144,256]{2,1,0:T(8,128)(2,1)S(1)} %all-to-all-done.got_ref, bf16[256,256]{1,0:T(8,128)(2,1)S(1)} %get-tuple-element.9.refs_0_, bf16[256,256]{1,0:T(8,128)(2,1)S(1)} %shard_map.65.refs_1_), custom_call_target="tpu_custom_call" | custom-call | tf_op jit(solution)/shard_map/pallas_call | solution.py:201
  22.0 8.5 %all_to_all.10 = bf16[8,32,256]{2,1,0:T(8,128)(2,1)S(1)} all-to-all(bf16[8,32,256]{2,1,0:T(8,128)(2,1)S(1)} %shard_map.66), channel_id=1, replica_groups={{0,2,4,6,8,10,12,14},{16,18,20,22,24,26,28,30},{1,3,5,7,9,11,13,15},{17..., dimensions={0} | all-to-all | bytes 262144 | tf_op jit(solution)/shard_map/all_to_all | solution.py:208
  30.6 0.7 %collective-permute-start.1 = (bf16[16,256]{1,0:T(8,128)(2,1)S(1)}, bf16[16,256]{1,0:T(8,128)(2,1)S(1)}, u32[]{:S(2)}, u32[]{:S(2)}) collective-permute-start(bf16[16,256]{1,0:T(8,128)(2,1)S(1)} %get-tuple-element.12), channel_id=1, source_target_pairs={{0,16},{1,17},{2,18},{3,19},{4,20},{5,21},{6,22},{7,23},{8,24},{9,... | collective-permute-start | bytes 24584 | tf_op jit(solution)/shard_map/ppermute | solution.py:215
  31.2 0.2 collective-permute-start.2
  31.4 2.2 %collective-permute-start.3 = (bf16[16,256]{1,0:T(8,128)(2,1)S(1)}, bf16[16,256]{1,0:T(8,128)(2,1)S(1)}, u32[]{:S(2)}, u32[]{:S(2)}) collective-permute-start(bf16[16,256]{1,0:T(8,128)(2,1)S(1)} %get-tuple-element.11), channel_id=1, source_target_pairs={{0,1},{1,0},{2,3},{3,2},{4,5},{5,4},{6,7},{7,6},{8,9},{9,8},{10,11... | collective-permute-start | bytes 24584 | tf_op jit(solution)/shard_map/ppermute | solution.py:215
  33.7 1.6 %collective-permute-done.1.refs_0_ = bf16[16,256]{1,0:T(8,128)(2,1)S(1)} collective-permute-done((bf16[16,256]{1,0:T(8,128)(2,1)S(1)}, bf16[16,256]{1,0:T(8,128)(2,1)S(1)}, u32[]{:S(2)}, u32[]{:S(2)}) %collective-permute-start.1) | collective-permute-done | bytes 8224 | tf_op jit(solution)/shard_map/ppermute | solution.py:215
  35.2 0.0 collective-permute-done.2.refs_1_
  35.3 0.0 collective-permute-done.3.refs_2_
  35.3 1.2 %shard_map.67 = f32[16,4096]{1,0:T(8,128)} custom-call(f32[16,256]{1,0:T(8,128)S(1)} %slice.10.mine_ref, bf16[16,256]{1,0:T(8,128)(2,1)S(1)} %collective-permute-done.1.refs_0_, bf16[16,256]{1,0:T(8,128)(2,1)S(1)} %collective-permute-done.2.refs_1_, bf16[16,256]{1,0:T(8,128)(2,1)S(1)} %collective-permute-done.3.refs_2_, ...), custom_call_target="tpu_custom_call" | custom-call | tf_op jit(solution)/shard_map/pallas_call | solution.py:219
  (4 shorter events, 0.0 us)
Async XLA Ops:
  0.0 11.5 %collective-permute-start = (bf16[256,256]{1,0:T(8,128)(2,1)}, bf16[256,256]{1,0:T(8,128)(2,1)S(1)}, u32[]{:S(2)}, u32[]{:S(2)}) collective-permute-start(bf16[256,256]{1,0:T(8,128)(2,1)} %bitcast.5), channel_id=1, source_target_pairs={{0,16},{2,18},{4,20},{6,22},{8,24},{10,26},{12,28},{14,30},{16,0},... | collective-permute-start | bytes 393224 | tf_op jit(solution)/shard_map/ppermute | solution.py:159
  6.8 14.2 %all-to-all-start = ((bf16[8,144,256]{2,1,0:T(8,128)(2,1)}), bf16[8,144,256]{2,1,0:T(8,128)(2,1)S(1)}, u32[]{:S(2)}, u32[]{:S(2)}) async-start(bf16[8,144,256]{2,1,0:T(8,128)(2,1)} %get-tuple-element.8), calls=%async_computation | async-start | bytes 1179648 | tf_op jit(solution)/shard_map/all_to_all | solution.py:187
  30.6 4.7 %collective-permute-start.1 = (bf16[16,256]{1,0:T(8,128)(2,1)S(1)}, bf16[16,256]{1,0:T(8,128)(2,1)S(1)}, u32[]{:S(2)}, u32[]{:S(2)}) collective-permute-start(bf16[16,256]{1,0:T(8,128)(2,1)S(1)} %get-tuple-element.12), channel_id=1, source_target_pairs={{0,16},{1,17},{2,18},{3,19},{4,20},{5,21},{6,22},{7,23},{8,24},{9,... | collective-permute-start | bytes 24584 | tf_op jit(solution)/shard_map/ppermute | solution.py:215
  31.2 4.1 %collective-permute-start.2 = (bf16[16,256]{1,0:T(8,128)(2,1)S(1)}, bf16[16,256]{1,0:T(8,128)(2,1)S(1)}, u32[]{:S(2)}, u32[]{:S(2)}) collective-permute-start(bf16[16,256]{1,0:T(8,128)(2,1)S(1)} %get-tuple-element.12), channel_id=1, source_target_pairs={{0,17},{1,16},{2,19},{3,18},{4,21},{5,20},{6,23},{7,22},{8,25},{9,... | collective-permute-start | bytes 24584 | tf_op jit(solution)/shard_map/ppermute | solution.py:215
  31.4 3.9 %collective-permute-start.3 = (bf16[16,256]{1,0:T(8,128)(2,1)S(1)}, bf16[16,256]{1,0:T(8,128)(2,1)S(1)}, u32[]{:S(2)}, u32[]{:S(2)}) collective-permute-start(bf16[16,256]{1,0:T(8,128)(2,1)S(1)} %get-tuple-element.11), channel_id=1, source_target_pairs={{0,1},{1,0},{2,3},{3,2},{4,5},{5,4},{6,7},{7,6},{8,9},{9,8},{10,11... | collective-permute-start | bytes 24584 | tf_op jit(solution)/shard_map/ppermute | solution.py:215

commit v10 on v6

--- a/solution.py
+++ b/solution.py
@@ -11,6 +11,7 @@
 META_ROWS = 16
 RAY_BASE = 32
 LANES = 128
+LINE_CHUNKS = 4
 OVERLAP_FLOPS = 10**10
 VMEM_LIMIT = 32 * 1024 * 1024
 F32 = jnp.float32
@@ -102,14 +103,23 @@
     out_ref[...] = total.astype(BF16)
 
 
-def line_kernel(mine_ref, theirs_ref, line_ref, out_ref):
+def line_kernel(mine_ref, theirs_ref, line_ref, out_hbm, out_ref, sems):
     sums = mine_ref[...] + theirs_ref[...]
     rows = sums.shape[0]
     high = sums.astype(BF16)
     low = (sums - high.astype(F32)).astype(BF16)
     both = jnp.concatenate([high, low], axis=0)
-    got = jnp.dot(both, line_ref[...], preferred_element_type=F32)
-    out_ref[...] = got[:rows] + got[rows:]
+    chunks = sems.shape[0]
+    width = out_ref.shape[1] // chunks
+    copies = []
+    for i in range(chunks):
+        part = pl.ds(i * width, width)
+        got = jnp.dot(both, line_ref[:, part], preferred_element_type=F32)
+        out_ref[:, part] = got[:rows] + got[rows:]
+        copies.append(pltpu.make_async_copy(out_ref.at[:, part], out_hbm.at[:, part], sems.at[i]))
+        copies[-1].start()
+    for copy in copies:
+        copy.wait()
 
 
 class Plan:
@@ -146,7 +156,7 @@
     outgoing, own, held_line = pl.pallas_call(
         functools.partial(pack_kernel, plan),
         out_shape=[
-            jax.ShapeDtypeStruct(a, BF16)
+            pltpu.VMEM(a, BF16)
             for a in ((plan.targets, rows, levels), rate_tables.shape[1:], line_table.shape)
         ],
         in_specs=[smem] + [hbm] * 6,
@@ -204,11 +214,13 @@
         total = total + theirs if step > 1 else total
         theirs = lax.ppermute(total, "wave", [(i, i ^ step) for i in range(wave_total)])
         step *= 2
+    out_shape = (ray_rows, line_table.shape[1])
     return pl.pallas_call(
         line_kernel,
-        out_shape=jax.ShapeDtypeStruct((ray_rows, line_table.shape[1]), F32),
+        out_shape=jax.ShapeDtypeStruct(out_shape, F32),
         in_specs=[vmem, vmem, vmem],
-        out_specs=vmem,
+        out_specs=hbm,
+        scratch_shapes=[pltpu.VMEM(out_shape, F32), pltpu.SemaphoreType.DMA((LINE_CHUNKS,))],
         compiler_params=params,
     )(total, theirs, held_line)
 

time: 35.1 us -> 35 us (level)
  no operation moved by 1% of the time
where the time goes in v10:
time: 35 us; the launch traced here: 34.8 us
  waiting for transfers between devices  10.6 us (30%)
  blocking collectives  10.4 us (30%)
  starting transfers between devices  8.85 us (25%)
  Pallas kernels  4.88 us (14%)
    all_to_all x1, blocking collectives, per_device(): lax.all_to_all(partial_sums.reshape(bin_total, ray_rows, levels), 'bin',...  10.4 us
    all_to_all x1, waiting for transfers between devices, per_device(): lax.all_to_all(outgoing, 'bin', split_axis=0, concat_axis=0, tiled=True,...  9.42 us
    all_to_all x1, starting transfers between devices, per_device(): lax.all_to_all(outgoing, 'bin', split_axis=0, concat_axis=0, tiled=True,...  4.75 us
    ppermute x1, starting transfers between devices, per_device(): arrived = lax.ppermute(rate_tables[0], 'bin', plan.table_moves())  4.04 us
    pallas_call x1, Pallas kernels, per_device(): pl.pallas_call(functools.partial(pack_kernel, plan), out_shape=[pltpu.VME...  2.71 us
    ppermute x1, waiting for transfers between devices, per_device(): lax.ppermute(total, 'wave', [(i, i ^ step) for i in range(wave_total)])  1.17 us
    pallas_call x1, Pallas kernels, per_device(): pl.pallas_call(line_kernel, out_shape=jax.ShapeDtypeStruct(out_shape, F32...  1.13 us
    pallas_call x1, Pallas kernels, per_device(): pl.pallas_call(functools.partial(level_kernel, plan, rays), out_shape=jax...  1.04 us
  transfers between devices with their start and end apart: 3, of which 2 were waited for; matrix products, arithmetic and copies ran while one was open for 0% of the time, Pallas kernels for 8%

profile of v10, /device:TPU:0, one launch (start us, length us, event | category | flops | bytes accessed | tf_op | source)
XLA Modules:
  0.0 34.8 jit_solution(7969489045136848823)
XLA Ops:
  0.0 4.0 %collective-permute-start = (bf16[256,256]{1,0:T(8,128)(2,1)}, bf16[256,256]{1,0:T(8,128)(2,1)S(1)}, u32[]{:S(2)}, u32[]{:S(2)}) collective-permute-start(bf16[256,256]{1,0:T(8,128)(2,1)} %bitcast.7), channel_id=1, source_target_pairs={{0,16},{2,18},{4,20},{6,22},{8,24},{10,26},{12,28},{14,30},{16,0},... | collective-permute-start | bytes 393224 | tf_op jit(solution)/shard_map/ppermute | solution.py:153
  4.0 2.7 %shard_map.64 = (bf16[8,144,256]{2,1,0:T(8,128)(2,1)}, bf16[256,256]{1,0:T(8,128)(2,1)S(1)}, bf16[256,4096]{1,0:T(8,128)(2,1)S(1)}) custom-call(s32[1]{0:T(128)} %bitcast.me_ref, bf16[512,256]{1,0:T(8,128)(2,1)} %src_hbm.1, bf16[4,128]{1,0:T(4,128)(2,1)} %bitcast.11, s32[1,512]{1,0:T(1,128)} %bitcast.9, s32[1,512]{1,0:T(1,128)} %bitcast.10, ...), custom_call_target="tpu_custom_call" | custom-call | tf_op jit(solution)/shard_map/pallas_call | solution.py:156
  6.8 4.7 %all-to-all-start = ((bf16[8,144,256]{2,1,0:T(8,128)(2,1)}), bf16[8,144,256]{2,1,0:T(8,128)(2,1)S(1)}, u32[]{:S(2)}, u32[]{:S(2)}) async-start(bf16[8,144,256]{2,1,0:T(8,128)(2,1)} %get-tuple-element.8), calls=%async_computation | async-start | bytes 1179648 | tf_op jit(solution)/shard_map/all_to_all | solution.py:181
  11.5 0.0 collective-permute-done.table_ref
  11.5 9.4 %all-to-all-done.got_ref = bf16[8,144,256]{2,1,0:T(8,128)(2,1)S(1)} async-done(((bf16[8,144,256]{2,1,0:T(8,128)(2,1)}), bf16[8,144,256]{2,1,0:T(8,128)(2,1)S(1)}, u32[]{:S(2)}, u32[]{:S(2)}) %all-to-all-start) | async-done | bytes 589856 | tf_op jit(solution)/shard_map/all_to_all | solution.py:181
  20.9 1.0 %shard_map.66 = bf16[256,256]{1,0:T(8,128)(2,1)S(1)} custom-call(bf16[8,144,256]{2,1,0:T(8,128)(2,1)S(1)} %all-to-all-done.got_ref, bf16[256,256]{1,0:T(8,128)(2,1)S(1)} %get-tuple-element.9.refs_0_, bf16[256,256]{1,0:T(8,128)(2,1)S(1)} %shard_map.65.refs_1_), custom_call_target="tpu_custom_call" | custom-call | tf_op jit(solution)/shard_map/pallas_call | solution.py:196
  22.0 10.4 %all_to_all.10 = bf16[16,16,256]{2,1,0:T(8,128)(2,1)S(1)} all-to-all(bf16[16,16,256]{2,1,0:T(8,128)(2,1)S(1)} %bitcast.6), channel_id=1, replica_groups=mesh['bin'=16,'wave'=2] {'bin'}, dimensions={0} | all-to-all | bytes 262144 | tf_op jit(solution)/shard_map/all_to_all | solution.py:203
  32.4 0.1 collective-permute-start.1
  32.5 1.2 %collective-permute-done.1.theirs_ref = f32[16,256]{1,0:T(8,128)S(1)} collective-permute-done((f32[16,256]{1,0:T(8,128)S(1)}, f32[16,256]{1,0:T(8,128)S(1)}, u32[]{:S(2)}, u32[]{:S(2)}) %collective-permute-start.1) | collective-permute-done | bytes 16416 | tf_op jit(solution)/shard_map/ppermute | solution.py:215
  33.7 1.1 %shard_map.67 = f32[16,4096]{1,0:T(8,128)} custom-call(f32[16,256]{1,0:T(8,128)S(1)} %convert_reduce_fusion.mine_ref, f32[16,256]{1,0:T(8,128)S(1)} %collective-permute-done.1.theirs_ref, bf16[256,4096]{1,0:T(8,128)(2,1)S(1)} %get-tuple-element.10.line_ref), custom_call_target="tpu_custom_call" | custom-call | tf_op jit(solution)/shard_map/pallas_call | solution.py:218
  (2 shorter events, 0.0 us)
Async XLA Ops:
  0.0 11.5 %collective-permute-start = (bf16[256,256]{1,0:T(8,128)(2,1)}, bf16[256,256]{1,0:T(8,128)(2,1)S(1)}, u32[]{:S(2)}, u32[]{:S(2)}) collective-permute-start(bf16[256,256]{1,0:T(8,128)(2,1)} %bitcast.7), channel_id=1, source_target_pairs={{0,16},{2,18},{4,20},{6,22},{8,24},{10,26},{12,28},{14,30},{16,0},... | collective-permute-start | bytes 393224 | tf_op jit(solution)/shard_map/ppermute | solution.py:153
  6.8 14.2 %all-to-all-start = ((bf16[8,144,256]{2,1,0:T(8,128)(2,1)}), bf16[8,144,256]{2,1,0:T(8,128)(2,1)S(1)}, u32[]{:S(2)}, u32[]{:S(2)}) async-start(bf16[8,144,256]{2,1,0:T(8,128)(2,1)} %get-tuple-element.8), calls=%async_computation | async-start | bytes 1179648 | tf_op jit(solution)/shard_map/all_to_all | solution.py:181
  32.4 1.2 %collective-permute-start.1 = (f32[16,256]{1,0:T(8,128)S(1)}, f32[16,256]{1,0:T(8,128)S(1)}, u32[]{:S(2)}, u32[]{:S(2)}) collective-permute-start(f32[16,256]{1,0:T(8,128)S(1)} %convert_reduce_fusion.mine_ref), channel_id=1, source_target_pairs={{0,1},{1,0},{2,3},{3,2},{4,5},{5,4},{6,7},{7,6},{8,9},{9,8},{10,11... | collective-permute-start | bytes 49160 | tf_op jit(solution)/shard_map/ppermute | solution.py:215

commit v11 on v6

--- a/solution.py
+++ b/solution.py
@@ -28,7 +28,8 @@
 
 def pack_kernel(plan, me_ref, src_hbm, den_hbm, bin_hbm, ray_hbm, table_hbm, line_hbm, *rest):
     targets, block = plan.targets, plan.block
-    out, table_out, line_out, src_ref, den_ref, bin_ref, ray_ref, sems = rest
+    outs, table_out, line_out = rest[:targets], rest[targets], rest[targets + 1]
+    src_ref, den_ref, bin_ref, ray_ref, sems = rest[targets + 2 :]
     copies = [
         pltpu.make_async_copy(a, b, sems.at[i])
         for i, (a, b) in enumerate(
@@ -46,15 +47,15 @@
         copy.start()
     cells, levels = src_ref.shape
     earlier = (iota((cells, cells), 0) < iota((cells, cells), 1)).astype(F32).astype(BF16)
-    my_half = me_ref[0] // targets
     for copy in copies[:3]:
         copy.wait()
     bins = bin_ref[...]
     hot = (iota((plan.bins, cells), 0) == bins).astype(F32)
     before = jnp.dot(hot.astype(BF16), earlier, preferred_element_type=F32)
     position = jnp.sum(hot * before, axis=0, keepdims=True).astype(I32)
-    half = bins // targets
-    slot = (bins - half * targets) * block + (half ^ my_half) * plan.capacity + position
+    turn = bins ^ me_ref[0]
+    half = turn // targets
+    slot = (turn - half * targets) * block + half * plan.capacity + position
     rays = ray_ref[...]
     ray_high = rays // RAY_BASE
     ray_low = rays - ray_high * RAY_BASE
@@ -68,10 +69,11 @@
     moved = nt_dot(meta, place).astype(BF16)
     copies[3].wait()
     rows = jnp.dot(place, src_ref[...], preferred_element_type=F32).astype(BF16)
-    out[:, :block, :] = rows.reshape(targets, block, levels)
-    out[:, block:, :] = jnp.zeros((targets, META_ROWS, levels), BF16)
     for t in range(targets):
-        out[t, block:, :block] = moved[:, t * block : (t + 1) * block]
+        first, last = t * block, (t + 1) * block
+        outs[t][:block, :] = rows[first:last]
+        outs[t][block:, :] = jnp.zeros((META_ROWS, levels), BF16)
+        outs[t][block:, :block] = moved[:, first:last]
     for copy in copies[4:]:
         copy.wait()
 
@@ -80,15 +82,15 @@
     out_ref[...] = table_ref[...]
 
 
-def level_kernel(plan, rays, got_ref, *refs):
-    table_refs, out_ref = refs[:-1], refs[-1]
-    targets, block = plan.targets, plan.block
-    meta = [got_ref[s, block:, :block].astype(F32) for s in range(targets)]
+def level_kernel(plan, rays, *refs):
+    got, table_refs, out_ref = refs[: plan.targets], refs[plan.targets : -1], refs[-1]
+    block = plan.block
+    meta = [g[block:, :block].astype(F32) for g in got]
     columns = [jnp.transpose(m[:8]) for m in meta]
     total = jnp.zeros(out_ref.shape, F32)
     for part, table_ref in enumerate(table_refs):
         low, high = part * plan.capacity, (part + 1) * plan.capacity
-        src = got_ref[:, low:high, :].reshape(targets * plan.capacity, got_ref.shape[2])
+        src = jnp.concatenate([g[low:high, :] for g in got], axis=0)
         den = jnp.concatenate([c[low:high, 0:1] for c in columns], axis=0)
         ray = jnp.concatenate(
             [m[1:2, low:high] * RAY_BASE + m[2:3, low:high] for m in meta], axis=1
@@ -122,8 +124,11 @@
     def table_moves(self):
         return [(i, (i + self.targets) % self.bins) for i in range(self.bins)]
 
-    def halves(self):
-        return [list(range(self.targets)), list(range(self.targets, self.bins))]
+    def order(self):
+        return sorted(range(1, self.targets), key=lambda k: -bin(k).count("1"))
+
+    def moves(self, k):
+        return [(i, i ^ k) for i in range(self.bins)]
 
 
 def per_device(sources, density, temp_bins, ray_index, rate_tables, line_table):
@@ -143,14 +148,14 @@
     arrived = lax.ppermute(rate_tables[0], "bin", plan.table_moves())
     me = lax.axis_index("bin").astype(I32).reshape(1)
     den_rows = cells // min(cells, LANES)
-    outgoing, own, held_line = pl.pallas_call(
+    *outgoing, own, held_line = pl.pallas_call(
         functools.partial(pack_kernel, plan),
         out_shape=[
             jax.ShapeDtypeStruct(a, BF16)
-            for a in ((plan.targets, rows, levels), rate_tables.shape[1:], line_table.shape)
+            for a in [(rows, levels)] * plan.targets + [rate_tables.shape[1:], line_table.shape]
         ],
         in_specs=[smem] + [hbm] * 6,
-        out_specs=[vmem] * 3,
+        out_specs=[vmem] * (plan.targets + 2),
         scratch_shapes=[
             pltpu.VMEM((cells, levels), BF16),
             pltpu.VMEM((den_rows, cells // den_rows), BF16),
@@ -168,9 +173,7 @@
         in_hbm(rate_tables[0]),
         in_hbm(line_table),
     )
-    got = lax.all_to_all(
-        outgoing, "bin", split_axis=0, concat_axis=0, tiled=True, axis_index_groups=plan.halves()
-    )
+    got = [lax.ppermute(outgoing[k], "bin", plan.moves(k)) for k in plan.order()]
     other = pl.pallas_call(
         keep_kernel,
         out_shape=jax.ShapeDtypeStruct(arrived.shape, BF16),
@@ -186,10 +189,10 @@
     partial_sums = pl.pallas_call(
         functools.partial(level_kernel, plan, rays),
         out_shape=jax.ShapeDtypeStruct((rays, levels), BF16),
-        in_specs=[vmem] * 3,
+        in_specs=[vmem] * (plan.targets + 2),
         out_specs=vmem,
         compiler_params=params,
-    )(got, own, other)
+    )(*got, outgoing[0], own, other)
     held = lax.all_to_all(
         partial_sums.reshape(bin_total, ray_rows, levels),
         "bin",

time: 35.1 us -> 36.6 us (1.043)
  starting transfers between devices: 8.85 us -> 15.3 us
  waiting for transfers between devices: 10.6 us -> 6.15 us
  Pallas kernels: 4.92 us -> 4.11 us
  blocking collectives: 10.4 us -> 10.8 us
    ppermute x0 -> x7, starting transfers between devices: none -> 11.2 us  [per_device(): lax.ppermute(outgoing[k], 'bin', plan.moves(k))]
    all_to_all x1 -> x0, waiting for transfers between devices: 9.42 us -> none  [per_device(): lax.all_to_all(outgoing, 'bin', split_axis=0, concat_axis=0, tiled=True,...]
    ppermute x0 -> x7, waiting for transfers between devices: none -> 4.97 us  [per_device(): lax.ppermute(outgoing[k], 'bin', plan.moves(k))]
    all_to_all x1 -> x0, starting transfers between devices: 4.75 us -> none  [per_device(): lax.all_to_all(outgoing, 'bin', split_axis=0, concat_axis=0, tiled=True,...]
    pallas_call x1, Pallas kernels: 2.71 us -> 1.9 us  [per_device(): pl.pallas_call(functools.partial(pack_kernel, plan), out_shape=[jax.Shape...]
    all_to_all x1, blocking collectives: 10.4 us -> 10.8 us  [per_device(): lax.all_to_all(partial_sums.reshape(bin_total, ray_rows, levels), 'bin',...]
  transfers between devices with their start and end apart: 3 -> 9, of which waited for: 2 -> 4; matrix products, arithmetic and copies ran while one was open for 0% -> 0% of each run, Pallas kernels for 8% -> 5%
where the time goes in v11:
time: 36.6 us; the launch traced here: 36.5 us
  starting transfers between devices  15.3 us (42%)
  blocking collectives  10.8 us (30%)
  waiting for transfers between devices  6.15 us (17%)
  Pallas kernels  4.11 us (11%)
    ppermute x7, starting transfers between devices, per_device(): lax.ppermute(outgoing[k], 'bin', plan.moves(k))  11.2 us
    all_to_all x1, blocking collectives, per_device(): lax.all_to_all(partial_sums.reshape(bin_total, ray_rows, levels), 'bin',...  10.8 us
    ppermute x7, waiting for transfers between devices, per_device(): lax.ppermute(outgoing[k], 'bin', plan.moves(k))  4.97 us
    ppermute x1, starting transfers between devices, per_device(): arrived = lax.ppermute(rate_tables[0], 'bin', plan.table_moves())  4.04 us
    pallas_call x1, Pallas kernels, per_device(): pl.pallas_call(functools.partial(pack_kernel, plan), out_shape=[jax.Shape...  1.9 us
    ppermute x1, waiting for transfers between devices, per_device(): lax.ppermute(total, 'wave', [(i, i ^ step) for i in range(wave_total)])  1.17 us
    pallas_call x1, Pallas kernels, per_device(): pl.pallas_call(line_kernel, out_shape=jax.ShapeDtypeStruct((ray_rows, lin...  1.17 us
    pallas_call x1, Pallas kernels, per_device(): pl.pallas_call(functools.partial(level_kernel, plan, rays), out_shape=jax...  1.04 us
  transfers between devices with their start and end apart: 9, of which 4 were waited for; matrix products, arithmetic and copies ran while one was open for 0% of the time, Pallas kernels for 5%

profile of v11, /device:TPU:0, one launch (start us, length us, event | category | flops | bytes accessed | tf_op | source)
XLA Modules:
  0.0 36.5 jit_solution(18429886970088378821)
XLA Ops:
  0.0 4.0 %collective-permute-start.7 = (bf16[256,256]{1,0:T(8,128)(2,1)}, bf16[256,256]{1,0:T(8,128)(2,1)S(1)}, u32[]{:S(2)}, u32[]{:S(2)}) collective-permute-start(bf16[256,256]{1,0:T(8,128)(2,1)} %bitcast.7), channel_id=1, source_target_pairs={{0,16},{2,18},{4,20},{6,22},{8,24},{10,26},{12,28},{14,30},{16,0},... | collective-permute-start | bytes 393224 | tf_op jit(solution)/shard_map/ppermute | solution.py:148
  4.0 1.9 %shard_map.64 = (bf16[144,256]{1,0:T(8,128)(2,1)S(1)}, bf16[144,256]{1,0:T(8,128)(2,1)S(1)}, bf16[144,256]{1,0:T(8,128)(2,1)S(1)}, bf16[144,256]{1,0:T(8,128)(2,...) custom-call(s32[1]{0:T(128)} %bitcast.me_ref, ...), custom_call_target="tpu_custom_call" | custom-call | tf_op jit(solution)/shard_map/pallas_call | solution.py:151
  5.9 3.5 %collective-permute-start = (bf16[144,256]{1,0:T(8,128)(2,1)S(1)}, bf16[144,256]{1,0:T(8,128)(2,1)S(1)}, u32[]{:S(2)}, u32[]{:S(2)}) collective-permute-start(bf16[144,256]{1,0:T(8,128)(2,1)S(1)} %get-tuple-element.15), channel_id=1, source_target_pairs={{0,14},{2,12},{4,10},{6,8},{8,6},{10,4},{12,2},{14,0},{16,30},{18,... | collective-permute-start | bytes 221192 | tf_op jit(solution)/shard_map/ppermute | solution.py:176
  9.5 0.5 %collective-permute-start.1 = (bf16[144,256]{1,0:T(8,128)(2,1)S(1)}, bf16[144,256]{1,0:T(8,128)(2,1)S(1)}, u32[]{:S(2)}, u32[]{:S(2)}) collective-permute-start(bf16[144,256]{1,0:T(8,128)(2,1)S(1)} %get-tuple-element.16), channel_id=1, source_target_pairs={{0,6},{2,4},{4,2},{6,0},{8,14},{10,12},{12,10},{14,8},{16,22},{18,... | collective-permute-start | bytes 221192 | tf_op jit(solution)/shard_map/ppermute | solution.py:176
  9.9 1.4 %collective-permute-start.2 = (bf16[144,256]{1,0:T(8,128)(2,1)S(1)}, bf16[144,256]{1,0:T(8,128)(2,1)S(1)}, u32[]{:S(2)}, u32[]{:S(2)}) collective-permute-start(bf16[144,256]{1,0:T(8,128)(2,1)S(1)} %get-tuple-element.17), channel_id=1, source_target_pairs={{0,10},{2,8},{4,14},{6,12},{8,2},{10,0},{12,6},{14,4},{16,26},{18,... | collective-permute-start | bytes 221192 | tf_op jit(solution)/shard_map/ppermute | solution.py:176
  11.3 2.5 %collective-permute-start.3 = (bf16[144,256]{1,0:T(8,128)(2,1)S(1)}, bf16[144,256]{1,0:T(8,128)(2,1)S(1)}, u32[]{:S(2)}, u32[]{:S(2)}) collective-permute-start(bf16[144,256]{1,0:T(8,128)(2,1)S(1)} %get-tuple-element.18), channel_id=1, source_target_pairs={{0,12},{2,14},{4,8},{6,10},{8,4},{10,6},{12,0},{14,2},{16,28},{18,... | collective-permute-start | bytes 221192 | tf_op jit(solution)/shard_map/ppermute | solution.py:176
  13.9 0.0 collective-permute-done.refs_0_
  13.9 0.8 %collective-permute-start.4 = (bf16[144,256]{1,0:T(8,128)(2,1)S(1)}, bf16[144,256]{1,0:T(8,128)(2,1)S(1)}, u32[]{:S(2)}, u32[]{:S(2)}) collective-permute-start(bf16[144,256]{1,0:T(8,128)(2,1)S(1)} %get-tuple-element.19), channel_id=1, source_target_pairs={{0,2},{2,0},{4,6},{6,4},{8,10},{10,8},{12,14},{14,12},{16,18},{18,... | collective-permute-start | bytes 221192 | tf_op jit(solution)/shard_map/ppermute | solution.py:176
  14.7 1.2 %collective-permute-done.1.refs_1_ = bf16[144,256]{1,0:T(8,128)(2,1)S(1)} collective-permute-done((bf16[144,256]{1,0:T(8,128)(2,1)S(1)}, bf16[144,256]{1,0:T(8,128)(2,1)S(1)}, u32[]{:S(2)}, u32[]{:S(2)}) %collective-permute-start.1) | collective-permute-done | bytes 73760 | tf_op jit(solution)/shard_map/ppermute | solution.py:176
  16.0 1.8 %collective-permute-start.5 = (bf16[144,256]{1,0:T(8,128)(2,1)S(1)}, bf16[144,256]{1,0:T(8,128)(2,1)S(1)}, u32[]{:S(2)}, u32[]{:S(2)}) collective-permute-start(bf16[144,256]{1,0:T(8,128)(2,1)S(1)} %get-tuple-element.20), channel_id=1, source_target_pairs={{0,4},{2,6},{4,0},{6,2},{8,12},{10,14},{12,8},{14,10},{16,20},{18,... | collective-permute-start | bytes 221192 | tf_op jit(solution)/shard_map/ppermute | solution.py:176
  17.8 0.0 collective-permute-done.7.table_ref
  17.8 0.6 %collective-permute-start.6 = (bf16[144,256]{1,0:T(8,128)(2,1)S(1)}, bf16[144,256]{1,0:T(8,128)(2,1)S(1)}, u32[]{:S(2)}, u32[]{:S(2)}) collective-permute-start(bf16[144,256]{1,0:T(8,128)(2,1)S(1)} %get-tuple-element.21), channel_id=1, source_target_pairs={{0,8},{2,10},{4,12},{6,14},{8,0},{10,2},{12,4},{14,6},{16,24},{18,... | collective-permute-start | bytes 221192 | tf_op jit(solution)/shard_map/ppermute | solution.py:176
  18.4 0.0 collective-permute-done.2.refs_2_
  18.4 0.0 collective-permute-done.3.refs_3_
  18.4 0.0 collective-permute-done.4.refs_4_
  18.4 1.9 %collective-permute-done.5.refs_5_ = bf16[144,256]{1,0:T(8,128)(2,1)S(1)} collective-permute-done((bf16[144,256]{1,0:T(8,128)(2,1)S(1)}, bf16[144,256]{1,0:T(8,128)(2,1)S(1)}, u32[]{:S(2)}, u32[]{:S(2)}) %collective-permute-start.5) | collective-permute-done | bytes 73760 | tf_op jit(solution)/shard_map/ppermute | solution.py:176
  20.3 1.8 %collective-permute-done.6.refs_6_ = bf16[144,256]{1,0:T(8,128)(2,1)S(1)} collective-permute-done((bf16[144,256]{1,0:T(8,128)(2,1)S(1)}, bf16[144,256]{1,0:T(8,128)(2,1)S(1)}, u32[]{:S(2)}, u32[]{:S(2)}) %collective-permute-start.6) | collective-permute-done | bytes 73760 | tf_op jit(solution)/shard_map/ppermute | solution.py:176
  22.1 1.0 %shard_map.66 = bf16[256,256]{1,0:T(8,128)(2,1)S(1)} custom-call(bf16[144,256]{1,0:T(8,128)(2,1)S(1)} %collective-permute-done.refs_0_, bf16[144,256]{1,0:T(8,128)(2,1)S(1)} %collective-permute-done.1.refs_1_, bf16[144,256]{1,0:T(8,128)(2,1)S(1)} %collective-permute-done.2.refs_2_, bf16[144,256]{1,0:T(8,128)(2,1)S(1)} %collective-permute-done.3.refs_3_, ...), custom_call_target="tpu_custom_call" | custom-call | tf_op jit(solution)/shard_map/pallas_call | solution.py:189
  23.2 10.8 %all_to_all.5 = bf16[16,16,256]{2,1,0:T(8,128)(2,1)S(1)} all-to-all(bf16[16,16,256]{2,1,0:T(8,128)(2,1)S(1)} %bitcast.6), channel_id=1, replica_groups=mesh['bin'=16,'wave'=2] {'bin'}, dimensions={0} | all-to-all | bytes 262144 | tf_op jit(solution)/shard_map/all_to_all | solution.py:196
  34.0 0.1 collective-permute-start.8
  34.1 1.2 %collective-permute-done.8.theirs_ref = f32[16,256]{1,0:T(8,128)S(1)} collective-permute-done((f32[16,256]{1,0:T(8,128)S(1)}, f32[16,256]{1,0:T(8,128)S(1)}, u32[]{:S(2)}, u32[]{:S(2)}) %collective-permute-start.8) | collective-permute-done | bytes 16416 | tf_op jit(solution)/shard_map/ppermute | solution.py:208
  35.3 1.2 %shard_map.67 = f32[16,4096]{1,0:T(8,128)} custom-call(f32[16,256]{1,0:T(8,128)S(1)} %convert_reduce_fusion.mine_ref, f32[16,256]{1,0:T(8,128)S(1)} %collective-permute-done.8.theirs_ref, bf16[256,4096]{1,0:T(8,128)(2,1)S(1)} %get-tuple-element.24.line_ref), custom_call_target="tpu_custom_call" | custom-call | tf_op jit(solution)/shard_map/pallas_call | solution.py:210
  (2 shorter events, 0.0 us)
Async XLA Ops:
  0.0 17.8 %collective-permute-start.7 = (bf16[256,256]{1,0:T(8,128)(2,1)}, bf16[256,256]{1,0:T(8,128)(2,1)S(1)}, u32[]{:S(2)}, u32[]{:S(2)}) collective-permute-start(bf16[256,256]{1,0:T(8,128)(2,1)} %bitcast.7), channel_id=1, source_target_pairs={{0,16},{2,18},{4,20},{6,22},{8,24},{10,26},{12,28},{14,30},{16,0},... | collective-permute-start | bytes 393224 | tf_op jit(solution)/shard_map/ppermute | solution.py:148
  5.9 7.9 %collective-permute-start = (bf16[144,256]{1,0:T(8,128)(2,1)S(1)}, bf16[144,256]{1,0:T(8,128)(2,1)S(1)}, u32[]{:S(2)}, u32[]{:S(2)}) collective-permute-start(bf16[144,256]{1,0:T(8,128)(2,1)S(1)} %get-tuple-element.15), channel_id=1, source_target_pairs={{0,14},{2,12},{4,10},{6,8},{8,6},{10,4},{12,2},{14,0},{16,30},{18,... | collective-permute-start | bytes 221192 | tf_op jit(solution)/shard_map/ppermute | solution.py:176
  9.5 6.5 %collective-permute-start.1 = (bf16[144,256]{1,0:T(8,128)(2,1)S(1)}, bf16[144,256]{1,0:T(8,128)(2,1)S(1)}, u32[]{:S(2)}, u32[]{:S(2)}) collective-permute-start(bf16[144,256]{1,0:T(8,128)(2,1)S(1)} %get-tuple-element.16), channel_id=1, source_target_pairs={{0,6},{2,4},{4,2},{6,0},{8,14},{10,12},{12,10},{14,8},{16,22},{18,... | collective-permute-start | bytes 221192 | tf_op jit(solution)/shard_map/ppermute | solution.py:176
  9.9 8.4 %collective-permute-start.2 = (bf16[144,256]{1,0:T(8,128)(2,1)S(1)}, bf16[144,256]{1,0:T(8,128)(2,1)S(1)}, u32[]{:S(2)}, u32[]{:S(2)}) collective-permute-start(bf16[144,256]{1,0:T(8,128)(2,1)S(1)} %get-tuple-element.17), channel_id=1, source_target_pairs={{0,10},{2,8},{4,14},{6,12},{8,2},{10,0},{12,6},{14,4},{16,26},{18,... | collective-permute-start | bytes 221192 | tf_op jit(solution)/shard_map/ppermute | solution.py:176
  11.3 7.1 %collective-permute-start.3 = (bf16[144,256]{1,0:T(8,128)(2,1)S(1)}, bf16[144,256]{1,0:T(8,128)(2,1)S(1)}, u32[]{:S(2)}, u32[]{:S(2)}) collective-permute-start(bf16[144,256]{1,0:T(8,128)(2,1)S(1)} %get-tuple-element.18), channel_id=1, source_target_pairs={{0,12},{2,14},{4,8},{6,10},{8,4},{10,6},{12,0},{14,2},{16,28},{18,... | collective-permute-start | bytes 221192 | tf_op jit(solution)/shard_map/ppermute | solution.py:176
  13.9 4.5 %collective-permute-start.4 = (bf16[144,256]{1,0:T(8,128)(2,1)S(1)}, bf16[144,256]{1,0:T(8,128)(2,1)S(1)}, u32[]{:S(2)}, u32[]{:S(2)}) collective-permute-start(bf16[144,256]{1,0:T(8,128)(2,1)S(1)} %get-tuple-element.19), channel_id=1, source_target_pairs={{0,2},{2,0},{4,6},{6,4},{8,10},{10,8},{12,14},{14,12},{16,18},{18,... | collective-permute-start | bytes 221192 | tf_op jit(solution)/shard_map/ppermute | solution.py:176
  16.0 4.4 %collective-permute-start.5 = (bf16[144,256]{1,0:T(8,128)(2,1)S(1)}, bf16[144,256]{1,0:T(8,128)(2,1)S(1)}, u32[]{:S(2)}, u32[]{:S(2)}) collective-permute-start(bf16[144,256]{1,0:T(8,128)(2,1)S(1)} %get-tuple-element.20), channel_id=1, source_target_pairs={{0,4},{2,6},{4,0},{6,2},{8,12},{10,14},{12,8},{14,10},{16,20},{18,... | collective-permute-start | bytes 221192 | tf_op jit(solution)/shard_map/ppermute | solution.py:176
  17.8 4.4 %collective-permute-start.6 = (bf16[144,256]{1,0:T(8,128)(2,1)S(1)}, bf16[144,256]{1,0:T(8,128)(2,1)S(1)}, u32[]{:S(2)}, u32[]{:S(2)}) collective-permute-start(bf16[144,256]{1,0:T(8,128)(2,1)S(1)} %get-tuple-element.21), channel_id=1, source_target_pairs={{0,8},{2,10},{4,12},{6,14},{8,0},{10,2},{12,4},{14,6},{16,24},{18,... | collective-permute-start | bytes 221192 | tf_op jit(solution)/shard_map/ppermute | solution.py:176
  34.0 1.2 %collective-permute-start.8 = (f32[16,256]{1,0:T(8,128)S(1)}, f32[16,256]{1,0:T(8,128)S(1)}, u32[]{:S(2)}, u32[]{:S(2)}) collective-permute-start(f32[16,256]{1,0:T(8,128)S(1)} %convert_reduce_fusion.mine_ref), channel_id=1, source_target_pairs={{0,1},{1,0},{2,3},{3,2},{4,5},{5,4},{6,7},{7,6},{8,9},{9,8},{10,11... | collective-permute-start | bytes 49160 | tf_op jit(solution)/shard_map/ppermute | solution.py:208

commit v12 on v6

--- a/solution.py
+++ b/solution.py
@@ -11,6 +11,7 @@
 META_ROWS = 16
 RAY_BASE = 32
 LANES = 128
+PACK_GROUPS = 2
 OVERLAP_FLOPS = 10**10
 VMEM_LIMIT = 32 * 1024 * 1024
 F32 = jnp.float32
@@ -26,29 +27,34 @@
     return lax.broadcasted_iota(I32, shape, dim)
 
 
-def pack_kernel(plan, me_ref, src_hbm, den_hbm, bin_hbm, ray_hbm, table_hbm, line_hbm, *rest):
-    targets, block = plan.targets, plan.block
-    out, table_out, line_out, src_ref, den_ref, bin_ref, ray_ref, sems = rest
+def load_kernel(plan, me_ref, *refs):
+    hbm_refs, vmem_refs, out_hbm = refs[:5], refs[5:10], refs[10]
+    held, in_sems, out_sems = refs[11:]
     copies = [
-        pltpu.make_async_copy(a, b, sems.at[i])
-        for i, (a, b) in enumerate(
-            (
-                (bin_hbm, bin_ref),
-                (ray_hbm, ray_ref),
-                (den_hbm, den_ref),
-                (src_hbm, src_ref),
-                (table_hbm, table_out),
-                (line_hbm, line_out),
-            )
-        )
+        pltpu.make_async_copy(a, b, in_sems.at[i])
+        for i, (a, b) in enumerate(zip(hbm_refs, vmem_refs))
     ]
     for copy in copies:
         copy.start()
+    for copy in copies:
+        copy.wait()
+
+    @pl.when(me_ref[0] < plan.targets)
+    def _():
+        pack(plan, 0, *vmem_refs[:4], out_hbm, held, out_sems)
+
+
+def pack_kernel(plan, me_ref, src_ref, den_ref, bin_ref, ray_ref, _, out_hbm, held, out_sems):
+    @pl.when(me_ref[0] >= plan.targets)
+    def _():
+        pack(plan, 1, src_ref, den_ref, bin_ref, ray_ref, out_hbm, held, out_sems)
+
+
+def pack(plan, my_half, src_ref, den_ref, bin_ref, ray_ref, out_hbm, held, out_sems):
+    targets, block = plan.targets, plan.block
     cells, levels = src_ref.shape
     earlier = (iota((cells, cells), 0) < iota((cells, cells), 1)).astype(F32).astype(BF16)
-    my_half = me_ref[0] // targets
-    for copy in copies[:3]:
-        copy.wait()
+    held[:, block:, :] = jnp.zeros((targets, META_ROWS, levels), BF16)
     bins = bin_ref[...]
     hot = (iota((plan.bins, cells), 0) == bins).astype(F32)
     before = jnp.dot(hot.astype(BF16), earlier, preferred_element_type=F32)
@@ -66,18 +72,28 @@
     ).astype(BF16)
     place = (iota((targets * block, cells), 0) == slot).astype(F32).astype(BF16)
     moved = nt_dot(meta, place).astype(BF16)
-    copies[3].wait()
-    rows = jnp.dot(place, src_ref[...], preferred_element_type=F32).astype(BF16)
-    out[:, :block, :] = rows.reshape(targets, block, levels)
-    out[:, block:, :] = jnp.zeros((targets, META_ROWS, levels), BF16)
-    for t in range(targets):
-        out[t, block:, :block] = moved[:, t * block : (t + 1) * block]
-    for copy in copies[4:]:
+    src = src_ref[...]
+    leaving = []
+    group = max(1, targets // PACK_GROUPS)
+    for first in range(0, targets, group):
+        last = first + group
+        rows = jnp.dot(place[first * block : last * block], src, preferred_element_type=F32)
+        held[first:last, :block, :] = rows.astype(BF16).reshape(group, block, levels)
+        for t in range(first, last):
+            held[t, block:, :block] = moved[:, t * block : (t + 1) * block]
+        part = pl.ds(first, group)
+        copy = pltpu.make_async_copy(held.at[part], out_hbm.at[part], out_sems.at[len(leaving)])
+        copy.start()
+        leaving.append(copy)
+    for copy in leaving:
         copy.wait()
 
 
-def keep_kernel(table_ref, out_ref):
-    out_ref[...] = table_ref[...]
+def keep_kernel(arrived_ref, line_hbm, other_ref, line_ref, sem):
+    copy = pltpu.make_async_copy(line_hbm, line_ref, sem)
+    copy.start()
+    other_ref[...] = arrived_ref[...]
+    copy.wait()
 
 
 def level_kernel(plan, rays, got_ref, *refs):
@@ -140,47 +156,56 @@
     def in_hbm(x):
         return pltpu.with_memory_space_constraint(x, pltpu.HBM)
 
-    arrived = lax.ppermute(rate_tables[0], "bin", plan.table_moves())
     me = lax.axis_index("bin").astype(I32).reshape(1)
     den_rows = cells // min(cells, LANES)
-    outgoing, own, held_line = pl.pallas_call(
+    inputs = [
+        in_hbm(x)
+        for x in (
+            sources,
+            density.reshape(den_rows, cells // den_rows),
+            temp_bins.reshape(1, cells),
+            ray_index.reshape(1, cells),
+            rate_tables[0],
+        )
+    ]
+    blocks = jax.ShapeDtypeStruct((plan.targets, rows, levels), BF16)
+    scratch = [
+        pltpu.VMEM(blocks.shape, BF16),
+        pltpu.SemaphoreType.DMA((len(inputs),)),
+        pltpu.SemaphoreType.DMA((PACK_GROUPS,)),
+    ]
+    *loaded, own, outgoing = pl.pallas_call(
+        functools.partial(load_kernel, plan),
+        out_shape=[jax.ShapeDtypeStruct(x.shape, x.dtype) for x in inputs] + [blocks],
+        in_specs=[smem] + [hbm] * len(inputs),
+        out_specs=[vmem] * len(inputs) + [hbm],
+        scratch_shapes=scratch,
+        compiler_params=params,
+    )(me, *inputs)
+    arrived = lax.ppermute(own, "bin", plan.table_moves())
+    outgoing = pl.pallas_call(
         functools.partial(pack_kernel, plan),
-        out_shape=[
-            jax.ShapeDtypeStruct(a, BF16)
-            for a in ((plan.targets, rows, levels), rate_tables.shape[1:], line_table.shape)
-        ],
-        in_specs=[smem] + [hbm] * 6,
-        out_specs=[vmem] * 3,
-        scratch_shapes=[
-            pltpu.VMEM((cells, levels), BF16),
-            pltpu.VMEM((den_rows, cells // den_rows), BF16),
-            pltpu.VMEM((1, cells), I32),
-            pltpu.VMEM((1, cells), I32),
-            pltpu.SemaphoreType.DMA((6,)),
-        ],
-        compiler_params=params,
-    )(
-        me,
-        in_hbm(sources),
-        in_hbm(density.reshape(den_rows, cells // den_rows)),
-        in_hbm(temp_bins.reshape(1, cells)),
-        in_hbm(ray_index.reshape(1, cells)),
-        in_hbm(rate_tables[0]),
-        in_hbm(line_table),
-    )
+        out_shape=blocks,
+        in_specs=[smem] + [vmem] * len(loaded) + [hbm],
+        out_specs=hbm,
+        input_output_aliases={1 + len(loaded): 0},
+        scratch_shapes=[scratch[0], scratch[2]],
+        compiler_params=params,
+    )(me, *loaded, outgoing)
     got = lax.all_to_all(
         outgoing, "bin", split_axis=0, concat_axis=0, tiled=True, axis_index_groups=plan.halves()
     )
-    other = pl.pallas_call(
+    other, held_line = pl.pallas_call(
         keep_kernel,
-        out_shape=jax.ShapeDtypeStruct(arrived.shape, BF16),
-        in_specs=[vmem],
-        out_specs=vmem,
+        out_shape=[jax.ShapeDtypeStruct(a, BF16) for a in (arrived.shape, line_table.shape)],
+        in_specs=[vmem, hbm],
+        out_specs=[vmem] * 2,
+        scratch_shapes=[pltpu.SemaphoreType.DMA],
         compiler_params=params,
         cost_estimate=pl.CostEstimate(
             flops=OVERLAP_FLOPS, bytes_accessed=4 * arrived.size, transcendentals=0
         ),
-    )(arrived)
+    )(arrived, in_hbm(line_table))
     ray_rows = RAY_DEV
     rays = ray_rows * bin_total
     partial_sums = pl.pallas_call(

time: 35.1 us -> 36.9 us (1.051)
  blocking collectives: 10.4 us -> 12.7 us
  Pallas kernels: 4.92 us -> 6.71 us
  starting transfers between devices: 8.85 us -> 7.12 us
  waiting for transfers between devices: 10.6 us -> 9.98 us
    all_to_all x1, waiting for transfers between devices: 9.42 us -> 6.21 us  [per_device(): lax.all_to_all(outgoing, 'bin', split_axis=0, concat_axis=0, tiled=True,...]
    ppermute x1, waiting for transfers between devices: 0.01 us -> 2.6 us  [per_device(): arrived = lax.ppermute(own, 'bin', plan.table_moves())]
    all_to_all x1, blocking collectives: 10.4 us -> 12.7 us  [per_device(): lax.all_to_all(partial_sums.reshape(bin_total, ray_rows, levels), 'bin',...]
    pallas_call x2 -> x3, Pallas kernels: 2.72 us -> 4.51 us  [the longest x1 2.89 us: per_device(): pl.pallas_call(functools.partial(load_kernel, plan), out_shape=[jax.Shape...]
    ppermute x1, starting transfers between devices: 4.04 us -> 2.3 us  [per_device(): arrived = lax.ppermute(own, 'bin', plan.table_moves())]
  transfers between devices with their start and end apart: 3 -> 3, of which waited for: 2 -> 3; matrix products, arithmetic and copies ran while one was open for 0% -> 0% of each run, Pallas kernels for 8% -> 4%
where the time goes in v12:
time: 36.9 us; the launch traced here: 36.6 us
  blocking collectives  12.7 us (34%)
  waiting for transfers between devices  9.98 us (27%)
  starting transfers between devices  7.12 us (19%)
  Pallas kernels  6.71 us (18%)
    all_to_all x1, blocking collectives, per_device(): lax.all_to_all(partial_sums.reshape(bin_total, ray_rows, levels), 'bin',...  12.7 us
    all_to_all x1, waiting for transfers between devices, per_device(): lax.all_to_all(outgoing, 'bin', split_axis=0, concat_axis=0, tiled=True,...  6.21 us
    all_to_all x1, starting transfers between devices, per_device(): lax.all_to_all(outgoing, 'bin', split_axis=0, concat_axis=0, tiled=True,...  4.75 us
    pallas_call x1, Pallas kernels, per_device(): pl.pallas_call(functools.partial(load_kernel, plan), out_shape=[jax.Shape...  2.89 us
    ppermute x1, waiting for transfers between devices, per_device(): arrived = lax.ppermute(own, 'bin', plan.table_moves())  2.6 us
    ppermute x1, starting transfers between devices, per_device(): arrived = lax.ppermute(own, 'bin', plan.table_moves())  2.3 us
    pallas_call x1, Pallas kernels, per_device(): pl.pallas_call(keep_kernel, out_shape=[jax.ShapeDtypeStruct(a, BF16) for...  1.6 us
    ppermute x1, waiting for transfers between devices, per_device(): lax.ppermute(total, 'wave', [(i, i ^ step) for i in range(wave_total)])  1.17 us
  transfers between devices with their start and end apart: 3, of which 3 were waited for; matrix products, arithmetic and copies ran while one was open for 0% of the time, Pallas kernels for 4%

profile of v12, /device:TPU:0, one launch (start us, length us, event | category | flops | bytes accessed | tf_op | source)
XLA Modules:
  0.0 36.6 jit_solution(16070940799792580786)
XLA Ops:
  0.0 2.9 %shard_map.64 = (bf16[512,256]{1,0:T(8,128)(2,1)S(1)}, bf16[4,128]{1,0:T(4,128)(2,1)S(1)}, s32[1,512]{1,0:T(1,128)S(1)}, s32[1,512]{1,0:T(1,128)S(1)}, bf16[256,...) custom-call(s32[1]{0:T(128)} %bitcast.me_ref, bf16[512,256]{1,0:T(8,128)(2,1)} %refs_0_.1, bf16[4,128]{1,0:T(4,128)(2,1)} %bitcast.10, ...), custom_call_target="tpu_custom_call" | custom-call | tf_op jit(solution)/shard_map/pallas_call | solution.py:177
  2.9 2.3 %collective-permute-start = (bf16[256,256]{1,0:T(8,128)(2,1)S(1)}, bf16[256,256]{1,0:T(8,128)(2,1)S(1)}, u32[]{:S(2)}, u32[]{:S(2)}) collective-permute-start(bf16[256,256]{1,0:T(8,128)(2,1)S(1)} %get-tuple-element.18.refs_0_), channel_id=1, source_target_pairs={{0,16},{2,18},{4,20},{6,22},{8,24},{10,26},{12,28},{14,30},{16,0},... | collective-permute-start | bytes 393224 | tf_op jit(solution)/shard_map/ppermute | solution.py:185
  5.2 4.7 %all-to-all-start = ((bf16[8,144,256]{2,1,0:T(8,128)(2,1)}), bf16[8,144,256]{2,1,0:T(8,128)(2,1)S(1)}, u32[]{:S(2)}, u32[]{:S(2)}) async-start(bf16[8,144,256]{2,1,0:T(8,128)(2,1)} %shard_map.65), calls=%async_computation | async-start | bytes 1179648 | tf_op jit(solution)/shard_map/all_to_all | solution.py:195
  10.0 2.6 %collective-permute-done.arrived_ref = bf16[256,256]{1,0:T(8,128)(2,1)S(1)} collective-permute-done((bf16[256,256]{1,0:T(8,128)(2,1)S(1)}, bf16[256,256]{1,0:T(8,128)(2,1)S(1)}, u32[]{:S(2)}, u32[]{:S(2)}) %collective-permute-start) | collective-permute-done | bytes 131104 | tf_op jit(solution)/shard_map/ppermute | solution.py:185
  12.6 1.6 %shard_map.66 = (bf16[256,256]{1,0:T(8,128)(2,1)S(1)}, bf16[256,4096]{1,0:T(8,128)(2,1)S(1)}) custom-call(bf16[256,256]{1,0:T(8,128)(2,1)S(1)} %collective-permute-done.arrived_ref, bf16[256,4096]{1,0:T(8,128)(2,1)} %line_hbm.1), custom_call_target="tpu_custom_call" | custom-call | flops 10000000000 | bytes 262144 | tf_op jit(solution)/shard_map/pallas_call | solution.py:198
  14.2 6.2 %all-to-all-done.got_ref = bf16[8,144,256]{2,1,0:T(8,128)(2,1)S(1)} async-done(((bf16[8,144,256]{2,1,0:T(8,128)(2,1)}), bf16[8,144,256]{2,1,0:T(8,128)(2,1)S(1)}, u32[]{:S(2)}, u32[]{:S(2)}) %all-to-all-start) | async-done | bytes 589856 | tf_op jit(solution)/shard_map/all_to_all | solution.py:195
  20.4 1.0 %shard_map.67 = bf16[256,256]{1,0:T(8,128)(2,1)S(1)} custom-call(bf16[8,144,256]{2,1,0:T(8,128)(2,1)S(1)} %all-to-all-done.got_ref, bf16[256,256]{1,0:T(8,128)(2,1)S(1)} %get-tuple-element.18.refs_0_, bf16[256,256]{1,0:T(8,128)(2,1)S(1)} %get-tuple-element.19.refs_1_), custom_call_target="tpu_custom_call" | custom-call | tf_op jit(solution)/shard_map/pallas_call | solution.py:211
  21.4 12.7 %all_to_all.10 = bf16[16,16,256]{2,1,0:T(8,128)(2,1)S(1)} all-to-all(bf16[16,16,256]{2,1,0:T(8,128)(2,1)S(1)} %bitcast.6), channel_id=1, replica_groups=mesh['bin'=16,'wave'=2] {'bin'}, dimensions={0} | all-to-all | bytes 262144 | tf_op jit(solution)/shard_map/all_to_all | solution.py:218
  34.2 0.1 collective-permute-start.1
  34.3 1.2 %collective-permute-done.1.theirs_ref = f32[16,256]{1,0:T(8,128)S(1)} collective-permute-done((f32[16,256]{1,0:T(8,128)S(1)}, f32[16,256]{1,0:T(8,128)S(1)}, u32[]{:S(2)}, u32[]{:S(2)}) %collective-permute-start.1) | collective-permute-done | bytes 16416 | tf_op jit(solution)/shard_map/ppermute | solution.py:230
  35.4 1.2 %shard_map.68 = f32[16,4096]{1,0:T(8,128)} custom-call(f32[16,256]{1,0:T(8,128)S(1)} %convert_reduce_fusion.mine_ref, f32[16,256]{1,0:T(8,128)S(1)} %collective-permute-done.1.theirs_ref, bf16[256,4096]{1,0:T(8,128)(2,1)S(1)} %get-tuple-element.20.line_ref), custom_call_target="tpu_custom_call" | custom-call | tf_op jit(solution)/shard_map/pallas_call | solution.py:232
  (2 shorter events, 0.0 us)
Async XLA Ops:
  2.9 9.7 %collective-permute-start = (bf16[256,256]{1,0:T(8,128)(2,1)S(1)}, bf16[256,256]{1,0:T(8,128)(2,1)S(1)}, u32[]{:S(2)}, u32[]{:S(2)}) collective-permute-start(bf16[256,256]{1,0:T(8,128)(2,1)S(1)} %get-tuple-element.18.refs_0_), channel_id=1, source_target_pairs={{0,16},{2,18},{4,20},{6,22},{8,24},{10,26},{12,28},{14,30},{16,0},... | collective-permute-start | bytes 393224 | tf_op jit(solution)/shard_map/ppermute | solution.py:185
  5.2 15.2 %all-to-all-start = ((bf16[8,144,256]{2,1,0:T(8,128)(2,1)}), bf16[8,144,256]{2,1,0:T(8,128)(2,1)S(1)}, u32[]{:S(2)}, u32[]{:S(2)}) async-start(bf16[8,144,256]{2,1,0:T(8,128)(2,1)} %shard_map.65), calls=%async_computation | async-start | bytes 1179648 | tf_op jit(solution)/shard_map/all_to_all | solution.py:195
  34.2 1.2 %collective-permute-start.1 = (f32[16,256]{1,0:T(8,128)S(1)}, f32[16,256]{1,0:T(8,128)S(1)}, u32[]{:S(2)}, u32[]{:S(2)}) collective-permute-start(f32[16,256]{1,0:T(8,128)S(1)} %convert_reduce_fusion.mine_ref), channel_id=1, source_target_pairs={{0,1},{1,0},{2,3},{3,2},{4,5},{5,4},{6,7},{7,6},{8,9},{9,8},{10,11... | collective-permute-start | bytes 49160 | tf_op jit(solution)/shard_map/ppermute | solution.py:230

commit v13 on v11

--- a/solution.py
+++ b/solution.py
@@ -125,7 +125,7 @@
         return [(i, (i + self.targets) % self.bins) for i in range(self.bins)]
 
     def order(self):
-        return sorted(range(1, self.targets), key=lambda k: -bin(k).count("1"))
+        return sorted(range(1, self.targets), key=lambda k: bin(k).count("1"))
 
     def moves(self, k):
         return [(i, i ^ k) for i in range(self.bins)]

time: 36.6 us -> 35.3 us (0.964)
  starting transfers between devices: 15.3 us -> 13.9 us
  blocking collectives: 10.8 us -> 10.4 us
  waiting for transfers between devices: 6.15 us -> 6.53 us
    ppermute x7, starting transfers between devices: 11.2 us -> 9.81 us  [per_device(): lax.ppermute(outgoing[k], 'bin', plan.moves(k))]
    all_to_all x1, blocking collectives: 10.8 us -> 10.4 us  [per_device(): lax.all_to_all(partial_sums.reshape(bin_total, ray_rows, levels), 'bin',...]
    ppermute x7, waiting for transfers between devices: 4.97 us -> 5.36 us  [per_device(): lax.ppermute(outgoing[k], 'bin', plan.moves(k))]
where the time goes in v13:
time: 35.3 us; the launch traced here: 35.1 us
  starting transfers between devices  13.9 us (39%)
  blocking collectives  10.4 us (29%)
  waiting for transfers between devices  6.53 us (18%)
  Pallas kernels  4.11 us (12%)
    all_to_all x1, blocking collectives, per_device(): lax.all_to_all(partial_sums.reshape(bin_total, ray_rows, levels), 'bin',...  10.4 us
    ppermute x7, starting transfers between devices, per_device(): lax.ppermute(outgoing[k], 'bin', plan.moves(k))  9.81 us
    ppermute x7, waiting for transfers between devices, per_device(): lax.ppermute(outgoing[k], 'bin', plan.moves(k))  5.36 us
    ppermute x1, starting transfers between devices, per_device(): arrived = lax.ppermute(rate_tables[0], 'bin', plan.table_moves())  4.04 us
    pallas_call x1, Pallas kernels, per_device(): pl.pallas_call(functools.partial(pack_kernel, plan), out_shape=[jax.Shape...  1.9 us
    ppermute x1, waiting for transfers between devices, per_device(): lax.ppermute(total, 'wave', [(i, i ^ step) for i in range(wave_total)])  1.17 us
    pallas_call x1, Pallas kernels, per_device(): pl.pallas_call(line_kernel, out_shape=jax.ShapeDtypeStruct((ray_rows, lin...  1.16 us
    pallas_call x1, Pallas kernels, per_device(): pl.pallas_call(functools.partial(level_kernel, plan, rays), out_shape=jax...  1.04 us
  transfers between devices with their start and end apart: 9, of which 4 were waited for; matrix products, arithmetic and copies ran while one was open for 0% of the time, Pallas kernels for 5%

profile of v13, /device:TPU:0, one launch (start us, length us, event | category | flops | bytes accessed | tf_op | source)
XLA Modules:
  0.0 35.1 jit_solution(4471793604663128457)
XLA Ops:
  0.0 4.0 %collective-permute-start.7 = (bf16[256,256]{1,0:T(8,128)(2,1)}, bf16[256,256]{1,0:T(8,128)(2,1)S(1)}, u32[]{:S(2)}, u32[]{:S(2)}) collective-permute-start(bf16[256,256]{1,0:T(8,128)(2,1)} %bitcast.7), channel_id=1, source_target_pairs={{0,16},{2,18},{4,20},{6,22},{8,24},{10,26},{12,28},{14,30},{16,0},... | collective-permute-start | bytes 393224 | tf_op jit(solution)/shard_map/ppermute | solution.py:148
  4.0 1.9 %shard_map.64 = (bf16[144,256]{1,0:T(8,128)(2,1)S(1)}, bf16[144,256]{1,0:T(8,128)(2,1)S(1)}, bf16[144,256]{1,0:T(8,128)(2,1)S(1)}, bf16[144,256]{1,0:T(8,128)(2,...) custom-call(s32[1]{0:T(128)} %bitcast.me_ref, ...), custom_call_target="tpu_custom_call" | custom-call | tf_op jit(solution)/shard_map/pallas_call | solution.py:151
  5.9 1.6 %collective-permute-start = (bf16[144,256]{1,0:T(8,128)(2,1)S(1)}, bf16[144,256]{1,0:T(8,128)(2,1)S(1)}, u32[]{:S(2)}, u32[]{:S(2)}) collective-permute-start(bf16[144,256]{1,0:T(8,128)(2,1)S(1)} %get-tuple-element.15), channel_id=1, source_target_pairs={{0,2},{2,0},{4,6},{6,4},{8,10},{10,8},{12,14},{14,12},{16,18},{18,... | collective-permute-start | bytes 221192 | tf_op jit(solution)/shard_map/ppermute | solution.py:176
  7.5 1.5 %collective-permute-start.1 = (bf16[144,256]{1,0:T(8,128)(2,1)S(1)}, bf16[144,256]{1,0:T(8,128)(2,1)S(1)}, u32[]{:S(2)}, u32[]{:S(2)}) collective-permute-start(bf16[144,256]{1,0:T(8,128)(2,1)S(1)} %get-tuple-element.16), channel_id=1, source_target_pairs={{0,4},{2,6},{4,0},{6,2},{8,12},{10,14},{12,8},{14,10},{16,20},{18,... | collective-permute-start | bytes 221192 | tf_op jit(solution)/shard_map/ppermute | solution.py:176
  9.0 1.6 %collective-permute-start.2 = (bf16[144,256]{1,0:T(8,128)(2,1)S(1)}, bf16[144,256]{1,0:T(8,128)(2,1)S(1)}, u32[]{:S(2)}, u32[]{:S(2)}) collective-permute-start(bf16[144,256]{1,0:T(8,128)(2,1)S(1)} %get-tuple-element.17), channel_id=1, source_target_pairs={{0,8},{2,10},{4,12},{6,14},{8,0},{10,2},{12,4},{14,6},{16,24},{18,... | collective-permute-start | bytes 221192 | tf_op jit(solution)/shard_map/ppermute | solution.py:176
  10.6 0.5 %collective-permute-start.3 = (bf16[144,256]{1,0:T(8,128)(2,1)S(1)}, bf16[144,256]{1,0:T(8,128)(2,1)S(1)}, u32[]{:S(2)}, u32[]{:S(2)}) collective-permute-start(bf16[144,256]{1,0:T(8,128)(2,1)S(1)} %get-tuple-element.18), channel_id=1, source_target_pairs={{0,6},{2,4},{4,2},{6,0},{8,14},{10,12},{12,10},{14,8},{16,22},{18,... | collective-permute-start | bytes 221192 | tf_op jit(solution)/shard_map/ppermute | solution.py:176
  11.1 0.0 collective-permute-done.refs_0_
  11.1 2.4 %collective-permute-start.4 = (bf16[144,256]{1,0:T(8,128)(2,1)S(1)}, bf16[144,256]{1,0:T(8,128)(2,1)S(1)}, u32[]{:S(2)}, u32[]{:S(2)}) collective-permute-start(bf16[144,256]{1,0:T(8,128)(2,1)S(1)} %get-tuple-element.19), channel_id=1, source_target_pairs={{0,10},{2,8},{4,14},{6,12},{8,2},{10,0},{12,6},{14,4},{16,26},{18,... | collective-permute-start | bytes 221192 | tf_op jit(solution)/shard_map/ppermute | solution.py:176
  13.5 0.0 collective-permute-done.1.refs_1_
  13.5 1.5 %collective-permute-start.5 = (bf16[144,256]{1,0:T(8,128)(2,1)S(1)}, bf16[144,256]{1,0:T(8,128)(2,1)S(1)}, u32[]{:S(2)}, u32[]{:S(2)}) collective-permute-start(bf16[144,256]{1,0:T(8,128)(2,1)S(1)} %get-tuple-element.20), channel_id=1, source_target_pairs={{0,12},{2,14},{4,8},{6,10},{8,4},{10,6},{12,0},{14,2},{16,28},{18,... | collective-permute-start | bytes 221192 | tf_op jit(solution)/shard_map/ppermute | solution.py:176
  15.0 0.0 collective-permute-done.7.table_ref
  15.0 0.8 %collective-permute-start.6 = (bf16[144,256]{1,0:T(8,128)(2,1)S(1)}, bf16[144,256]{1,0:T(8,128)(2,1)S(1)}, u32[]{:S(2)}, u32[]{:S(2)}) collective-permute-start(bf16[144,256]{1,0:T(8,128)(2,1)S(1)} %get-tuple-element.21), channel_id=1, source_target_pairs={{0,14},{2,12},{4,10},{6,8},{8,6},{10,4},{12,2},{14,0},{16,30},{18,... | collective-permute-start | bytes 221192 | tf_op jit(solution)/shard_map/ppermute | solution.py:176
  15.8 0.0 collective-permute-done.2.refs_2_
  15.8 0.6 %collective-permute-done.3.refs_3_ = bf16[144,256]{1,0:T(8,128)(2,1)S(1)} collective-permute-done((bf16[144,256]{1,0:T(8,128)(2,1)S(1)}, bf16[144,256]{1,0:T(8,128)(2,1)S(1)}, u32[]{:S(2)}, u32[]{:S(2)}) %collective-permute-start.3) | collective-permute-done | bytes 73760 | tf_op jit(solution)/shard_map/ppermute | solution.py:176
  16.4 0.0 collective-permute-done.4.refs_4_
  16.4 2.7 %collective-permute-done.5.refs_5_ = bf16[144,256]{1,0:T(8,128)(2,1)S(1)} collective-permute-done((bf16[144,256]{1,0:T(8,128)(2,1)S(1)}, bf16[144,256]{1,0:T(8,128)(2,1)S(1)}, u32[]{:S(2)}, u32[]{:S(2)}) %collective-permute-start.5) | collective-permute-done | bytes 73760 | tf_op jit(solution)/shard_map/ppermute | solution.py:176
  19.1 2.0 %collective-permute-done.6.refs_6_ = bf16[144,256]{1,0:T(8,128)(2,1)S(1)} collective-permute-done((bf16[144,256]{1,0:T(8,128)(2,1)S(1)}, bf16[144,256]{1,0:T(8,128)(2,1)S(1)}, u32[]{:S(2)}, u32[]{:S(2)}) %collective-permute-start.6) | collective-permute-done | bytes 73760 | tf_op jit(solution)/shard_map/ppermute | solution.py:176
  21.1 1.0 %shard_map.66 = bf16[256,256]{1,0:T(8,128)(2,1)S(1)} custom-call(bf16[144,256]{1,0:T(8,128)(2,1)S(1)} %collective-permute-done.refs_0_, bf16[144,256]{1,0:T(8,128)(2,1)S(1)} %collective-permute-done.1.refs_1_, bf16[144,256]{1,0:T(8,128)(2,1)S(1)} %collective-permute-done.2.refs_2_, bf16[144,256]{1,0:T(8,128)(2,1)S(1)} %collective-permute-done.3.refs_3_, ...), custom_call_target="tpu_custom_call" | custom-call | tf_op jit(solution)/shard_map/pallas_call | solution.py:189
  22.2 10.4 %all_to_all.5 = bf16[16,16,256]{2,1,0:T(8,128)(2,1)S(1)} all-to-all(bf16[16,16,256]{2,1,0:T(8,128)(2,1)S(1)} %bitcast.6), channel_id=1, replica_groups=mesh['bin'=16,'wave'=2] {'bin'}, dimensions={0} | all-to-all | bytes 262144 | tf_op jit(solution)/shard_map/all_to_all | solution.py:196
  32.6 0.1 collective-permute-start.8
  32.7 1.2 %collective-permute-done.8.theirs_ref = f32[16,256]{1,0:T(8,128)S(1)} collective-permute-done((f32[16,256]{1,0:T(8,128)S(1)}, f32[16,256]{1,0:T(8,128)S(1)}, u32[]{:S(2)}, u32[]{:S(2)}) %collective-permute-start.8) | collective-permute-done | bytes 16416 | tf_op jit(solution)/shard_map/ppermute | solution.py:208
  33.9 1.2 %shard_map.67 = f32[16,4096]{1,0:T(8,128)} custom-call(f32[16,256]{1,0:T(8,128)S(1)} %convert_reduce_fusion.mine_ref, f32[16,256]{1,0:T(8,128)S(1)} %collective-permute-done.8.theirs_ref, bf16[256,4096]{1,0:T(8,128)(2,1)S(1)} %get-tuple-element.24.line_ref), custom_call_target="tpu_custom_call" | custom-call | tf_op jit(solution)/shard_map/pallas_call | solution.py:210
  (2 shorter events, 0.0 us)
Async XLA Ops:
  0.0 15.0 %collective-permute-start.7 = (bf16[256,256]{1,0:T(8,128)(2,1)}, bf16[256,256]{1,0:T(8,128)(2,1)S(1)}, u32[]{:S(2)}, u32[]{:S(2)}) collective-permute-start(bf16[256,256]{1,0:T(8,128)(2,1)} %bitcast.7), channel_id=1, source_target_pairs={{0,16},{2,18},{4,20},{6,22},{8,24},{10,26},{12,28},{14,30},{16,0},... | collective-permute-start | bytes 393224 | tf_op jit(solution)/shard_map/ppermute | solution.py:148
  5.9 5.1 %collective-permute-start = (bf16[144,256]{1,0:T(8,128)(2,1)S(1)}, bf16[144,256]{1,0:T(8,128)(2,1)S(1)}, u32[]{:S(2)}, u32[]{:S(2)}) collective-permute-start(bf16[144,256]{1,0:T(8,128)(2,1)S(1)} %get-tuple-element.15), channel_id=1, source_target_pairs={{0,2},{2,0},{4,6},{6,4},{8,10},{10,8},{12,14},{14,12},{16,18},{18,... | collective-permute-start | bytes 221192 | tf_op jit(solution)/shard_map/ppermute | solution.py:176
  7.5 6.0 %collective-permute-start.1 = (bf16[144,256]{1,0:T(8,128)(2,1)S(1)}, bf16[144,256]{1,0:T(8,128)(2,1)S(1)}, u32[]{:S(2)}, u32[]{:S(2)}) collective-permute-start(bf16[144,256]{1,0:T(8,128)(2,1)S(1)} %get-tuple-element.16), channel_id=1, source_target_pairs={{0,4},{2,6},{4,0},{6,2},{8,12},{10,14},{12,8},{14,10},{16,20},{18,... | collective-permute-start | bytes 221192 | tf_op jit(solution)/shard_map/ppermute | solution.py:176
  9.0 6.8 %collective-permute-start.2 = (bf16[144,256]{1,0:T(8,128)(2,1)S(1)}, bf16[144,256]{1,0:T(8,128)(2,1)S(1)}, u32[]{:S(2)}, u32[]{:S(2)}) collective-permute-start(bf16[144,256]{1,0:T(8,128)(2,1)S(1)} %get-tuple-element.17), channel_id=1, source_target_pairs={{0,8},{2,10},{4,12},{6,14},{8,0},{10,2},{12,4},{14,6},{16,24},{18,... | collective-permute-start | bytes 221192 | tf_op jit(solution)/shard_map/ppermute | solution.py:176
  10.6 5.8 %collective-permute-start.3 = (bf16[144,256]{1,0:T(8,128)(2,1)S(1)}, bf16[144,256]{1,0:T(8,128)(2,1)S(1)}, u32[]{:S(2)}, u32[]{:S(2)}) collective-permute-start(bf16[144,256]{1,0:T(8,128)(2,1)S(1)} %get-tuple-element.18), channel_id=1, source_target_pairs={{0,6},{2,4},{4,2},{6,0},{8,14},{10,12},{12,10},{14,8},{16,22},{18,... | collective-permute-start | bytes 221192 | tf_op jit(solution)/shard_map/ppermute | solution.py:176
  11.1 5.3 %collective-permute-start.4 = (bf16[144,256]{1,0:T(8,128)(2,1)S(1)}, bf16[144,256]{1,0:T(8,128)(2,1)S(1)}, u32[]{:S(2)}, u32[]{:S(2)}) collective-permute-start(bf16[144,256]{1,0:T(8,128)(2,1)S(1)} %get-tuple-element.19), channel_id=1, source_target_pairs={{0,10},{2,8},{4,14},{6,12},{8,2},{10,0},{12,6},{14,4},{16,26},{18,... | collective-permute-start | bytes 221192 | tf_op jit(solution)/shard_map/ppermute | solution.py:176
  13.5 5.6 %collective-permute-start.5 = (bf16[144,256]{1,0:T(8,128)(2,1)S(1)}, bf16[144,256]{1,0:T(8,128)(2,1)S(1)}, u32[]{:S(2)}, u32[]{:S(2)}) collective-permute-start(bf16[144,256]{1,0:T(8,128)(2,1)S(1)} %get-tuple-element.20), channel_id=1, source_target_pairs={{0,12},{2,14},{4,8},{6,10},{8,4},{10,6},{12,0},{14,2},{16,28},{18,... | collective-permute-start | bytes 221192 | tf_op jit(solution)/shard_map/ppermute | solution.py:176
  15.0 6.2 %collective-permute-start.6 = (bf16[144,256]{1,0:T(8,128)(2,1)S(1)}, bf16[144,256]{1,0:T(8,128)(2,1)S(1)}, u32[]{:S(2)}, u32[]{:S(2)}) collective-permute-start(bf16[144,256]{1,0:T(8,128)(2,1)S(1)} %get-tuple-element.21), channel_id=1, source_target_pairs={{0,14},{2,12},{4,10},{6,8},{8,6},{10,4},{12,2},{14,0},{16,30},{18,... | collective-permute-start | bytes 221192 | tf_op jit(solution)/shard_map/ppermute | solution.py:176
  32.6 1.2 %collective-permute-start.8 = (f32[16,256]{1,0:T(8,128)S(1)}, f32[16,256]{1,0:T(8,128)S(1)}, u32[]{:S(2)}, u32[]{:S(2)}) collective-permute-start(f32[16,256]{1,0:T(8,128)S(1)} %convert_reduce_fusion.mine_ref), channel_id=1, source_target_pairs={{0,1},{1,0},{2,3},{3,2},{4,5},{5,4},{6,7},{7,6},{8,9},{9,8},{10,11... | collective-permute-start | bytes 49160 | tf_op jit(solution)/shard_map/ppermute | solution.py:208

commit v14 on v13

--- a/solution.py
+++ b/solution.py
@@ -78,7 +78,8 @@
         copy.wait()
 
 
-def keep_kernel(table_ref, out_ref):
+def keep_kernel(table_ref, *refs):
+    out_ref = refs[-1]
     out_ref[...] = table_ref[...]
 
 
@@ -125,7 +126,9 @@
         return [(i, (i + self.targets) % self.bins) for i in range(self.bins)]
 
     def order(self):
-        return sorted(range(1, self.targets), key=lambda k: bin(k).count("1"))
+        near = [k for k in range(1, self.targets) if k & (k - 1) == 0]
+        far = [k for k in range(1, self.targets) if k & (k - 1)]
+        return near + sorted(far, key=lambda k: (k != self.targets - 1, k))
 
     def moves(self, k):
         return [(i, i ^ k) for i in range(self.bins)]
@@ -174,16 +177,17 @@
         in_hbm(line_table),
     )
     got = [lax.ppermute(outgoing[k], "bin", plan.moves(k)) for k in plan.order()]
+    nearest = got[: plan.targets.bit_length() - 1]
     other = pl.pallas_call(
         keep_kernel,
         out_shape=jax.ShapeDtypeStruct(arrived.shape, BF16),
-        in_specs=[vmem],
+        in_specs=[vmem] * (1 + len(nearest)),
         out_specs=vmem,
         compiler_params=params,
         cost_estimate=pl.CostEstimate(
             flops=OVERLAP_FLOPS, bytes_accessed=4 * arrived.size, transcendentals=0
         ),
-    )(arrived)
+    )(arrived, *nearest)
     ray_rows = RAY_DEV
     rays = ray_rows * bin_total
     partial_sums = pl.pallas_call(

time: 35.3 us -> 35.5 us (level)
  blocking collectives: 10.4 us -> 11.6 us
  waiting for transfers between devices: 6.53 us -> 6.02 us
  starting transfers between devices: 13.9 us -> 13.5 us
    all_to_all x1, blocking collectives: 10.4 us -> 11.6 us  [per_device(): lax.all_to_all(partial_sums.reshape(bin_total, ray_rows, levels), 'bin',...]
    ppermute x7, waiting for transfers between devices: 5.36 us -> 4.85 us  [per_device(): lax.ppermute(outgoing[k], 'bin', plan.moves(k))]
    ppermute x7, starting transfers between devices: 9.81 us -> 9.4 us  [per_device(): lax.ppermute(outgoing[k], 'bin', plan.moves(k))]
  transfers between devices with their start and end apart: 9 -> 9, of which waited for: 4 -> 5; matrix products, arithmetic and copies ran while one was open for 0% -> 0% of each run, Pallas kernels for 5% -> 5%
where the time goes in v14:
time: 35.5 us; the launch traced here: 35.3 us
  starting transfers between devices  13.5 us (38%)
  blocking collectives  11.6 us (33%)
  waiting for transfers between devices  6.02 us (17%)
  Pallas kernels  4.11 us (12%)
    all_to_all x1, blocking collectives, per_device(): lax.all_to_all(partial_sums.reshape(bin_total, ray_rows, levels), 'bin',...  11.6 us
    ppermute x7, starting transfers between devices, per_device(): lax.ppermute(outgoing[k], 'bin', plan.moves(k))  9.4 us
    ppermute x7, waiting for transfers between devices, per_device(): lax.ppermute(outgoing[k], 'bin', plan.moves(k))  4.85 us
    ppermute x1, starting transfers between devices, per_device(): arrived = lax.ppermute(rate_tables[0], 'bin', plan.table_moves())  4.04 us
    pallas_call x1, Pallas kernels, per_device(): pl.pallas_call(functools.partial(pack_kernel, plan), out_shape=[jax.Shape...  1.9 us
    ppermute x1, waiting for transfers between devices, per_device(): lax.ppermute(total, 'wave', [(i, i ^ step) for i in range(wave_total)])  1.17 us
    pallas_call x1, Pallas kernels, per_device(): pl.pallas_call(line_kernel, out_shape=jax.ShapeDtypeStruct((ray_rows, lin...  1.17 us
    pallas_call x1, Pallas kernels, per_device(): pl.pallas_call(functools.partial(level_kernel, plan, rays), out_shape=jax...  1.04 us
  transfers between devices with their start and end apart: 9, of which 5 were waited for; matrix products, arithmetic and copies ran while one was open for 0% of the time, Pallas kernels for 5%

profile of v14, /device:TPU:0, one launch (start us, length us, event | category | flops | bytes accessed | tf_op | source)
XLA Modules:
  0.0 35.3 jit_solution(7019789053694588363)
XLA Ops:
  0.0 4.0 %collective-permute-start.7 = (bf16[256,256]{1,0:T(8,128)(2,1)}, bf16[256,256]{1,0:T(8,128)(2,1)S(1)}, u32[]{:S(2)}, u32[]{:S(2)}) collective-permute-start(bf16[256,256]{1,0:T(8,128)(2,1)} %bitcast.7), channel_id=1, source_target_pairs={{0,16},{2,18},{4,20},{6,22},{8,24},{10,26},{12,28},{14,30},{16,0},... | collective-permute-start | bytes 393224 | tf_op jit(solution)/shard_map/ppermute | solution.py:151
  4.0 1.9 %shard_map.64 = (bf16[144,256]{1,0:T(8,128)(2,1)S(1)}, bf16[144,256]{1,0:T(8,128)(2,1)S(1)}, bf16[144,256]{1,0:T(8,128)(2,1)S(1)}, bf16[144,256]{1,0:T(8,128)(2,...) custom-call(s32[1]{0:T(128)} %bitcast.me_ref, ...), custom_call_target="tpu_custom_call" | custom-call | tf_op jit(solution)/shard_map/pallas_call | solution.py:154
  5.9 1.6 %collective-permute-start = (bf16[144,256]{1,0:T(8,128)(2,1)S(1)}, bf16[144,256]{1,0:T(8,128)(2,1)S(1)}, u32[]{:S(2)}, u32[]{:S(2)}) collective-permute-start(bf16[144,256]{1,0:T(8,128)(2,1)S(1)} %get-tuple-element.15), channel_id=1, source_target_pairs={{0,2},{2,0},{4,6},{6,4},{8,10},{10,8},{12,14},{14,12},{16,18},{18,... | collective-permute-start | bytes 221192 | tf_op jit(solution)/shard_map/ppermute | solution.py:179
  7.5 1.5 %collective-permute-start.1 = (bf16[144,256]{1,0:T(8,128)(2,1)S(1)}, bf16[144,256]{1,0:T(8,128)(2,1)S(1)}, u32[]{:S(2)}, u32[]{:S(2)}) collective-permute-start(bf16[144,256]{1,0:T(8,128)(2,1)S(1)} %get-tuple-element.16), channel_id=1, source_target_pairs={{0,4},{2,6},{4,0},{6,2},{8,12},{10,14},{12,8},{14,10},{16,20},{18,... | collective-permute-start | bytes 221192 | tf_op jit(solution)/shard_map/ppermute | solution.py:179
  9.0 1.6 %collective-permute-start.2 = (bf16[144,256]{1,0:T(8,128)(2,1)S(1)}, bf16[144,256]{1,0:T(8,128)(2,1)S(1)}, u32[]{:S(2)}, u32[]{:S(2)}) collective-permute-start(bf16[144,256]{1,0:T(8,128)(2,1)S(1)} %get-tuple-element.17), channel_id=1, source_target_pairs={{0,8},{2,10},{4,12},{6,14},{8,0},{10,2},{12,4},{14,6},{16,24},{18,... | collective-permute-start | bytes 221192 | tf_op jit(solution)/shard_map/ppermute | solution.py:179
  10.6 0.4 %collective-permute-start.3 = (bf16[144,256]{1,0:T(8,128)(2,1)S(1)}, bf16[144,256]{1,0:T(8,128)(2,1)S(1)}, u32[]{:S(2)}, u32[]{:S(2)}) collective-permute-start(bf16[144,256]{1,0:T(8,128)(2,1)S(1)} %get-tuple-element.18), channel_id=1, source_target_pairs={{0,14},{2,12},{4,10},{6,8},{8,6},{10,4},{12,2},{14,0},{16,30},{18,... | collective-permute-start | bytes 221192 | tf_op jit(solution)/shard_map/ppermute | solution.py:179
  11.0 0.0 collective-permute-done.refs_0_
  11.0 2.4 %collective-permute-start.4 = (bf16[144,256]{1,0:T(8,128)(2,1)S(1)}, bf16[144,256]{1,0:T(8,128)(2,1)S(1)}, u32[]{:S(2)}, u32[]{:S(2)}) collective-permute-start(bf16[144,256]{1,0:T(8,128)(2,1)S(1)} %get-tuple-element.19), channel_id=1, source_target_pairs={{0,6},{2,4},{4,2},{6,0},{8,14},{10,12},{12,10},{14,8},{16,22},{18,... | collective-permute-start | bytes 221192 | tf_op jit(solution)/shard_map/ppermute | solution.py:179
  13.4 0.0 collective-permute-done.1.refs_1_
  13.4 1.5 %collective-permute-start.5 = (bf16[144,256]{1,0:T(8,128)(2,1)S(1)}, bf16[144,256]{1,0:T(8,128)(2,1)S(1)}, u32[]{:S(2)}, u32[]{:S(2)}) collective-permute-start(bf16[144,256]{1,0:T(8,128)(2,1)S(1)} %get-tuple-element.20), channel_id=1, source_target_pairs={{0,10},{2,8},{4,14},{6,12},{8,2},{10,0},{12,6},{14,4},{16,26},{18,... | collective-permute-start | bytes 221192 | tf_op jit(solution)/shard_map/ppermute | solution.py:179
  15.0 0.0 collective-permute-done.2.refs_2_
  15.0 0.4 %collective-permute-start.6 = (bf16[144,256]{1,0:T(8,128)(2,1)S(1)}, bf16[144,256]{1,0:T(8,128)(2,1)S(1)}, u32[]{:S(2)}, u32[]{:S(2)}) collective-permute-start(bf16[144,256]{1,0:T(8,128)(2,1)S(1)} %get-tuple-element.21), channel_id=1, source_target_pairs={{0,12},{2,14},{4,8},{6,10},{8,4},{10,6},{12,0},{14,2},{16,28},{18,... | collective-permute-start | bytes 221192 | tf_op jit(solution)/shard_map/ppermute | solution.py:179
  15.4 0.0 collective-permute-done.7.table_ref
  15.4 1.8 %collective-permute-done.3.refs_3_ = bf16[144,256]{1,0:T(8,128)(2,1)S(1)} collective-permute-done((bf16[144,256]{1,0:T(8,128)(2,1)S(1)}, bf16[144,256]{1,0:T(8,128)(2,1)S(1)}, u32[]{:S(2)}, u32[]{:S(2)}) %collective-permute-start.3) | collective-permute-done | bytes 73760 | tf_op jit(solution)/shard_map/ppermute | solution.py:179
  17.2 1.0 %collective-permute-done.4.refs_4_ = bf16[144,256]{1,0:T(8,128)(2,1)S(1)} collective-permute-done((bf16[144,256]{1,0:T(8,128)(2,1)S(1)}, bf16[144,256]{1,0:T(8,128)(2,1)S(1)}, u32[]{:S(2)}, u32[]{:S(2)}) %collective-permute-start.4) | collective-permute-done | bytes 73760 | tf_op jit(solution)/shard_map/ppermute | solution.py:179
  18.2 0.5 %collective-permute-done.5.refs_5_ = bf16[144,256]{1,0:T(8,128)(2,1)S(1)} collective-permute-done((bf16[144,256]{1,0:T(8,128)(2,1)S(1)}, bf16[144,256]{1,0:T(8,128)(2,1)S(1)}, u32[]{:S(2)}, u32[]{:S(2)}) %collective-permute-start.5) | collective-permute-done | bytes 73760 | tf_op jit(solution)/shard_map/ppermute | solution.py:179
  18.7 1.6 %collective-permute-done.6.refs_6_ = bf16[144,256]{1,0:T(8,128)(2,1)S(1)} collective-permute-done((bf16[144,256]{1,0:T(8,128)(2,1)S(1)}, bf16[144,256]{1,0:T(8,128)(2,1)S(1)}, u32[]{:S(2)}, u32[]{:S(2)}) %collective-permute-start.6) | collective-permute-done | bytes 73760 | tf_op jit(solution)/shard_map/ppermute | solution.py:179
  20.2 1.0 %shard_map.66 = bf16[256,256]{1,0:T(8,128)(2,1)S(1)} custom-call(bf16[144,256]{1,0:T(8,128)(2,1)S(1)} %collective-permute-done.refs_0_, bf16[144,256]{1,0:T(8,128)(2,1)S(1)} %collective-permute-done.1.refs_1_, bf16[144,256]{1,0:T(8,128)(2,1)S(1)} %collective-permute-done.2.refs_2_, bf16[144,256]{1,0:T(8,128)(2,1)S(1)} %collective-permute-done.3.refs_3_, ...), custom_call_target="tpu_custom_call" | custom-call | tf_op jit(solution)/shard_map/pallas_call | solution.py:193
  21.3 11.6 %all_to_all.5 = bf16[16,16,256]{2,1,0:T(8,128)(2,1)S(1)} all-to-all(bf16[16,16,256]{2,1,0:T(8,128)(2,1)S(1)} %bitcast.6), channel_id=1, replica_groups=mesh['bin'=16,'wave'=2] {'bin'}, dimensions={0} | all-to-all | bytes 262144 | tf_op jit(solution)/shard_map/all_to_all | solution.py:200
  32.9 0.1 collective-permute-start.8
  32.9 1.2 %collective-permute-done.8.theirs_ref = f32[16,256]{1,0:T(8,128)S(1)} collective-permute-done((f32[16,256]{1,0:T(8,128)S(1)}, f32[16,256]{1,0:T(8,128)S(1)}, u32[]{:S(2)}, u32[]{:S(2)}) %collective-permute-start.8) | collective-permute-done | bytes 16416 | tf_op jit(solution)/shard_map/ppermute | solution.py:212
  34.1 1.2 %shard_map.67 = f32[16,4096]{1,0:T(8,128)} custom-call(f32[16,256]{1,0:T(8,128)S(1)} %convert_reduce_fusion.mine_ref, f32[16,256]{1,0:T(8,128)S(1)} %collective-permute-done.8.theirs_ref, bf16[256,4096]{1,0:T(8,128)(2,1)S(1)} %get-tuple-element.24.line_ref), custom_call_target="tpu_custom_call" | custom-call | tf_op jit(solution)/shard_map/pallas_call | solution.py:214
  (2 shorter events, 0.0 us)
Async XLA Ops:
  0.0 15.4 %collective-permute-start.7 = (bf16[256,256]{1,0:T(8,128)(2,1)}, bf16[256,256]{1,0:T(8,128)(2,1)S(1)}, u32[]{:S(2)}, u32[]{:S(2)}) collective-permute-start(bf16[256,256]{1,0:T(8,128)(2,1)} %bitcast.7), channel_id=1, source_target_pairs={{0,16},{2,18},{4,20},{6,22},{8,24},{10,26},{12,28},{14,30},{16,0},... | collective-permute-start | bytes 393224 | tf_op jit(solution)/shard_map/ppermute | solution.py:151
  5.9 5.0 %collective-permute-start = (bf16[144,256]{1,0:T(8,128)(2,1)S(1)}, bf16[144,256]{1,0:T(8,128)(2,1)S(1)}, u32[]{:S(2)}, u32[]{:S(2)}) collective-permute-start(bf16[144,256]{1,0:T(8,128)(2,1)S(1)} %get-tuple-element.15), channel_id=1, source_target_pairs={{0,2},{2,0},{4,6},{6,4},{8,10},{10,8},{12,14},{14,12},{16,18},{18,... | collective-permute-start | bytes 221192 | tf_op jit(solution)/shard_map/ppermute | solution.py:179
  7.5 5.9 %collective-permute-start.1 = (bf16[144,256]{1,0:T(8,128)(2,1)S(1)}, bf16[144,256]{1,0:T(8,128)(2,1)S(1)}, u32[]{:S(2)}, u32[]{:S(2)}) collective-permute-start(bf16[144,256]{1,0:T(8,128)(2,1)S(1)} %get-tuple-element.16), channel_id=1, source_target_pairs={{0,4},{2,6},{4,0},{6,2},{8,12},{10,14},{12,8},{14,10},{16,20},{18,... | collective-permute-start | bytes 221192 | tf_op jit(solution)/shard_map/ppermute | solution.py:179
  9.0 5.9 %collective-permute-start.2 = (bf16[144,256]{1,0:T(8,128)(2,1)S(1)}, bf16[144,256]{1,0:T(8,128)(2,1)S(1)}, u32[]{:S(2)}, u32[]{:S(2)}) collective-permute-start(bf16[144,256]{1,0:T(8,128)(2,1)S(1)} %get-tuple-element.17), channel_id=1, source_target_pairs={{0,8},{2,10},{4,12},{6,14},{8,0},{10,2},{12,4},{14,6},{16,24},{18,... | collective-permute-start | bytes 221192 | tf_op jit(solution)/shard_map/ppermute | solution.py:179
  10.6 6.6 %collective-permute-start.3 = (bf16[144,256]{1,0:T(8,128)(2,1)S(1)}, bf16[144,256]{1,0:T(8,128)(2,1)S(1)}, u32[]{:S(2)}, u32[]{:S(2)}) collective-permute-start(bf16[144,256]{1,0:T(8,128)(2,1)S(1)} %get-tuple-element.18), channel_id=1, source_target_pairs={{0,14},{2,12},{4,10},{6,8},{8,6},{10,4},{12,2},{14,0},{16,30},{18,... | collective-permute-start | bytes 221192 | tf_op jit(solution)/shard_map/ppermute | solution.py:179
  11.0 7.2 %collective-permute-start.4 = (bf16[144,256]{1,0:T(8,128)(2,1)S(1)}, bf16[144,256]{1,0:T(8,128)(2,1)S(1)}, u32[]{:S(2)}, u32[]{:S(2)}) collective-permute-start(bf16[144,256]{1,0:T(8,128)(2,1)S(1)} %get-tuple-element.19), channel_id=1, source_target_pairs={{0,6},{2,4},{4,2},{6,0},{8,14},{10,12},{12,10},{14,8},{16,22},{18,... | collective-permute-start | bytes 221192 | tf_op jit(solution)/shard_map/ppermute | solution.py:179
  13.4 5.3 %collective-permute-start.5 = (bf16[144,256]{1,0:T(8,128)(2,1)S(1)}, bf16[144,256]{1,0:T(8,128)(2,1)S(1)}, u32[]{:S(2)}, u32[]{:S(2)}) collective-permute-start(bf16[144,256]{1,0:T(8,128)(2,1)S(1)} %get-tuple-element.20), channel_id=1, source_target_pairs={{0,10},{2,8},{4,14},{6,12},{8,2},{10,0},{12,6},{14,4},{16,26},{18,... | collective-permute-start | bytes 221192 | tf_op jit(solution)/shard_map/ppermute | solution.py:179
  15.0 5.3 %collective-permute-start.6 = (bf16[144,256]{1,0:T(8,128)(2,1)S(1)}, bf16[144,256]{1,0:T(8,128)(2,1)S(1)}, u32[]{:S(2)}, u32[]{:S(2)}) collective-permute-start(bf16[144,256]{1,0:T(8,128)(2,1)S(1)} %get-tuple-element.21), channel_id=1, source_target_pairs={{0,12},{2,14},{4,8},{6,10},{8,4},{10,6},{12,0},{14,2},{16,28},{18,... | collective-permute-start | bytes 221192 | tf_op jit(solution)/shard_map/ppermute | solution.py:179
  32.9 1.2 %collective-permute-start.8 = (f32[16,256]{1,0:T(8,128)S(1)}, f32[16,256]{1,0:T(8,128)S(1)}, u32[]{:S(2)}, u32[]{:S(2)}) collective-permute-start(f32[16,256]{1,0:T(8,128)S(1)} %convert_reduce_fusion.mine_ref), channel_id=1, source_target_pairs={{0,1},{1,0},{2,3},{3,2},{4,5},{5,4},{6,7},{7,6},{8,9},{9,8},{10,11... | collective-permute-start | bytes 49160 | tf_op jit(solution)/shard_map/ppermute | solution.py:212

commit v15 on v6

--- a/solution.py
+++ b/solution.py
@@ -76,8 +76,8 @@
         copy.wait()
 
 
-def keep_kernel(table_ref, out_ref):
-    out_ref[...] = table_ref[...]
+def keep_kernel(core_ref, arrived_ref, passed_ref, out_ref):
+    out_ref[...] = jnp.where(core_ref[0] % 2 == 1, arrived_ref[...], passed_ref[...])
 
 
 def level_kernel(plan, rays, got_ref, *refs):
@@ -119,8 +119,13 @@
         self.capacity = max(2, 2 * cells // bin_total)
         self.block = 2 * self.capacity
 
-    def table_moves(self):
-        return [(i, (i + self.targets) % self.bins) for i in range(self.bins)]
+    def table_moves(self, wave_total):
+        moves = []
+        for b in range(self.bins):
+            for w in range(wave_total):
+                to = (b + self.targets) % self.bins if w % 2 else b ^ 1
+                moves.append((b * wave_total + w, to * wave_total + w))
+        return moves
 
     def halves(self):
         return [list(range(self.targets)), list(range(self.targets, self.bins))]
@@ -140,7 +145,8 @@
     def in_hbm(x):
         return pltpu.with_memory_space_constraint(x, pltpu.HBM)
 
-    arrived = lax.ppermute(rate_tables[0], "bin", plan.table_moves())
+    arrived = lax.ppermute(rate_tables[0], ("bin", "wave"), plan.table_moves(wave_total))
+    passed = lax.ppermute(arrived, "wave", [(i, i ^ 1) for i in range(wave_total)])
     me = lax.axis_index("bin").astype(I32).reshape(1)
     den_rows = cells // min(cells, LANES)
     outgoing, own, held_line = pl.pallas_call(
@@ -174,13 +180,13 @@
     other = pl.pallas_call(
         keep_kernel,
         out_shape=jax.ShapeDtypeStruct(arrived.shape, BF16),
-        in_specs=[vmem],
+        in_specs=[smem, vmem, vmem],
         out_specs=vmem,
         compiler_params=params,
         cost_estimate=pl.CostEstimate(
             flops=OVERLAP_FLOPS, bytes_accessed=4 * arrived.size, transcendentals=0
         ),
-    )(arrived)
+    )(lax.axis_index("wave").astype(I32).reshape(1), arrived, passed)
     ray_rows = RAY_DEV
     rays = ray_rows * bin_total
     partial_sums = pl.pallas_call(

time: 35.1 us -> 41 us (1.17)
  waiting for transfers between devices: 10.6 us -> 14.2 us
  blocking collectives: 10.4 us -> 12.8 us
    ppermute x1 -> x2, waiting for transfers between devices: 0.01 us -> 3.16 us  [the longest x1 3.15 us: per_device(): lax.ppermute(rate_tables[0], ('bin', 'wave'), plan.table_moves(wave_total))]
    all_to_all x1, blocking collectives: 10.4 us -> 12.8 us  [per_device(): lax.all_to_all(partial_sums.reshape(bin_total, ray_rows, levels), 'bin',...]
    all_to_all x1, starting transfers between devices: 4.75 us -> 4.3 us  [per_device(): lax.all_to_all(outgoing, 'bin', split_axis=0, concat_axis=0, tiled=True,...]
    all_to_all x1, waiting for transfers between devices: 9.42 us -> 9.84 us  [per_device(): lax.all_to_all(outgoing, 'bin', split_axis=0, concat_axis=0, tiled=True,...]
    ppermute x1 -> x2, starting transfers between devices: 4.04 us -> 4.41 us  [the longest x1 2.94 us: per_device(): lax.ppermute(rate_tables[0], ('bin', 'wave'), plan.table_moves(wave_total))]
  transfers between devices with their start and end apart: 3 -> 4, of which waited for: 2 -> 3; matrix products, arithmetic and copies ran while one was open for 0% -> 0% of each run, Pallas kernels for 8% -> 7%
where the time goes in v15:
time: 41 us; the launch traced here: 40.8 us
  waiting for transfers between devices  14.2 us (35%)
  blocking collectives  12.8 us (31%)
  starting transfers between devices  8.77 us (21%)
  Pallas kernels  4.93 us (12%)
    all_to_all x1, blocking collectives, per_device(): lax.all_to_all(partial_sums.reshape(bin_total, ray_rows, levels), 'bin',...  12.8 us
    all_to_all x1, waiting for transfers between devices, per_device(): lax.all_to_all(outgoing, 'bin', split_axis=0, concat_axis=0, tiled=True,...  9.84 us
    all_to_all x1, starting transfers between devices, per_device(): lax.all_to_all(outgoing, 'bin', split_axis=0, concat_axis=0, tiled=True,...  4.3 us
    ppermute x1, waiting for transfers between devices, per_device(): lax.ppermute(rate_tables[0], ('bin', 'wave'), plan.table_moves(wave_total))  3.15 us
    ppermute x1, starting transfers between devices, per_device(): lax.ppermute(rate_tables[0], ('bin', 'wave'), plan.table_moves(wave_total))  2.94 us
    pallas_call x1, Pallas kernels, per_device(): pl.pallas_call(functools.partial(pack_kernel, plan), out_shape=[jax.Shape...  2.71 us
    ppermute x1, starting transfers between devices, per_device(): lax.ppermute(arrived, 'wave', [(i, i ^ 1) for i in range(wave_total)])  1.47 us
    ppermute x1, waiting for transfers between devices, per_device(): lax.ppermute(total, 'wave', [(i, i ^ step) for i in range(wave_total)])  1.17 us
  transfers between devices with their start and end apart: 4, of which 3 were waited for; matrix products, arithmetic and copies ran while one was open for 0% of the time, Pallas kernels for 7%

profile of v15, /device:TPU:0, one launch (start us, length us, event | category | flops | bytes accessed | tf_op | source)
XLA Modules:
  0.0 40.8 jit_solution(15328108631735711049)
XLA Ops:
  0.0 2.9 %collective-permute-start = (bf16[256,256]{1,0:T(8,128)(2,1)}, bf16[256,256]{1,0:T(8,128)(2,1)S(1)}, u32[]{:S(2)}, u32[]{:S(2)}) collective-permute-start(bf16[256,256]{1,0:T(8,128)(2,1)} %bitcast.8), channel_id=1, source_target_pairs={{0,2},{1,17},{2,0},{3,19},{4,6},{5,21},{6,4},{7,23},{8,10},{9,25},... | collective-permute-start | bytes 393224 | tf_op jit(solution)/shard_map/ppermute | solution.py:148
  2.9 3.2 %collective-permute-done.arrived_ref = bf16[256,256]{1,0:T(8,128)(2,1)S(1)} collective-permute-done((bf16[256,256]{1,0:T(8,128)(2,1)}, bf16[256,256]{1,0:T(8,128)(2,1)S(1)}, u32[]{:S(2)}, u32[]{:S(2)}) %collective-permute-start) | collective-permute-done | bytes 131104 | tf_op jit(solution)/shard_map/ppermute | solution.py:148
  6.1 1.5 %collective-permute-start.1 = (bf16[256,256]{1,0:T(8,128)(2,1)S(1)}, bf16[256,256]{1,0:T(8,128)(2,1)S(1)}, u32[]{:S(2)}, u32[]{:S(2)}) collective-permute-start(bf16[256,256]{1,0:T(8,128)(2,1)S(1)} %collective-permute-done.arrived_ref), channel_id=1, source_target_pairs={{0,1},{1,0},{2,3},{3,2},{4,5},{5,4},{6,7},{7,6},{8,9},{9,8},{10,11... | collective-permute-start | bytes 393224 | tf_op jit(solution)/shard_map/ppermute | solution.py:149
  7.6 2.7 %shard_map.64 = (bf16[8,144,256]{2,1,0:T(8,128)(2,1)}, bf16[256,256]{1,0:T(8,128)(2,1)S(1)}, bf16[256,4096]{1,0:T(8,128)(2,1)S(1)}) custom-call(s32[1]{0:T(128)} %bitcast.me_ref, bf16[512,256]{1,0:T(8,128)(2,1)} %src_hbm.1, bf16[4,128]{1,0:T(4,128)(2,1)} %bitcast.12, s32[1,512]{1,0:T(1,128)} %bitcast.10, s32[1,512]{1,0:T(1,128)} %bitcast.11, ...), custom_call_target="tpu_custom_call" | custom-call | tf_op jit(solution)/shard_map/pallas_call | solution.py:152
  10.3 4.3 %all-to-all-start = ((bf16[8,144,256]{2,1,0:T(8,128)(2,1)}), bf16[8,144,256]{2,1,0:T(8,128)(2,1)S(1)}, u32[]{:S(2)}, u32[]{:S(2)}) async-start(bf16[8,144,256]{2,1,0:T(8,128)(2,1)} %get-tuple-element.8), calls=%async_computation | async-start | bytes 1179648 | tf_op jit(solution)/shard_map/all_to_all | solution.py:177
  14.6 0.0 collective-permute-done.1.passed_ref
  14.6 9.8 %all-to-all-done.got_ref = bf16[8,144,256]{2,1,0:T(8,128)(2,1)S(1)} async-done(((bf16[8,144,256]{2,1,0:T(8,128)(2,1)}), bf16[8,144,256]{2,1,0:T(8,128)(2,1)S(1)}, u32[]{:S(2)}, u32[]{:S(2)}) %all-to-all-start) | async-done | bytes 589856 | tf_op jit(solution)/shard_map/all_to_all | solution.py:177
  24.5 1.0 %shard_map.66 = bf16[256,256]{1,0:T(8,128)(2,1)S(1)} custom-call(bf16[8,144,256]{2,1,0:T(8,128)(2,1)S(1)} %all-to-all-done.got_ref, bf16[256,256]{1,0:T(8,128)(2,1)S(1)} %get-tuple-element.9.refs_0_, bf16[256,256]{1,0:T(8,128)(2,1)S(1)} %shard_map.65.refs_1_), custom_call_target="tpu_custom_call" | custom-call | tf_op jit(solution)/shard_map/pallas_call | solution.py:192
  25.5 12.8 %all_to_all.10 = bf16[16,16,256]{2,1,0:T(8,128)(2,1)S(1)} all-to-all(bf16[16,16,256]{2,1,0:T(8,128)(2,1)S(1)} %bitcast.7), channel_id=1, replica_groups=mesh['bin'=16,'wave'=2] {'bin'}, dimensions={0} | all-to-all | bytes 262144 | tf_op jit(solution)/shard_map/all_to_all | solution.py:199
  38.4 0.1 collective-permute-start.2
  38.4 1.2 %collective-permute-done.2.theirs_ref = f32[16,256]{1,0:T(8,128)S(1)} collective-permute-done((f32[16,256]{1,0:T(8,128)S(1)}, f32[16,256]{1,0:T(8,128)S(1)}, u32[]{:S(2)}, u32[]{:S(2)}) %collective-permute-start.2) | collective-permute-done | bytes 16416 | tf_op jit(solution)/shard_map/ppermute | solution.py:211
  39.6 1.2 %shard_map.67 = f32[16,4096]{1,0:T(8,128)} custom-call(f32[16,256]{1,0:T(8,128)S(1)} %convert_reduce_fusion.mine_ref, f32[16,256]{1,0:T(8,128)S(1)} %collective-permute-done.2.theirs_ref, bf16[256,4096]{1,0:T(8,128)(2,1)S(1)} %get-tuple-element.10.line_ref), custom_call_target="tpu_custom_call" | custom-call | tf_op jit(solution)/shard_map/pallas_call | solution.py:213
  (2 shorter events, 0.0 us)
Async XLA Ops:
  0.0 6.1 %collective-permute-start = (bf16[256,256]{1,0:T(8,128)(2,1)}, bf16[256,256]{1,0:T(8,128)(2,1)S(1)}, u32[]{:S(2)}, u32[]{:S(2)}) collective-permute-start(bf16[256,256]{1,0:T(8,128)(2,1)} %bitcast.8), channel_id=1, source_target_pairs={{0,2},{1,17},{2,0},{3,19},{4,6},{5,21},{6,4},{7,23},{8,10},{9,25},... | collective-permute-start | bytes 393224 | tf_op jit(solution)/shard_map/ppermute | solution.py:148
  6.1 8.5 %collective-permute-start.1 = (bf16[256,256]{1,0:T(8,128)(2,1)S(1)}, bf16[256,256]{1,0:T(8,128)(2,1)S(1)}, u32[]{:S(2)}, u32[]{:S(2)}) collective-permute-start(bf16[256,256]{1,0:T(8,128)(2,1)S(1)} %collective-permute-done.arrived_ref), channel_id=1, source_target_pairs={{0,1},{1,0},{2,3},{3,2},{4,5},{5,4},{6,7},{7,6},{8,9},{9,8},{10,11... | collective-permute-start | bytes 393224 | tf_op jit(solution)/shard_map/ppermute | solution.py:149
  10.3 14.2 %all-to-all-start = ((bf16[8,144,256]{2,1,0:T(8,128)(2,1)}), bf16[8,144,256]{2,1,0:T(8,128)(2,1)S(1)}, u32[]{:S(2)}, u32[]{:S(2)}) async-start(bf16[8,144,256]{2,1,0:T(8,128)(2,1)} %get-tuple-element.8), calls=%async_computation | async-start | bytes 1179648 | tf_op jit(solution)/shard_map/all_to_all | solution.py:177
  38.4 1.2 %collective-permute-start.2 = (f32[16,256]{1,0:T(8,128)S(1)}, f32[16,256]{1,0:T(8,128)S(1)}, u32[]{:S(2)}, u32[]{:S(2)}) collective-permute-start(f32[16,256]{1,0:T(8,128)S(1)} %convert_reduce_fusion.mine_ref), channel_id=1, source_target_pairs={{0,1},{1,0},{2,3},{3,2},{4,5},{5,4},{6,7},{7,6},{8,9},{9,8},{10,11... | collective-permute-start | bytes 49160 | tf_op jit(solution)/shard_map/ppermute | solution.py:211

commit v16 on v6

--- a/solution.py
+++ b/solution.py
@@ -11,7 +11,6 @@
 META_ROWS = 16
 RAY_BASE = 32
 LANES = 128
-OVERLAP_FLOPS = 10**10
 VMEM_LIMIT = 32 * 1024 * 1024
 F32 = jnp.float32
 BF16 = jnp.bfloat16
@@ -28,7 +27,9 @@
 
 def pack_kernel(plan, me_ref, src_hbm, den_hbm, bin_hbm, ray_hbm, table_hbm, line_hbm, *rest):
     targets, block = plan.targets, plan.block
-    out, table_out, line_out, src_ref, den_ref, bin_ref, ray_ref, sems = rest
+    out, table_out, line_out, share_out, src_ref, den_ref, bin_ref, ray_ref, sems = rest
+    share = share_out.shape[0]
+    share_rows = pl.ds(pl.multiple_of(me_ref[0] % 2 * share, share), share)
     copies = [
         pltpu.make_async_copy(a, b, sems.at[i])
         for i, (a, b) in enumerate(
@@ -39,6 +40,7 @@
                 (src_hbm, src_ref),
                 (table_hbm, table_out),
                 (line_hbm, line_out),
+                (table_hbm.at[share_rows], share_out),
             )
         )
     ]
@@ -46,7 +48,7 @@
         copy.start()
     cells, levels = src_ref.shape
     earlier = (iota((cells, cells), 0) < iota((cells, cells), 1)).astype(F32).astype(BF16)
-    my_half = me_ref[0] // targets
+    my_half = me_ref[0] // (targets * plan.wave)
     for copy in copies[:3]:
         copy.wait()
     bins = bin_ref[...]
@@ -76,17 +78,17 @@
         copy.wait()
 
 
-def keep_kernel(table_ref, out_ref):
-    out_ref[...] = table_ref[...]
-
-
-def level_kernel(plan, rays, got_ref, *refs):
-    table_refs, out_ref = refs[:-1], refs[-1]
+def level_kernel(plan, rays, me_ref, got_ref, own_ref, arrived_ref, passed_ref, out_ref):
+    upper = me_ref[0] % 2 == 1
+    arrived, passed = arrived_ref[...], passed_ref[...]
+    other = jnp.concatenate(
+        [jnp.where(upper, passed, arrived), jnp.where(upper, arrived, passed)], axis=0
+    )
     targets, block = plan.targets, plan.block
     meta = [got_ref[s, block:, :block].astype(F32) for s in range(targets)]
     columns = [jnp.transpose(m[:8]) for m in meta]
     total = jnp.zeros(out_ref.shape, F32)
-    for part, table_ref in enumerate(table_refs):
+    for part, table in enumerate((own_ref[...], other)):
         low, high = part * plan.capacity, (part + 1) * plan.capacity
         src = got_ref[:, low:high, :].reshape(targets * plan.capacity, got_ref.shape[2])
         den = jnp.concatenate([c[low:high, 0:1] for c in columns], axis=0)
@@ -94,7 +96,6 @@
             [m[1:2, low:high] * RAY_BASE + m[2:3, low:high] for m in meta], axis=1
         ).astype(I32)
         wide = src.astype(F32)
-        table = table_ref[...]
         first = (den * jnp.dot(src, table, preferred_element_type=F32) + wide).astype(BF16)
         pops = (den * jnp.dot(first, table, preferred_element_type=F32) + wide).astype(BF16)
         pick = (iota((rays, src.shape[0]), 0) == ray).astype(F32).astype(BF16)
@@ -113,8 +114,9 @@
 
 
 class Plan:
-    def __init__(self, bin_total, cells):
+    def __init__(self, bin_total, wave_total, cells):
         self.bins = bin_total
+        self.wave = wave_total
         self.targets = bin_total // 2
         self.capacity = max(2, 2 * cells // bin_total)
         self.block = 2 * self.capacity
@@ -130,7 +132,7 @@
     cells, levels = sources.shape
     bin_total = lax.axis_size("bin")
     wave_total = lax.axis_size("wave")
-    plan = Plan(bin_total, cells)
+    plan = Plan(bin_total, wave_total, cells)
     rows = plan.block + META_ROWS
     params = pltpu.CompilerParams(vmem_limit_bytes=VMEM_LIMIT)
     vmem = pl.BlockSpec(memory_space=pltpu.VMEM)
@@ -140,23 +142,23 @@
     def in_hbm(x):
         return pltpu.with_memory_space_constraint(x, pltpu.HBM)
 
-    arrived = lax.ppermute(rate_tables[0], "bin", plan.table_moves())
-    me = lax.axis_index("bin").astype(I32).reshape(1)
+    me = lax.axis_index(("bin", "wave")).astype(I32).reshape(1)
+    share = (levels // 2, levels)
     den_rows = cells // min(cells, LANES)
-    outgoing, own, held_line = pl.pallas_call(
+    outgoing, own, held_line, own_share = pl.pallas_call(
         functools.partial(pack_kernel, plan),
         out_shape=[
             jax.ShapeDtypeStruct(a, BF16)
-            for a in ((plan.targets, rows, levels), rate_tables.shape[1:], line_table.shape)
+            for a in ((plan.targets, rows, levels), (levels, levels), line_table.shape, share)
         ],
         in_specs=[smem] + [hbm] * 6,
-        out_specs=[vmem] * 3,
+        out_specs=[vmem] * 4,
         scratch_shapes=[
             pltpu.VMEM((cells, levels), BF16),
             pltpu.VMEM((den_rows, cells // den_rows), BF16),
             pltpu.VMEM((1, cells), I32),
             pltpu.VMEM((1, cells), I32),
-            pltpu.SemaphoreType.DMA((6,)),
+            pltpu.SemaphoreType.DMA((7,)),
         ],
         compiler_params=params,
     )(
@@ -171,25 +173,17 @@
     got = lax.all_to_all(
         outgoing, "bin", split_axis=0, concat_axis=0, tiled=True, axis_index_groups=plan.halves()
     )
-    other = pl.pallas_call(
-        keep_kernel,
-        out_shape=jax.ShapeDtypeStruct(arrived.shape, BF16),
-        in_specs=[vmem],
-        out_specs=vmem,
-        compiler_params=params,
-        cost_estimate=pl.CostEstimate(
-            flops=OVERLAP_FLOPS, bytes_accessed=4 * arrived.size, transcendentals=0
-        ),
-    )(arrived)
+    arrived = lax.ppermute(own_share, "bin", plan.table_moves())
+    passed = lax.ppermute(arrived, "wave", [(i, i ^ 1) for i in range(wave_total)])
     ray_rows = RAY_DEV
     rays = ray_rows * bin_total
     partial_sums = pl.pallas_call(
         functools.partial(level_kernel, plan, rays),
         out_shape=jax.ShapeDtypeStruct((rays, levels), BF16),
-        in_specs=[vmem] * 3,
+        in_specs=[smem] + [vmem] * 4,
         out_specs=vmem,
         compiler_params=params,
-    )(got, own, other)
+    )(me, got, own, arrived, passed)
     held = lax.all_to_all(
         partial_sums.reshape(bin_total, ray_rows, levels),
         "bin",

time: 35.1 us -> 37.4 us (1.066)
  blocking collectives: 10.4 us -> 13.7 us
  waiting for transfers between devices: 10.6 us -> 9.67 us
    all_to_all x1, waiting for transfers between devices: 9.42 us -> 1.95 us  [per_device(): lax.all_to_all(outgoing, 'bin', split_axis=0, concat_axis=0, tiled=True,...]
    ppermute x1 -> x2, waiting for transfers between devices: 0.01 us -> 6.54 us  [the longest x1 5.29 us: per_device(): arrived = lax.ppermute(own_share, 'bin', plan.table_moves())]
    all_to_all x1, blocking collectives: 10.4 us -> 13.7 us  [per_device(): lax.all_to_all(partial_sums.reshape(bin_total, ray_rows, levels), 'bin',...]
    all_to_all x1, starting transfers between devices: 4.75 us -> 6.2 us  [per_device(): lax.all_to_all(outgoing, 'bin', split_axis=0, concat_axis=0, tiled=True,...]
    ppermute x1 -> x2, starting transfers between devices: 4.04 us -> 2.59 us  [the longest x1 2.59 us: per_device(): arrived = lax.ppermute(own_share, 'bin', plan.table_moves())]
  transfers between devices with their start and end apart: 3 -> 4, of which waited for: 2 -> 4; matrix products, arithmetic and copies ran while one was open for 0% -> 0% of each run, Pallas kernels for 8% -> 0%
where the time goes in v16:
time: 37.4 us; the launch traced here: 37.2 us
  blocking collectives  13.7 us (37%)
  waiting for transfers between devices  9.67 us (26%)
  starting transfers between devices  8.86 us (24%)
  Pallas kernels  4.92 us (13%)
    all_to_all x1, blocking collectives, per_device(): lax.all_to_all(partial_sums.reshape(bin_total, ray_rows, levels), 'bin',...  13.7 us
    all_to_all x1, starting transfers between devices, per_device(): lax.all_to_all(outgoing, 'bin', split_axis=0, concat_axis=0, tiled=True,...  6.2 us
    ppermute x1, waiting for transfers between devices, per_device(): arrived = lax.ppermute(own_share, 'bin', plan.table_moves())  5.29 us
    pallas_call x1, Pallas kernels, per_device(): pl.pallas_call(functools.partial(pack_kernel, plan), out_shape=[jax.Shape...  2.72 us
    ppermute x1, starting transfers between devices, per_device(): arrived = lax.ppermute(own_share, 'bin', plan.table_moves())  2.59 us
    all_to_all x1, waiting for transfers between devices, per_device(): lax.all_to_all(outgoing, 'bin', split_axis=0, concat_axis=0, tiled=True,...  1.95 us
    ppermute x1, waiting for transfers between devices, per_device(): lax.ppermute(arrived, 'wave', [(i, i ^ 1) for i in range(wave_total)])  1.25 us
    ppermute x1, waiting for transfers between devices, per_device(): lax.ppermute(total, 'wave', [(i, i ^ step) for i in range(wave_total)])  1.17 us
  transfers between devices with their start and end apart: 4, of which 4 were waited for; matrix products, arithmetic and copies ran while one was open for 0% of the time, Pallas kernels for 0%

profile of v16, /device:TPU:0, one launch (start us, length us, event | category | flops | bytes accessed | tf_op | source)
XLA Modules:
  0.0 37.2 jit_solution(14649398377331222107)
XLA Ops:
  0.0 2.7 %shard_map.64 = (bf16[8,144,256]{2,1,0:T(8,128)(2,1)}, bf16[256,256]{1,0:T(8,128)(2,1)S(1)}, bf16[256,4096]{1,0:T(8,128)(2,1)S(1)}, bf16[128,256]{1,0:T(8,128)(2,1)S(1)}) custom-call(s32[1]{0:T(128)} %bitcast.me_ref, bf16[512,256]{1,0:T(8,128)(2,1)} %src_hbm.1, bf16[4,128]{1,0:T(4,128)(2,1)} %bitcast.10, s32[1,512]{1,0:T(1,128)} %bitcast.8, ...), custom_call_target="tpu_custom_call" | custom-call | tf_op jit(solution)/shard_map/pallas_call | solution.py:148
  2.7 6.2 %all-to-all-start = ((bf16[8,144,256]{2,1,0:T(8,128)(2,1)}), bf16[8,144,256]{2,1,0:T(8,128)(2,1)S(1)}, u32[]{:S(2)}, u32[]{:S(2)}) async-start(bf16[8,144,256]{2,1,0:T(8,128)(2,1)} %get-tuple-element.9), calls=%async_computation | async-start | bytes 1179648 | tf_op jit(solution)/shard_map/all_to_all | solution.py:173
  8.9 2.6 %collective-permute-start = (bf16[128,256]{1,0:T(8,128)(2,1)S(1)}, bf16[128,256]{1,0:T(8,128)(2,1)S(1)}, u32[]{:S(2)}, u32[]{:S(2)}) collective-permute-start(bf16[128,256]{1,0:T(8,128)(2,1)S(1)} %get-tuple-element.11), channel_id=1, source_target_pairs={{0,16},{2,18},{4,20},{6,22},{8,24},{10,26},{12,28},{14,30},{16,0},... | collective-permute-start | bytes 196616 | tf_op jit(solution)/shard_map/ppermute | solution.py:176
  11.5 5.3 %collective-permute-done.arrived_ref = bf16[128,256]{1,0:T(8,128)(2,1)S(1)} collective-permute-done((bf16[128,256]{1,0:T(8,128)(2,1)S(1)}, bf16[128,256]{1,0:T(8,128)(2,1)S(1)}, u32[]{:S(2)}, u32[]{:S(2)}) %collective-permute-start) | collective-permute-done | bytes 65568 | tf_op jit(solution)/shard_map/ppermute | solution.py:176
  16.8 0.0 collective-permute-start.1
  16.8 1.3 %collective-permute-done.1.passed_ref = bf16[128,256]{1,0:T(8,128)(2,1)S(1)} collective-permute-done((bf16[128,256]{1,0:T(8,128)(2,1)S(1)}, bf16[128,256]{1,0:T(8,128)(2,1)S(1)}, u32[]{:S(2)}, u32[]{:S(2)}) %collective-permute-start.1) | collective-permute-done | bytes 65568 | tf_op jit(solution)/shard_map/ppermute | solution.py:177
  18.1 2.0 %all-to-all-done.got_ref = bf16[8,144,256]{2,1,0:T(8,128)(2,1)S(1)} async-done(((bf16[8,144,256]{2,1,0:T(8,128)(2,1)}), bf16[8,144,256]{2,1,0:T(8,128)(2,1)S(1)}, u32[]{:S(2)}, u32[]{:S(2)}) %all-to-all-start) | async-done | bytes 589856 | tf_op jit(solution)/shard_map/all_to_all | solution.py:173
  20.0 1.0 %shard_map.65 = bf16[256,256]{1,0:T(8,128)(2,1)S(1)} custom-call(s32[1]{0:T(128)} %bitcast.me_ref, bf16[8,144,256]{2,1,0:T(8,128)(2,1)S(1)} %all-to-all-done.got_ref, bf16[256,256]{1,0:T(8,128)(2,1)S(1)} %get-tuple-element.10.own_ref, bf16[128,256]{1,0:T(8,128)(2,1)S(1)} %collective-permute-done.arrived_ref, ...), custom_call_target="tpu_custom_call" | custom-call | tf_op jit(solution)/shard_map/pallas_call | solution.py:180
  21.1 13.7 %all_to_all.10 = bf16[16,16,256]{2,1,0:T(8,128)(2,1)S(1)} all-to-all(bf16[16,16,256]{2,1,0:T(8,128)(2,1)S(1)} %bitcast.6), channel_id=1, replica_groups=mesh['bin'=16,'wave'=2] {'bin'}, dimensions={0} | all-to-all | bytes 262144 | tf_op jit(solution)/shard_map/all_to_all | solution.py:187
  34.7 0.1 collective-permute-start.2
  34.8 1.2 %collective-permute-done.2.theirs_ref = f32[16,256]{1,0:T(8,128)S(1)} collective-permute-done((f32[16,256]{1,0:T(8,128)S(1)}, f32[16,256]{1,0:T(8,128)S(1)}, u32[]{:S(2)}, u32[]{:S(2)}) %collective-permute-start.2) | collective-permute-done | bytes 16416 | tf_op jit(solution)/shard_map/ppermute | solution.py:199
  36.0 1.2 %shard_map.66 = f32[16,4096]{1,0:T(8,128)} custom-call(f32[16,256]{1,0:T(8,128)S(1)} %convert_reduce_fusion.mine_ref, f32[16,256]{1,0:T(8,128)S(1)} %collective-permute-done.2.theirs_ref, bf16[256,4096]{1,0:T(8,128)(2,1)S(1)} %get-tuple-element.12.line_ref), custom_call_target="tpu_custom_call" | custom-call | tf_op jit(solution)/shard_map/pallas_call | solution.py:201
  (1 shorter events, 0.0 us)
Async XLA Ops:
  2.7 17.3 %all-to-all-start = ((bf16[8,144,256]{2,1,0:T(8,128)(2,1)}), bf16[8,144,256]{2,1,0:T(8,128)(2,1)S(1)}, u32[]{:S(2)}, u32[]{:S(2)}) async-start(bf16[8,144,256]{2,1,0:T(8,128)(2,1)} %get-tuple-element.9), calls=%async_computation | async-start | bytes 1179648 | tf_op jit(solution)/shard_map/all_to_all | solution.py:173
  8.9 7.9 %collective-permute-start = (bf16[128,256]{1,0:T(8,128)(2,1)S(1)}, bf16[128,256]{1,0:T(8,128)(2,1)S(1)}, u32[]{:S(2)}, u32[]{:S(2)}) collective-permute-start(bf16[128,256]{1,0:T(8,128)(2,1)S(1)} %get-tuple-element.11), channel_id=1, source_target_pairs={{0,16},{2,18},{4,20},{6,22},{8,24},{10,26},{12,28},{14,30},{16,0},... | collective-permute-start | bytes 196616 | tf_op jit(solution)/shard_map/ppermute | solution.py:176
  16.8 1.3 %collective-permute-start.1 = (bf16[128,256]{1,0:T(8,128)(2,1)S(1)}, bf16[128,256]{1,0:T(8,128)(2,1)S(1)}, u32[]{:S(2)}, u32[]{:S(2)}) collective-permute-start(bf16[128,256]{1,0:T(8,128)(2,1)S(1)} %collective-permute-done.arrived_ref), channel_id=1, source_target_pairs={{0,1},{1,0},{2,3},{3,2},{4,5},{5,4},{6,7},{7,6},{8,9},{9,8},{10,11... | collective-permute-start | bytes 196616 | tf_op jit(solution)/shard_map/ppermute | solution.py:177
  34.7 1.2 %collective-permute-start.2 = (f32[16,256]{1,0:T(8,128)S(1)}, f32[16,256]{1,0:T(8,128)S(1)}, u32[]{:S(2)}, u32[]{:S(2)}) collective-permute-start(f32[16,256]{1,0:T(8,128)S(1)} %convert_reduce_fusion.mine_ref), channel_id=1, source_target_pairs={{0,1},{1,0},{2,3},{3,2},{4,5},{5,4},{6,7},{7,6},{8,9},{9,8},{10,11... | collective-permute-start | bytes 49160 | tf_op jit(solution)/shard_map/ppermute | solution.py:199

commit v17 on v8

--- a/solution.py
+++ b/solution.py
@@ -51,8 +51,8 @@
     hot = (iota((plan.bins, cells), 0) == bins).astype(F32)
     before = jnp.dot(hot.astype(BF16), earlier, preferred_element_type=F32)
     position = jnp.sum(hot * before, axis=0, keepdims=True).astype(I32)
-    half = bins // targets
-    slot = (bins - half * targets) * block + half * plan.capacity + position
+    part = bins // targets
+    slot = (bins - part * targets) * block + part * plan.capacity + position
     rays = ray_ref[...]
     ray_high = rays // RAY_BASE
     ray_low = rays - ray_high * RAY_BASE
@@ -83,7 +83,7 @@
     meta = [got_ref[s, block:, :block].astype(F32) for s in range(targets)]
     columns = [jnp.transpose(m[:8]) for m in meta]
     total = jnp.zeros(out_ref.shape, F32)
-    for part in range(2):
+    for part in range(plan.parts):
         low, high = part * plan.capacity, (part + 1) * plan.capacity
         src = got_ref[:, low:high, :].reshape(targets * plan.capacity, got_ref.shape[2])
         den = jnp.concatenate([c[low:high, 0:1] for c in columns], axis=0)
@@ -112,15 +112,16 @@
 class Plan:
     def __init__(self, bin_total, cells):
         self.bins = bin_total
-        self.targets = bin_total // 2
+        self.parts = 1 << (bin_total.bit_length() // 2)
+        self.targets = bin_total // self.parts
         self.capacity = max(2, 2 * cells // bin_total)
-        self.block = 2 * self.capacity
-
-    def pairs(self):
-        return [[i, i + self.targets] for i in range(self.targets)]
-
-    def halves(self):
-        return [list(range(self.targets)), list(range(self.targets, self.bins))]
+        self.block = self.parts * self.capacity
+
+    def lines(self):
+        return [[p * self.targets + t for p in range(self.parts)] for t in range(self.targets)]
+
+    def planes(self):
+        return [[p * self.targets + t for t in range(self.targets)] for p in range(self.parts)]
 
 
 def per_device(sources, density, temp_bins, ray_index, rate_tables, line_table):
@@ -136,7 +137,7 @@
     def in_hbm(x):
         return pltpu.with_memory_space_constraint(x, pltpu.HBM)
 
-    arrived = lax.all_gather(rate_tables[0], "bin", axis_index_groups=plan.pairs())
+    arrived = lax.all_gather(rate_tables[0], "bin", axis_index_groups=plan.lines())
     den_rows = cells // min(cells, LANES)
     outgoing, held_line = pl.pallas_call(
         functools.partial(pack_kernel, plan),
@@ -162,7 +163,7 @@
         in_hbm(line_table),
     )
     got = lax.all_to_all(
-        outgoing, "bin", split_axis=0, concat_axis=0, tiled=True, axis_index_groups=plan.halves()
+        outgoing, "bin", split_axis=0, concat_axis=0, tiled=True, axis_index_groups=plan.planes()
     )
     tables = pl.pallas_call(
         keep_kernel,

time: 37.6 us -> 42.7 us (1.14)
  blocking collectives: 21.7 us -> 30.9 us
  waiting for transfers between devices: 4.36 us -> 1.17 us
  starting transfers between devices: 6.27 us -> 5.25 us
    all_gather x1, blocking collectives: 9.28 us -> 15.9 us  [per_device(): lax.all_gather(rate_tables[0], 'bin', axis_index_groups=plan.lines())]
    all_to_all x1, waiting for transfers between devices: 3.19 us -> 0.01 us  [per_device(): lax.all_to_all(outgoing, 'bin', split_axis=0, concat_axis=0, tiled=True,...]
    all_to_all x1, blocking collectives: 12.4 us -> 15 us  [per_device(): lax.all_to_all(partial_sums.reshape(bin_total, ray_rows, levels), 'bin',...]
    all_to_all x1, starting transfers between devices: 6.2 us -> 5.18 us  [per_device(): lax.all_to_all(outgoing, 'bin', split_axis=0, concat_axis=0, tiled=True,...]
  transfers between devices with their start and end apart: 2 -> 2, of which waited for: 2 -> 1; matrix products, arithmetic and copies ran while one was open for 0% -> 0% of each run, Pallas kernels for 0% -> 0%
where the time goes in v17:
time: 42.7 us; the launch traced here: 42.5 us
  blocking collectives  30.9 us (72%)
  starting transfers between devices  5.25 us (12%)
  Pallas kernels  5.08 us (12%)
  waiting for transfers between devices  1.17 us (3%)
    all_gather x1, blocking collectives, per_device(): lax.all_gather(rate_tables[0], 'bin', axis_index_groups=plan.lines())  15.9 us
    all_to_all x1, blocking collectives, per_device(): lax.all_to_all(partial_sums.reshape(bin_total, ray_rows, levels), 'bin',...  15 us
    all_to_all x1, starting transfers between devices, per_device(): lax.all_to_all(outgoing, 'bin', split_axis=0, concat_axis=0, tiled=True,...  5.18 us
    pallas_call x1, Pallas kernels, per_device(): pl.pallas_call(functools.partial(pack_kernel, plan), out_shape=[jax.Shape...  2.72 us
    ppermute x1, waiting for transfers between devices, per_device(): lax.ppermute(total, 'wave', [(i, i ^ step) for i in range(wave_total)])  1.17 us
    pallas_call x1, Pallas kernels, per_device(): pl.pallas_call(line_kernel, out_shape=jax.ShapeDtypeStruct((ray_rows, lin...  1.17 us
    pallas_call x1, Pallas kernels, per_device(): pl.pallas_call(functools.partial(level_kernel, plan, rays), out_shape=jax...  1.16 us
  transfers between devices with their start and end apart: 2, of which 1 were waited for; matrix products, arithmetic and copies ran while one was open for 0% of the time, Pallas kernels for 0%

profile of v17, /device:TPU:0, one launch (start us, length us, event | category | flops | bytes accessed | tf_op | source)
XLA Modules:
  0.0 42.5 jit_solution(980742636386291067)
XLA Ops:
  0.0 0.0 copy-start
  0.0 2.7 %shard_map.64 = (bf16[4,272,256]{2,1,0:T(8,128)(2,1)}, bf16[256,4096]{1,0:T(8,128)(2,1)S(1)}) custom-call(bf16[512,256]{1,0:T(8,128)(2,1)} %src_hbm.1, bf16[4,128]{1,0:T(4,128)(2,1)} %bitcast.7, s32[1,512]{1,0:T(1,128)} %bitcast.5, s32[1,512]{1,0:T(1,128)} %bitcast.6, bf16[256,4096]{1,0:T(8,128)(2,1)} %line_hbm.1), custom_call_target="tpu_custom_call" | custom-call | tf_op jit(solution)/shard_map/pallas_call | solution.py:142
  2.7 5.2 %all-to-all-start = ((bf16[4,272,256]{2,1,0:T(8,128)(2,1)}), bf16[4,272,256]{2,1,0:T(8,128)(2,1)S(1)}, u32[]{:S(2)}, u32[]{:S(2)}) async-start(bf16[4,272,256]{2,1,0:T(8,128)(2,1)} %get-tuple-element.7), calls=%async_computation | async-start | bytes 1114112 | tf_op jit(solution)/shard_map/all_to_all | solution.py:165
  7.9 0.0 copy-done
  7.9 15.9 %all_gather.3.tables_ref = bf16[4,256,256]{2,1,0:T(8,128)(2,1)S(1)} all-gather(bf16[1,256,256]{2,1,0:T(8,128)(2,1)S(1)} %copy-done), channel_id=1, replica_groups={{0,8,16,24},{2,10,18,26},{4,12,20,28},{6,14,22,30},{1,9,17,25},{3,11,19..., dimensions={0}, use_global_device_ids=true | all-gather | bytes 655360 | tf_op jit(solution)/shard_map/all_gather | solution.py:140
  23.8 0.0 all-to-all-done.got_ref
  23.8 1.2 %shard_map.66 = bf16[256,256]{1,0:T(8,128)(2,1)S(1)} custom-call(bf16[4,272,256]{2,1,0:T(8,128)(2,1)S(1)} %all-to-all-done.got_ref, bf16[4,256,256]{2,1,0:T(8,128)(2,1)S(1)} %shard_map.65.tables_ref), custom_call_target="tpu_custom_call" | custom-call | tf_op jit(solution)/shard_map/pallas_call | solution.py:180
  25.0 15.0 %all_to_all.10 = bf16[16,16,256]{2,1,0:T(8,128)(2,1)S(1)} all-to-all(bf16[16,16,256]{2,1,0:T(8,128)(2,1)S(1)} %bitcast.4), channel_id=1, replica_groups=mesh['bin'=16,'wave'=2] {'bin'}, dimensions={0} | all-to-all | bytes 262144 | tf_op jit(solution)/shard_map/all_to_all | solution.py:187
  40.1 0.1 collective-permute-start
  40.1 1.2 %collective-permute-done.theirs_ref = f32[16,256]{1,0:T(8,128)S(1)} collective-permute-done((f32[16,256]{1,0:T(8,128)S(1)}, f32[16,256]{1,0:T(8,128)S(1)}, u32[]{:S(2)}, u32[]{:S(2)}) %collective-permute-start) | collective-permute-done | bytes 16416 | tf_op jit(solution)/shard_map/ppermute | solution.py:199
  41.3 1.2 %shard_map.67 = f32[16,4096]{1,0:T(8,128)} custom-call(f32[16,256]{1,0:T(8,128)S(1)} %convert_reduce_fusion.mine_ref, f32[16,256]{1,0:T(8,128)S(1)} %collective-permute-done.theirs_ref, bf16[256,4096]{1,0:T(8,128)(2,1)S(1)} %get-tuple-element.8.line_ref), custom_call_target="tpu_custom_call" | custom-call | tf_op jit(solution)/shard_map/pallas_call | solution.py:201
  (2 shorter events, 0.1 us)
Async XLA Ops:
  0.0 7.9 %copy-start = (bf16[1,256,256]{2,1,0:T(8,128)(2,1)S(1)}, bf16[1,256,256]{2,1,0:T(8,128)(2,1)}, u32[]{:S(2)}) copy-start(bf16[1,256,256]{2,1,0:T(8,128)(2,1)} %param.10) | copy-start | bytes 393220
  2.7 21.1 %all-to-all-start = ((bf16[4,272,256]{2,1,0:T(8,128)(2,1)}), bf16[4,272,256]{2,1,0:T(8,128)(2,1)S(1)}, u32[]{:S(2)}, u32[]{:S(2)}) async-start(bf16[4,272,256]{2,1,0:T(8,128)(2,1)} %get-tuple-element.7), calls=%async_computation | async-start | bytes 1114112 | tf_op jit(solution)/shard_map/all_to_all | solution.py:165
  40.1 1.2 %collective-permute-start = (f32[16,256]{1,0:T(8,128)S(1)}, f32[16,256]{1,0:T(8,128)S(1)}, u32[]{:S(2)}, u32[]{:S(2)}) collective-permute-start(f32[16,256]{1,0:T(8,128)S(1)} %convert_reduce_fusion.mine_ref), channel_id=1, source_target_pairs={{0,1},{1,0},{2,3},{3,2},{4,5},{5,4},{6,7},{7,6},{8,9},{9,8},{10,11... | collective-permute-start | bytes 49160 | tf_op jit(solution)/shard_map/ppermute | solution.py:199

commit v18 on v10

--- a/solution.py
+++ b/solution.py
@@ -27,9 +27,9 @@
     return lax.broadcasted_iota(I32, shape, dim)
 
 
-def pack_kernel(plan, me_ref, src_hbm, den_hbm, bin_hbm, ray_hbm, table_hbm, line_hbm, *rest):
+def pack_kernel(plan, me_ref, src_hbm, den_hbm, bin_hbm, ray_hbm, *rest):
     targets, block = plan.targets, plan.block
-    out, table_out, line_out, src_ref, den_ref, bin_ref, ray_ref, sems = rest
+    out, src_ref, den_ref, bin_ref, ray_ref, sems = rest
     copies = [
         pltpu.make_async_copy(a, b, sems.at[i])
         for i, (a, b) in enumerate(
@@ -38,22 +38,30 @@
                 (ray_hbm, ray_ref),
                 (den_hbm, den_ref),
                 (src_hbm, src_ref),
-                (table_hbm, table_out),
-                (line_hbm, line_out),
             )
         )
     ]
     for copy in copies:
         copy.start()
     cells, levels = src_ref.shape
-    earlier = (iota((cells, cells), 0) < iota((cells, cells), 1)).astype(F32).astype(BF16)
+    lanes = min(cells, LANES)
+    earlier = (iota((lanes, lanes), 0) < iota((lanes, lanes), 1)).astype(F32).astype(BF16)
     my_half = me_ref[0] // targets
     for copy in copies[:3]:
         copy.wait()
     bins = bin_ref[...]
     hot = (iota((plan.bins, cells), 0) == bins).astype(F32)
-    before = jnp.dot(hot.astype(BF16), earlier, preferred_element_type=F32)
-    position = jnp.sum(hot * before, axis=0, keepdims=True).astype(I32)
+    parts = [hot[:, i : i + lanes] for i in range(0, cells, lanes)]
+    ranks = jnp.dot(
+        jnp.concatenate(parts, axis=0).astype(BF16), earlier, preferred_element_type=F32
+    )
+    sofar = jnp.zeros((plan.bins, 1), F32)
+    places = []
+    for i, part in enumerate(parts):
+        rank = ranks[i * plan.bins : (i + 1) * plan.bins] + sofar
+        places.append(jnp.sum(part * rank, axis=0, keepdims=True))
+        sofar = sofar + jnp.sum(part, axis=1, keepdims=True)
+    position = jnp.concatenate(places, axis=1).astype(I32)
     half = bins // targets
     slot = (bins - half * targets) * block + (half ^ my_half) * plan.capacity + position
     rays = ray_ref[...]
@@ -73,21 +81,32 @@
     out[:, block:, :] = jnp.zeros((targets, META_ROWS, levels), BF16)
     for t in range(targets):
         out[t, block:, :block] = moved[:, t * block : (t + 1) * block]
-    for copy in copies[4:]:
-        copy.wait()
-
-
-def keep_kernel(table_ref, out_ref):
-    out_ref[...] = table_ref[...]
-
-
-def level_kernel(plan, rays, got_ref, *refs):
-    table_refs, out_ref = refs[:-1], refs[-1]
+
+
+def window_kernel(arrived_ref, table_hbm, line_hbm, powers_ref, line_ref, sems):
+    levels = arrived_ref.shape[0]
+    copies = [
+        pltpu.make_async_copy(table_hbm, powers_ref.at[0, :, pl.ds(0, levels)], sems.at[0]),
+        pltpu.make_async_copy(line_hbm, line_ref, sems.at[1]),
+    ]
+    for copy in copies:
+        copy.start()
+    powers_ref[1, :, :levels] = arrived_ref[...]
+    copies[0].wait()
+    for part in range(2):
+        table = powers_ref[part, :, :levels]
+        square = jnp.dot(table, table, preferred_element_type=F32)
+        powers_ref[part, :, levels:] = square.astype(BF16)
+    copies[1].wait()
+
+
+def level_kernel(plan, rays, got_ref, powers_ref, out_ref):
     targets, block = plan.targets, plan.block
     meta = [got_ref[s, block:, :block].astype(F32) for s in range(targets)]
     columns = [jnp.transpose(m[:8]) for m in meta]
     total = jnp.zeros(out_ref.shape, F32)
-    for part, table_ref in enumerate(table_refs):
+    levels = got_ref.shape[2]
+    for part in range(2):
         low, high = part * plan.capacity, (part + 1) * plan.capacity
         src = got_ref[:, low:high, :].reshape(targets * plan.capacity, got_ref.shape[2])
         den = jnp.concatenate([c[low:high, 0:1] for c in columns], axis=0)
@@ -95,9 +114,8 @@
             [m[1:2, low:high] * RAY_BASE + m[2:3, low:high] for m in meta], axis=1
         ).astype(I32)
         wide = src.astype(F32)
-        table = table_ref[...]
-        first = (den * jnp.dot(src, table, preferred_element_type=F32) + wide).astype(BF16)
-        pops = (den * jnp.dot(first, table, preferred_element_type=F32) + wide).astype(BF16)
+        steps = jnp.dot(src, powers_ref[part], preferred_element_type=F32)
+        pops = (wide + den * (steps[:, :levels] + den * steps[:, levels:])).astype(BF16)
         pick = (iota((rays, src.shape[0]), 0) == ray).astype(F32).astype(BF16)
         total = total + jnp.dot(pick, pops, preferred_element_type=F32)
     out_ref[...] = total.astype(BF16)
@@ -153,20 +171,17 @@
     arrived = lax.ppermute(rate_tables[0], "bin", plan.table_moves())
     me = lax.axis_index("bin").astype(I32).reshape(1)
     den_rows = cells // min(cells, LANES)
-    outgoing, own, held_line = pl.pallas_call(
+    outgoing = pl.pallas_call(
         functools.partial(pack_kernel, plan),
-        out_shape=[
-            pltpu.VMEM(a, BF16)
-            for a in ((plan.targets, rows, levels), rate_tables.shape[1:], line_table.shape)
-        ],
-        in_specs=[smem] + [hbm] * 6,
-        out_specs=[vmem] * 3,
+        out_shape=jax.ShapeDtypeStruct((plan.targets, rows, levels), BF16),
+        in_specs=[smem] + [hbm] * 4,
+        out_specs=vmem,
         scratch_shapes=[
             pltpu.VMEM((cells, levels), BF16),
             pltpu.VMEM((den_rows, cells // den_rows), BF16),
             pltpu.VMEM((1, cells), I32),
             pltpu.VMEM((1, cells), I32),
-            pltpu.SemaphoreType.DMA((6,)),
+            pltpu.SemaphoreType.DMA((4,)),
         ],
         compiler_params=params,
     )(
@@ -175,31 +190,32 @@
         in_hbm(density.reshape(den_rows, cells // den_rows)),
         in_hbm(temp_bins.reshape(1, cells)),
         in_hbm(ray_index.reshape(1, cells)),
-        in_hbm(rate_tables[0]),
-        in_hbm(line_table),
     )
     got = lax.all_to_all(
         outgoing, "bin", split_axis=0, concat_axis=0, tiled=True, axis_index_groups=plan.halves()
     )
-    other = pl.pallas_call(
-        keep_kernel,
-        out_shape=jax.ShapeDtypeStruct(arrived.shape, BF16),
-        in_specs=[vmem],
-        out_specs=vmem,
+    powers, held_line = pl.pallas_call(
+        window_kernel,
+        out_shape=[
+            jax.ShapeDtypeStruct(a, BF16) for a in ((2, levels, 2 * levels), line_table.shape)
+        ],
+        in_specs=[vmem, hbm, hbm],
+        out_specs=[vmem] * 2,
+        scratch_shapes=[pltpu.SemaphoreType.DMA((2,))],
         compiler_params=params,
         cost_estimate=pl.CostEstimate(
             flops=OVERLAP_FLOPS, bytes_accessed=4 * arrived.size, transcendentals=0
         ),
-    )(arrived)
+    )(arrived, in_hbm(rate_tables[0]), in_hbm(line_table))
     ray_rows = RAY_DEV
     rays = ray_rows * bin_total
     partial_sums = pl.pallas_call(
         functools.partial(level_kernel, plan, rays),
         out_shape=jax.ShapeDtypeStruct((rays, levels), BF16),
-        in_specs=[vmem] * 3,
+        in_specs=[vmem] * 2,
         out_specs=vmem,
         compiler_params=params,
-    )(got, own, other)
+    )(got, powers)
     held = lax.all_to_all(
         partial_sums.reshape(bin_total, ray_rows, levels),
         "bin",

time: 35 us -> 35 us (level)
  waiting for transfers between devices: 10.6 us -> 8.92 us
  Pallas kernels: 4.88 us -> 6.43 us
    all_to_all x1, waiting for transfers between devices: 9.42 us -> 7.74 us  [per_device(): lax.all_to_all(outgoing, 'bin', split_axis=0, concat_axis=0, tiled=True,...]
    pallas_call x2, Pallas kernels: 2.72 us -> 4.33 us  [the longest x1 2.64 us: per_device(): pl.pallas_call(functools.partial(pack_kernel, plan), out_shape=jax.ShapeD...]
  transfers between devices with their start and end apart: 3 -> 3, of which waited for: 2 -> 2; matrix products, arithmetic and copies ran while one was open for 0% -> 0% of each run, Pallas kernels for 8% -> 12%
where the time goes in v18:
time: 35 us; the launch traced here: 34.7 us
  blocking collectives  10.4 us (30%)
  waiting for transfers between devices  8.92 us (25%)
  starting transfers between devices  8.85 us (25%)
  Pallas kernels  6.43 us (18%)
    all_to_all x1, blocking collectives, per_device(): lax.all_to_all(partial_sums.reshape(bin_total, ray_rows, levels), 'bin',...  10.4 us
    all_to_all x1, waiting for transfers between devices, per_device(): lax.all_to_all(outgoing, 'bin', split_axis=0, concat_axis=0, tiled=True,...  7.74 us
    all_to_all x1, starting transfers between devices, per_device(): lax.all_to_all(outgoing, 'bin', split_axis=0, concat_axis=0, tiled=True,...  4.75 us
    ppermute x1, starting transfers between devices, per_device(): arrived = lax.ppermute(rate_tables[0], 'bin', plan.table_moves())  4.04 us
    pallas_call x1, Pallas kernels, per_device(): pl.pallas_call(functools.partial(pack_kernel, plan), out_shape=jax.ShapeD...  2.64 us
    pallas_call x1, Pallas kernels, per_device(): pl.pallas_call(window_kernel, out_shape=[jax.ShapeDtypeStruct(a, BF16) fo...  1.69 us
    ppermute x1, waiting for transfers between devices, per_device(): lax.ppermute(total, 'wave', [(i, i ^ step) for i in range(wave_total)])  1.17 us
    pallas_call x1, Pallas kernels, per_device(): pl.pallas_call(line_kernel, out_shape=jax.ShapeDtypeStruct(out_shape, F32...  1.13 us
  transfers between devices with their start and end apart: 3, of which 2 were waited for; matrix products, arithmetic and copies ran while one was open for 0% of the time, Pallas kernels for 12%

profile of v18, /device:TPU:0, one launch (start us, length us, event | category | flops | bytes accessed | tf_op | source)
XLA Modules:
  0.0 34.7 jit_solution(7473499885513033806)
XLA Ops:
  0.0 4.0 %collective-permute-start = (bf16[256,256]{1,0:T(8,128)(2,1)}, bf16[256,256]{1,0:T(8,128)(2,1)S(1)}, u32[]{:S(2)}, u32[]{:S(2)}) collective-permute-start(bf16[256,256]{1,0:T(8,128)(2,1)} %bitcast.10), channel_id=1, source_target_pairs={{0,16},{2,18},{4,20},{6,22},{8,24},{10,26},{12,28},{14,30},{16,0},... | collective-permute-start | bytes 393224 | tf_op jit(solution)/shard_map/ppermute | solution.py:171
  4.0 2.6 %shard_map.64 = bf16[8,144,256]{2,1,0:T(8,128)(2,1)} custom-call(s32[1]{0:T(128)} %bitcast.me_ref, bf16[512,256]{1,0:T(8,128)(2,1)} %src_hbm.1, bf16[4,128]{1,0:T(4,128)(2,1)} %bitcast.9, s32[1,512]{1,0:T(1,128)} %bitcast.7, s32[1,512]{1,0:T(1,128)} %bitcast.8), custom_call_target="tpu_custom_call" | custom-call | tf_op jit(solution)/shard_map/pallas_call | solution.py:174
  6.7 4.7 %all-to-all-start = ((bf16[8,144,256]{2,1,0:T(8,128)(2,1)}), bf16[8,144,256]{2,1,0:T(8,128)(2,1)S(1)}, u32[]{:S(2)}, u32[]{:S(2)}) async-start(bf16[8,144,256]{2,1,0:T(8,128)(2,1)} %shard_map.64), calls=%async_computation | async-start | bytes 1179648 | tf_op jit(solution)/shard_map/all_to_all | solution.py:194
  11.4 0.0 collective-permute-done.arrived_ref
  11.4 1.7 %shard_map.65 = (bf16[2,256,512]{2,1,0:T(8,128)(2,1)S(1)}, bf16[256,4096]{1,0:T(8,128)(2,1)S(1)}) custom-call(bf16[256,256]{1,0:T(8,128)(2,1)S(1)} %collective-permute-done.arrived_ref, bf16[256,256]{1,0:T(8,128)(2,1)} %bitcast.11, bf16[256,4096]{1,0:T(8,128)(2,1)} %line_hbm.1), custom_call_target="tpu_custom_call" | custom-call | flops 10000000000 | bytes 262144 | tf_op jit(solution)/shard_map/pallas_call | solution.py:197
  13.1 7.7 %all-to-all-done.got_ref = bf16[8,144,256]{2,1,0:T(8,128)(2,1)S(1)} async-done(((bf16[8,144,256]{2,1,0:T(8,128)(2,1)}), bf16[8,144,256]{2,1,0:T(8,128)(2,1)S(1)}, u32[]{:S(2)}, u32[]{:S(2)}) %all-to-all-start) | async-done | bytes 589856 | tf_op jit(solution)/shard_map/all_to_all | solution.py:194
  20.9 1.0 %shard_map.66 = bf16[256,256]{1,0:T(8,128)(2,1)S(1)} custom-call(bf16[8,144,256]{2,1,0:T(8,128)(2,1)S(1)} %all-to-all-done.got_ref, bf16[2,256,512]{2,1,0:T(8,128)(2,1)S(1)} %get-tuple-element.7.powers_ref), custom_call_target="tpu_custom_call" | custom-call | tf_op jit(solution)/shard_map/pallas_call | solution.py:212
  21.9 10.4 %all_to_all.10 = bf16[16,16,256]{2,1,0:T(8,128)(2,1)S(1)} all-to-all(bf16[16,16,256]{2,1,0:T(8,128)(2,1)S(1)} %bitcast.6), channel_id=1, replica_groups=mesh['bin'=16,'wave'=2] {'bin'}, dimensions={0} | all-to-all | bytes 262144 | tf_op jit(solution)/shard_map/all_to_all | solution.py:219
  32.3 0.1 collective-permute-start.1
  32.4 1.2 %collective-permute-done.1.theirs_ref = f32[16,256]{1,0:T(8,128)S(1)} collective-permute-done((f32[16,256]{1,0:T(8,128)S(1)}, f32[16,256]{1,0:T(8,128)S(1)}, u32[]{:S(2)}, u32[]{:S(2)}) %collective-permute-start.1) | collective-permute-done | bytes 16416 | tf_op jit(solution)/shard_map/ppermute | solution.py:231
  33.6 1.1 %shard_map.67 = f32[16,4096]{1,0:T(8,128)} custom-call(f32[16,256]{1,0:T(8,128)S(1)} %convert_reduce_fusion.mine_ref, f32[16,256]{1,0:T(8,128)S(1)} %collective-permute-done.1.theirs_ref, bf16[256,4096]{1,0:T(8,128)(2,1)S(1)} %get-tuple-element.8.line_ref), custom_call_target="tpu_custom_call" | custom-call | tf_op jit(solution)/shard_map/pallas_call | solution.py:234
  (1 shorter events, 0.0 us)
Async XLA Ops:
  0.0 11.4 %collective-permute-start = (bf16[256,256]{1,0:T(8,128)(2,1)}, bf16[256,256]{1,0:T(8,128)(2,1)S(1)}, u32[]{:S(2)}, u32[]{:S(2)}) collective-permute-start(bf16[256,256]{1,0:T(8,128)(2,1)} %bitcast.10), channel_id=1, source_target_pairs={{0,16},{2,18},{4,20},{6,22},{8,24},{10,26},{12,28},{14,30},{16,0},... | collective-permute-start | bytes 393224 | tf_op jit(solution)/shard_map/ppermute | solution.py:171
  6.7 14.2 %all-to-all-start = ((bf16[8,144,256]{2,1,0:T(8,128)(2,1)}), bf16[8,144,256]{2,1,0:T(8,128)(2,1)S(1)}, u32[]{:S(2)}, u32[]{:S(2)}) async-start(bf16[8,144,256]{2,1,0:T(8,128)(2,1)} %shard_map.64), calls=%async_computation | async-start | bytes 1179648 | tf_op jit(solution)/shard_map/all_to_all | solution.py:194
  32.3 1.2 %collective-permute-start.1 = (f32[16,256]{1,0:T(8,128)S(1)}, f32[16,256]{1,0:T(8,128)S(1)}, u32[]{:S(2)}, u32[]{:S(2)}) collective-permute-start(f32[16,256]{1,0:T(8,128)S(1)} %convert_reduce_fusion.mine_ref), channel_id=1, source_target_pairs={{0,1},{1,0},{2,3},{3,2},{4,5},{5,4},{6,7},{7,6},{8,9},{9,8},{10,11... | collective-permute-start | bytes 49160 | tf_op jit(solution)/shard_map/ppermute | solution.py:231

commit v19 on v18

--- a/solution.py
+++ b/solution.py
@@ -8,7 +8,7 @@
 from jax.sharding import PartitionSpec as P
 
 RAY_DEV = 16
-META_ROWS = 16
+META_ROWS = 8
 RAY_BASE = 32
 LANES = 128
 LINE_CHUNKS = 4

time: 35 us -> 34.6 us (0.989)
  transfers between devices with their start and end apart: 3 -> 3, of which waited for: 2 -> 2; matrix products, arithmetic and copies ran while one was open for 0% -> 0% of each run, Pallas kernels for 12% -> 13%
where the time goes in v19:
time: 34.6 us; the launch traced here: 34.4 us
  blocking collectives  10.4 us (30%)
  starting transfers between devices  8.86 us (26%)
  waiting for transfers between devices  8.6 us (25%)
  Pallas kernels  6.42 us (19%)
    all_to_all x1, blocking collectives, per_device(): lax.all_to_all(partial_sums.reshape(bin_total, ray_rows, levels), 'bin',...  10.4 us
    all_to_all x1, waiting for transfers between devices, per_device(): lax.all_to_all(outgoing, 'bin', split_axis=0, concat_axis=0, tiled=True,...  7.43 us
    all_to_all x1, starting transfers between devices, per_device(): lax.all_to_all(outgoing, 'bin', split_axis=0, concat_axis=0, tiled=True,...  4.76 us
    ppermute x1, starting transfers between devices, per_device(): arrived = lax.ppermute(rate_tables[0], 'bin', plan.table_moves())  4.04 us
    pallas_call x1, Pallas kernels, per_device(): pl.pallas_call(functools.partial(pack_kernel, plan), out_shape=jax.ShapeD...  2.63 us
    pallas_call x1, Pallas kernels, per_device(): pl.pallas_call(window_kernel, out_shape=[jax.ShapeDtypeStruct(a, BF16) fo...  1.69 us
    ppermute x1, waiting for transfers between devices, per_device(): lax.ppermute(total, 'wave', [(i, i ^ step) for i in range(wave_total)])  1.17 us
    pallas_call x1, Pallas kernels, per_device(): pl.pallas_call(line_kernel, out_shape=jax.ShapeDtypeStruct(out_shape, F32...  1.13 us
  transfers between devices with their start and end apart: 3, of which 2 were waited for; matrix products, arithmetic and copies ran while one was open for 0% of the time, Pallas kernels for 13%

profile of v19, /device:TPU:0, one launch (start us, length us, event | category | flops | bytes accessed | tf_op | source)
XLA Modules:
  0.0 34.4 jit_solution(14546009513835936751)
XLA Ops:
  0.0 4.0 %collective-permute-start = (bf16[256,256]{1,0:T(8,128)(2,1)}, bf16[256,256]{1,0:T(8,128)(2,1)S(1)}, u32[]{:S(2)}, u32[]{:S(2)}) collective-permute-start(bf16[256,256]{1,0:T(8,128)(2,1)} %bitcast.10), channel_id=1, source_target_pairs={{0,16},{2,18},{4,20},{6,22},{8,24},{10,26},{12,28},{14,30},{16,0},... | collective-permute-start | bytes 393224 | tf_op jit(solution)/shard_map/ppermute | solution.py:171
  4.0 2.6 %shard_map.64 = bf16[8,136,256]{2,1,0:T(8,128)(2,1)} custom-call(s32[1]{0:T(128)} %bitcast.me_ref, bf16[512,256]{1,0:T(8,128)(2,1)} %src_hbm.1, bf16[4,128]{1,0:T(4,128)(2,1)} %bitcast.9, s32[1,512]{1,0:T(1,128)} %bitcast.7, s32[1,512]{1,0:T(1,128)} %bitcast.8), custom_call_target="tpu_custom_call" | custom-call | tf_op jit(solution)/shard_map/pallas_call | solution.py:174
  6.7 4.8 %all-to-all-start = ((bf16[8,136,256]{2,1,0:T(8,128)(2,1)}), bf16[8,136,256]{2,1,0:T(8,128)(2,1)S(1)}, u32[]{:S(2)}, u32[]{:S(2)}) async-start(bf16[8,136,256]{2,1,0:T(8,128)(2,1)} %shard_map.64), calls=%async_computation | async-start | bytes 1114112 | tf_op jit(solution)/shard_map/all_to_all | solution.py:194
  11.4 0.0 collective-permute-done.arrived_ref
  11.4 1.7 %shard_map.65 = (bf16[2,256,512]{2,1,0:T(8,128)(2,1)S(1)}, bf16[256,4096]{1,0:T(8,128)(2,1)S(1)}) custom-call(bf16[256,256]{1,0:T(8,128)(2,1)S(1)} %collective-permute-done.arrived_ref, bf16[256,256]{1,0:T(8,128)(2,1)} %bitcast.11, bf16[256,4096]{1,0:T(8,128)(2,1)} %line_hbm.1), custom_call_target="tpu_custom_call" | custom-call | flops 10000000000 | bytes 262144 | tf_op jit(solution)/shard_map/pallas_call | solution.py:197
  13.1 7.4 %all-to-all-done.got_ref = bf16[8,136,256]{2,1,0:T(8,128)(2,1)S(1)} async-done(((bf16[8,136,256]{2,1,0:T(8,128)(2,1)}), bf16[8,136,256]{2,1,0:T(8,128)(2,1)S(1)}, u32[]{:S(2)}, u32[]{:S(2)}) %all-to-all-start) | async-done | bytes 557088 | tf_op jit(solution)/shard_map/all_to_all | solution.py:194
  20.6 1.0 %shard_map.66 = bf16[256,256]{1,0:T(8,128)(2,1)S(1)} custom-call(bf16[8,136,256]{2,1,0:T(8,128)(2,1)S(1)} %all-to-all-done.got_ref, bf16[2,256,512]{2,1,0:T(8,128)(2,1)S(1)} %get-tuple-element.7.powers_ref), custom_call_target="tpu_custom_call" | custom-call | tf_op jit(solution)/shard_map/pallas_call | solution.py:212
  21.5 10.4 %all_to_all.10 = bf16[16,16,256]{2,1,0:T(8,128)(2,1)S(1)} all-to-all(bf16[16,16,256]{2,1,0:T(8,128)(2,1)S(1)} %bitcast.6), channel_id=1, replica_groups=mesh['bin'=16,'wave'=2] {'bin'}, dimensions={0} | all-to-all | bytes 262144 | tf_op jit(solution)/shard_map/all_to_all | solution.py:219
  32.0 0.1 collective-permute-start.1
  32.1 1.2 %collective-permute-done.1.theirs_ref = f32[16,256]{1,0:T(8,128)S(1)} collective-permute-done((f32[16,256]{1,0:T(8,128)S(1)}, f32[16,256]{1,0:T(8,128)S(1)}, u32[]{:S(2)}, u32[]{:S(2)}) %collective-permute-start.1) | collective-permute-done | bytes 16416 | tf_op jit(solution)/shard_map/ppermute | solution.py:231
  33.2 1.1 %shard_map.67 = f32[16,4096]{1,0:T(8,128)} custom-call(f32[16,256]{1,0:T(8,128)S(1)} %convert_reduce_fusion.mine_ref, f32[16,256]{1,0:T(8,128)S(1)} %collective-permute-done.1.theirs_ref, bf16[256,4096]{1,0:T(8,128)(2,1)S(1)} %get-tuple-element.8.line_ref), custom_call_target="tpu_custom_call" | custom-call | tf_op jit(solution)/shard_map/pallas_call | solution.py:234
  (1 shorter events, 0.0 us)
Async XLA Ops:
  0.0 11.4 %collective-permute-start = (bf16[256,256]{1,0:T(8,128)(2,1)}, bf16[256,256]{1,0:T(8,128)(2,1)S(1)}, u32[]{:S(2)}, u32[]{:S(2)}) collective-permute-start(bf16[256,256]{1,0:T(8,128)(2,1)} %bitcast.10), channel_id=1, source_target_pairs={{0,16},{2,18},{4,20},{6,22},{8,24},{10,26},{12,28},{14,30},{16,0},... | collective-permute-start | bytes 393224 | tf_op jit(solution)/shard_map/ppermute | solution.py:171
  6.7 13.9 %all-to-all-start = ((bf16[8,136,256]{2,1,0:T(8,128)(2,1)}), bf16[8,136,256]{2,1,0:T(8,128)(2,1)S(1)}, u32[]{:S(2)}, u32[]{:S(2)}) async-start(bf16[8,136,256]{2,1,0:T(8,128)(2,1)} %shard_map.64), calls=%async_computation | async-start | bytes 1114112 | tf_op jit(solution)/shard_map/all_to_all | solution.py:194
  32.0 1.2 %collective-permute-start.1 = (f32[16,256]{1,0:T(8,128)S(1)}, f32[16,256]{1,0:T(8,128)S(1)}, u32[]{:S(2)}, u32[]{:S(2)}) collective-permute-start(f32[16,256]{1,0:T(8,128)S(1)} %convert_reduce_fusion.mine_ref), channel_id=1, source_target_pairs={{0,1},{1,0},{2,3},{3,2},{4,5},{5,4},{6,7},{7,6},{8,9},{9,8},{10,11... | collective-permute-start | bytes 49160 | tf_op jit(solution)/shard_map/ppermute | solution.py:231

commit v20 on v19

--- a/solution.py
+++ b/solution.py
@@ -63,7 +63,8 @@
         sofar = sofar + jnp.sum(part, axis=1, keepdims=True)
     position = jnp.concatenate(places, axis=1).astype(I32)
     half = bins // targets
-    slot = (bins - half * targets) * block + (half ^ my_half) * plan.capacity + position
+    target = bins - half * targets
+    within = (half ^ my_half) * plan.capacity + position
     rays = ray_ref[...]
     ray_high = rays // RAY_BASE
     ray_low = rays - ray_high * RAY_BASE
@@ -73,51 +74,52 @@
         [den_row, ray_high.astype(F32), ray_low.astype(F32), jnp.zeros((META_ROWS - 3, cells), F32)],
         axis=0,
     ).astype(BF16)
-    place = (iota((targets * block, cells), 0) == slot).astype(F32).astype(BF16)
-    moved = nt_dot(meta, place).astype(BF16)
+    base = (iota((block, cells), 0) == within).astype(F32).astype(BF16)
+    masks = [(target == t).astype(F32).astype(BF16) for t in range(targets)]
+    place = jnp.concatenate([base * mask for mask in masks], axis=0)
+    moved = nt_dot(jnp.concatenate([meta * mask for mask in masks], axis=0), base).astype(BF16)
     copies[3].wait()
     rows = jnp.dot(place, src_ref[...], preferred_element_type=F32).astype(BF16)
     out[:, :block, :] = rows.reshape(targets, block, levels)
     out[:, block:, :] = jnp.zeros((targets, META_ROWS, levels), BF16)
     for t in range(targets):
-        out[t, block:, :block] = moved[:, t * block : (t + 1) * block]
+        out[t, block:, :block] = moved[t * META_ROWS : (t + 1) * META_ROWS]
 
 
 def window_kernel(arrived_ref, table_hbm, line_hbm, powers_ref, line_ref, sems):
     levels = arrived_ref.shape[0]
     copies = [
-        pltpu.make_async_copy(table_hbm, powers_ref.at[0, :, pl.ds(0, levels)], sems.at[0]),
+        pltpu.make_async_copy(table_hbm, powers_ref.at[0, pl.ds(0, levels)], sems.at[0]),
         pltpu.make_async_copy(line_hbm, line_ref, sems.at[1]),
     ]
     for copy in copies:
         copy.start()
-    powers_ref[1, :, :levels] = arrived_ref[...]
+    powers_ref[1, :levels] = arrived_ref[...]
     copies[0].wait()
     for part in range(2):
-        table = powers_ref[part, :, :levels]
+        table = powers_ref[part, :levels]
         square = jnp.dot(table, table, preferred_element_type=F32)
-        powers_ref[part, :, levels:] = square.astype(BF16)
+        powers_ref[part, levels:] = square.astype(BF16)
     copies[1].wait()
 
 
 def level_kernel(plan, rays, got_ref, powers_ref, out_ref):
-    targets, block = plan.targets, plan.block
+    targets, block, levels = plan.targets, plan.block, got_ref.shape[2]
     meta = [got_ref[s, block:, :block].astype(F32) for s in range(targets)]
-    columns = [jnp.transpose(m[:8]) for m in meta]
-    total = jnp.zeros(out_ref.shape, F32)
-    levels = got_ref.shape[2]
+    total = jnp.zeros((rays, levels), F32)
     for part in range(2):
         low, high = part * plan.capacity, (part + 1) * plan.capacity
-        src = got_ref[:, low:high, :].reshape(targets * plan.capacity, got_ref.shape[2])
-        den = jnp.concatenate([c[low:high, 0:1] for c in columns], axis=0)
-        ray = jnp.concatenate(
-            [m[1:2, low:high] * RAY_BASE + m[2:3, low:high] for m in meta], axis=1
-        ).astype(I32)
-        wide = src.astype(F32)
-        steps = jnp.dot(src, powers_ref[part], preferred_element_type=F32)
-        pops = (wide + den * (steps[:, :levels] + den * steps[:, levels:])).astype(BF16)
+        src = got_ref[:, low:high, :].reshape(targets * plan.capacity, levels)
+        rows = jnp.concatenate([m[:, low:high] for m in meta], axis=1)
+        den = rows[0:1].astype(BF16)
+        ray = (rows[1:2] * RAY_BASE + rows[2:3]).astype(I32)
         pick = (iota((rays, src.shape[0]), 0) == ray).astype(F32).astype(BF16)
-        total = total + jnp.dot(pick, pops, preferred_element_type=F32)
+        once = pick * den
+        weights = jnp.concatenate([pick, once, once * den], axis=0)
+        sums = jnp.dot(weights, src, preferred_element_type=F32)
+        powers = jnp.concatenate([sums[rays : 2 * rays], sums[2 * rays :]], axis=1).astype(BF16)
+        steps = jnp.dot(powers, powers_ref[part], preferred_element_type=F32)
+        total = total + sums[:rays] + steps
     out_ref[...] = total.astype(BF16)
 
 
@@ -197,7 +199,7 @@
     powers, held_line = pl.pallas_call(
         window_kernel,
         out_shape=[
-            jax.ShapeDtypeStruct(a, BF16) for a in ((2, levels, 2 * levels), line_table.shape)
+            jax.ShapeDtypeStruct(a, BF16) for a in ((2, 2 * levels, levels), line_table.shape)
         ],
         in_specs=[vmem, hbm, hbm],
         out_specs=[vmem] * 2,

time: 34.6 us -> 34.8 us (level)
  transfers between devices with their start and end apart: 3 -> 3, of which waited for: 2 -> 2; matrix products, arithmetic and copies ran while one was open for 0% -> 0% of each run, Pallas kernels for 13% -> 12%
where the time goes in v20:
time: 34.8 us; the launch traced here: 34.5 us
  blocking collectives  10.6 us (30%)
  starting transfers between devices  8.86 us (25%)
  waiting for transfers between devices  8.61 us (25%)
  Pallas kernels  6.35 us (18%)
    all_to_all x1, blocking collectives, per_device(): lax.all_to_all(partial_sums.reshape(bin_total, ray_rows, levels), 'bin',...  10.6 us
    all_to_all x1, waiting for transfers between devices, per_device(): lax.all_to_all(outgoing, 'bin', split_axis=0, concat_axis=0, tiled=True,...  7.44 us
    all_to_all x1, starting transfers between devices, per_device(): lax.all_to_all(outgoing, 'bin', split_axis=0, concat_axis=0, tiled=True,...  4.75 us
    ppermute x1, starting transfers between devices, per_device(): arrived = lax.ppermute(rate_tables[0], 'bin', plan.table_moves())  4.04 us
    pallas_call x1, Pallas kernels, per_device(): pl.pallas_call(functools.partial(pack_kernel, plan), out_shape=jax.ShapeD...  2.36 us
    pallas_call x1, Pallas kernels, per_device(): pl.pallas_call(window_kernel, out_shape=[jax.ShapeDtypeStruct(a, BF16) fo...  1.69 us
    pallas_call x1, Pallas kernels, per_device(): pl.pallas_call(functools.partial(level_kernel, plan, rays), out_shape=jax...  1.17 us
    ppermute x1, waiting for transfers between devices, per_device(): lax.ppermute(total, 'wave', [(i, i ^ step) for i in range(wave_total)])  1.17 us
  transfers between devices with their start and end apart: 3, of which 2 were waited for; matrix products, arithmetic and copies ran while one was open for 0% of the time, Pallas kernels for 12%

profile of v20, /device:TPU:0, one launch (start us, length us, event | category | flops | bytes accessed | tf_op | source)
XLA Modules:
  0.0 34.5 jit_solution(18342585449499432071)
XLA Ops:
  0.0 4.0 %collective-permute-start = (bf16[256,256]{1,0:T(8,128)(2,1)}, bf16[256,256]{1,0:T(8,128)(2,1)S(1)}, u32[]{:S(2)}, u32[]{:S(2)}) collective-permute-start(bf16[256,256]{1,0:T(8,128)(2,1)} %bitcast.10), channel_id=1, source_target_pairs={{0,16},{2,18},{4,20},{6,22},{8,24},{10,26},{12,28},{14,30},{16,0},... | collective-permute-start | bytes 393224 | tf_op jit(solution)/shard_map/ppermute | solution.py:173
  4.0 2.4 %shard_map.64 = bf16[8,136,256]{2,1,0:T(8,128)(2,1)} custom-call(s32[1]{0:T(128)} %bitcast.me_ref, bf16[512,256]{1,0:T(8,128)(2,1)} %src_hbm.1, bf16[4,128]{1,0:T(4,128)(2,1)} %bitcast.9, s32[1,512]{1,0:T(1,128)} %bitcast.7, s32[1,512]{1,0:T(1,128)} %bitcast.8), custom_call_target="tpu_custom_call" | custom-call | tf_op jit(solution)/shard_map/pallas_call | solution.py:176
  6.4 4.7 %all-to-all-start = ((bf16[8,136,256]{2,1,0:T(8,128)(2,1)}), bf16[8,136,256]{2,1,0:T(8,128)(2,1)S(1)}, u32[]{:S(2)}, u32[]{:S(2)}) async-start(bf16[8,136,256]{2,1,0:T(8,128)(2,1)} %shard_map.64), calls=%async_computation | async-start | bytes 1114112 | tf_op jit(solution)/shard_map/all_to_all | solution.py:196
  11.2 0.0 collective-permute-done.arrived_ref
  11.2 1.7 %shard_map.65 = (bf16[2,512,256]{2,1,0:T(8,128)(2,1)S(1)}, bf16[256,4096]{1,0:T(8,128)(2,1)S(1)}) custom-call(bf16[256,256]{1,0:T(8,128)(2,1)S(1)} %collective-permute-done.arrived_ref, bf16[256,256]{1,0:T(8,128)(2,1)} %bitcast.11, bf16[256,4096]{1,0:T(8,128)(2,1)} %line_hbm.1), custom_call_target="tpu_custom_call" | custom-call | flops 10000000000 | bytes 262144 | tf_op jit(solution)/shard_map/pallas_call | solution.py:199
  12.9 7.4 %all-to-all-done.got_ref = bf16[8,136,256]{2,1,0:T(8,128)(2,1)S(1)} async-done(((bf16[8,136,256]{2,1,0:T(8,128)(2,1)}), bf16[8,136,256]{2,1,0:T(8,128)(2,1)S(1)}, u32[]{:S(2)}, u32[]{:S(2)}) %all-to-all-start) | async-done | bytes 557088 | tf_op jit(solution)/shard_map/all_to_all | solution.py:196
  20.3 1.2 %shard_map.66 = bf16[256,256]{1,0:T(8,128)(2,1)S(1)} custom-call(bf16[8,136,256]{2,1,0:T(8,128)(2,1)S(1)} %all-to-all-done.got_ref, bf16[2,512,256]{2,1,0:T(8,128)(2,1)S(1)} %get-tuple-element.7.powers_ref), custom_call_target="tpu_custom_call" | custom-call | tf_op jit(solution)/shard_map/pallas_call | solution.py:214
  21.5 10.6 %all_to_all.10 = bf16[16,16,256]{2,1,0:T(8,128)(2,1)S(1)} all-to-all(bf16[16,16,256]{2,1,0:T(8,128)(2,1)S(1)} %bitcast.6), channel_id=1, replica_groups=mesh['bin'=16,'wave'=2] {'bin'}, dimensions={0} | all-to-all | bytes 262144 | tf_op jit(solution)/shard_map/all_to_all | solution.py:221
  32.1 0.1 collective-permute-start.1
  32.2 1.2 %collective-permute-done.1.theirs_ref = f32[16,256]{1,0:T(8,128)S(1)} collective-permute-done((f32[16,256]{1,0:T(8,128)S(1)}, f32[16,256]{1,0:T(8,128)S(1)}, u32[]{:S(2)}, u32[]{:S(2)}) %collective-permute-start.1) | collective-permute-done | bytes 16416 | tf_op jit(solution)/shard_map/ppermute | solution.py:233
  33.4 1.1 %shard_map.67 = f32[16,4096]{1,0:T(8,128)} custom-call(f32[16,256]{1,0:T(8,128)S(1)} %convert_reduce_fusion.mine_ref, f32[16,256]{1,0:T(8,128)S(1)} %collective-permute-done.1.theirs_ref, bf16[256,4096]{1,0:T(8,128)(2,1)S(1)} %get-tuple-element.8.line_ref), custom_call_target="tpu_custom_call" | custom-call | tf_op jit(solution)/shard_map/pallas_call | solution.py:236
  (1 shorter events, 0.0 us)
Async XLA Ops:
  0.0 11.2 %collective-permute-start = (bf16[256,256]{1,0:T(8,128)(2,1)}, bf16[256,256]{1,0:T(8,128)(2,1)S(1)}, u32[]{:S(2)}, u32[]{:S(2)}) collective-permute-start(bf16[256,256]{1,0:T(8,128)(2,1)} %bitcast.10), channel_id=1, source_target_pairs={{0,16},{2,18},{4,20},{6,22},{8,24},{10,26},{12,28},{14,30},{16,0},... | collective-permute-start | bytes 393224 | tf_op jit(solution)/shard_map/ppermute | solution.py:173
  6.4 13.9 %all-to-all-start = ((bf16[8,136,256]{2,1,0:T(8,128)(2,1)}), bf16[8,136,256]{2,1,0:T(8,128)(2,1)S(1)}, u32[]{:S(2)}, u32[]{:S(2)}) async-start(bf16[8,136,256]{2,1,0:T(8,128)(2,1)} %shard_map.64), calls=%async_computation | async-start | bytes 1114112 | tf_op jit(solution)/shard_map/all_to_all | solution.py:196
  32.1 1.2 %collective-permute-start.1 = (f32[16,256]{1,0:T(8,128)S(1)}, f32[16,256]{1,0:T(8,128)S(1)}, u32[]{:S(2)}, u32[]{:S(2)}) collective-permute-start(f32[16,256]{1,0:T(8,128)S(1)} %convert_reduce_fusion.mine_ref), channel_id=1, source_target_pairs={{0,1},{1,0},{2,3},{3,2},{4,5},{5,4},{6,7},{7,6},{8,9},{9,8},{10,11... | collective-permute-start | bytes 49160 | tf_op jit(solution)/shard_map/ppermute | solution.py:233

commit v21 on v19

--- a/solution.py
+++ b/solution.py
@@ -63,7 +63,8 @@
         sofar = sofar + jnp.sum(part, axis=1, keepdims=True)
     position = jnp.concatenate(places, axis=1).astype(I32)
     half = bins // targets
-    slot = (bins - half * targets) * block + (half ^ my_half) * plan.capacity + position
+    target = bins - half * targets
+    within = (half ^ my_half) * plan.capacity + position
     rays = ray_ref[...]
     ray_high = rays // RAY_BASE
     ray_low = rays - ray_high * RAY_BASE
@@ -73,14 +74,16 @@
         [den_row, ray_high.astype(F32), ray_low.astype(F32), jnp.zeros((META_ROWS - 3, cells), F32)],
         axis=0,
     ).astype(BF16)
-    place = (iota((targets * block, cells), 0) == slot).astype(F32).astype(BF16)
-    moved = nt_dot(meta, place).astype(BF16)
+    base = (iota((block, cells), 0) == within).astype(F32).astype(BF16)
+    masks = [(target == t).astype(F32).astype(BF16) for t in range(targets)]
+    place = jnp.concatenate([base * mask for mask in masks], axis=0)
+    moved = nt_dot(jnp.concatenate([meta * mask for mask in masks], axis=0), base).astype(BF16)
     copies[3].wait()
     rows = jnp.dot(place, src_ref[...], preferred_element_type=F32).astype(BF16)
     out[:, :block, :] = rows.reshape(targets, block, levels)
     out[:, block:, :] = jnp.zeros((targets, META_ROWS, levels), BF16)
     for t in range(targets):
-        out[t, block:, :block] = moved[:, t * block : (t + 1) * block]
+        out[t, block:, :block] = moved[t * META_ROWS : (t + 1) * META_ROWS]
 
 
 def window_kernel(arrived_ref, table_hbm, line_hbm, powers_ref, line_ref, sems):

time: 34.6 us -> 34.6 us (level)
  transfers between devices with their start and end apart: 3 -> 3, of which waited for: 2 -> 2; matrix products, arithmetic and copies ran while one was open for 0% -> 0% of each run, Pallas kernels for 13% -> 12%
where the time goes in v21:
time: 34.6 us; the launch traced here: 34.3 us
  blocking collectives  10.6 us (31%)
  starting transfers between devices  8.86 us (26%)
  waiting for transfers between devices  8.61 us (25%)
  Pallas kernels  6.15 us (18%)
    all_to_all x1, blocking collectives, per_device(): lax.all_to_all(partial_sums.reshape(bin_total, ray_rows, levels), 'bin',...  10.6 us
    all_to_all x1, waiting for transfers between devices, per_device(): lax.all_to_all(outgoing, 'bin', split_axis=0, concat_axis=0, tiled=True,...  7.44 us
    all_to_all x1, starting transfers between devices, per_device(): lax.all_to_all(outgoing, 'bin', split_axis=0, concat_axis=0, tiled=True,...  4.75 us
    ppermute x1, starting transfers between devices, per_device(): arrived = lax.ppermute(rate_tables[0], 'bin', plan.table_moves())  4.04 us
    pallas_call x1, Pallas kernels, per_device(): pl.pallas_call(functools.partial(pack_kernel, plan), out_shape=jax.ShapeD...  2.36 us
    pallas_call x1, Pallas kernels, per_device(): pl.pallas_call(window_kernel, out_shape=[jax.ShapeDtypeStruct(a, BF16) fo...  1.69 us
    ppermute x1, waiting for transfers between devices, per_device(): lax.ppermute(total, 'wave', [(i, i ^ step) for i in range(wave_total)])  1.17 us
    pallas_call x1, Pallas kernels, per_device(): pl.pallas_call(line_kernel, out_shape=jax.ShapeDtypeStruct(out_shape, F32...  1.13 us
  transfers between devices with their start and end apart: 3, of which 2 were waited for; matrix products, arithmetic and copies ran while one was open for 0% of the time, Pallas kernels for 12%

profile of v21, /device:TPU:0, one launch (start us, length us, event | category | flops | bytes accessed | tf_op | source)
XLA Modules:
  0.0 34.3 jit_solution(18184733421618154485)
XLA Ops:
  0.0 4.0 %collective-permute-start = (bf16[256,256]{1,0:T(8,128)(2,1)}, bf16[256,256]{1,0:T(8,128)(2,1)S(1)}, u32[]{:S(2)}, u32[]{:S(2)}) collective-permute-start(bf16[256,256]{1,0:T(8,128)(2,1)} %bitcast.10), channel_id=1, source_target_pairs={{0,16},{2,18},{4,20},{6,22},{8,24},{10,26},{12,28},{14,30},{16,0},... | collective-permute-start | bytes 393224 | tf_op jit(solution)/shard_map/ppermute | solution.py:174
  4.0 2.4 %shard_map.64 = bf16[8,136,256]{2,1,0:T(8,128)(2,1)} custom-call(s32[1]{0:T(128)} %bitcast.me_ref, bf16[512,256]{1,0:T(8,128)(2,1)} %src_hbm.1, bf16[4,128]{1,0:T(4,128)(2,1)} %bitcast.9, s32[1,512]{1,0:T(1,128)} %bitcast.7, s32[1,512]{1,0:T(1,128)} %bitcast.8), custom_call_target="tpu_custom_call" | custom-call | tf_op jit(solution)/shard_map/pallas_call | solution.py:177
  6.4 4.7 %all-to-all-start = ((bf16[8,136,256]{2,1,0:T(8,128)(2,1)}), bf16[8,136,256]{2,1,0:T(8,128)(2,1)S(1)}, u32[]{:S(2)}, u32[]{:S(2)}) async-start(bf16[8,136,256]{2,1,0:T(8,128)(2,1)} %shard_map.64), calls=%async_computation | async-start | bytes 1114112 | tf_op jit(solution)/shard_map/all_to_all | solution.py:197
  11.2 0.0 collective-permute-done.arrived_ref
  11.2 1.7 %shard_map.65 = (bf16[2,256,512]{2,1,0:T(8,128)(2,1)S(1)}, bf16[256,4096]{1,0:T(8,128)(2,1)S(1)}) custom-call(bf16[256,256]{1,0:T(8,128)(2,1)S(1)} %collective-permute-done.arrived_ref, bf16[256,256]{1,0:T(8,128)(2,1)} %bitcast.11, bf16[256,4096]{1,0:T(8,128)(2,1)} %line_hbm.1), custom_call_target="tpu_custom_call" | custom-call | flops 10000000000 | bytes 262144 | tf_op jit(solution)/shard_map/pallas_call | solution.py:200
  12.9 7.4 %all-to-all-done.got_ref = bf16[8,136,256]{2,1,0:T(8,128)(2,1)S(1)} async-done(((bf16[8,136,256]{2,1,0:T(8,128)(2,1)}), bf16[8,136,256]{2,1,0:T(8,128)(2,1)S(1)}, u32[]{:S(2)}, u32[]{:S(2)}) %all-to-all-start) | async-done | bytes 557088 | tf_op jit(solution)/shard_map/all_to_all | solution.py:197
  20.3 1.0 %shard_map.66 = bf16[256,256]{1,0:T(8,128)(2,1)S(1)} custom-call(bf16[8,136,256]{2,1,0:T(8,128)(2,1)S(1)} %all-to-all-done.got_ref, bf16[2,256,512]{2,1,0:T(8,128)(2,1)S(1)} %get-tuple-element.7.powers_ref), custom_call_target="tpu_custom_call" | custom-call | tf_op jit(solution)/shard_map/pallas_call | solution.py:215
  21.3 10.6 %all_to_all.10 = bf16[16,16,256]{2,1,0:T(8,128)(2,1)S(1)} all-to-all(bf16[16,16,256]{2,1,0:T(8,128)(2,1)S(1)} %bitcast.6), channel_id=1, replica_groups=mesh['bin'=16,'wave'=2] {'bin'}, dimensions={0} | all-to-all | bytes 262144 | tf_op jit(solution)/shard_map/all_to_all | solution.py:222
  31.9 0.1 collective-permute-start.1
  32.0 1.2 %collective-permute-done.1.theirs_ref = f32[16,256]{1,0:T(8,128)S(1)} collective-permute-done((f32[16,256]{1,0:T(8,128)S(1)}, f32[16,256]{1,0:T(8,128)S(1)}, u32[]{:S(2)}, u32[]{:S(2)}) %collective-permute-start.1) | collective-permute-done | bytes 16416 | tf_op jit(solution)/shard_map/ppermute | solution.py:234
  33.2 1.1 %shard_map.67 = f32[16,4096]{1,0:T(8,128)} custom-call(f32[16,256]{1,0:T(8,128)S(1)} %convert_reduce_fusion.mine_ref, f32[16,256]{1,0:T(8,128)S(1)} %collective-permute-done.1.theirs_ref, bf16[256,4096]{1,0:T(8,128)(2,1)S(1)} %get-tuple-element.8.line_ref), custom_call_target="tpu_custom_call" | custom-call | tf_op jit(solution)/shard_map/pallas_call | solution.py:237
  (1 shorter events, 0.0 us)
Async XLA Ops:
  0.0 11.2 %collective-permute-start = (bf16[256,256]{1,0:T(8,128)(2,1)}, bf16[256,256]{1,0:T(8,128)(2,1)S(1)}, u32[]{:S(2)}, u32[]{:S(2)}) collective-permute-start(bf16[256,256]{1,0:T(8,128)(2,1)} %bitcast.10), channel_id=1, source_target_pairs={{0,16},{2,18},{4,20},{6,22},{8,24},{10,26},{12,28},{14,30},{16,0},... | collective-permute-start | bytes 393224 | tf_op jit(solution)/shard_map/ppermute | solution.py:174
  6.4 13.9 %all-to-all-start = ((bf16[8,136,256]{2,1,0:T(8,128)(2,1)}), bf16[8,136,256]{2,1,0:T(8,128)(2,1)S(1)}, u32[]{:S(2)}, u32[]{:S(2)}) async-start(bf16[8,136,256]{2,1,0:T(8,128)(2,1)} %shard_map.64), calls=%async_computation | async-start | bytes 1114112 | tf_op jit(solution)/shard_map/all_to_all | solution.py:197
  31.9 1.2 %collective-permute-start.1 = (f32[16,256]{1,0:T(8,128)S(1)}, f32[16,256]{1,0:T(8,128)S(1)}, u32[]{:S(2)}, u32[]{:S(2)}) collective-permute-start(f32[16,256]{1,0:T(8,128)S(1)} %convert_reduce_fusion.mine_ref), channel_id=1, source_target_pairs={{0,1},{1,0},{2,3},{3,2},{4,5},{5,4},{6,7},{7,6},{8,9},{9,8},{10,11... | collective-permute-start | bytes 49160 | tf_op jit(solution)/shard_map/ppermute | solution.py:234

commit v22 on v21

--- a/solution.py
+++ b/solution.py
@@ -12,6 +12,7 @@
 RAY_BASE = 32
 LANES = 128
 LINE_CHUNKS = 4
+LINE_PARTS = 2
 OVERLAP_FLOPS = 10**10
 VMEM_LIMIT = 32 * 1024 * 1024
 F32 = jnp.float32
@@ -27,9 +28,9 @@
     return lax.broadcasted_iota(I32, shape, dim)
 
 
-def pack_kernel(plan, me_ref, src_hbm, den_hbm, bin_hbm, ray_hbm, *rest):
+def pack_kernel(plan, me_ref, src_hbm, den_hbm, bin_hbm, ray_hbm, line_hbm, *rest):
     targets, block = plan.targets, plan.block
-    out, src_ref, den_ref, bin_ref, ray_ref, sems = rest
+    out, line_out, src_ref, den_ref, bin_ref, ray_ref, sems, line_sems = rest
     copies = [
         pltpu.make_async_copy(a, b, sems.at[i])
         for i, (a, b) in enumerate(
@@ -46,7 +47,7 @@
     cells, levels = src_ref.shape
     lanes = min(cells, LANES)
     earlier = (iota((lanes, lanes), 0) < iota((lanes, lanes), 1)).astype(F32).astype(BF16)
-    my_half = me_ref[0] // targets
+    my_half = me_ref[0] // (targets * plan.wave)
     for copy in copies[:3]:
         copy.wait()
     bins = bin_ref[...]
@@ -85,22 +86,43 @@
     for t in range(targets):
         out[t, block:, :block] = moved[t * META_ROWS : (t + 1) * META_ROWS]
 
-
-def window_kernel(arrived_ref, table_hbm, line_hbm, powers_ref, line_ref, sems):
+    @pl.when(me_ref[0] % 2 == 1)
+    def _():
+        width = line_out.shape[1] // LINE_PARTS
+        for i in range(LINE_PARTS):
+            part = pl.ds(i * width, width)
+            copy = pltpu.make_async_copy(
+                line_hbm.at[:, part], line_out.at[:, part], line_sems.at[i]
+            )
+            copy.start()
+            copy.wait()
+
+
+def window_kernel(me_ref, arrived_ref, loaded_ref, table_hbm, line_hbm, powers_ref, line_ref, sems):
     levels = arrived_ref.shape[0]
-    copies = [
-        pltpu.make_async_copy(table_hbm, powers_ref.at[0, :, pl.ds(0, levels)], sems.at[0]),
-        pltpu.make_async_copy(line_hbm, line_ref, sems.at[1]),
-    ]
-    for copy in copies:
-        copy.start()
+    even = me_ref[0] % 2 == 0
+    table_copy = pltpu.make_async_copy(table_hbm, powers_ref.at[0, :, pl.ds(0, levels)], sems.at[0])
+    line_copy = pltpu.make_async_copy(line_hbm, line_ref, sems.at[1])
+    table_copy.start()
+
+    @pl.when(even)
+    def _():
+        line_copy.start()
+
+    @pl.when(jnp.logical_not(even))
+    def _():
+        line_ref[...] = loaded_ref[...]
+
     powers_ref[1, :, :levels] = arrived_ref[...]
-    copies[0].wait()
+    table_copy.wait()
     for part in range(2):
         table = powers_ref[part, :, :levels]
         square = jnp.dot(table, table, preferred_element_type=F32)
         powers_ref[part, :, levels:] = square.astype(BF16)
-    copies[1].wait()
+
+    @pl.when(even)
+    def _():
+        line_copy.wait()
 
 
 def level_kernel(plan, rays, got_ref, powers_ref, out_ref):
@@ -144,8 +166,9 @@
 
 
 class Plan:
-    def __init__(self, bin_total, cells):
+    def __init__(self, bin_total, wave_total, cells):
         self.bins = bin_total
+        self.wave = wave_total
         self.targets = bin_total // 2
         self.capacity = max(2, 2 * cells // bin_total)
         self.block = 2 * self.capacity
@@ -161,7 +184,7 @@
     cells, levels = sources.shape
     bin_total = lax.axis_size("bin")
     wave_total = lax.axis_size("wave")
-    plan = Plan(bin_total, cells)
+    plan = Plan(bin_total, wave_total, cells)
     rows = plan.block + META_ROWS
     params = pltpu.CompilerParams(vmem_limit_bytes=VMEM_LIMIT)
     vmem = pl.BlockSpec(memory_space=pltpu.VMEM)
@@ -172,19 +195,22 @@
         return pltpu.with_memory_space_constraint(x, pltpu.HBM)
 
     arrived = lax.ppermute(rate_tables[0], "bin", plan.table_moves())
-    me = lax.axis_index("bin").astype(I32).reshape(1)
+    me = lax.axis_index(("bin", "wave")).astype(I32).reshape(1)
     den_rows = cells // min(cells, LANES)
-    outgoing = pl.pallas_call(
+    outgoing, loaded = pl.pallas_call(
         functools.partial(pack_kernel, plan),
-        out_shape=jax.ShapeDtypeStruct((plan.targets, rows, levels), BF16),
-        in_specs=[smem] + [hbm] * 4,
-        out_specs=vmem,
+        out_shape=[
+            jax.ShapeDtypeStruct(a, BF16) for a in ((plan.targets, rows, levels), line_table.shape)
+        ],
+        in_specs=[smem] + [hbm] * 5,
+        out_specs=[vmem] * 2,
         scratch_shapes=[
             pltpu.VMEM((cells, levels), BF16),
             pltpu.VMEM((den_rows, cells // den_rows), BF16),
             pltpu.VMEM((1, cells), I32),
             pltpu.VMEM((1, cells), I32),
             pltpu.SemaphoreType.DMA((4,)),
+            pltpu.SemaphoreType.DMA((LINE_PARTS,)),
         ],
         compiler_params=params,
     )(
@@ -193,6 +219,7 @@
         in_hbm(density.reshape(den_rows, cells // den_rows)),
         in_hbm(temp_bins.reshape(1, cells)),
         in_hbm(ray_index.reshape(1, cells)),
+        in_hbm(line_table),
     )
     got = lax.all_to_all(
         outgoing, "bin", split_axis=0, concat_axis=0, tiled=True, axis_index_groups=plan.halves()
@@ -202,14 +229,14 @@
         out_shape=[
             jax.ShapeDtypeStruct(a, BF16) for a in ((2, levels, 2 * levels), line_table.shape)
         ],
-        in_specs=[vmem, hbm, hbm],
+        in_specs=[smem, vmem, vmem, hbm, hbm],
         out_specs=[vmem] * 2,
         scratch_shapes=[pltpu.SemaphoreType.DMA((2,))],
         compiler_params=params,
         cost_estimate=pl.CostEstimate(
             flops=OVERLAP_FLOPS, bytes_accessed=4 * arrived.size, transcendentals=0
         ),
-    )(arrived, in_hbm(rate_tables[0]), in_hbm(line_table))
+    )(me, arrived, loaded, in_hbm(rate_tables[0]), in_hbm(line_table))
     ray_rows = RAY_DEV
     rays = ray_rows * bin_total
     partial_sums = pl.pallas_call(

time: 34.6 us -> 37.5 us (1.084)
  local copies, waits for them, and re-layouts: 0 us -> 2.92 us
  waiting for transfers between devices: 8.61 us -> 8.05 us
  blocking collectives: 10.6 us -> 11.1 us
    unnamed x0 -> x4, local copies, waits for them, and re-layouts: none -> 2.92 us
    all_to_all x1, waiting for transfers between devices: 7.44 us -> 6.88 us  [per_device(): lax.all_to_all(outgoing, 'bin', split_axis=0, concat_axis=0, tiled=True,...]
    all_to_all x1, blocking collectives: 10.6 us -> 11.1 us  [per_device(): lax.all_to_all(partial_sums.reshape(bin_total, ray_rows, levels), 'bin',...]
  transfers between devices with their start and end apart: 3 -> 3, of which waited for: 2 -> 2; matrix products, arithmetic and copies ran while one was open for 0% -> 0% of each run, Pallas kernels for 12% -> 11%
where the time goes in v22:
time: 37.5 us; the launch traced here: 37.1 us
  blocking collectives  11.1 us (30%)
  starting transfers between devices  8.84 us (24%)
  waiting for transfers between devices  8.05 us (21%)
  Pallas kernels  6.17 us (16%)
  local copies, waits for them, and re-layouts  2.92 us (8%)
    all_to_all x1, blocking collectives, per_device(): lax.all_to_all(partial_sums.reshape(bin_total, ray_rows, levels), 'bin',...  11.1 us
    all_to_all x1, waiting for transfers between devices, per_device(): lax.all_to_all(outgoing, 'bin', split_axis=0, concat_axis=0, tiled=True,...  6.88 us
    all_to_all x1, starting transfers between devices, per_device(): lax.all_to_all(outgoing, 'bin', split_axis=0, concat_axis=0, tiled=True,...  4.74 us
    ppermute x1, starting transfers between devices, per_device(): arrived = lax.ppermute(rate_tables[0], 'bin', plan.table_moves())  4.04 us
    unnamed x4, local copies, waits for them, and re-layouts  2.92 us
    pallas_call x1, Pallas kernels, per_device(): pl.pallas_call(functools.partial(pack_kernel, plan), out_shape=[jax.Shape...  2.39 us
    pallas_call x1, Pallas kernels, per_device(): pl.pallas_call(window_kernel, out_shape=[jax.ShapeDtypeStruct(a, BF16) fo...  1.69 us
    ppermute x1, waiting for transfers between devices, per_device(): lax.ppermute(total, 'wave', [(i, i ^ step) for i in range(wave_total)])  1.17 us
  transfers between devices with their start and end apart: 3, of which 2 were waited for; matrix products, arithmetic and copies ran while one was open for 0% of the time, Pallas kernels for 11%

profile of v22, /device:TPU:0, one launch (start us, length us, event | category | flops | bytes accessed | tf_op | source)
XLA Modules:
  0.0 37.1 jit_solution(8231751210622635547)
XLA Ops:
  0.0 4.0 %collective-permute-start = (bf16[256,256]{1,0:T(8,128)(2,1)}, bf16[256,256]{1,0:T(8,128)(2,1)S(1)}, u32[]{:S(2)}, u32[]{:S(2)}) collective-permute-start(bf16[256,256]{1,0:T(8,128)(2,1)} %bitcast.10), channel_id=1, source_target_pairs={{0,16},{2,18},{4,20},{6,22},{8,24},{10,26},{12,28},{14,30},{16,0},... | collective-permute-start | bytes 393224 | tf_op jit(solution)/shard_map/ppermute | solution.py:197
  4.0 2.4 %shard_map.64 = (bf16[8,136,256]{2,1,0:T(8,128)(2,1)}, bf16[256,4096]{1,0:T(8,128)(2,1)S(1)}) custom-call(s32[1]{0:T(128)} %bitcast.me_ref, bf16[512,256]{1,0:T(8,128)(2,1)} %src_hbm.1, bf16[4,128]{1,0:T(4,128)(2,1)} %bitcast.9, s32[1,512]{1,0:T(1,128)} %bitcast.7, s32[1,512]{1,0:T(1,128)} %bitcast.8, bf16[256,4096]{1,0:T(8,128)(2,1)} %line_hbm.3), custom_call_target="tpu_custom_call" | custom-call | tf_op jit(solution)/shard_map/pallas_call | solution.py:200
  6.4 0.0 copy-start
  6.4 1.3 %copy-done = bf16[256,4096]{1,0:T(8,128)(2,1)} copy-done((bf16[256,4096]{1,0:T(8,128)(2,1)}, bf16[256,4096]{1,0:T(8,128)(2,1)S(1)}, u32[]{:S(2)}) %copy-start) | copy-done | bytes 2097176
  7.8 4.7 %all-to-all-start = ((bf16[8,136,256]{2,1,0:T(8,128)(2,1)}), bf16[8,136,256]{2,1,0:T(8,128)(2,1)S(1)}, u32[]{:S(2)}, u32[]{:S(2)}) async-start(bf16[8,136,256]{2,1,0:T(8,128)(2,1)} %get-tuple-element.9), calls=%async_computation | async-start | bytes 1114112 | tf_op jit(solution)/shard_map/all_to_all | solution.py:224
  12.5 0.0 collective-permute-done.arrived_ref
  12.5 0.0 copy-start.1
  12.5 1.6 %copy-done.1 = bf16[256,4096]{1,0:T(8,128)(2,1)S(1)} copy-done((bf16[256,4096]{1,0:T(8,128)(2,1)S(1)}, bf16[256,4096]{1,0:T(8,128)(2,1)}, u32[]{:S(2)}) %copy-start.1) | copy-done | bytes 2097176
  14.1 1.7 %shard_map.65 = (bf16[2,256,512]{2,1,0:T(8,128)(2,1)S(1)}, bf16[256,4096]{1,0:T(8,128)(2,1)S(1)}) custom-call(s32[1]{0:T(128)} %bitcast.me_ref, bf16[256,256]{1,0:T(8,128)(2,1)S(1)} %collective-permute-done.arrived_ref, bf16[256,4096]{1,0:T(8,128)(2,1)S(1)} %copy-done.1, bf16[256,256]{1,0:T(8,128)(2,1)} %bitcast.11, bf16[256,4096]{1,0:T(8,128)(2,1)} %line_hbm.3), custom_call_target="tpu_custom_call" | custom-call | flops 10000000000 | bytes 262144 | tf_op jit(solution)/shard_map/pallas_call | solution.py:227
  15.8 6.9 %all-to-all-done.got_ref = bf16[8,136,256]{2,1,0:T(8,128)(2,1)S(1)} async-done(((bf16[8,136,256]{2,1,0:T(8,128)(2,1)}), bf16[8,136,256]{2,1,0:T(8,128)(2,1)S(1)}, u32[]{:S(2)}, u32[]{:S(2)}) %all-to-all-start) | async-done | bytes 557088 | tf_op jit(solution)/shard_map/all_to_all | solution.py:224
  22.7 1.0 %shard_map.66 = bf16[256,256]{1,0:T(8,128)(2,1)S(1)} custom-call(bf16[8,136,256]{2,1,0:T(8,128)(2,1)S(1)} %all-to-all-done.got_ref, bf16[2,256,512]{2,1,0:T(8,128)(2,1)S(1)} %get-tuple-element.11.powers_ref), custom_call_target="tpu_custom_call" | custom-call | tf_op jit(solution)/shard_map/pallas_call | solution.py:242
  23.7 11.1 %all_to_all.10 = bf16[16,16,256]{2,1,0:T(8,128)(2,1)S(1)} all-to-all(bf16[16,16,256]{2,1,0:T(8,128)(2,1)S(1)} %bitcast.6), channel_id=1, replica_groups=mesh['bin'=16,'wave'=2] {'bin'}, dimensions={0} | all-to-all | bytes 262144 | tf_op jit(solution)/shard_map/all_to_all | solution.py:249
  34.8 0.1 collective-permute-start.1
  34.8 1.2 %collective-permute-done.1.theirs_ref = f32[16,256]{1,0:T(8,128)S(1)} collective-permute-done((f32[16,256]{1,0:T(8,128)S(1)}, f32[16,256]{1,0:T(8,128)S(1)}, u32[]{:S(2)}, u32[]{:S(2)}) %collective-permute-start.1) | collective-permute-done | bytes 16416 | tf_op jit(solution)/shard_map/ppermute | solution.py:261
  36.0 1.1 %shard_map.67 = f32[16,4096]{1,0:T(8,128)} custom-call(f32[16,256]{1,0:T(8,128)S(1)} %convert_reduce_fusion.mine_ref, f32[16,256]{1,0:T(8,128)S(1)} %collective-permute-done.1.theirs_ref, bf16[256,4096]{1,0:T(8,128)(2,1)S(1)} %get-tuple-element.12.line_ref), custom_call_target="tpu_custom_call" | custom-call | tf_op jit(solution)/shard_map/pallas_call | solution.py:264
  (1 shorter events, 0.0 us)
Async XLA Ops:
  0.0 12.5 %collective-permute-start = (bf16[256,256]{1,0:T(8,128)(2,1)}, bf16[256,256]{1,0:T(8,128)(2,1)S(1)}, u32[]{:S(2)}, u32[]{:S(2)}) collective-permute-start(bf16[256,256]{1,0:T(8,128)(2,1)} %bitcast.10), channel_id=1, source_target_pairs={{0,16},{2,18},{4,20},{6,22},{8,24},{10,26},{12,28},{14,30},{16,0},... | collective-permute-start | bytes 393224 | tf_op jit(solution)/shard_map/ppermute | solution.py:197
  6.4 1.3 %copy-start = (bf16[256,4096]{1,0:T(8,128)(2,1)}, bf16[256,4096]{1,0:T(8,128)(2,1)S(1)}, u32[]{:S(2)}) copy-start(bf16[256,4096]{1,0:T(8,128)(2,1)S(1)} %get-tuple-element.10.loaded_ref) | copy-start | bytes 6291460
  7.8 14.9 %all-to-all-start = ((bf16[8,136,256]{2,1,0:T(8,128)(2,1)}), bf16[8,136,256]{2,1,0:T(8,128)(2,1)S(1)}, u32[]{:S(2)}, u32[]{:S(2)}) async-start(bf16[8,136,256]{2,1,0:T(8,128)(2,1)} %get-tuple-element.9), calls=%async_computation | async-start | bytes 1114112 | tf_op jit(solution)/shard_map/all_to_all | solution.py:224
  12.5 1.6 %copy-start.1 = (bf16[256,4096]{1,0:T(8,128)(2,1)S(1)}, bf16[256,4096]{1,0:T(8,128)(2,1)}, u32[]{:S(2)}) copy-start(bf16[256,4096]{1,0:T(8,128)(2,1)} %copy-done) | copy-start | bytes 6291460
  34.8 1.2 %collective-permute-start.1 = (f32[16,256]{1,0:T(8,128)S(1)}, f32[16,256]{1,0:T(8,128)S(1)}, u32[]{:S(2)}, u32[]{:S(2)}) collective-permute-start(f32[16,256]{1,0:T(8,128)S(1)} %convert_reduce_fusion.mine_ref), channel_id=1, source_target_pairs={{0,1},{1,0},{2,3},{3,2},{4,5},{5,4},{6,7},{7,6},{8,9},{9,8},{10,11... | collective-permute-start | bytes 49160 | tf_op jit(solution)/shard_map/ppermute | solution.py:261

commit v23 on v21

--- a/solution.py
+++ b/solution.py
@@ -144,8 +144,9 @@
 
 
 class Plan:
-    def __init__(self, bin_total, cells):
+    def __init__(self, bin_total, wave_total, cells):
         self.bins = bin_total
+        self.wave = wave_total
         self.targets = bin_total // 2
         self.capacity = max(2, 2 * cells // bin_total)
         self.block = 2 * self.capacity
@@ -153,20 +154,25 @@
     def table_moves(self):
         return [(i, (i + self.targets) % self.bins) for i in range(self.bins)]
 
-    def halves(self):
-        return [list(range(self.targets)), list(range(self.targets, self.bins))]
+    def groups(self, size):
+        return [
+            [b * self.wave + (w ^ (bin(b).count("1") % 2)) for b in range(first, first + size)]
+            for first in range(0, self.bins, size)
+            for w in range(self.wave)
+        ]
 
 
 def per_device(sources, density, temp_bins, ray_index, rate_tables, line_table):
     cells, levels = sources.shape
     bin_total = lax.axis_size("bin")
     wave_total = lax.axis_size("wave")
-    plan = Plan(bin_total, cells)
+    plan = Plan(bin_total, wave_total, cells)
     rows = plan.block + META_ROWS
     params = pltpu.CompilerParams(vmem_limit_bytes=VMEM_LIMIT)
     vmem = pl.BlockSpec(memory_space=pltpu.VMEM)
     smem = pl.BlockSpec(memory_space=pltpu.SMEM)
     hbm = pl.BlockSpec(memory_space=pltpu.HBM)
+    both = ("bin", "wave")
 
     def in_hbm(x):
         return pltpu.with_memory_space_constraint(x, pltpu.HBM)
@@ -195,7 +201,12 @@
         in_hbm(ray_index.reshape(1, cells)),
     )
     got = lax.all_to_all(
-        outgoing, "bin", split_axis=0, concat_axis=0, tiled=True, axis_index_groups=plan.halves()
+        outgoing,
+        both,
+        split_axis=0,
+        concat_axis=0,
+        tiled=True,
+        axis_index_groups=plan.groups(plan.targets),
     )
     powers, held_line = pl.pallas_call(
         window_kernel,
@@ -221,10 +232,11 @@
     )(got, powers)
     held = lax.all_to_all(
         partial_sums.reshape(bin_total, ray_rows, levels),
-        "bin",
+        both,
         split_axis=0,
         concat_axis=0,
         tiled=True,
+        axis_index_groups=plan.groups(bin_total),
     )
     total = jnp.sum(held.astype(F32), axis=0)
     theirs = jnp.zeros_like(total)

time: 34.6 us -> 35.6 us (1.029)
  waiting for transfers between devices: 8.61 us -> 10.1 us
  starting transfers between devices: 8.86 us -> 8.01 us
    all_to_all x1, waiting for transfers between devices: 7.44 us -> 8.74 us  [per_device(): lax.all_to_all(outgoing, both, split_axis=0, concat_axis=0, tiled=True, a...]
    all_to_all x1, starting transfers between devices: 4.75 us -> 3.91 us  [per_device(): lax.all_to_all(outgoing, both, split_axis=0, concat_axis=0, tiled=True, a...]
  transfers between devices with their start and end apart: 3 -> 3, of which waited for: 2 -> 3; matrix products, arithmetic and copies ran while one was open for 0% -> 0% of each run, Pallas kernels for 12% -> 11%
where the time goes in v23:
time: 35.6 us; the launch traced here: 35.3 us
  blocking collectives  10.9 us (31%)
  waiting for transfers between devices  10.1 us (28%)
  starting transfers between devices  8.01 us (22%)
  Pallas kernels  6.15 us (17%)
    all_to_all x1, blocking collectives, per_device(): lax.all_to_all(partial_sums.reshape(bin_total, ray_rows, levels), both, s...  10.9 us
    all_to_all x1, waiting for transfers between devices, per_device(): lax.all_to_all(outgoing, both, split_axis=0, concat_axis=0, tiled=True, a...  8.74 us
    ppermute x1, starting transfers between devices, per_device(): arrived = lax.ppermute(rate_tables[0], 'bin', plan.table_moves())  4.04 us
    all_to_all x1, starting transfers between devices, per_device(): lax.all_to_all(outgoing, both, split_axis=0, concat_axis=0, tiled=True, a...  3.91 us
    pallas_call x1, Pallas kernels, per_device(): pl.pallas_call(functools.partial(pack_kernel, plan), out_shape=jax.ShapeD...  2.36 us
    pallas_call x1, Pallas kernels, per_device(): pl.pallas_call(window_kernel, out_shape=[jax.ShapeDtypeStruct(a, BF16) fo...  1.69 us
    ppermute x1, waiting for transfers between devices, per_device(): lax.ppermute(total, 'wave', [(i, i ^ step) for i in range(wave_total)])  1.17 us
    pallas_call x1, Pallas kernels, per_device(): pl.pallas_call(line_kernel, out_shape=jax.ShapeDtypeStruct(out_shape, F32...  1.13 us
  transfers between devices with their start and end apart: 3, of which 3 were waited for; matrix products, arithmetic and copies ran while one was open for 0% of the time, Pallas kernels for 11%

profile of v23, /device:TPU:0, one launch (start us, length us, event | category | flops | bytes accessed | tf_op | source)
XLA Modules:
  0.0 35.3 jit_solution(8121751187560654659)
XLA Ops:
  0.0 4.0 %collective-permute-start = (bf16[256,256]{1,0:T(8,128)(2,1)}, bf16[256,256]{1,0:T(8,128)(2,1)S(1)}, u32[]{:S(2)}, u32[]{:S(2)}) collective-permute-start(bf16[256,256]{1,0:T(8,128)(2,1)} %bitcast.10), channel_id=1, source_target_pairs={{0,16},{2,18},{4,20},{6,22},{8,24},{10,26},{12,28},{14,30},{16,0},... | collective-permute-start | bytes 393224 | tf_op jit(solution)/shard_map/ppermute | solution.py:180
  4.0 2.4 %shard_map.64 = bf16[8,136,256]{2,1,0:T(8,128)(2,1)} custom-call(s32[1]{0:T(128)} %bitcast.me_ref, bf16[512,256]{1,0:T(8,128)(2,1)} %src_hbm.1, bf16[4,128]{1,0:T(4,128)(2,1)} %bitcast.9, s32[1,512]{1,0:T(1,128)} %bitcast.7, s32[1,512]{1,0:T(1,128)} %bitcast.8), custom_call_target="tpu_custom_call" | custom-call | tf_op jit(solution)/shard_map/pallas_call | solution.py:183
  6.4 3.9 %all-to-all-start = ((bf16[8,136,256]{2,1,0:T(8,128)(2,1)}), bf16[8,136,256]{2,1,0:T(8,128)(2,1)S(1)}, u32[]{:S(2)}, u32[]{:S(2)}) async-start(bf16[8,136,256]{2,1,0:T(8,128)(2,1)} %shard_map.64), calls=%async_computation | async-start | bytes 1114112 | tf_op jit(solution)/shard_map/all_to_all | solution.py:203
  10.3 0.2 collective-permute-done.arrived_ref
  10.6 1.7 %shard_map.65 = (bf16[2,256,512]{2,1,0:T(8,128)(2,1)S(1)}, bf16[256,4096]{1,0:T(8,128)(2,1)S(1)}) custom-call(bf16[256,256]{1,0:T(8,128)(2,1)S(1)} %collective-permute-done.arrived_ref, bf16[256,256]{1,0:T(8,128)(2,1)} %bitcast.11, bf16[256,4096]{1,0:T(8,128)(2,1)} %line_hbm.1), custom_call_target="tpu_custom_call" | custom-call | flops 10000000000 | bytes 262144 | tf_op jit(solution)/shard_map/pallas_call | solution.py:211
  12.2 8.7 %all-to-all-done.got_ref = bf16[8,136,256]{2,1,0:T(8,128)(2,1)S(1)} async-done(((bf16[8,136,256]{2,1,0:T(8,128)(2,1)}), bf16[8,136,256]{2,1,0:T(8,128)(2,1)S(1)}, u32[]{:S(2)}, u32[]{:S(2)}) %all-to-all-start) | async-done | bytes 557088 | tf_op jit(solution)/shard_map/all_to_all | solution.py:203
  21.0 1.0 %shard_map.66 = bf16[256,256]{1,0:T(8,128)(2,1)S(1)} custom-call(bf16[8,136,256]{2,1,0:T(8,128)(2,1)S(1)} %all-to-all-done.got_ref, bf16[2,256,512]{2,1,0:T(8,128)(2,1)S(1)} %get-tuple-element.7.powers_ref), custom_call_target="tpu_custom_call" | custom-call | tf_op jit(solution)/shard_map/pallas_call | solution.py:226
  22.0 10.9 %all_to_all.10 = bf16[16,16,256]{2,1,0:T(8,128)(2,1)S(1)} all-to-all(bf16[16,16,256]{2,1,0:T(8,128)(2,1)S(1)} %bitcast.6), channel_id=1, replica_groups={{0,3,5,6,9,10,12,15,17,18,20,23,24,27,29,30},{1,2,4,7,8,11,13,14,16,19,..., dimensions={0} | all-to-all | bytes 262144 | tf_op jit(solution)/shard_map/all_to_all | solution.py:233
  32.9 0.1 collective-permute-start.1
  33.0 1.2 %collective-permute-done.1.theirs_ref = f32[16,256]{1,0:T(8,128)S(1)} collective-permute-done((f32[16,256]{1,0:T(8,128)S(1)}, f32[16,256]{1,0:T(8,128)S(1)}, u32[]{:S(2)}, u32[]{:S(2)}) %collective-permute-start.1) | collective-permute-done | bytes 16416 | tf_op jit(solution)/shard_map/ppermute | solution.py:246
  34.2 1.1 %shard_map.67 = f32[16,4096]{1,0:T(8,128)} custom-call(f32[16,256]{1,0:T(8,128)S(1)} %convert_reduce_fusion.mine_ref, f32[16,256]{1,0:T(8,128)S(1)} %collective-permute-done.1.theirs_ref, bf16[256,4096]{1,0:T(8,128)(2,1)S(1)} %get-tuple-element.8.line_ref), custom_call_target="tpu_custom_call" | custom-call | tf_op jit(solution)/shard_map/pallas_call | solution.py:249
  (1 shorter events, 0.0 us)
Async XLA Ops:
  0.0 10.5 %collective-permute-start = (bf16[256,256]{1,0:T(8,128)(2,1)}, bf16[256,256]{1,0:T(8,128)(2,1)S(1)}, u32[]{:S(2)}, u32[]{:S(2)}) collective-permute-start(bf16[256,256]{1,0:T(8,128)(2,1)} %bitcast.10), channel_id=1, source_target_pairs={{0,16},{2,18},{4,20},{6,22},{8,24},{10,26},{12,28},{14,30},{16,0},... | collective-permute-start | bytes 393224 | tf_op jit(solution)/shard_map/ppermute | solution.py:180
  6.4 14.6 %all-to-all-start = ((bf16[8,136,256]{2,1,0:T(8,128)(2,1)}), bf16[8,136,256]{2,1,0:T(8,128)(2,1)S(1)}, u32[]{:S(2)}, u32[]{:S(2)}) async-start(bf16[8,136,256]{2,1,0:T(8,128)(2,1)} %shard_map.64), calls=%async_computation | async-start | bytes 1114112 | tf_op jit(solution)/shard_map/all_to_all | solution.py:203
  32.9 1.2 %collective-permute-start.1 = (f32[16,256]{1,0:T(8,128)S(1)}, f32[16,256]{1,0:T(8,128)S(1)}, u32[]{:S(2)}, u32[]{:S(2)}) collective-permute-start(f32[16,256]{1,0:T(8,128)S(1)} %convert_reduce_fusion.mine_ref), channel_id=1, source_target_pairs={{0,1},{1,0},{2,3},{3,2},{4,5},{5,4},{6,7},{7,6},{8,9},{9,8},{10,11... | collective-permute-start | bytes 49160 | tf_op jit(solution)/shard_map/ppermute | solution.py:246

commit v24 on v21

--- a/solution.py
+++ b/solution.py
@@ -12,6 +12,7 @@
 RAY_BASE = 32
 LANES = 128
 LINE_CHUNKS = 4
+PACK_GROUPS = 2
 OVERLAP_FLOPS = 10**10
 VMEM_LIMIT = 32 * 1024 * 1024
 F32 = jnp.float32
@@ -29,7 +30,7 @@
 
 def pack_kernel(plan, me_ref, src_hbm, den_hbm, bin_hbm, ray_hbm, *rest):
     targets, block = plan.targets, plan.block
-    out, src_ref, den_ref, bin_ref, ray_ref, sems = rest
+    out_hbm, src_ref, den_ref, bin_ref, ray_ref, held, sems, out_sems = rest
     copies = [
         pltpu.make_async_copy(a, b, sems.at[i])
         for i, (a, b) in enumerate(
@@ -76,14 +77,24 @@
     ).astype(BF16)
     base = (iota((block, cells), 0) == within).astype(F32).astype(BF16)
     masks = [(target == t).astype(F32).astype(BF16) for t in range(targets)]
-    place = jnp.concatenate([base * mask for mask in masks], axis=0)
     moved = nt_dot(jnp.concatenate([meta * mask for mask in masks], axis=0), base).astype(BF16)
+    held[:, block:, :] = jnp.zeros((targets, META_ROWS, levels), BF16)
+    for t in range(targets):
+        held[t, block:, :block] = moved[t * META_ROWS : (t + 1) * META_ROWS]
     copies[3].wait()
-    rows = jnp.dot(place, src_ref[...], preferred_element_type=F32).astype(BF16)
-    out[:, :block, :] = rows.reshape(targets, block, levels)
-    out[:, block:, :] = jnp.zeros((targets, META_ROWS, levels), BF16)
-    for t in range(targets):
-        out[t, block:, :block] = moved[t * META_ROWS : (t + 1) * META_ROWS]
+    src = src_ref[...]
+    size = max(1, targets // PACK_GROUPS)
+    leaving = []
+    for first in range(0, targets, size):
+        place = jnp.concatenate([base * mask for mask in masks[first : first + size]], axis=0)
+        rows = jnp.dot(place, src, preferred_element_type=F32).astype(BF16)
+        part = pl.ds(first, size)
+        held[part, :block, :] = rows.reshape(size, block, levels)
+        copy = pltpu.make_async_copy(held.at[part], out_hbm.at[part], out_sems.at[len(leaving)])
+        copy.start()
+        leaving.append(copy)
+    for copy in leaving:
+        copy.wait()
 
 
 def window_kernel(arrived_ref, table_hbm, line_hbm, powers_ref, line_ref, sems):
@@ -178,13 +189,15 @@
         functools.partial(pack_kernel, plan),
         out_shape=jax.ShapeDtypeStruct((plan.targets, rows, levels), BF16),
         in_specs=[smem] + [hbm] * 4,
-        out_specs=vmem,
+        out_specs=hbm,
         scratch_shapes=[
             pltpu.VMEM((cells, levels), BF16),
             pltpu.VMEM((den_rows, cells // den_rows), BF16),
             pltpu.VMEM((1, cells), I32),
             pltpu.VMEM((1, cells), I32),
+            pltpu.VMEM((plan.targets, rows, levels), BF16),
             pltpu.SemaphoreType.DMA((4,)),
+            pltpu.SemaphoreType.DMA((PACK_GROUPS,)),
         ],
         compiler_params=params,
     )(

time: 34.6 us -> 34.6 us (level)
  no operation moved by 1% of the time
where the time goes in v24:
time: 34.6 us; the launch traced here: 34.3 us
  blocking collectives  10.6 us (31%)
  starting transfers between devices  8.85 us (26%)
  waiting for transfers between devices  8.61 us (25%)
  Pallas kernels  6.15 us (18%)
    all_to_all x1, blocking collectives, per_device(): lax.all_to_all(partial_sums.reshape(bin_total, ray_rows, levels), 'bin',...  10.6 us
    all_to_all x1, waiting for transfers between devices, per_device(): lax.all_to_all(outgoing, 'bin', split_axis=0, concat_axis=0, tiled=True,...  7.44 us
    all_to_all x1, starting transfers between devices, per_device(): lax.all_to_all(outgoing, 'bin', split_axis=0, concat_axis=0, tiled=True,...  4.75 us
    ppermute x1, starting transfers between devices, per_device(): arrived = lax.ppermute(rate_tables[0], 'bin', plan.table_moves())  4.04 us
    pallas_call x1, Pallas kernels, per_device(): pl.pallas_call(functools.partial(pack_kernel, plan), out_shape=jax.ShapeD...  2.37 us
    pallas_call x1, Pallas kernels, per_device(): pl.pallas_call(window_kernel, out_shape=[jax.ShapeDtypeStruct(a, BF16) fo...  1.69 us
    ppermute x1, waiting for transfers between devices, per_device(): lax.ppermute(total, 'wave', [(i, i ^ step) for i in range(wave_total)])  1.17 us
    pallas_call x1, Pallas kernels, per_device(): pl.pallas_call(line_kernel, out_shape=jax.ShapeDtypeStruct(out_shape, F32...  1.13 us
  transfers between devices with their start and end apart: 3, of which 2 were waited for; matrix products, arithmetic and copies ran while one was open for 0% of the time, Pallas kernels for 12%

profile of v24, /device:TPU:0, one launch (start us, length us, event | category | flops | bytes accessed | tf_op | source)
XLA Modules:
  0.0 34.3 jit_solution(14950913974084748288)
XLA Ops:
  0.0 4.0 %collective-permute-start = (bf16[256,256]{1,0:T(8,128)(2,1)}, bf16[256,256]{1,0:T(8,128)(2,1)S(1)}, u32[]{:S(2)}, u32[]{:S(2)}) collective-permute-start(bf16[256,256]{1,0:T(8,128)(2,1)} %bitcast.10), channel_id=1, source_target_pairs={{0,16},{2,18},{4,20},{6,22},{8,24},{10,26},{12,28},{14,30},{16,0},... | collective-permute-start | bytes 393224 | tf_op jit(solution)/shard_map/ppermute | solution.py:185
  4.0 2.4 %shard_map.64 = bf16[8,136,256]{2,1,0:T(8,128)(2,1)} custom-call(s32[1]{0:T(128)} %bitcast.me_ref, bf16[512,256]{1,0:T(8,128)(2,1)} %src_hbm.1, bf16[4,128]{1,0:T(4,128)(2,1)} %bitcast.9, s32[1,512]{1,0:T(1,128)} %bitcast.7, s32[1,512]{1,0:T(1,128)} %bitcast.8), custom_call_target="tpu_custom_call" | custom-call | tf_op jit(solution)/shard_map/pallas_call | solution.py:188
  6.4 4.7 %all-to-all-start = ((bf16[8,136,256]{2,1,0:T(8,128)(2,1)}), bf16[8,136,256]{2,1,0:T(8,128)(2,1)S(1)}, u32[]{:S(2)}, u32[]{:S(2)}) async-start(bf16[8,136,256]{2,1,0:T(8,128)(2,1)} %shard_map.64), calls=%async_computation | async-start | bytes 1114112 | tf_op jit(solution)/shard_map/all_to_all | solution.py:210
  11.2 0.0 collective-permute-done.arrived_ref
  11.2 1.7 %shard_map.65 = (bf16[2,256,512]{2,1,0:T(8,128)(2,1)S(1)}, bf16[256,4096]{1,0:T(8,128)(2,1)S(1)}) custom-call(bf16[256,256]{1,0:T(8,128)(2,1)S(1)} %collective-permute-done.arrived_ref, bf16[256,256]{1,0:T(8,128)(2,1)} %bitcast.11, bf16[256,4096]{1,0:T(8,128)(2,1)} %line_hbm.1), custom_call_target="tpu_custom_call" | custom-call | flops 10000000000 | bytes 262144 | tf_op jit(solution)/shard_map/pallas_call | solution.py:213
  12.9 7.4 %all-to-all-done.got_ref = bf16[8,136,256]{2,1,0:T(8,128)(2,1)S(1)} async-done(((bf16[8,136,256]{2,1,0:T(8,128)(2,1)}), bf16[8,136,256]{2,1,0:T(8,128)(2,1)S(1)}, u32[]{:S(2)}, u32[]{:S(2)}) %all-to-all-start) | async-done | bytes 557088 | tf_op jit(solution)/shard_map/all_to_all | solution.py:210
  20.3 1.0 %shard_map.66 = bf16[256,256]{1,0:T(8,128)(2,1)S(1)} custom-call(bf16[8,136,256]{2,1,0:T(8,128)(2,1)S(1)} %all-to-all-done.got_ref, bf16[2,256,512]{2,1,0:T(8,128)(2,1)S(1)} %get-tuple-element.7.powers_ref), custom_call_target="tpu_custom_call" | custom-call | tf_op jit(solution)/shard_map/pallas_call | solution.py:228
  21.3 10.6 %all_to_all.10 = bf16[16,16,256]{2,1,0:T(8,128)(2,1)S(1)} all-to-all(bf16[16,16,256]{2,1,0:T(8,128)(2,1)S(1)} %bitcast.6), channel_id=1, replica_groups=mesh['bin'=16,'wave'=2] {'bin'}, dimensions={0} | all-to-all | bytes 262144 | tf_op jit(solution)/shard_map/all_to_all | solution.py:235
  31.9 0.1 collective-permute-start.1
  32.0 1.2 %collective-permute-done.1.theirs_ref = f32[16,256]{1,0:T(8,128)S(1)} collective-permute-done((f32[16,256]{1,0:T(8,128)S(1)}, f32[16,256]{1,0:T(8,128)S(1)}, u32[]{:S(2)}, u32[]{:S(2)}) %collective-permute-start.1) | collective-permute-done | bytes 16416 | tf_op jit(solution)/shard_map/ppermute | solution.py:247
  33.2 1.1 %shard_map.67 = f32[16,4096]{1,0:T(8,128)} custom-call(f32[16,256]{1,0:T(8,128)S(1)} %convert_reduce_fusion.mine_ref, f32[16,256]{1,0:T(8,128)S(1)} %collective-permute-done.1.theirs_ref, bf16[256,4096]{1,0:T(8,128)(2,1)S(1)} %get-tuple-element.8.line_ref), custom_call_target="tpu_custom_call" | custom-call | tf_op jit(solution)/shard_map/pallas_call | solution.py:250
  (1 shorter events, 0.0 us)
Async XLA Ops:
  0.0 11.2 %collective-permute-start = (bf16[256,256]{1,0:T(8,128)(2,1)}, bf16[256,256]{1,0:T(8,128)(2,1)S(1)}, u32[]{:S(2)}, u32[]{:S(2)}) collective-permute-start(bf16[256,256]{1,0:T(8,128)(2,1)} %bitcast.10), channel_id=1, source_target_pairs={{0,16},{2,18},{4,20},{6,22},{8,24},{10,26},{12,28},{14,30},{16,0},... | collective-permute-start | bytes 393224 | tf_op jit(solution)/shard_map/ppermute | solution.py:185
  6.4 13.9 %all-to-all-start = ((bf16[8,136,256]{2,1,0:T(8,128)(2,1)}), bf16[8,136,256]{2,1,0:T(8,128)(2,1)S(1)}, u32[]{:S(2)}, u32[]{:S(2)}) async-start(bf16[8,136,256]{2,1,0:T(8,128)(2,1)} %shard_map.64), calls=%async_computation | async-start | bytes 1114112 | tf_op jit(solution)/shard_map/all_to_all | solution.py:210
  31.9 1.2 %collective-permute-start.1 = (f32[16,256]{1,0:T(8,128)S(1)}, f32[16,256]{1,0:T(8,128)S(1)}, u32[]{:S(2)}, u32[]{:S(2)}) collective-permute-start(f32[16,256]{1,0:T(8,128)S(1)} %convert_reduce_fusion.mine_ref), channel_id=1, source_target_pairs={{0,1},{1,0},{2,3},{3,2},{4,5},{5,4},{6,7},{7,6},{8,9},{9,8},{10,11... | collective-permute-start | bytes 49160 | tf_op jit(solution)/shard_map/ppermute | solution.py:247

commit v25 on v21

--- a/solution.py
+++ b/solution.py
@@ -25,6 +25,14 @@
 
 def iota(shape, dim):
     return lax.broadcasted_iota(I32, shape, dim)
+
+
+def gray_place(index, size):
+    place, shift = index, 1
+    while 1 << shift < size:
+        place = place ^ (index >> shift)
+        shift += 1
+    return place
 
 
 def pack_kernel(plan, me_ref, src_hbm, den_hbm, bin_hbm, ray_hbm, *rest):
@@ -63,7 +71,7 @@
         sofar = sofar + jnp.sum(part, axis=1, keepdims=True)
     position = jnp.concatenate(places, axis=1).astype(I32)
     half = bins // targets
-    target = bins - half * targets
+    target = gray_place(bins - half * targets, targets)
     within = (half ^ my_half) * plan.capacity + position
     rays = ray_ref[...]
     ray_high = rays // RAY_BASE
@@ -103,8 +111,9 @@
     copies[1].wait()
 
 
-def level_kernel(plan, rays, got_ref, powers_ref, out_ref):
+def level_kernel(plan, ray_rows, got_ref, powers_ref, out_ref):
     targets, block = plan.targets, plan.block
+    rays = plan.bins * ray_rows
     meta = [got_ref[s, block:, :block].astype(F32) for s in range(targets)]
     columns = [jnp.transpose(m[:8]) for m in meta]
     total = jnp.zeros(out_ref.shape, F32)
@@ -116,10 +125,12 @@
         ray = jnp.concatenate(
             [m[1:2, low:high] * RAY_BASE + m[2:3, low:high] for m in meta], axis=1
         ).astype(I32)
+        owner = ray // ray_rows
+        row = gray_place(owner, plan.bins) * ray_rows + (ray - owner * ray_rows)
         wide = src.astype(F32)
         steps = jnp.dot(src, powers_ref[part], preferred_element_type=F32)
         pops = (wide + den * (steps[:, :levels] + den * steps[:, levels:])).astype(BF16)
-        pick = (iota((rays, src.shape[0]), 0) == ray).astype(F32).astype(BF16)
+        pick = (iota((rays, src.shape[0]), 0) == row).astype(F32).astype(BF16)
         total = total + jnp.dot(pick, pops, preferred_element_type=F32)
     out_ref[...] = total.astype(BF16)
 
@@ -154,7 +165,11 @@
         return [(i, (i + self.targets) % self.bins) for i in range(self.bins)]
 
     def halves(self):
-        return [list(range(self.targets)), list(range(self.targets, self.bins))]
+        order = [i ^ (i >> 1) for i in range(self.targets)]
+        return [order, [self.targets + i for i in order]]
+
+    def everyone(self):
+        return [[i ^ (i >> 1) for i in range(self.bins)]]
 
 
 def per_device(sources, density, temp_bins, ray_index, rate_tables, line_table):
@@ -213,7 +228,7 @@
     ray_rows = RAY_DEV
     rays = ray_rows * bin_total
     partial_sums = pl.pallas_call(
-        functools.partial(level_kernel, plan, rays),
+        functools.partial(level_kernel, plan, ray_rows),
         out_shape=jax.ShapeDtypeStruct((rays, levels), BF16),
         in_specs=[vmem] * 2,
         out_specs=vmem,
@@ -225,6 +240,7 @@
         split_axis=0,
         concat_axis=0,
         tiled=True,
+        axis_index_groups=plan.everyone(),
     )
     total = jnp.sum(held.astype(F32), axis=0)
     theirs = jnp.zeros_like(total)

time: 34.6 us -> 34.8 us (level)
  blocking collectives: 10.6 us -> 11.1 us
    all_to_all x1, blocking collectives: 10.6 us -> 11.1 us  [per_device(): lax.all_to_all(partial_sums.reshape(bin_total, ray_rows, levels), 'bin',...]
where the time goes in v25:
time: 34.8 us; the launch traced here: 34.5 us
  blocking collectives  11.1 us (32%)
  starting transfers between devices  8.86 us (25%)
  waiting for transfers between devices  8.41 us (24%)
  Pallas kernels  6.14 us (18%)
    all_to_all x1, blocking collectives, per_device(): lax.all_to_all(partial_sums.reshape(bin_total, ray_rows, levels), 'bin',...  11.1 us
    all_to_all x1, waiting for transfers between devices, per_device(): lax.all_to_all(outgoing, 'bin', split_axis=0, concat_axis=0, tiled=True,...  7.23 us
    all_to_all x1, starting transfers between devices, per_device(): lax.all_to_all(outgoing, 'bin', split_axis=0, concat_axis=0, tiled=True,...  4.75 us
    ppermute x1, starting transfers between devices, per_device(): arrived = lax.ppermute(rate_tables[0], 'bin', plan.table_moves())  4.04 us
    pallas_call x1, Pallas kernels, per_device(): pl.pallas_call(functools.partial(pack_kernel, plan), out_shape=jax.ShapeD...  2.36 us
    pallas_call x1, Pallas kernels, per_device(): pl.pallas_call(window_kernel, out_shape=[jax.ShapeDtypeStruct(a, BF16) fo...  1.69 us
    ppermute x1, waiting for transfers between devices, per_device(): lax.ppermute(total, 'wave', [(i, i ^ step) for i in range(wave_total)])  1.17 us
    pallas_call x1, Pallas kernels, per_device(): pl.pallas_call(line_kernel, out_shape=jax.ShapeDtypeStruct(out_shape, F32...  1.13 us
  transfers between devices with their start and end apart: 3, of which 2 were waited for; matrix products, arithmetic and copies ran while one was open for 0% of the time, Pallas kernels for 12%

profile of v25, /device:TPU:0, one launch (start us, length us, event | category | flops | bytes accessed | tf_op | source)
XLA Modules:
  0.0 34.5 jit_solution(4377231344787280114)
XLA Ops:
  0.0 4.0 %collective-permute-start = (bf16[256,256]{1,0:T(8,128)(2,1)}, bf16[256,256]{1,0:T(8,128)(2,1)S(1)}, u32[]{:S(2)}, u32[]{:S(2)}) collective-permute-start(bf16[256,256]{1,0:T(8,128)(2,1)} %bitcast.10), channel_id=1, source_target_pairs={{0,16},{2,18},{4,20},{6,22},{8,24},{10,26},{12,28},{14,30},{16,0},... | collective-permute-start | bytes 393224 | tf_op jit(solution)/shard_map/ppermute | solution.py:189
  4.0 2.4 %shard_map.64 = bf16[8,136,256]{2,1,0:T(8,128)(2,1)} custom-call(s32[1]{0:T(128)} %bitcast.me_ref, bf16[512,256]{1,0:T(8,128)(2,1)} %src_hbm.1, bf16[4,128]{1,0:T(4,128)(2,1)} %bitcast.9, s32[1,512]{1,0:T(1,128)} %bitcast.7, s32[1,512]{1,0:T(1,128)} %bitcast.8), custom_call_target="tpu_custom_call" | custom-call | tf_op jit(solution)/shard_map/pallas_call | solution.py:192
  6.4 4.7 %all-to-all-start = ((bf16[8,136,256]{2,1,0:T(8,128)(2,1)}), bf16[8,136,256]{2,1,0:T(8,128)(2,1)S(1)}, u32[]{:S(2)}, u32[]{:S(2)}) async-start(bf16[8,136,256]{2,1,0:T(8,128)(2,1)} %shard_map.64), calls=%async_computation | async-start | bytes 1114112 | tf_op jit(solution)/shard_map/all_to_all | solution.py:212
  11.2 0.0 collective-permute-done.arrived_ref
  11.2 1.7 %shard_map.65 = (bf16[2,256,512]{2,1,0:T(8,128)(2,1)S(1)}, bf16[256,4096]{1,0:T(8,128)(2,1)S(1)}) custom-call(bf16[256,256]{1,0:T(8,128)(2,1)S(1)} %collective-permute-done.arrived_ref, bf16[256,256]{1,0:T(8,128)(2,1)} %bitcast.11, bf16[256,4096]{1,0:T(8,128)(2,1)} %line_hbm.1), custom_call_target="tpu_custom_call" | custom-call | flops 10000000000 | bytes 262144 | tf_op jit(solution)/shard_map/pallas_call | solution.py:215
  12.9 7.2 %all-to-all-done.got_ref = bf16[8,136,256]{2,1,0:T(8,128)(2,1)S(1)} async-done(((bf16[8,136,256]{2,1,0:T(8,128)(2,1)}), bf16[8,136,256]{2,1,0:T(8,128)(2,1)S(1)}, u32[]{:S(2)}, u32[]{:S(2)}) %all-to-all-start) | async-done | bytes 557088 | tf_op jit(solution)/shard_map/all_to_all | solution.py:212
  20.1 1.0 %shard_map.66 = bf16[256,256]{1,0:T(8,128)(2,1)S(1)} custom-call(bf16[8,136,256]{2,1,0:T(8,128)(2,1)S(1)} %all-to-all-done.got_ref, bf16[2,256,512]{2,1,0:T(8,128)(2,1)S(1)} %get-tuple-element.7.powers_ref), custom_call_target="tpu_custom_call" | custom-call | tf_op jit(solution)/shard_map/pallas_call | solution.py:230
  21.1 11.1 %all_to_all.10 = bf16[16,16,256]{2,1,0:T(8,128)(2,1)S(1)} all-to-all(bf16[16,16,256]{2,1,0:T(8,128)(2,1)S(1)} %bitcast.6), channel_id=1, replica_groups={{0,2,6,4,12,14,10,8,24,26,30,28,20,22,18,16},{1,3,7,5,13,15,11,9,25,27,..., dimensions={0} | all-to-all | bytes 262144 | tf_op jit(solution)/shard_map/all_to_all | solution.py:237
  32.1 0.1 collective-permute-start.1
  32.2 1.2 %collective-permute-done.1.theirs_ref = f32[16,256]{1,0:T(8,128)S(1)} collective-permute-done((f32[16,256]{1,0:T(8,128)S(1)}, f32[16,256]{1,0:T(8,128)S(1)}, u32[]{:S(2)}, u32[]{:S(2)}) %collective-permute-start.1) | collective-permute-done | bytes 16416 | tf_op jit(solution)/shard_map/ppermute | solution.py:250
  33.4 1.1 %shard_map.67 = f32[16,4096]{1,0:T(8,128)} custom-call(f32[16,256]{1,0:T(8,128)S(1)} %convert_reduce_fusion.mine_ref, f32[16,256]{1,0:T(8,128)S(1)} %collective-permute-done.1.theirs_ref, bf16[256,4096]{1,0:T(8,128)(2,1)S(1)} %get-tuple-element.8.line_ref), custom_call_target="tpu_custom_call" | custom-call | tf_op jit(solution)/shard_map/pallas_call | solution.py:253
  (1 shorter events, 0.0 us)
Async XLA Ops:
  0.0 11.2 %collective-permute-start = (bf16[256,256]{1,0:T(8,128)(2,1)}, bf16[256,256]{1,0:T(8,128)(2,1)S(1)}, u32[]{:S(2)}, u32[]{:S(2)}) collective-permute-start(bf16[256,256]{1,0:T(8,128)(2,1)} %bitcast.10), channel_id=1, source_target_pairs={{0,16},{2,18},{4,20},{6,22},{8,24},{10,26},{12,28},{14,30},{16,0},... | collective-permute-start | bytes 393224 | tf_op jit(solution)/shard_map/ppermute | solution.py:189
  6.4 13.7 %all-to-all-start = ((bf16[8,136,256]{2,1,0:T(8,128)(2,1)}), bf16[8,136,256]{2,1,0:T(8,128)(2,1)S(1)}, u32[]{:S(2)}, u32[]{:S(2)}) async-start(bf16[8,136,256]{2,1,0:T(8,128)(2,1)} %shard_map.64), calls=%async_computation | async-start | bytes 1114112 | tf_op jit(solution)/shard_map/all_to_all | solution.py:212
  32.1 1.2 %collective-permute-start.1 = (f32[16,256]{1,0:T(8,128)S(1)}, f32[16,256]{1,0:T(8,128)S(1)}, u32[]{:S(2)}, u32[]{:S(2)}) collective-permute-start(f32[16,256]{1,0:T(8,128)S(1)} %convert_reduce_fusion.mine_ref), channel_id=1, source_target_pairs={{0,1},{1,0},{2,3},{3,2},{4,5},{5,4},{6,7},{7,6},{8,9},{9,8},{10,11... | collective-permute-start | bytes 49160 | tf_op jit(solution)/shard_map/ppermute | solution.py:250

commit v26 on v25

--- a/solution.py
+++ b/solution.py
@@ -27,12 +27,12 @@
     return lax.broadcasted_iota(I32, shape, dim)
 
 
-def gray_place(index, size):
-    place, shift = index, 1
-    while 1 << shift < size:
-        place = place ^ (index >> shift)
-        shift += 1
-    return place
+def far_place(index, size):
+    return jnp.where(index < size // 2, 2 * index, 2 * (size - 1 - index) + 1)
+
+
+def far_order(size):
+    return [i // 2 if i % 2 == 0 else size - 1 - i // 2 for i in range(size)]
 
 
 def pack_kernel(plan, me_ref, src_hbm, den_hbm, bin_hbm, ray_hbm, *rest):
@@ -71,7 +71,7 @@
         sofar = sofar + jnp.sum(part, axis=1, keepdims=True)
     position = jnp.concatenate(places, axis=1).astype(I32)
     half = bins // targets
-    target = gray_place(bins - half * targets, targets)
+    target = far_place(bins - half * targets, targets)
     within = (half ^ my_half) * plan.capacity + position
     rays = ray_ref[...]
     ray_high = rays // RAY_BASE
@@ -126,7 +126,7 @@
             [m[1:2, low:high] * RAY_BASE + m[2:3, low:high] for m in meta], axis=1
         ).astype(I32)
         owner = ray // ray_rows
-        row = gray_place(owner, plan.bins) * ray_rows + (ray - owner * ray_rows)
+        row = far_place(owner, plan.bins) * ray_rows + (ray - owner * ray_rows)
         wide = src.astype(F32)
         steps = jnp.dot(src, powers_ref[part], preferred_element_type=F32)
         pops = (wide + den * (steps[:, :levels] + den * steps[:, levels:])).astype(BF16)
@@ -165,11 +165,11 @@
         return [(i, (i + self.targets) % self.bins) for i in range(self.bins)]
 
     def halves(self):
-        order = [i ^ (i >> 1) for i in range(self.targets)]
+        order = far_order(self.targets)
         return [order, [self.targets + i for i in order]]
 
     def everyone(self):
-        return [[i ^ (i >> 1) for i in range(self.bins)]]
+        return [far_order(self.bins)]
 
 
 def per_device(sources, density, temp_bins, ray_index, rate_tables, line_table):

time: 34.8 us -> 35.1 us (level)
  no operation moved by 1% of the time
where the time goes in v26:
time: 35.1 us; the launch traced here: 34.8 us
  blocking collectives  11.3 us (32%)
  starting transfers between devices  8.86 us (25%)
  waiting for transfers between devices  8.45 us (24%)
  Pallas kernels  6.14 us (17%)
    all_to_all x1, blocking collectives, per_device(): lax.all_to_all(partial_sums.reshape(bin_total, ray_rows, levels), 'bin',...  11.3 us
    all_to_all x1, waiting for transfers between devices, per_device(): lax.all_to_all(outgoing, 'bin', split_axis=0, concat_axis=0, tiled=True,...  7.28 us
    all_to_all x1, starting transfers between devices, per_device(): lax.all_to_all(outgoing, 'bin', split_axis=0, concat_axis=0, tiled=True,...  4.75 us
    ppermute x1, starting transfers between devices, per_device(): arrived = lax.ppermute(rate_tables[0], 'bin', plan.table_moves())  4.04 us
    pallas_call x1, Pallas kernels, per_device(): pl.pallas_call(functools.partial(pack_kernel, plan), out_shape=jax.ShapeD...  2.36 us
    pallas_call x1, Pallas kernels, per_device(): pl.pallas_call(window_kernel, out_shape=[jax.ShapeDtypeStruct(a, BF16) fo...  1.69 us
    ppermute x1, waiting for transfers between devices, per_device(): lax.ppermute(total, 'wave', [(i, i ^ step) for i in range(wave_total)])  1.17 us
    pallas_call x1, Pallas kernels, per_device(): pl.pallas_call(line_kernel, out_shape=jax.ShapeDtypeStruct(out_shape, F32...  1.13 us
  transfers between devices with their start and end apart: 3, of which 2 were waited for; matrix products, arithmetic and copies ran while one was open for 0% of the time, Pallas kernels for 12%

profile of v26, /device:TPU:0, one launch (start us, length us, event | category | flops | bytes accessed | tf_op | source)
XLA Modules:
  0.0 34.8 jit_solution(16510017082492806907)
XLA Ops:
  0.0 4.0 %collective-permute-start = (bf16[256,256]{1,0:T(8,128)(2,1)}, bf16[256,256]{1,0:T(8,128)(2,1)S(1)}, u32[]{:S(2)}, u32[]{:S(2)}) collective-permute-start(bf16[256,256]{1,0:T(8,128)(2,1)} %bitcast.10), channel_id=1, source_target_pairs={{0,16},{2,18},{4,20},{6,22},{8,24},{10,26},{12,28},{14,30},{16,0},... | collective-permute-start | bytes 393224 | tf_op jit(solution)/shard_map/ppermute | solution.py:189
  4.0 2.4 %shard_map.64 = bf16[8,136,256]{2,1,0:T(8,128)(2,1)} custom-call(s32[1]{0:T(128)} %bitcast.me_ref, bf16[512,256]{1,0:T(8,128)(2,1)} %src_hbm.1, bf16[4,128]{1,0:T(4,128)(2,1)} %bitcast.9, s32[1,512]{1,0:T(1,128)} %bitcast.7, s32[1,512]{1,0:T(1,128)} %bitcast.8), custom_call_target="tpu_custom_call" | custom-call | tf_op jit(solution)/shard_map/pallas_call | solution.py:192
  6.4 4.7 %all-to-all-start = ((bf16[8,136,256]{2,1,0:T(8,128)(2,1)}), bf16[8,136,256]{2,1,0:T(8,128)(2,1)S(1)}, u32[]{:S(2)}, u32[]{:S(2)}) async-start(bf16[8,136,256]{2,1,0:T(8,128)(2,1)} %shard_map.64), calls=%async_computation | async-start | bytes 1114112 | tf_op jit(solution)/shard_map/all_to_all | solution.py:212
  11.2 0.0 collective-permute-done.arrived_ref
  11.2 1.7 %shard_map.65 = (bf16[2,256,512]{2,1,0:T(8,128)(2,1)S(1)}, bf16[256,4096]{1,0:T(8,128)(2,1)S(1)}) custom-call(bf16[256,256]{1,0:T(8,128)(2,1)S(1)} %collective-permute-done.arrived_ref, bf16[256,256]{1,0:T(8,128)(2,1)} %bitcast.11, bf16[256,4096]{1,0:T(8,128)(2,1)} %line_hbm.1), custom_call_target="tpu_custom_call" | custom-call | flops 10000000000 | bytes 262144 | tf_op jit(solution)/shard_map/pallas_call | solution.py:215
  12.9 7.3 %all-to-all-done.got_ref = bf16[8,136,256]{2,1,0:T(8,128)(2,1)S(1)} async-done(((bf16[8,136,256]{2,1,0:T(8,128)(2,1)}), bf16[8,136,256]{2,1,0:T(8,128)(2,1)S(1)}, u32[]{:S(2)}, u32[]{:S(2)}) %all-to-all-start) | async-done | bytes 557088 | tf_op jit(solution)/shard_map/all_to_all | solution.py:212
  20.1 1.0 %shard_map.66 = bf16[256,256]{1,0:T(8,128)(2,1)S(1)} custom-call(bf16[8,136,256]{2,1,0:T(8,128)(2,1)S(1)} %all-to-all-done.got_ref, bf16[2,256,512]{2,1,0:T(8,128)(2,1)S(1)} %get-tuple-element.7.powers_ref), custom_call_target="tpu_custom_call" | custom-call | tf_op jit(solution)/shard_map/pallas_call | solution.py:230
  21.1 11.3 %all_to_all.10 = bf16[16,16,256]{2,1,0:T(8,128)(2,1)S(1)} all-to-all(bf16[16,16,256]{2,1,0:T(8,128)(2,1)S(1)} %bitcast.6), channel_id=1, replica_groups={{0,30,2,28,4,26,6,24,8,22,10,20,12,18,14,16},{1,31,3,29,5,27,7,25,9,23,..., dimensions={0} | all-to-all | bytes 262144 | tf_op jit(solution)/shard_map/all_to_all | solution.py:237
  32.4 0.1 collective-permute-start.1
  32.5 1.2 %collective-permute-done.1.theirs_ref = f32[16,256]{1,0:T(8,128)S(1)} collective-permute-done((f32[16,256]{1,0:T(8,128)S(1)}, f32[16,256]{1,0:T(8,128)S(1)}, u32[]{:S(2)}, u32[]{:S(2)}) %collective-permute-start.1) | collective-permute-done | bytes 16416 | tf_op jit(solution)/shard_map/ppermute | solution.py:250
  33.7 1.1 %shard_map.67 = f32[16,4096]{1,0:T(8,128)} custom-call(f32[16,256]{1,0:T(8,128)S(1)} %convert_reduce_fusion.mine_ref, f32[16,256]{1,0:T(8,128)S(1)} %collective-permute-done.1.theirs_ref, bf16[256,4096]{1,0:T(8,128)(2,1)S(1)} %get-tuple-element.8.line_ref), custom_call_target="tpu_custom_call" | custom-call | tf_op jit(solution)/shard_map/pallas_call | solution.py:253
  (1 shorter events, 0.0 us)
Async XLA Ops:
  0.0 11.2 %collective-permute-start = (bf16[256,256]{1,0:T(8,128)(2,1)}, bf16[256,256]{1,0:T(8,128)(2,1)S(1)}, u32[]{:S(2)}, u32[]{:S(2)}) collective-permute-start(bf16[256,256]{1,0:T(8,128)(2,1)} %bitcast.10), channel_id=1, source_target_pairs={{0,16},{2,18},{4,20},{6,22},{8,24},{10,26},{12,28},{14,30},{16,0},... | collective-permute-start | bytes 393224 | tf_op jit(solution)/shard_map/ppermute | solution.py:189
  6.4 13.7 %all-to-all-start = ((bf16[8,136,256]{2,1,0:T(8,128)(2,1)}), bf16[8,136,256]{2,1,0:T(8,128)(2,1)S(1)}, u32[]{:S(2)}, u32[]{:S(2)}) async-start(bf16[8,136,256]{2,1,0:T(8,128)(2,1)} %shard_map.64), calls=%async_computation | async-start | bytes 1114112 | tf_op jit(solution)/shard_map/all_to_all | solution.py:212
  32.4 1.2 %collective-permute-start.1 = (f32[16,256]{1,0:T(8,128)S(1)}, f32[16,256]{1,0:T(8,128)S(1)}, u32[]{:S(2)}, u32[]{:S(2)}) collective-permute-start(f32[16,256]{1,0:T(8,128)S(1)} %convert_reduce_fusion.mine_ref), channel_id=1, source_target_pairs={{0,1},{1,0},{2,3},{3,2},{4,5},{5,4},{6,7},{7,6},{8,9},{9,8},{10,11... | collective-permute-start | bytes 49160 | tf_op jit(solution)/shard_map/ppermute | solution.py:250

commit v27 on v21

--- a/solution.py
+++ b/solution.py
@@ -150,8 +150,12 @@
         self.capacity = max(2, 2 * cells // bin_total)
         self.block = 2 * self.capacity
 
-    def table_moves(self):
-        return [(i, (i + self.targets) % self.bins) for i in range(self.bins)]
+    def table_moves(self, wave_total):
+        return [
+            (b * wave_total + w, (b + self.targets) % self.bins * wave_total + (w ^ 1))
+            for b in range(self.bins)
+            for w in range(wave_total)
+        ]
 
     def halves(self):
         return [list(range(self.targets)), list(range(self.targets, self.bins))]
@@ -171,7 +175,7 @@
     def in_hbm(x):
         return pltpu.with_memory_space_constraint(x, pltpu.HBM)
 
-    arrived = lax.ppermute(rate_tables[0], "bin", plan.table_moves())
+    arrived = lax.ppermute(rate_tables[0], ("bin", "wave"), plan.table_moves(wave_total))
     me = lax.axis_index("bin").astype(I32).reshape(1)
     den_rows = cells // min(cells, LANES)
     outgoing = pl.pallas_call(

time: 34.6 us -> 35.5 us (1.026)
  waiting for transfers between devices: 8.61 us -> 9.61 us
  starting transfers between devices: 8.86 us -> 8.29 us
  blocking collectives: 10.6 us -> 11.1 us
    all_to_all x1, waiting for transfers between devices: 7.44 us -> 8.44 us  [per_device(): lax.all_to_all(outgoing, 'bin', split_axis=0, concat_axis=0, tiled=True,...]
    ppermute x1, starting transfers between devices: 4.04 us -> 3.48 us  [per_device(): lax.ppermute(rate_tables[0], ('bin', 'wave'), plan.table_moves(wave_total))]
    all_to_all x1, blocking collectives: 10.6 us -> 11.1 us  [per_device(): lax.all_to_all(partial_sums.reshape(bin_total, ray_rows, levels), 'bin',...]
where the time goes in v27:
time: 35.5 us; the launch traced here: 35.2 us
  blocking collectives  11.1 us (31%)
  waiting for transfers between devices  9.61 us (27%)
  starting transfers between devices  8.29 us (23%)
  Pallas kernels  6.15 us (17%)
    all_to_all x1, blocking collectives, per_device(): lax.all_to_all(partial_sums.reshape(bin_total, ray_rows, levels), 'bin',...  11.1 us
    all_to_all x1, waiting for transfers between devices, per_device(): lax.all_to_all(outgoing, 'bin', split_axis=0, concat_axis=0, tiled=True,...  8.44 us
    all_to_all x1, starting transfers between devices, per_device(): lax.all_to_all(outgoing, 'bin', split_axis=0, concat_axis=0, tiled=True,...  4.75 us
    ppermute x1, starting transfers between devices, per_device(): lax.ppermute(rate_tables[0], ('bin', 'wave'), plan.table_moves(wave_total))  3.48 us
    pallas_call x1, Pallas kernels, per_device(): pl.pallas_call(functools.partial(pack_kernel, plan), out_shape=jax.ShapeD...  2.36 us
    pallas_call x1, Pallas kernels, per_device(): pl.pallas_call(window_kernel, out_shape=[jax.ShapeDtypeStruct(a, BF16) fo...  1.69 us
    ppermute x1, waiting for transfers between devices, per_device(): lax.ppermute(total, 'wave', [(i, i ^ step) for i in range(wave_total)])  1.17 us
    pallas_call x1, Pallas kernels, per_device(): pl.pallas_call(line_kernel, out_shape=jax.ShapeDtypeStruct(out_shape, F32...  1.13 us
  transfers between devices with their start and end apart: 3, of which 2 were waited for; matrix products, arithmetic and copies ran while one was open for 0% of the time, Pallas kernels for 12%

profile of v27, /device:TPU:0, one launch (start us, length us, event | category | flops | bytes accessed | tf_op | source)
XLA Modules:
  0.0 35.2 jit_solution(2651004456261798305)
XLA Ops:
  0.0 3.5 %collective-permute-start = (bf16[256,256]{1,0:T(8,128)(2,1)}, bf16[256,256]{1,0:T(8,128)(2,1)S(1)}, u32[]{:S(2)}, u32[]{:S(2)}) collective-permute-start(bf16[256,256]{1,0:T(8,128)(2,1)} %bitcast.10), channel_id=1, source_target_pairs={{0,17},{1,16},{2,19},{3,18},{4,21},{5,20},{6,23},{7,22},{8,25},{9,... | collective-permute-start | bytes 393224 | tf_op jit(solution)/shard_map/ppermute | solution.py:178
  3.5 2.4 %shard_map.64 = bf16[8,136,256]{2,1,0:T(8,128)(2,1)} custom-call(s32[1]{0:T(128)} %bitcast.me_ref, bf16[512,256]{1,0:T(8,128)(2,1)} %src_hbm.1, bf16[4,128]{1,0:T(4,128)(2,1)} %bitcast.9, s32[1,512]{1,0:T(1,128)} %bitcast.7, s32[1,512]{1,0:T(1,128)} %bitcast.8), custom_call_target="tpu_custom_call" | custom-call | tf_op jit(solution)/shard_map/pallas_call | solution.py:181
  5.8 4.7 %all-to-all-start = ((bf16[8,136,256]{2,1,0:T(8,128)(2,1)}), bf16[8,136,256]{2,1,0:T(8,128)(2,1)S(1)}, u32[]{:S(2)}, u32[]{:S(2)}) async-start(bf16[8,136,256]{2,1,0:T(8,128)(2,1)} %shard_map.64), calls=%async_computation | async-start | bytes 1114112 | tf_op jit(solution)/shard_map/all_to_all | solution.py:201
  10.6 0.0 collective-permute-done.arrived_ref
  10.6 1.7 %shard_map.65 = (bf16[2,256,512]{2,1,0:T(8,128)(2,1)S(1)}, bf16[256,4096]{1,0:T(8,128)(2,1)S(1)}) custom-call(bf16[256,256]{1,0:T(8,128)(2,1)S(1)} %collective-permute-done.arrived_ref, bf16[256,256]{1,0:T(8,128)(2,1)} %bitcast.11, bf16[256,4096]{1,0:T(8,128)(2,1)} %line_hbm.1), custom_call_target="tpu_custom_call" | custom-call | flops 10000000000 | bytes 262144 | tf_op jit(solution)/shard_map/pallas_call | solution.py:204
  12.3 8.4 %all-to-all-done.got_ref = bf16[8,136,256]{2,1,0:T(8,128)(2,1)S(1)} async-done(((bf16[8,136,256]{2,1,0:T(8,128)(2,1)}), bf16[8,136,256]{2,1,0:T(8,128)(2,1)S(1)}, u32[]{:S(2)}, u32[]{:S(2)}) %all-to-all-start) | async-done | bytes 557088 | tf_op jit(solution)/shard_map/all_to_all | solution.py:201
  20.7 1.0 %shard_map.66 = bf16[256,256]{1,0:T(8,128)(2,1)S(1)} custom-call(bf16[8,136,256]{2,1,0:T(8,128)(2,1)S(1)} %all-to-all-done.got_ref, bf16[2,256,512]{2,1,0:T(8,128)(2,1)S(1)} %get-tuple-element.7.powers_ref), custom_call_target="tpu_custom_call" | custom-call | tf_op jit(solution)/shard_map/pallas_call | solution.py:219
  21.7 11.1 %all_to_all.10 = bf16[16,16,256]{2,1,0:T(8,128)(2,1)S(1)} all-to-all(bf16[16,16,256]{2,1,0:T(8,128)(2,1)S(1)} %bitcast.6), channel_id=1, replica_groups=mesh['bin'=16,'wave'=2] {'bin'}, dimensions={0} | all-to-all | bytes 262144 | tf_op jit(solution)/shard_map/all_to_all | solution.py:226
  32.9 0.1 collective-permute-start.1
  32.9 1.2 %collective-permute-done.1.theirs_ref = f32[16,256]{1,0:T(8,128)S(1)} collective-permute-done((f32[16,256]{1,0:T(8,128)S(1)}, f32[16,256]{1,0:T(8,128)S(1)}, u32[]{:S(2)}, u32[]{:S(2)}) %collective-permute-start.1) | collective-permute-done | bytes 16416 | tf_op jit(solution)/shard_map/ppermute | solution.py:238
  34.1 1.1 %shard_map.67 = f32[16,4096]{1,0:T(8,128)} custom-call(f32[16,256]{1,0:T(8,128)S(1)} %convert_reduce_fusion.mine_ref, f32[16,256]{1,0:T(8,128)S(1)} %collective-permute-done.1.theirs_ref, bf16[256,4096]{1,0:T(8,128)(2,1)S(1)} %get-tuple-element.8.line_ref), custom_call_target="tpu_custom_call" | custom-call | tf_op jit(solution)/shard_map/pallas_call | solution.py:241
  (1 shorter events, 0.0 us)
Async XLA Ops:
  0.0 10.6 %collective-permute-start = (bf16[256,256]{1,0:T(8,128)(2,1)}, bf16[256,256]{1,0:T(8,128)(2,1)S(1)}, u32[]{:S(2)}, u32[]{:S(2)}) collective-permute-start(bf16[256,256]{1,0:T(8,128)(2,1)} %bitcast.10), channel_id=1, source_target_pairs={{0,17},{1,16},{2,19},{3,18},{4,21},{5,20},{6,23},{7,22},{8,25},{9,... | collective-permute-start | bytes 393224 | tf_op jit(solution)/shard_map/ppermute | solution.py:178
  5.8 14.9 %all-to-all-start = ((bf16[8,136,256]{2,1,0:T(8,128)(2,1)}), bf16[8,136,256]{2,1,0:T(8,128)(2,1)S(1)}, u32[]{:S(2)}, u32[]{:S(2)}) async-start(bf16[8,136,256]{2,1,0:T(8,128)(2,1)} %shard_map.64), calls=%async_computation | async-start | bytes 1114112 | tf_op jit(solution)/shard_map/all_to_all | solution.py:201
  32.9 1.2 %collective-permute-start.1 = (f32[16,256]{1,0:T(8,128)S(1)}, f32[16,256]{1,0:T(8,128)S(1)}, u32[]{:S(2)}, u32[]{:S(2)}) collective-permute-start(f32[16,256]{1,0:T(8,128)S(1)} %convert_reduce_fusion.mine_ref), channel_id=1, source_target_pairs={{0,1},{1,0},{2,3},{3,2},{4,5},{5,4},{6,7},{7,6},{8,9},{9,8},{10,11... | collective-permute-start | bytes 49160 | tf_op jit(solution)/shard_map/ppermute | solution.py:238

commit v28 on v21

--- a/solution.py
+++ b/solution.py
@@ -29,7 +29,8 @@
 
 def pack_kernel(plan, me_ref, src_hbm, den_hbm, bin_hbm, ray_hbm, *rest):
     targets, block = plan.targets, plan.block
-    out, src_ref, den_ref, bin_ref, ray_ref, sems = rest
+    outs, near_out = rest[: len(plan.far)], rest[len(plan.far)]
+    src_ref, den_ref, bin_ref, ray_ref, sems = rest[len(plan.far) + 1 :]
     copies = [
         pltpu.make_async_copy(a, b, sems.at[i])
         for i, (a, b) in enumerate(
@@ -47,6 +48,7 @@
     lanes = min(cells, LANES)
     earlier = (iota((lanes, lanes), 0) < iota((lanes, lanes), 1)).astype(F32).astype(BF16)
     my_half = me_ref[0] // targets
+    my_place = me_ref[0] - my_half * targets
     for copy in copies[:3]:
         copy.wait()
     bins = bin_ref[...]
@@ -75,15 +77,28 @@
         axis=0,
     ).astype(BF16)
     base = (iota((block, cells), 0) == within).astype(F32).astype(BF16)
-    masks = [(target == t).astype(F32).astype(BF16) for t in range(targets)]
+    turn = target ^ my_place
+    flips = turn
+    for shift in range(1, targets.bit_length() - 1):
+        flips = flips ^ (turn >> shift)
+    pairs = jnp.where(flips % 2 == 0, target // 2, -1)
+    masks = [(pairs == p).astype(F32).astype(BF16) for p in range(targets // 2)]
+    masks = [(turn == k).astype(F32).astype(BF16) for k in plan.far] + masks
     place = jnp.concatenate([base * mask for mask in masks], axis=0)
     moved = nt_dot(jnp.concatenate([meta * mask for mask in masks], axis=0), base).astype(BF16)
     copies[3].wait()
     rows = jnp.dot(place, src_ref[...], preferred_element_type=F32).astype(BF16)
-    out[:, :block, :] = rows.reshape(targets, block, levels)
-    out[:, block:, :] = jnp.zeros((targets, META_ROWS, levels), BF16)
     for t in range(targets):
-        out[t, block:, :block] = moved[t * META_ROWS : (t + 1) * META_ROWS]
+        out = outs[t] if t < len(outs) else near_out.at[t - len(outs)]
+        out[:block, :] = rows[t * block : (t + 1) * block]
+        out[block:, :] = jnp.zeros((META_ROWS, levels), BF16)
+        out[block:, :block] = moved[t * META_ROWS : (t + 1) * META_ROWS]
+
+
+def stage_kernel(near_ref, out_hbm, sem):
+    copy = pltpu.make_async_copy(near_ref, out_hbm, sem)
+    copy.start()
+    copy.wait()
 
 
 def window_kernel(arrived_ref, table_hbm, line_hbm, powers_ref, line_ref, sems):
@@ -103,15 +118,15 @@
     copies[1].wait()
 
 
-def level_kernel(plan, rays, got_ref, powers_ref, out_ref):
-    targets, block = plan.targets, plan.block
-    meta = [got_ref[s, block:, :block].astype(F32) for s in range(targets)]
+def level_kernel(plan, rays, powers_ref, near_ref, *refs):
+    out_ref, block, levels = refs[-1], plan.block, near_ref.shape[2]
+    got = list(refs[:-1]) + [near_ref.at[i] for i in range(near_ref.shape[0])]
+    meta = [g[block:, :block].astype(F32) for g in got]
     columns = [jnp.transpose(m[:8]) for m in meta]
     total = jnp.zeros(out_ref.shape, F32)
-    levels = got_ref.shape[2]
     for part in range(2):
         low, high = part * plan.capacity, (part + 1) * plan.capacity
-        src = got_ref[:, low:high, :].reshape(targets * plan.capacity, got_ref.shape[2])
+        src = jnp.concatenate([g[low:high, :] for g in got], axis=0)
         den = jnp.concatenate([c[low:high, 0:1] for c in columns], axis=0)
         ray = jnp.concatenate(
             [m[1:2, low:high] * RAY_BASE + m[2:3, low:high] for m in meta], axis=1
@@ -149,12 +164,16 @@
         self.targets = bin_total // 2
         self.capacity = max(2, 2 * cells // bin_total)
         self.block = 2 * self.capacity
+        even = [k for k in range(self.targets) if bin(k).count("1") % 2 == 0]
+        odd = [k for k in range(self.targets) if bin(k).count("1") % 2]
+        self.far = sorted(odd, key=lambda k: (-bin(k).count("1"), k))
+        self.quads = [[h + k for k in ks] for h in (0, self.targets) for ks in (even, odd)]
 
     def table_moves(self):
         return [(i, (i + self.targets) % self.bins) for i in range(self.bins)]
 
-    def halves(self):
-        return [list(range(self.targets)), list(range(self.targets, self.bins))]
+    def moves(self, k):
+        return [(i, i ^ k) for i in range(self.bins)]
 
 
 def per_device(sources, density, temp_bins, ray_index, rate_tables, line_table):
@@ -174,11 +193,12 @@
     arrived = lax.ppermute(rate_tables[0], "bin", plan.table_moves())
     me = lax.axis_index("bin").astype(I32).reshape(1)
     den_rows = cells // min(cells, LANES)
-    outgoing = pl.pallas_call(
+    near_shape = jax.ShapeDtypeStruct((plan.targets // 2, rows, levels), BF16)
+    *outgoing, near = pl.pallas_call(
         functools.partial(pack_kernel, plan),
-        out_shape=jax.ShapeDtypeStruct((plan.targets, rows, levels), BF16),
+        out_shape=[jax.ShapeDtypeStruct((rows, levels), BF16)] * len(plan.far) + [near_shape],
         in_specs=[smem] + [hbm] * 4,
-        out_specs=vmem,
+        out_specs=[vmem] * (len(plan.far) + 1),
         scratch_shapes=[
             pltpu.VMEM((cells, levels), BF16),
             pltpu.VMEM((den_rows, cells // den_rows), BF16),
@@ -194,8 +214,17 @@
         in_hbm(temp_bins.reshape(1, cells)),
         in_hbm(ray_index.reshape(1, cells)),
     )
+    far = [lax.ppermute(x, "bin", plan.moves(k)) for x, k in zip(outgoing, plan.far)]
+    staged = pl.pallas_call(
+        stage_kernel,
+        out_shape=near_shape,
+        in_specs=[vmem],
+        out_specs=hbm,
+        scratch_shapes=[pltpu.SemaphoreType.DMA],
+        compiler_params=params,
+    )(near)
     got = lax.all_to_all(
-        outgoing, "bin", split_axis=0, concat_axis=0, tiled=True, axis_index_groups=plan.halves()
+        staged, "bin", split_axis=0, concat_axis=0, tiled=True, axis_index_groups=plan.quads
     )
     powers, held_line = pl.pallas_call(
         window_kernel,
@@ -215,10 +244,10 @@
     partial_sums = pl.pallas_call(
         functools.partial(level_kernel, plan, rays),
         out_shape=jax.ShapeDtypeStruct((rays, levels), BF16),
-        in_specs=[vmem] * 2,
+        in_specs=[vmem] * (2 + len(far)),
         out_specs=vmem,
         compiler_params=params,
-    )(got, powers)
+    )(powers, got, *far)
     held = lax.all_to_all(
         partial_sums.reshape(bin_total, ray_rows, levels),
         "bin",

time: 34.6 us -> 35.1 us (1.014)
  starting transfers between devices: 8.86 us -> 13.8 us
  waiting for transfers between devices: 8.61 us -> 3.78 us
  Pallas kernels: 6.15 us -> 6.69 us
    all_to_all x1, waiting for transfers between devices: 7.44 us -> 0.01 us  [per_device(): lax.all_to_all(staged, 'bin', split_axis=0, concat_axis=0, tiled=True, ax...]
    ppermute x0 -> x4, starting transfers between devices: none -> 5.88 us  [per_device(): lax.ppermute(x, 'bin', plan.moves(k))]
    ppermute x0 -> x4, waiting for transfers between devices: none -> 2.61 us  [per_device(): lax.ppermute(x, 'bin', plan.moves(k))]
    all_to_all x1, starting transfers between devices: 4.75 us -> 3.81 us  [per_device(): lax.all_to_all(staged, 'bin', split_axis=0, concat_axis=0, tiled=True, ax...]
    pallas_call x1 -> x2, Pallas kernels: 2.36 us -> 2.9 us  [the longest x1 2.19 us: per_device(): pl.pallas_call(functools.partial(pack_kernel, plan), out_shape=[jax.Shape...]
  transfers between devices with their start and end apart: 3 -> 7, of which waited for: 2 -> 4; matrix products, arithmetic and copies ran while one was open for 0% -> 0% of each run, Pallas kernels for 12% -> 13%
where the time goes in v28:
time: 35.1 us; the launch traced here: 34.8 us
  starting transfers between devices  13.8 us (39%)
  blocking collectives  10.4 us (30%)
  Pallas kernels  6.69 us (19%)
  waiting for transfers between devices  3.78 us (11%)
    all_to_all x1, blocking collectives, per_device(): lax.all_to_all(partial_sums.reshape(bin_total, ray_rows, levels), 'bin',...  10.4 us
    ppermute x4, starting transfers between devices, per_device(): lax.ppermute(x, 'bin', plan.moves(k))  5.88 us
    ppermute x1, starting transfers between devices, per_device(): arrived = lax.ppermute(rate_tables[0], 'bin', plan.table_moves())  4.04 us
    all_to_all x1, starting transfers between devices, per_device(): lax.all_to_all(staged, 'bin', split_axis=0, concat_axis=0, tiled=True, ax...  3.81 us
    ppermute x4, waiting for transfers between devices, per_device(): lax.ppermute(x, 'bin', plan.moves(k))  2.61 us
    pallas_call x1, Pallas kernels, per_device(): pl.pallas_call(functools.partial(pack_kernel, plan), out_shape=[jax.Shape...  2.19 us
    pallas_call x1, Pallas kernels, per_device(): pl.pallas_call(window_kernel, out_shape=[jax.ShapeDtypeStruct(a, BF16) fo...  1.69 us
    ppermute x1, waiting for transfers between devices, per_device(): lax.ppermute(total, 'wave', [(i, i ^ step) for i in range(wave_total)])  1.17 us
  transfers between devices with their start and end apart: 7, of which 4 were waited for; matrix products, arithmetic and copies ran while one was open for 0% of the time, Pallas kernels for 13%

profile of v28, /device:TPU:0, one launch (start us, length us, event | category | flops | bytes accessed | tf_op | source)
XLA Modules:
  0.0 34.8 jit_solution(6478793140619346667)
XLA Ops:
  0.0 4.0 %collective-permute-start = (bf16[256,256]{1,0:T(8,128)(2,1)}, bf16[256,256]{1,0:T(8,128)(2,1)S(1)}, u32[]{:S(2)}, u32[]{:S(2)}) collective-permute-start(bf16[256,256]{1,0:T(8,128)(2,1)} %bitcast.10), channel_id=1, source_target_pairs={{0,16},{2,18},{4,20},{6,22},{8,24},{10,26},{12,28},{14,30},{16,0},... | collective-permute-start | bytes 393224 | tf_op jit(solution)/shard_map/ppermute | solution.py:193
  4.0 2.2 %shard_map.65 = (bf16[136,256]{1,0:T(8,128)(2,1)}, bf16[136,256]{1,0:T(8,128)(2,1)S(1)}, bf16[136,256]{1,0:T(8,128)(2,1)S(1)}, bf16[136,256]{1,0:T(8,128)(2,1)S(1)}, bf16[4,136,256]{2,1,0:T(8,128)(2,1)S(1)}) custom-call(s32[1]{0:T(128)} %bitcast.1.me_ref, bf16[512,256]{1,0:T(8,128)(2,1)} %src_hbm.1, bf16[4,128]{1,0:T(4,128)(2,1)} %bitcast.9, ...), custom_call_target="tpu_custom_call" | custom-call | tf_op jit(solution)/shard_map/pallas_call | solution.py:197
  6.2 0.7 %shard_map.66 = bf16[4,136,256]{2,1,0:T(8,128)(2,1)} custom-call(bf16[4,136,256]{2,1,0:T(8,128)(2,1)S(1)} %get-tuple-element.13.near_ref), custom_call_target="tpu_custom_call" | custom-call | tf_op jit(solution)/shard_map/pallas_call | solution.py:218
  7.0 3.8 %all-to-all-start = ((bf16[4,136,256]{2,1,0:T(8,128)(2,1)}), bf16[4,136,256]{2,1,0:T(8,128)(2,1)S(1)}, u32[]{:S(2)}, u32[]{:S(2)}) async-start(bf16[4,136,256]{2,1,0:T(8,128)(2,1)} %shard_map.66), calls=%async_computation | async-start | bytes 557056 | tf_op jit(solution)/shard_map/all_to_all | solution.py:226
  10.8 3.9 %collective-permute-start.1 = (bf16[136,256]{1,0:T(8,128)(2,1)}, bf16[136,256]{1,0:T(8,128)(2,1)S(1)}, u32[]{:S(2)}, u32[]{:S(2)}) collective-permute-start(bf16[136,256]{1,0:T(8,128)(2,1)} %get-tuple-element.14), channel_id=1, source_target_pairs={{0,14},{2,12},{4,10},{6,8},{8,6},{10,4},{12,2},{14,0},{16,30},{18,... | collective-permute-start | bytes 208904 | tf_op jit(solution)/shard_map/ppermute | solution.py:217
  14.6 0.5 %collective-permute-start.2 = (bf16[136,256]{1,0:T(8,128)(2,1)S(1)}, bf16[136,256]{1,0:T(8,128)(2,1)S(1)}, u32[]{:S(2)}, u32[]{:S(2)}) collective-permute-start(bf16[136,256]{1,0:T(8,128)(2,1)S(1)} %get-tuple-element.15), channel_id=1, source_target_pairs={{0,2},{2,0},{4,6},{6,4},{8,10},{10,8},{12,14},{14,12},{16,18},{18,... | collective-permute-start | bytes 208904 | tf_op jit(solution)/shard_map/ppermute | solution.py:217
  15.2 1.5 %collective-permute-start.3 = (bf16[136,256]{1,0:T(8,128)(2,1)S(1)}, bf16[136,256]{1,0:T(8,128)(2,1)S(1)}, u32[]{:S(2)}, u32[]{:S(2)}) collective-permute-start(bf16[136,256]{1,0:T(8,128)(2,1)S(1)} %get-tuple-element.16), channel_id=1, source_target_pairs={{0,4},{2,6},{4,0},{6,2},{8,12},{10,14},{12,8},{14,10},{16,20},{18,... | collective-permute-start | bytes 208904 | tf_op jit(solution)/shard_map/ppermute | solution.py:217
  16.6 0.0 collective-permute-start.4
  16.6 0.0 collective-permute-done.arrived_ref
  16.6 1.7 %shard_map.64 = (bf16[2,256,512]{2,1,0:T(8,128)(2,1)S(1)}, bf16[256,4096]{1,0:T(8,128)(2,1)S(1)}) custom-call(bf16[256,256]{1,0:T(8,128)(2,1)S(1)} %collective-permute-done.arrived_ref, bf16[256,256]{1,0:T(8,128)(2,1)} %bitcast.11, bf16[256,4096]{1,0:T(8,128)(2,1)} %line_hbm.1), custom_call_target="tpu_custom_call" | custom-call | flops 10000000000 | bytes 262144 | tf_op jit(solution)/shard_map/pallas_call | solution.py:229
  18.3 1.5 %collective-permute-done.1.refs_0_ = bf16[136,256]{1,0:T(8,128)(2,1)S(1)} collective-permute-done((bf16[136,256]{1,0:T(8,128)(2,1)}, bf16[136,256]{1,0:T(8,128)(2,1)S(1)}, u32[]{:S(2)}, u32[]{:S(2)}) %collective-permute-start.1) | collective-permute-done | bytes 69664 | tf_op jit(solution)/shard_map/ppermute | solution.py:217
  19.9 0.0 collective-permute-done.2.refs_1_
  19.9 0.4 %collective-permute-done.3.refs_2_ = bf16[136,256]{1,0:T(8,128)(2,1)S(1)} collective-permute-done((bf16[136,256]{1,0:T(8,128)(2,1)S(1)}, bf16[136,256]{1,0:T(8,128)(2,1)S(1)}, u32[]{:S(2)}, u32[]{:S(2)}) %collective-permute-start.3) | collective-permute-done | bytes 69664 | tf_op jit(solution)/shard_map/ppermute | solution.py:217
  20.3 0.6 %collective-permute-done.4.refs_3_ = bf16[136,256]{1,0:T(8,128)(2,1)S(1)} collective-permute-done((bf16[136,256]{1,0:T(8,128)(2,1)S(1)}, bf16[136,256]{1,0:T(8,128)(2,1)S(1)}, u32[]{:S(2)}, u32[]{:S(2)}) %collective-permute-start.4) | collective-permute-done | bytes 69664 | tf_op jit(solution)/shard_map/ppermute | solution.py:217
  21.0 0.0 all-to-all-done.near_ref
  21.0 1.0 %shard_map.67 = bf16[256,256]{1,0:T(8,128)(2,1)S(1)} custom-call(bf16[2,256,512]{2,1,0:T(8,128)(2,1)S(1)} %get-tuple-element.12.powers_ref, bf16[4,136,256]{2,1,0:T(8,128)(2,1)S(1)} %all-to-all-done.near_ref, bf16[136,256]{1,0:T(8,128)(2,1)S(1)} %collective-permute-done.1.refs_0_, bf16[136,256]{1,0:T(8,128)(2,1)S(1)} %collective-permute-done.2.refs_1_, ...), custom_call_target="tpu_custom_call" | custom-call | tf_op jit(solution)/shard_map/pallas_call | solution.py:244
  21.9 10.4 %all_to_all.10 = bf16[16,16,256]{2,1,0:T(8,128)(2,1)S(1)} all-to-all(bf16[16,16,256]{2,1,0:T(8,128)(2,1)S(1)} %bitcast.6), channel_id=1, replica_groups=mesh['bin'=16,'wave'=2] {'bin'}, dimensions={0} | all-to-all | bytes 262144 | tf_op jit(solution)/shard_map/all_to_all | solution.py:251
  32.4 0.1 collective-permute-start.5
  32.5 1.2 %collective-permute-done.5.theirs_ref = f32[16,256]{1,0:T(8,128)S(1)} collective-permute-done((f32[16,256]{1,0:T(8,128)S(1)}, f32[16,256]{1,0:T(8,128)S(1)}, u32[]{:S(2)}, u32[]{:S(2)}) %collective-permute-start.5) | collective-permute-done | bytes 16416 | tf_op jit(solution)/shard_map/ppermute | solution.py:263
  33.7 1.1 %shard_map.68 = f32[16,4096]{1,0:T(8,128)} custom-call(f32[16,256]{1,0:T(8,128)S(1)} %convert_reduce_fusion.mine_ref, f32[16,256]{1,0:T(8,128)S(1)} %collective-permute-done.5.theirs_ref, bf16[256,4096]{1,0:T(8,128)(2,1)S(1)} %get-tuple-element.18.line_ref), custom_call_target="tpu_custom_call" | custom-call | tf_op jit(solution)/shard_map/pallas_call | solution.py:266
  (1 shorter events, 0.0 us)
Async XLA Ops:
  0.0 16.6 %collective-permute-start = (bf16[256,256]{1,0:T(8,128)(2,1)}, bf16[256,256]{1,0:T(8,128)(2,1)S(1)}, u32[]{:S(2)}, u32[]{:S(2)}) collective-permute-start(bf16[256,256]{1,0:T(8,128)(2,1)} %bitcast.10), channel_id=1, source_target_pairs={{0,16},{2,18},{4,20},{6,22},{8,24},{10,26},{12,28},{14,30},{16,0},... | collective-permute-start | bytes 393224 | tf_op jit(solution)/shard_map/ppermute | solution.py:193
  7.0 14.0 %all-to-all-start = ((bf16[4,136,256]{2,1,0:T(8,128)(2,1)}), bf16[4,136,256]{2,1,0:T(8,128)(2,1)S(1)}, u32[]{:S(2)}, u32[]{:S(2)}) async-start(bf16[4,136,256]{2,1,0:T(8,128)(2,1)} %shard_map.66), calls=%async_computation | async-start | bytes 557056 | tf_op jit(solution)/shard_map/all_to_all | solution.py:226
  10.8 9.1 %collective-permute-start.1 = (bf16[136,256]{1,0:T(8,128)(2,1)}, bf16[136,256]{1,0:T(8,128)(2,1)S(1)}, u32[]{:S(2)}, u32[]{:S(2)}) collective-permute-start(bf16[136,256]{1,0:T(8,128)(2,1)} %get-tuple-element.14), channel_id=1, source_target_pairs={{0,14},{2,12},{4,10},{6,8},{8,6},{10,4},{12,2},{14,0},{16,30},{18,... | collective-permute-start | bytes 208904 | tf_op jit(solution)/shard_map/ppermute | solution.py:217
  14.6 5.3 %collective-permute-start.2 = (bf16[136,256]{1,0:T(8,128)(2,1)S(1)}, bf16[136,256]{1,0:T(8,128)(2,1)S(1)}, u32[]{:S(2)}, u32[]{:S(2)}) collective-permute-start(bf16[136,256]{1,0:T(8,128)(2,1)S(1)} %get-tuple-element.15), channel_id=1, source_target_pairs={{0,2},{2,0},{4,6},{6,4},{8,10},{10,8},{12,14},{14,12},{16,18},{18,... | collective-permute-start | bytes 208904 | tf_op jit(solution)/shard_map/ppermute | solution.py:217
  15.2 5.2 %collective-permute-start.3 = (bf16[136,256]{1,0:T(8,128)(2,1)S(1)}, bf16[136,256]{1,0:T(8,128)(2,1)S(1)}, u32[]{:S(2)}, u32[]{:S(2)}) collective-permute-start(bf16[136,256]{1,0:T(8,128)(2,1)S(1)} %get-tuple-element.16), channel_id=1, source_target_pairs={{0,4},{2,6},{4,0},{6,2},{8,12},{10,14},{12,8},{14,10},{16,20},{18,... | collective-permute-start | bytes 208904 | tf_op jit(solution)/shard_map/ppermute | solution.py:217
  16.6 4.3 %collective-permute-start.4 = (bf16[136,256]{1,0:T(8,128)(2,1)S(1)}, bf16[136,256]{1,0:T(8,128)(2,1)S(1)}, u32[]{:S(2)}, u32[]{:S(2)}) collective-permute-start(bf16[136,256]{1,0:T(8,128)(2,1)S(1)} %get-tuple-element.17), channel_id=1, source_target_pairs={{0,8},{2,10},{4,12},{6,14},{8,0},{10,2},{12,4},{14,6},{16,24},{18,... | collective-permute-start | bytes 208904 | tf_op jit(solution)/shard_map/ppermute | solution.py:217
  32.4 1.2 %collective-permute-start.5 = (f32[16,256]{1,0:T(8,128)S(1)}, f32[16,256]{1,0:T(8,128)S(1)}, u32[]{:S(2)}, u32[]{:S(2)}) collective-permute-start(f32[16,256]{1,0:T(8,128)S(1)} %convert_reduce_fusion.mine_ref), channel_id=1, source_target_pairs={{0,1},{1,0},{2,3},{3,2},{4,5},{5,4},{6,7},{7,6},{8,9},{9,8},{10,11... | collective-permute-start | bytes 49160 | tf_op jit(solution)/shard_map/ppermute | solution.py:263

commit v29 on v28

--- a/solution.py
+++ b/solution.py
@@ -118,7 +118,11 @@
     copies[1].wait()
 
 
-def level_kernel(plan, rays, powers_ref, near_ref, *refs):
+def token_kernel(*refs):
+    refs[-1][...] = jnp.zeros_like(refs[-1])
+
+
+def level_kernel(plan, rays, token_ref, powers_ref, near_ref, *refs):
     out_ref, block, levels = refs[-1], plan.block, near_ref.shape[2]
     got = list(refs[:-1]) + [near_ref.at[i] for i in range(near_ref.shape[0])]
     meta = [g[block:, :block].astype(F32) for g in got]
@@ -239,15 +243,25 @@
             flops=OVERLAP_FLOPS, bytes_accessed=4 * arrived.size, transcendentals=0
         ),
     )(arrived, in_hbm(rate_tables[0]), in_hbm(line_table))
+    token = pl.pallas_call(
+        token_kernel,
+        out_shape=jax.ShapeDtypeStruct((8, LANES), F32),
+        in_specs=[vmem] * len(far),
+        out_specs=vmem,
+        compiler_params=params,
+        cost_estimate=pl.CostEstimate(
+            flops=OVERLAP_FLOPS, bytes_accessed=4 * arrived.size, transcendentals=0
+        ),
+    )(*far)
     ray_rows = RAY_DEV
     rays = ray_rows * bin_total
     partial_sums = pl.pallas_call(
         functools.partial(level_kernel, plan, rays),
         out_shape=jax.ShapeDtypeStruct((rays, levels), BF16),
-        in_specs=[vmem] * (2 + len(far)),
+        in_specs=[vmem] * (3 + len(far)),
         out_specs=vmem,
         compiler_params=params,
-    )(powers, got, *far)
+    )(token, powers, got, *far)
     held = lax.all_to_all(
         partial_sums.reshape(bin_total, ray_rows, levels),
         "bin",

time: 35.1 us -> 36.7 us (1.046)
  waiting for transfers between devices: 3.78 us -> 5.61 us
  blocking collectives: 10.4 us -> 11.7 us
  starting transfers between devices: 13.8 us -> 12.9 us
  Pallas kernels: 6.69 us -> 6.06 us
    all_to_all x1, waiting for transfers between devices: 0.01 us -> 3.36 us  [per_device(): lax.all_to_all(staged, 'bin', split_axis=0, concat_axis=0, tiled=True, ax...]
    ppermute x4, waiting for transfers between devices: 2.61 us -> 0.01 us  [per_device(): lax.ppermute(x, 'bin', plan.moves(k))]
    all_to_all x1, blocking collectives: 10.4 us -> 11.7 us  [per_device(): lax.all_to_all(partial_sums.reshape(bin_total, ray_rows, levels), 'bin',...]
    ppermute x1, starting transfers between devices: 4.04 us -> 2.88 us  [per_device(): arrived = lax.ppermute(rate_tables[0], 'bin', plan.table_moves())]
    ppermute x1, waiting for transfers between devices: 0.01 us -> 1.07 us  [per_device(): arrived = lax.ppermute(rate_tables[0], 'bin', plan.table_moves())]
    pallas_call x1, Pallas kernels: 2.19 us -> 1.56 us  [per_device(): pl.pallas_call(functools.partial(pack_kernel, plan), out_shape=[jax.Shape...]
  transfers between devices with their start and end apart: 7 -> 7, of which waited for: 4 -> 3; matrix products, arithmetic and copies ran while one was open for 0% -> 0% of each run, Pallas kernels for 13% -> 7%
where the time goes in v29:
time: 36.7 us; the launch traced here: 36.4 us
  starting transfers between devices  12.9 us (35%)
  blocking collectives  11.7 us (32%)
  Pallas kernels  6.06 us (17%)
  waiting for transfers between devices  5.61 us (15%)
    all_to_all x1, blocking collectives, per_device(): lax.all_to_all(partial_sums.reshape(bin_total, ray_rows, levels), 'bin',...  11.7 us
    ppermute x4, starting transfers between devices, per_device(): lax.ppermute(x, 'bin', plan.moves(k))  6.18 us
    all_to_all x1, starting transfers between devices, per_device(): lax.all_to_all(staged, 'bin', split_axis=0, concat_axis=0, tiled=True, ax...  3.81 us
    all_to_all x1, waiting for transfers between devices, per_device(): lax.all_to_all(staged, 'bin', split_axis=0, concat_axis=0, tiled=True, ax...  3.36 us
    ppermute x1, starting transfers between devices, per_device(): arrived = lax.ppermute(rate_tables[0], 'bin', plan.table_moves())  2.88 us
    pallas_call x1, Pallas kernels, per_device(): pl.pallas_call(window_kernel, out_shape=[jax.ShapeDtypeStruct(a, BF16) fo...  1.69 us
    pallas_call x1, Pallas kernels, per_device(): pl.pallas_call(functools.partial(pack_kernel, plan), out_shape=[jax.Shape...  1.56 us
    ppermute x1, waiting for transfers between devices, per_device(): lax.ppermute(total, 'wave', [(i, i ^ step) for i in range(wave_total)])  1.17 us
  transfers between devices with their start and end apart: 7, of which 3 were waited for; matrix products, arithmetic and copies ran while one was open for 0% of the time, Pallas kernels for 7%

profile of v29, /device:TPU:0, one launch (start us, length us, event | category | flops | bytes accessed | tf_op | source)
XLA Modules:
  0.0 36.4 jit_solution(10130909227131860197)
XLA Ops:
  0.0 1.6 %shard_map.64 = (bf16[136,256]{1,0:T(8,128)(2,1)S(1)}, bf16[136,256]{1,0:T(8,128)(2,1)S(1)}, bf16[136,256]{1,0:T(8,128)(2,1)S(1)}, bf16[136,256]{1,0:T(8,128)(2,1)S(1)}, bf16[4,136,256]{2,1,0:T(8,128)(2,1)S(1)}) custom-call(s32[1]{0:T(128)} %bitcast.me_ref, bf16[512,256]{1,0:T(8,128)(2,1)} %src_hbm.1, bf16[4,128]{1,0:T(4,128)(2,1)} %bitcast.9, ...), custom_call_target="tpu_custom_call" | custom-call | tf_op jit(solution)/shard_map/pallas_call | solution.py:201
  1.6 5.0 %collective-permute-start = (bf16[136,256]{1,0:T(8,128)(2,1)S(1)}, bf16[136,256]{1,0:T(8,128)(2,1)S(1)}, u32[]{:S(2)}, u32[]{:S(2)}) collective-permute-start(bf16[136,256]{1,0:T(8,128)(2,1)S(1)} %get-tuple-element.12), channel_id=1, source_target_pairs={{0,14},{2,12},{4,10},{6,8},{8,6},{10,4},{12,2},{14,0},{16,30},{18,... | collective-permute-start | bytes 208904 | tf_op jit(solution)/shard_map/ppermute | solution.py:221
  6.5 0.5 %collective-permute-start.1 = (bf16[136,256]{1,0:T(8,128)(2,1)S(1)}, bf16[136,256]{1,0:T(8,128)(2,1)S(1)}, u32[]{:S(2)}, u32[]{:S(2)}) collective-permute-start(bf16[136,256]{1,0:T(8,128)(2,1)S(1)} %get-tuple-element.13), channel_id=1, source_target_pairs={{0,2},{2,0},{4,6},{6,4},{8,10},{10,8},{12,14},{14,12},{16,18},{18,... | collective-permute-start | bytes 208904 | tf_op jit(solution)/shard_map/ppermute | solution.py:221
  7.1 0.5 %collective-permute-start.2 = (bf16[136,256]{1,0:T(8,128)(2,1)S(1)}, bf16[136,256]{1,0:T(8,128)(2,1)S(1)}, u32[]{:S(2)}, u32[]{:S(2)}) collective-permute-start(bf16[136,256]{1,0:T(8,128)(2,1)S(1)} %get-tuple-element.14), channel_id=1, source_target_pairs={{0,4},{2,6},{4,0},{6,2},{8,12},{10,14},{12,8},{14,10},{16,20},{18,... | collective-permute-start | bytes 208904 | tf_op jit(solution)/shard_map/ppermute | solution.py:221
  7.6 0.2 collective-permute-start.3
  7.7 2.9 %collective-permute-start.4 = (bf16[256,256]{1,0:T(8,128)(2,1)}, bf16[256,256]{1,0:T(8,128)(2,1)S(1)}, u32[]{:S(2)}, u32[]{:S(2)}) collective-permute-start(bf16[256,256]{1,0:T(8,128)(2,1)} %bitcast.10), channel_id=1, source_target_pairs={{0,16},{2,18},{4,20},{6,22},{8,24},{10,26},{12,28},{14,30},{16,0},... | collective-permute-start | bytes 393224 | tf_op jit(solution)/shard_map/ppermute | solution.py:197
  10.6 0.7 %shard_map.67 = bf16[4,136,256]{2,1,0:T(8,128)(2,1)} custom-call(bf16[4,136,256]{2,1,0:T(8,128)(2,1)S(1)} %get-tuple-element.17.near_ref), custom_call_target="tpu_custom_call" | custom-call | tf_op jit(solution)/shard_map/pallas_call | solution.py:222
  11.3 3.8 %all-to-all-start = ((bf16[4,136,256]{2,1,0:T(8,128)(2,1)}), bf16[4,136,256]{2,1,0:T(8,128)(2,1)S(1)}, u32[]{:S(2)}, u32[]{:S(2)}) async-start(bf16[4,136,256]{2,1,0:T(8,128)(2,1)} %shard_map.67), calls=%async_computation | async-start | bytes 557056 | tf_op jit(solution)/shard_map/all_to_all | solution.py:230
  15.2 0.0 collective-permute-done.refs_0_
  15.2 0.0 collective-permute-done.1.refs_1_
  15.2 0.0 collective-permute-done.2.refs_2_
  15.2 0.0 collective-permute-done.3.refs_3_
  15.2 1.1 %collective-permute-done.4.arrived_ref = bf16[256,256]{1,0:T(8,128)(2,1)S(1)} collective-permute-done((bf16[256,256]{1,0:T(8,128)(2,1)}, bf16[256,256]{1,0:T(8,128)(2,1)S(1)}, u32[]{:S(2)}, u32[]{:S(2)}) %collective-permute-start.4) | collective-permute-done | bytes 131104 | tf_op jit(solution)/shard_map/ppermute | solution.py:197
  16.3 1.7 %shard_map.66 = (bf16[2,256,512]{2,1,0:T(8,128)(2,1)S(1)}, bf16[256,4096]{1,0:T(8,128)(2,1)S(1)}) custom-call(bf16[256,256]{1,0:T(8,128)(2,1)S(1)} %collective-permute-done.4.arrived_ref, bf16[256,256]{1,0:T(8,128)(2,1)} %bitcast.11, bf16[256,4096]{1,0:T(8,128)(2,1)} %line_hbm.1), custom_call_target="tpu_custom_call" | custom-call | flops 10000000000 | bytes 262144 | tf_op jit(solution)/shard_map/pallas_call | solution.py:233
  18.0 3.4 %all-to-all-done.near_ref = bf16[4,136,256]{2,1,0:T(8,128)(2,1)S(1)} async-done(((bf16[4,136,256]{2,1,0:T(8,128)(2,1)}), bf16[4,136,256]{2,1,0:T(8,128)(2,1)S(1)}, u32[]{:S(2)}, u32[]{:S(2)}) %all-to-all-start) | async-done | bytes 278560 | tf_op jit(solution)/shard_map/all_to_all | solution.py:230
  21.3 1.0 %shard_map.68 = bf16[256,256]{1,0:T(8,128)(2,1)S(1)} custom-call(f32[8,128]{1,0:T(8,128)S(1)} %shard_map.65.token_ref, bf16[2,256,512]{2,1,0:T(8,128)(2,1)S(1)} %get-tuple-element.16.powers_ref, bf16[4,136,256]{2,1,0:T(8,128)(2,1)S(1)} %all-to-all-done.near_ref, bf16[136,256]{1,0:T(8,128)(2,1)S(1)} %collective-permute-done.refs_0_, ...), custom_call_target="tpu_custom_call" | custom-call | tf_op jit(solution)/shard_map/pallas_call | solution.py:258
  22.3 11.7 %all_to_all.10 = bf16[16,16,256]{2,1,0:T(8,128)(2,1)S(1)} all-to-all(bf16[16,16,256]{2,1,0:T(8,128)(2,1)S(1)} %bitcast.6), channel_id=1, replica_groups=mesh['bin'=16,'wave'=2] {'bin'}, dimensions={0} | all-to-all | bytes 262144 | tf_op jit(solution)/shard_map/all_to_all | solution.py:265
  34.0 0.1 collective-permute-start.5
  34.1 1.2 %collective-permute-done.5.theirs_ref = f32[16,256]{1,0:T(8,128)S(1)} collective-permute-done((f32[16,256]{1,0:T(8,128)S(1)}, f32[16,256]{1,0:T(8,128)S(1)}, u32[]{:S(2)}, u32[]{:S(2)}) %collective-permute-start.5) | collective-permute-done | bytes 16416 | tf_op jit(solution)/shard_map/ppermute | solution.py:277
  35.3 1.1 %shard_map.69 = f32[16,4096]{1,0:T(8,128)} custom-call(f32[16,256]{1,0:T(8,128)S(1)} %convert_reduce_fusion.mine_ref, f32[16,256]{1,0:T(8,128)S(1)} %collective-permute-done.5.theirs_ref, bf16[256,4096]{1,0:T(8,128)(2,1)S(1)} %get-tuple-element.18.line_ref), custom_call_target="tpu_custom_call" | custom-call | tf_op jit(solution)/shard_map/pallas_call | solution.py:280
  (2 shorter events, 0.0 us)
Async XLA Ops:
  1.6 13.6 %collective-permute-start = (bf16[136,256]{1,0:T(8,128)(2,1)S(1)}, bf16[136,256]{1,0:T(8,128)(2,1)S(1)}, u32[]{:S(2)}, u32[]{:S(2)}) collective-permute-start(bf16[136,256]{1,0:T(8,128)(2,1)S(1)} %get-tuple-element.12), channel_id=1, source_target_pairs={{0,14},{2,12},{4,10},{6,8},{8,6},{10,4},{12,2},{14,0},{16,30},{18,... | collective-permute-start | bytes 208904 | tf_op jit(solution)/shard_map/ppermute | solution.py:221
  6.5 8.6 %collective-permute-start.1 = (bf16[136,256]{1,0:T(8,128)(2,1)S(1)}, bf16[136,256]{1,0:T(8,128)(2,1)S(1)}, u32[]{:S(2)}, u32[]{:S(2)}) collective-permute-start(bf16[136,256]{1,0:T(8,128)(2,1)S(1)} %get-tuple-element.13), channel_id=1, source_target_pairs={{0,2},{2,0},{4,6},{6,4},{8,10},{10,8},{12,14},{14,12},{16,18},{18,... | collective-permute-start | bytes 208904 | tf_op jit(solution)/shard_map/ppermute | solution.py:221
  7.1 8.1 %collective-permute-start.2 = (bf16[136,256]{1,0:T(8,128)(2,1)S(1)}, bf16[136,256]{1,0:T(8,128)(2,1)S(1)}, u32[]{:S(2)}, u32[]{:S(2)}) collective-permute-start(bf16[136,256]{1,0:T(8,128)(2,1)S(1)} %get-tuple-element.14), channel_id=1, source_target_pairs={{0,4},{2,6},{4,0},{6,2},{8,12},{10,14},{12,8},{14,10},{16,20},{18,... | collective-permute-start | bytes 208904 | tf_op jit(solution)/shard_map/ppermute | solution.py:221
  7.6 7.6 %collective-permute-start.3 = (bf16[136,256]{1,0:T(8,128)(2,1)S(1)}, bf16[136,256]{1,0:T(8,128)(2,1)S(1)}, u32[]{:S(2)}, u32[]{:S(2)}) collective-permute-start(bf16[136,256]{1,0:T(8,128)(2,1)S(1)} %get-tuple-element.15), channel_id=1, source_target_pairs={{0,8},{2,10},{4,12},{6,14},{8,0},{10,2},{12,4},{14,6},{16,24},{18,... | collective-permute-start | bytes 208904 | tf_op jit(solution)/shard_map/ppermute | solution.py:221
  7.7 8.5 %collective-permute-start.4 = (bf16[256,256]{1,0:T(8,128)(2,1)}, bf16[256,256]{1,0:T(8,128)(2,1)S(1)}, u32[]{:S(2)}, u32[]{:S(2)}) collective-permute-start(bf16[256,256]{1,0:T(8,128)(2,1)} %bitcast.10), channel_id=1, source_target_pairs={{0,16},{2,18},{4,20},{6,22},{8,24},{10,26},{12,28},{14,30},{16,0},... | collective-permute-start | bytes 393224 | tf_op jit(solution)/shard_map/ppermute | solution.py:197
  11.3 10.0 %all-to-all-start = ((bf16[4,136,256]{2,1,0:T(8,128)(2,1)}), bf16[4,136,256]{2,1,0:T(8,128)(2,1)S(1)}, u32[]{:S(2)}, u32[]{:S(2)}) async-start(bf16[4,136,256]{2,1,0:T(8,128)(2,1)} %shard_map.67), calls=%async_computation | async-start | bytes 557056 | tf_op jit(solution)/shard_map/all_to_all | solution.py:230
  34.0 1.2 %collective-permute-start.5 = (f32[16,256]{1,0:T(8,128)S(1)}, f32[16,256]{1,0:T(8,128)S(1)}, u32[]{:S(2)}, u32[]{:S(2)}) collective-permute-start(f32[16,256]{1,0:T(8,128)S(1)} %convert_reduce_fusion.mine_ref), channel_id=1, source_target_pairs={{0,1},{1,0},{2,3},{3,2},{4,5},{5,4},{6,7},{7,6},{8,9},{9,8},{10,11... | collective-permute-start | bytes 49160 | tf_op jit(solution)/shard_map/ppermute | solution.py:277

commit v30 on v21

--- a/solution.py
+++ b/solution.py
@@ -86,24 +86,37 @@
         out[t, block:, :block] = moved[t * META_ROWS : (t + 1) * META_ROWS]
 
 
-def window_kernel(arrived_ref, table_hbm, line_hbm, powers_ref, line_ref, sems):
+def window_kernel(core_ref, arrived_ref, table_hbm, line_hbm, powers_ref, line_ref, sems):
     levels = arrived_ref.shape[0]
-    copies = [
-        pltpu.make_async_copy(table_hbm, powers_ref.at[0, :, pl.ds(0, levels)], sems.at[0]),
-        pltpu.make_async_copy(line_hbm, line_ref, sems.at[1]),
-    ]
-    for copy in copies:
-        copy.start()
+    even = core_ref[0] % 2 == 0
+    table_copy = pltpu.make_async_copy(table_hbm, powers_ref.at[0, :, pl.ds(0, levels)], sems.at[0])
+    line_copy = pltpu.make_async_copy(line_hbm, line_ref, sems.at[1])
+    table_copy.start()
+
+    @pl.when(even)
+    def _():
+        line_copy.start()
+
     powers_ref[1, :, :levels] = arrived_ref[...]
-    copies[0].wait()
+    table_copy.wait()
     for part in range(2):
         table = powers_ref[part, :, :levels]
         square = jnp.dot(table, table, preferred_element_type=F32)
         powers_ref[part, :, levels:] = square.astype(BF16)
-    copies[1].wait()
-
-
-def level_kernel(plan, rays, got_ref, powers_ref, out_ref):
+
+    @pl.when(even)
+    def _():
+        line_copy.wait()
+
+
+def level_kernel(plan, rays, core_ref, got_ref, powers_ref, line_hbm, out_ref, line_ref, sem):
+    odd = core_ref[0] % 2 == 1
+    line_copy = pltpu.make_async_copy(line_hbm, line_ref, sem)
+
+    @pl.when(odd)
+    def _():
+        line_copy.start()
+
     targets, block = plan.targets, plan.block
     meta = [got_ref[s, block:, :block].astype(F32) for s in range(targets)]
     columns = [jnp.transpose(m[:8]) for m in meta]
@@ -123,8 +136,20 @@
         total = total + jnp.dot(pick, pops, preferred_element_type=F32)
     out_ref[...] = total.astype(BF16)
 
-
-def line_kernel(mine_ref, theirs_ref, line_ref, out_hbm, out_ref, sems):
+    @pl.when(odd)
+    def _():
+        line_copy.wait()
+
+
+def line_kernel(core_ref, mine_ref, theirs_ref, even_ref, odd_ref, out_hbm, out_ref, sems):
+    for parity, line_ref in ((0, even_ref), (1, odd_ref)):
+
+        @pl.when(core_ref[0] % 2 == parity)
+        def _(line_ref=line_ref):
+            line_product(mine_ref, theirs_ref, line_ref, out_hbm, out_ref, sems)
+
+
+def line_product(mine_ref, theirs_ref, line_ref, out_hbm, out_ref, sems):
     sums = mine_ref[...] + theirs_ref[...]
     rows = sums.shape[0]
     high = sums.astype(BF16)
@@ -197,28 +222,32 @@
     got = lax.all_to_all(
         outgoing, "bin", split_axis=0, concat_axis=0, tiled=True, axis_index_groups=plan.halves()
     )
-    powers, held_line = pl.pallas_call(
+    core = lax.axis_index("wave").astype(I32).reshape(1)
+    powers, even_line = pl.pallas_call(
         window_kernel,
         out_shape=[
             jax.ShapeDtypeStruct(a, BF16) for a in ((2, levels, 2 * levels), line_table.shape)
         ],
-        in_specs=[vmem, hbm, hbm],
+        in_specs=[smem, vmem, hbm, hbm],
         out_specs=[vmem] * 2,
         scratch_shapes=[pltpu.SemaphoreType.DMA((2,))],
         compiler_params=params,
         cost_estimate=pl.CostEstimate(
             flops=OVERLAP_FLOPS, bytes_accessed=4 * arrived.size, transcendentals=0
         ),
-    )(arrived, in_hbm(rate_tables[0]), in_hbm(line_table))
+    )(core, arrived, in_hbm(rate_tables[0]), in_hbm(line_table))
     ray_rows = RAY_DEV
     rays = ray_rows * bin_total
-    partial_sums = pl.pallas_call(
+    partial_sums, odd_line = pl.pallas_call(
         functools.partial(level_kernel, plan, rays),
-        out_shape=jax.ShapeDtypeStruct((rays, levels), BF16),
-        in_specs=[vmem] * 2,
-        out_specs=vmem,
-        compiler_params=params,
-    )(got, powers)
+        out_shape=[
+            jax.ShapeDtypeStruct(a, BF16) for a in ((rays, levels), line_table.shape)
+        ],
+        in_specs=[smem, vmem, vmem, hbm],
+        out_specs=[vmem] * 2,
+        scratch_shapes=[pltpu.SemaphoreType.DMA],
+        compiler_params=params,
+    )(core, got, powers, in_hbm(line_table))
     held = lax.all_to_all(
         partial_sums.reshape(bin_total, ray_rows, levels),
         "bin",
@@ -237,11 +266,11 @@
     return pl.pallas_call(
         line_kernel,
         out_shape=jax.ShapeDtypeStruct(out_shape, F32),
-        in_specs=[vmem, vmem, vmem],
+        in_specs=[smem] + [vmem] * 4,
         out_specs=hbm,
         scratch_shapes=[pltpu.VMEM(out_shape, F32), pltpu.SemaphoreType.DMA((LINE_CHUNKS,))],
         compiler_params=params,
-    )(total, theirs, held_line)
+    )(core, total, theirs, even_line, odd_line)
 
 
 def solution(mesh):

time: 34.6 us -> 35 us (1.012)
  blocking collectives: 10.6 us -> 11.1 us
    all_to_all x1, blocking collectives: 10.6 us -> 11.1 us  [per_device(): lax.all_to_all(partial_sums.reshape(bin_total, ray_rows, levels), 'bin',...]
where the time goes in v30:
time: 35 us; the launch traced here: 34.8 us
  blocking collectives  11.1 us (32%)
  starting transfers between devices  8.86 us (25%)
  waiting for transfers between devices  8.61 us (25%)
  Pallas kernels  6.16 us (18%)
    all_to_all x1, blocking collectives, per_device(): lax.all_to_all(partial_sums.reshape(bin_total, ray_rows, levels), 'bin',...  11.1 us
    all_to_all x1, waiting for transfers between devices, per_device(): lax.all_to_all(outgoing, 'bin', split_axis=0, concat_axis=0, tiled=True,...  7.44 us
    all_to_all x1, starting transfers between devices, per_device(): lax.all_to_all(outgoing, 'bin', split_axis=0, concat_axis=0, tiled=True,...  4.75 us
    ppermute x1, starting transfers between devices, per_device(): arrived = lax.ppermute(rate_tables[0], 'bin', plan.table_moves())  4.04 us
    pallas_call x1, Pallas kernels, per_device(): pl.pallas_call(functools.partial(pack_kernel, plan), out_shape=jax.ShapeD...  2.36 us
    pallas_call x1, Pallas kernels, per_device(): pl.pallas_call(window_kernel, out_shape=[jax.ShapeDtypeStruct(a, BF16) fo...  1.69 us
    ppermute x1, waiting for transfers between devices, per_device(): lax.ppermute(total, 'wave', [(i, i ^ step) for i in range(wave_total)])  1.17 us
    pallas_call x1, Pallas kernels, per_device(): pl.pallas_call(line_kernel, out_shape=jax.ShapeDtypeStruct(out_shape, F32...  1.13 us
  transfers between devices with their start and end apart: 3, of which 2 were waited for; matrix products, arithmetic and copies ran while one was open for 0% of the time, Pallas kernels for 12%

profile of v30, /device:TPU:0, one launch (start us, length us, event | category | flops | bytes accessed | tf_op | source)
XLA Modules:
  0.0 34.8 jit_solution(3891594595813427244)
XLA Ops:
  0.0 4.0 %collective-permute-start = (bf16[256,256]{1,0:T(8,128)(2,1)}, bf16[256,256]{1,0:T(8,128)(2,1)S(1)}, u32[]{:S(2)}, u32[]{:S(2)}) collective-permute-start(bf16[256,256]{1,0:T(8,128)(2,1)} %bitcast.11), channel_id=1, source_target_pairs={{0,16},{2,18},{4,20},{6,22},{8,24},{10,26},{12,28},{14,30},{16,0},... | collective-permute-start | bytes 393224 | tf_op jit(solution)/shard_map/ppermute | solution.py:199
  4.0 2.4 %shard_map.64 = bf16[8,136,256]{2,1,0:T(8,128)(2,1)} custom-call(s32[1]{0:T(128)} %bitcast.1.me_ref, bf16[512,256]{1,0:T(8,128)(2,1)} %src_hbm.1, bf16[4,128]{1,0:T(4,128)(2,1)} %bitcast.10, s32[1,512]{1,0:T(1,128)} %bitcast.8, s32[1,512]{1,0:T(1,128)} %bitcast.9), custom_call_target="tpu_custom_call" | custom-call | tf_op jit(solution)/shard_map/pallas_call | solution.py:202
  6.4 4.7 %all-to-all-start = ((bf16[8,136,256]{2,1,0:T(8,128)(2,1)}), bf16[8,136,256]{2,1,0:T(8,128)(2,1)S(1)}, u32[]{:S(2)}, u32[]{:S(2)}) async-start(bf16[8,136,256]{2,1,0:T(8,128)(2,1)} %shard_map.64), calls=%async_computation | async-start | bytes 1114112 | tf_op jit(solution)/shard_map/all_to_all | solution.py:222
  11.2 0.0 collective-permute-done.arrived_ref
  11.2 1.7 %shard_map.65 = (bf16[2,256,512]{2,1,0:T(8,128)(2,1)S(1)}, bf16[256,4096]{1,0:T(8,128)(2,1)S(1)}) custom-call(s32[1]{0:T(128)} %bitcast.core_ref, bf16[256,256]{1,0:T(8,128)(2,1)S(1)} %collective-permute-done.arrived_ref, bf16[256,256]{1,0:T(8,128)(2,1)} %bitcast.12, bf16[256,4096]{1,0:T(8,128)(2,1)} %line_hbm.3), custom_call_target="tpu_custom_call" | custom-call | flops 10000000000 | bytes 262144 | tf_op jit(solution)/shard_map/pallas_call | solution.py:226
  12.9 7.4 %all-to-all-done.got_ref = bf16[8,136,256]{2,1,0:T(8,128)(2,1)S(1)} async-done(((bf16[8,136,256]{2,1,0:T(8,128)(2,1)}), bf16[8,136,256]{2,1,0:T(8,128)(2,1)S(1)}, u32[]{:S(2)}, u32[]{:S(2)}) %all-to-all-start) | async-done | bytes 557088 | tf_op jit(solution)/shard_map/all_to_all | solution.py:222
  20.3 1.0 %shard_map.66 = (bf16[256,256]{1,0:T(8,128)(2,1)S(1)}, bf16[256,4096]{1,0:T(8,128)(2,1)S(1)}) custom-call(s32[1]{0:T(128)} %bitcast.core_ref, bf16[8,136,256]{2,1,0:T(8,128)(2,1)S(1)} %all-to-all-done.got_ref, bf16[2,256,512]{2,1,0:T(8,128)(2,1)S(1)} %get-tuple-element.9.powers_ref, bf16[256,4096]{1,0:T(8,128)(2,1)} %line_hbm.3), custom_call_target="tpu_custom_call" | custom-call | tf_op jit(solution)/shard_map/pallas_call | solution.py:241
  21.3 11.1 %all_to_all.10 = bf16[16,16,256]{2,1,0:T(8,128)(2,1)S(1)} all-to-all(bf16[16,16,256]{2,1,0:T(8,128)(2,1)S(1)} %bitcast.7), channel_id=1, replica_groups=mesh['bin'=16,'wave'=2] {'bin'}, dimensions={0} | all-to-all | bytes 262144 | tf_op jit(solution)/shard_map/all_to_all | solution.py:251
  32.4 0.1 collective-permute-start.1
  32.5 1.2 %collective-permute-done.1.theirs_ref = f32[16,256]{1,0:T(8,128)S(1)} collective-permute-done((f32[16,256]{1,0:T(8,128)S(1)}, f32[16,256]{1,0:T(8,128)S(1)}, u32[]{:S(2)}, u32[]{:S(2)}) %collective-permute-start.1) | collective-permute-done | bytes 16416 | tf_op jit(solution)/shard_map/ppermute | solution.py:263
  33.6 1.1 %shard_map.67 = f32[16,4096]{1,0:T(8,128)} custom-call(s32[1]{0:T(128)} %bitcast.core_ref, f32[16,256]{1,0:T(8,128)S(1)} %convert_reduce_fusion.mine_ref, f32[16,256]{1,0:T(8,128)S(1)} %collective-permute-done.1.theirs_ref, bf16[256,4096]{1,0:T(8,128)(2,1)S(1)} %get-tuple-element.11.even_ref, bf16[256,4096]{1,0:T(8,128)(2,1)S(1)} %get-tuple-element.12.odd_ref), custom_call_target="tpu_custom_call" | custom-call | tf_op jit(solution)/shard_map/pallas_call | solution.py:266
  (1 shorter events, 0.0 us)
Async XLA Ops:
  0.0 11.2 %collective-permute-start = (bf16[256,256]{1,0:T(8,128)(2,1)}, bf16[256,256]{1,0:T(8,128)(2,1)S(1)}, u32[]{:S(2)}, u32[]{:S(2)}) collective-permute-start(bf16[256,256]{1,0:T(8,128)(2,1)} %bitcast.11), channel_id=1, source_target_pairs={{0,16},{2,18},{4,20},{6,22},{8,24},{10,26},{12,28},{14,30},{16,0},... | collective-permute-start | bytes 393224 | tf_op jit(solution)/shard_map/ppermute | solution.py:199
  6.4 13.9 %all-to-all-start = ((bf16[8,136,256]{2,1,0:T(8,128)(2,1)}), bf16[8,136,256]{2,1,0:T(8,128)(2,1)S(1)}, u32[]{:S(2)}, u32[]{:S(2)}) async-start(bf16[8,136,256]{2,1,0:T(8,128)(2,1)} %shard_map.64), calls=%async_computation | async-start | bytes 1114112 | tf_op jit(solution)/shard_map/all_to_all | solution.py:222
  32.4 1.2 %collective-permute-start.1 = (f32[16,256]{1,0:T(8,128)S(1)}, f32[16,256]{1,0:T(8,128)S(1)}, u32[]{:S(2)}, u32[]{:S(2)}) collective-permute-start(f32[16,256]{1,0:T(8,128)S(1)} %convert_reduce_fusion.mine_ref), channel_id=1, source_target_pairs={{0,1},{1,0},{2,3},{3,2},{4,5},{5,4},{6,7},{7,6},{8,9},{9,8},{10,11... | collective-permute-start | bytes 49160 | tf_op jit(solution)/shard_map/ppermute | solution.py:263

commit v31 on v22

--- a/solution.py
+++ b/solution.py
@@ -12,7 +12,6 @@
 RAY_BASE = 32
 LANES = 128
 LINE_CHUNKS = 4
-LINE_PARTS = 2
 OVERLAP_FLOPS = 10**10
 VMEM_LIMIT = 32 * 1024 * 1024
 F32 = jnp.float32
@@ -30,7 +29,7 @@
 
 def pack_kernel(plan, me_ref, src_hbm, den_hbm, bin_hbm, ray_hbm, line_hbm, *rest):
     targets, block = plan.targets, plan.block
-    out, line_out, src_ref, den_ref, bin_ref, ray_ref, sems, line_sems = rest
+    out, line_out, src_ref, den_ref, bin_ref, ray_ref, sems = rest
     copies = [
         pltpu.make_async_copy(a, b, sems.at[i])
         for i, (a, b) in enumerate(
@@ -44,12 +43,24 @@
     ]
     for copy in copies:
         copy.start()
+    line_copy = pltpu.make_async_copy(line_hbm, line_out, sems.at[len(copies)])
+    even = me_ref[0] % 2 == 0
+
+    @pl.when(jnp.logical_not(even))
+    def _():
+        line_copy.start()
+
     cells, levels = src_ref.shape
     lanes = min(cells, LANES)
     earlier = (iota((lanes, lanes), 0) < iota((lanes, lanes), 1)).astype(F32).astype(BF16)
     my_half = me_ref[0] // (targets * plan.wave)
     for copy in copies[:3]:
         copy.wait()
+
+    @pl.when(even)
+    def _():
+        line_copy.start()
+
     bins = bin_ref[...]
     hot = (iota((plan.bins, cells), 0) == bins).astype(F32)
     parts = [hot[:, i : i + lanes] for i in range(0, cells, lanes)]
@@ -85,44 +96,19 @@
     out[:, block:, :] = jnp.zeros((targets, META_ROWS, levels), BF16)
     for t in range(targets):
         out[t, block:, :block] = moved[t * META_ROWS : (t + 1) * META_ROWS]
-
-    @pl.when(me_ref[0] % 2 == 1)
-    def _():
-        width = line_out.shape[1] // LINE_PARTS
-        for i in range(LINE_PARTS):
-            part = pl.ds(i * width, width)
-            copy = pltpu.make_async_copy(
-                line_hbm.at[:, part], line_out.at[:, part], line_sems.at[i]
-            )
-            copy.start()
-            copy.wait()
-
-
-def window_kernel(me_ref, arrived_ref, loaded_ref, table_hbm, line_hbm, powers_ref, line_ref, sems):
+    line_copy.wait()
+
+
+def window_kernel(arrived_ref, table_hbm, powers_ref, sem):
     levels = arrived_ref.shape[0]
-    even = me_ref[0] % 2 == 0
-    table_copy = pltpu.make_async_copy(table_hbm, powers_ref.at[0, :, pl.ds(0, levels)], sems.at[0])
-    line_copy = pltpu.make_async_copy(line_hbm, line_ref, sems.at[1])
-    table_copy.start()
-
-    @pl.when(even)
-    def _():
-        line_copy.start()
-
-    @pl.when(jnp.logical_not(even))
-    def _():
-        line_ref[...] = loaded_ref[...]
-
+    copy = pltpu.make_async_copy(table_hbm, powers_ref.at[0, :, pl.ds(0, levels)], sem)
+    copy.start()
     powers_ref[1, :, :levels] = arrived_ref[...]
-    table_copy.wait()
+    copy.wait()
     for part in range(2):
         table = powers_ref[part, :, :levels]
         square = jnp.dot(table, table, preferred_element_type=F32)
         powers_ref[part, :, levels:] = square.astype(BF16)
-
-    @pl.when(even)
-    def _():
-        line_copy.wait()
 
 
 def level_kernel(plan, rays, got_ref, powers_ref, out_ref):
@@ -197,7 +183,7 @@
     arrived = lax.ppermute(rate_tables[0], "bin", plan.table_moves())
     me = lax.axis_index(("bin", "wave")).astype(I32).reshape(1)
     den_rows = cells // min(cells, LANES)
-    outgoing, loaded = pl.pallas_call(
+    outgoing, held_line = pl.pallas_call(
         functools.partial(pack_kernel, plan),
         out_shape=[
             jax.ShapeDtypeStruct(a, BF16) for a in ((plan.targets, rows, levels), line_table.shape)
@@ -209,8 +195,7 @@
             pltpu.VMEM((den_rows, cells // den_rows), BF16),
             pltpu.VMEM((1, cells), I32),
             pltpu.VMEM((1, cells), I32),
-            pltpu.SemaphoreType.DMA((4,)),
-            pltpu.SemaphoreType.DMA((LINE_PARTS,)),
+            pltpu.SemaphoreType.DMA((5,)),
         ],
         compiler_params=params,
     )(
@@ -224,19 +209,17 @@
     got = lax.all_to_all(
         outgoing, "bin", split_axis=0, concat_axis=0, tiled=True, axis_index_groups=plan.halves()
     )
-    powers, held_line = pl.pallas_call(
+    powers = pl.pallas_call(
         window_kernel,
-        out_shape=[
-            jax.ShapeDtypeStruct(a, BF16) for a in ((2, levels, 2 * levels), line_table.shape)
-        ],
-        in_specs=[smem, vmem, vmem, hbm, hbm],
-        out_specs=[vmem] * 2,
-        scratch_shapes=[pltpu.SemaphoreType.DMA((2,))],
+        out_shape=jax.ShapeDtypeStruct((2, levels, 2 * levels), BF16),
+        in_specs=[vmem, hbm],
+        out_specs=vmem,
+        scratch_shapes=[pltpu.SemaphoreType.DMA],
         compiler_params=params,
         cost_estimate=pl.CostEstimate(
             flops=OVERLAP_FLOPS, bytes_accessed=4 * arrived.size, transcendentals=0
         ),
-    )(me, arrived, loaded, in_hbm(rate_tables[0]), in_hbm(line_table))
+    )(arrived, in_hbm(rate_tables[0]))
     ray_rows = RAY_DEV
     rays = ray_rows * bin_total
     partial_sums = pl.pallas_call(

time: 37.5 us -> 34.6 us (0.923)
  local copies, waits for them, and re-layouts: 2.92 us -> 0 us
  blocking collectives: 11.1 us -> 10.5 us
  waiting for transfers between devices: 8.05 us -> 8.52 us
    unnamed x4 -> x0, local copies, waits for them, and re-layouts: 2.92 us -> none
    pallas_call x1, Pallas kernels: 2.39 us -> 3.17 us  [per_device(): pl.pallas_call(functools.partial(pack_kernel, plan), out_shape=[jax.Shape...]
    all_to_all x1, blocking collectives: 11.1 us -> 10.5 us  [per_device(): lax.all_to_all(partial_sums.reshape(bin_total, ray_rows, levels), 'bin',...]
    pallas_call x1, Pallas kernels: 1.69 us -> 1.15 us  [per_device(): pl.pallas_call(window_kernel, out_shape=jax.ShapeDtypeStruct((2, levels,...]
    all_to_all x1, waiting for transfers between devices: 6.88 us -> 7.34 us  [per_device(): lax.all_to_all(outgoing, 'bin', split_axis=0, concat_axis=0, tiled=True,...]
  transfers between devices with their start and end apart: 3 -> 3, of which waited for: 2 -> 2; matrix products, arithmetic and copies ran while one was open for 0% -> 0% of each run, Pallas kernels for 11% -> 13%
where the time goes in v31:
time: 34.6 us; the launch traced here: 34.3 us
  blocking collectives  10.5 us (30%)
  starting transfers between devices  8.86 us (26%)
  waiting for transfers between devices  8.52 us (25%)
  Pallas kernels  6.41 us (19%)
    all_to_all x1, blocking collectives, per_device(): lax.all_to_all(partial_sums.reshape(bin_total, ray_rows, levels), 'bin',...  10.5 us
    all_to_all x1, waiting for transfers between devices, per_device(): lax.all_to_all(outgoing, 'bin', split_axis=0, concat_axis=0, tiled=True,...  7.34 us
    all_to_all x1, starting transfers between devices, per_device(): lax.all_to_all(outgoing, 'bin', split_axis=0, concat_axis=0, tiled=True,...  4.75 us
    ppermute x1, starting transfers between devices, per_device(): arrived = lax.ppermute(rate_tables[0], 'bin', plan.table_moves())  4.04 us
    pallas_call x1, Pallas kernels, per_device(): pl.pallas_call(functools.partial(pack_kernel, plan), out_shape=[jax.Shape...  3.17 us
    ppermute x1, waiting for transfers between devices, per_device(): lax.ppermute(total, 'wave', [(i, i ^ step) for i in range(wave_total)])  1.17 us
    pallas_call x1, Pallas kernels, per_device(): pl.pallas_call(window_kernel, out_shape=jax.ShapeDtypeStruct((2, levels,...  1.15 us
    pallas_call x1, Pallas kernels, per_device(): pl.pallas_call(line_kernel, out_shape=jax.ShapeDtypeStruct(out_shape, F32...  1.13 us
  transfers between devices with their start and end apart: 3, of which 2 were waited for; matrix products, arithmetic and copies ran while one was open for 0% of the time, Pallas kernels for 13%

profile of v31, /device:TPU:0, one launch (start us, length us, event | category | flops | bytes accessed | tf_op | source)
XLA Modules:
  0.0 34.3 jit_solution(7907998589394229969)
XLA Ops:
  0.0 4.0 %collective-permute-start = (bf16[256,256]{1,0:T(8,128)(2,1)}, bf16[256,256]{1,0:T(8,128)(2,1)S(1)}, u32[]{:S(2)}, u32[]{:S(2)}) collective-permute-start(bf16[256,256]{1,0:T(8,128)(2,1)} %bitcast.10), channel_id=1, source_target_pairs={{0,16},{2,18},{4,20},{6,22},{8,24},{10,26},{12,28},{14,30},{16,0},... | collective-permute-start | bytes 393224 | tf_op jit(solution)/shard_map/ppermute | solution.py:183
  4.0 3.2 %shard_map.64 = (bf16[8,136,256]{2,1,0:T(8,128)(2,1)}, bf16[256,4096]{1,0:T(8,128)(2,1)S(1)}) custom-call(s32[1]{0:T(128)} %bitcast.me_ref, bf16[512,256]{1,0:T(8,128)(2,1)} %src_hbm.1, bf16[4,128]{1,0:T(4,128)(2,1)} %bitcast.9, s32[1,512]{1,0:T(1,128)} %bitcast.7, s32[1,512]{1,0:T(1,128)} %bitcast.8, bf16[256,4096]{1,0:T(8,128)(2,1)} %line_hbm.1), custom_call_target="tpu_custom_call" | custom-call | tf_op jit(solution)/shard_map/pallas_call | solution.py:186
  7.2 4.7 %all-to-all-start = ((bf16[8,136,256]{2,1,0:T(8,128)(2,1)}), bf16[8,136,256]{2,1,0:T(8,128)(2,1)S(1)}, u32[]{:S(2)}, u32[]{:S(2)}) async-start(bf16[8,136,256]{2,1,0:T(8,128)(2,1)} %get-tuple-element.7), calls=%async_computation | async-start | bytes 1114112 | tf_op jit(solution)/shard_map/all_to_all | solution.py:209
  12.0 0.0 collective-permute-done.arrived_ref
  12.0 1.1 %shard_map.65.powers_ref = bf16[2,256,512]{2,1,0:T(8,128)(2,1)S(1)} custom-call(bf16[256,256]{1,0:T(8,128)(2,1)S(1)} %collective-permute-done.arrived_ref, bf16[256,256]{1,0:T(8,128)(2,1)} %bitcast.11), custom_call_target="tpu_custom_call" | custom-call | flops 10000000000 | bytes 262144 | tf_op jit(solution)/shard_map/pallas_call | solution.py:212
  13.1 7.3 %all-to-all-done.got_ref = bf16[8,136,256]{2,1,0:T(8,128)(2,1)S(1)} async-done(((bf16[8,136,256]{2,1,0:T(8,128)(2,1)}), bf16[8,136,256]{2,1,0:T(8,128)(2,1)S(1)}, u32[]{:S(2)}, u32[]{:S(2)}) %all-to-all-start) | async-done | bytes 557088 | tf_op jit(solution)/shard_map/all_to_all | solution.py:209
  20.5 1.0 %shard_map.66 = bf16[256,256]{1,0:T(8,128)(2,1)S(1)} custom-call(bf16[8,136,256]{2,1,0:T(8,128)(2,1)S(1)} %all-to-all-done.got_ref, bf16[2,256,512]{2,1,0:T(8,128)(2,1)S(1)} %shard_map.65.powers_ref), custom_call_target="tpu_custom_call" | custom-call | tf_op jit(solution)/shard_map/pallas_call | solution.py:225
  21.4 10.5 %all_to_all.10 = bf16[16,16,256]{2,1,0:T(8,128)(2,1)S(1)} all-to-all(bf16[16,16,256]{2,1,0:T(8,128)(2,1)S(1)} %bitcast.6), channel_id=1, replica_groups=mesh['bin'=16,'wave'=2] {'bin'}, dimensions={0} | all-to-all | bytes 262144 | tf_op jit(solution)/shard_map/all_to_all | solution.py:232
  32.0 0.1 collective-permute-start.1
  32.0 1.2 %collective-permute-done.1.theirs_ref = f32[16,256]{1,0:T(8,128)S(1)} collective-permute-done((f32[16,256]{1,0:T(8,128)S(1)}, f32[16,256]{1,0:T(8,128)S(1)}, u32[]{:S(2)}, u32[]{:S(2)}) %collective-permute-start.1) | collective-permute-done | bytes 16416 | tf_op jit(solution)/shard_map/ppermute | solution.py:244
  33.2 1.1 %shard_map.67 = f32[16,4096]{1,0:T(8,128)} custom-call(f32[16,256]{1,0:T(8,128)S(1)} %convert_reduce_fusion.mine_ref, f32[16,256]{1,0:T(8,128)S(1)} %collective-permute-done.1.theirs_ref, bf16[256,4096]{1,0:T(8,128)(2,1)S(1)} %get-tuple-element.8.line_ref), custom_call_target="tpu_custom_call" | custom-call | tf_op jit(solution)/shard_map/pallas_call | solution.py:247
  (1 shorter events, 0.0 us)
Async XLA Ops:
  0.0 12.0 %collective-permute-start = (bf16[256,256]{1,0:T(8,128)(2,1)}, bf16[256,256]{1,0:T(8,128)(2,1)S(1)}, u32[]{:S(2)}, u32[]{:S(2)}) collective-permute-start(bf16[256,256]{1,0:T(8,128)(2,1)} %bitcast.10), channel_id=1, source_target_pairs={{0,16},{2,18},{4,20},{6,22},{8,24},{10,26},{12,28},{14,30},{16,0},... | collective-permute-start | bytes 393224 | tf_op jit(solution)/shard_map/ppermute | solution.py:183
  7.2 13.3 %all-to-all-start = ((bf16[8,136,256]{2,1,0:T(8,128)(2,1)}), bf16[8,136,256]{2,1,0:T(8,128)(2,1)S(1)}, u32[]{:S(2)}, u32[]{:S(2)}) async-start(bf16[8,136,256]{2,1,0:T(8,128)(2,1)} %get-tuple-element.7), calls=%async_computation | async-start | bytes 1114112 | tf_op jit(solution)/shard_map/all_to_all | solution.py:209
  32.0 1.2 %collective-permute-start.1 = (f32[16,256]{1,0:T(8,128)S(1)}, f32[16,256]{1,0:T(8,128)S(1)}, u32[]{:S(2)}, u32[]{:S(2)}) collective-permute-start(f32[16,256]{1,0:T(8,128)S(1)} %convert_reduce_fusion.mine_ref), channel_id=1, source_target_pairs={{0,1},{1,0},{2,3},{3,2},{4,5},{5,4},{6,7},{7,6},{8,9},{9,8},{10,11... | collective-permute-start | bytes 49160 | tf_op jit(solution)/shard_map/ppermute | solution.py:244

commit v32 on v27

--- a/solution.py
+++ b/solution.py
@@ -86,30 +86,31 @@
         out[t, block:, :block] = moved[t * META_ROWS : (t + 1) * META_ROWS]
 
 
-def window_kernel(arrived_ref, table_hbm, line_hbm, powers_ref, line_ref, sems):
+def window_kernel(arrived_ref, table_hbm, line_hbm, own_ref, other_ref, line_ref, sems):
     levels = arrived_ref.shape[0]
     copies = [
-        pltpu.make_async_copy(table_hbm, powers_ref.at[0, :, pl.ds(0, levels)], sems.at[0]),
+        pltpu.make_async_copy(table_hbm, own_ref.at[:, pl.ds(0, levels)], sems.at[0]),
         pltpu.make_async_copy(line_hbm, line_ref, sems.at[1]),
     ]
     for copy in copies:
         copy.start()
-    powers_ref[1, :, :levels] = arrived_ref[...]
+    other_ref[:, :levels] = arrived_ref[...]
     copies[0].wait()
-    for part in range(2):
-        table = powers_ref[part, :, :levels]
+    for ref in (own_ref, other_ref):
+        table = ref[:, :levels]
         square = jnp.dot(table, table, preferred_element_type=F32)
-        powers_ref[part, :, levels:] = square.astype(BF16)
+        ref[:, levels:] = square.astype(BF16)
     copies[1].wait()
 
 
-def level_kernel(plan, rays, got_ref, powers_ref, out_ref):
+def level_kernel(plan, rays, core_ref, got_ref, own_ref, other_ref, passed_ref, out_ref):
+    other = jnp.where(core_ref[0] % 2 == 1, passed_ref[...], other_ref[...])
     targets, block = plan.targets, plan.block
     meta = [got_ref[s, block:, :block].astype(F32) for s in range(targets)]
     columns = [jnp.transpose(m[:8]) for m in meta]
     total = jnp.zeros(out_ref.shape, F32)
     levels = got_ref.shape[2]
-    for part in range(2):
+    for part, powers in enumerate((own_ref[...], other)):
         low, high = part * plan.capacity, (part + 1) * plan.capacity
         src = got_ref[:, low:high, :].reshape(targets * plan.capacity, got_ref.shape[2])
         den = jnp.concatenate([c[low:high, 0:1] for c in columns], axis=0)
@@ -117,7 +118,7 @@
             [m[1:2, low:high] * RAY_BASE + m[2:3, low:high] for m in meta], axis=1
         ).astype(I32)
         wide = src.astype(F32)
-        steps = jnp.dot(src, powers_ref[part], preferred_element_type=F32)
+        steps = jnp.dot(src, powers, preferred_element_type=F32)
         pops = (wide + den * (steps[:, :levels] + den * steps[:, levels:])).astype(BF16)
         pick = (iota((rays, src.shape[0]), 0) == ray).astype(F32).astype(BF16)
         total = total + jnp.dot(pick, pops, preferred_element_type=F32)
@@ -151,11 +152,12 @@
         self.block = 2 * self.capacity
 
     def table_moves(self, wave_total):
-        return [
-            (b * wave_total + w, (b + self.targets) % self.bins * wave_total + (w ^ 1))
-            for b in range(self.bins)
-            for w in range(wave_total)
-        ]
+        moves = []
+        for b in range(self.bins):
+            for w in range(wave_total):
+                to = b ^ 1 if w % 2 else (b + self.targets) % self.bins
+                moves.append((b * wave_total + w, to * wave_total + w))
+        return moves
 
     def halves(self):
         return [list(range(self.targets)), list(range(self.targets, self.bins))]
@@ -176,6 +178,7 @@
         return pltpu.with_memory_space_constraint(x, pltpu.HBM)
 
     arrived = lax.ppermute(rate_tables[0], ("bin", "wave"), plan.table_moves(wave_total))
+    core = lax.axis_index("wave").astype(I32).reshape(1)
     me = lax.axis_index("bin").astype(I32).reshape(1)
     den_rows = cells // min(cells, LANES)
     outgoing = pl.pallas_call(
@@ -201,28 +204,30 @@
     got = lax.all_to_all(
         outgoing, "bin", split_axis=0, concat_axis=0, tiled=True, axis_index_groups=plan.halves()
     )
-    powers, held_line = pl.pallas_call(
+    own, other, held_line = pl.pallas_call(
         window_kernel,
         out_shape=[
-            jax.ShapeDtypeStruct(a, BF16) for a in ((2, levels, 2 * levels), line_table.shape)
+            jax.ShapeDtypeStruct(a, BF16)
+            for a in ((levels, 2 * levels), (levels, 2 * levels), line_table.shape)
         ],
         in_specs=[vmem, hbm, hbm],
-        out_specs=[vmem] * 2,
+        out_specs=[vmem] * 3,
         scratch_shapes=[pltpu.SemaphoreType.DMA((2,))],
         compiler_params=params,
         cost_estimate=pl.CostEstimate(
             flops=OVERLAP_FLOPS, bytes_accessed=4 * arrived.size, transcendentals=0
         ),
     )(arrived, in_hbm(rate_tables[0]), in_hbm(line_table))
+    passed = lax.ppermute(other, "wave", [(i, i ^ 1) for i in range(wave_total)])
     ray_rows = RAY_DEV
     rays = ray_rows * bin_total
     partial_sums = pl.pallas_call(
         functools.partial(level_kernel, plan, rays),
         out_shape=jax.ShapeDtypeStruct((rays, levels), BF16),
-        in_specs=[vmem] * 2,
+        in_specs=[smem] + [vmem] * 4,
         out_specs=vmem,
         compiler_params=params,
-    )(got, powers)
+    )(core, got, own, other, passed)
     held = lax.all_to_all(
         partial_sums.reshape(bin_total, ray_rows, levels),
         "bin",

time: 35.5 us -> 34.2 us (0.963)
  waiting for transfers between devices: 9.61 us -> 7.19 us
  starting transfers between devices: 8.29 us -> 8.93 us
  blocking collectives: 11.1 us -> 11.6 us
    all_to_all x1, waiting for transfers between devices: 8.44 us -> 4.5 us  [per_device(): lax.all_to_all(outgoing, 'bin', split_axis=0, concat_axis=0, tiled=True,...]
    ppermute x0 -> x1, waiting for transfers between devices: none -> 1.52 us  [per_device(): lax.ppermute(other, 'wave', [(i, i ^ 1) for i in range(wave_total)])]
    ppermute x1, starting transfers between devices: 3.48 us -> 4.04 us  [per_device(): lax.ppermute(rate_tables[0], ('bin', 'wave'), plan.table_moves(wave_total))]
    all_to_all x1, blocking collectives: 11.1 us -> 11.6 us  [per_device(): lax.all_to_all(partial_sums.reshape(bin_total, ray_rows, levels), 'bin',...]
  transfers between devices with their start and end apart: 3 -> 4, of which waited for: 2 -> 3; matrix products, arithmetic and copies ran while one was open for 0% -> 0% of each run, Pallas kernels for 12% -> 12%
where the time goes in v32:
time: 34.2 us; the launch traced here: 34 us
  blocking collectives  11.6 us (34%)
  starting transfers between devices  8.93 us (26%)
  waiting for transfers between devices  7.19 us (21%)
  Pallas kernels  6.14 us (18%)
    all_to_all x1, blocking collectives, per_device(): lax.all_to_all(partial_sums.reshape(bin_total, ray_rows, levels), 'bin',...  11.6 us
    all_to_all x1, starting transfers between devices, per_device(): lax.all_to_all(outgoing, 'bin', split_axis=0, concat_axis=0, tiled=True,...  4.75 us
    all_to_all x1, waiting for transfers between devices, per_device(): lax.all_to_all(outgoing, 'bin', split_axis=0, concat_axis=0, tiled=True,...  4.5 us
    ppermute x1, starting transfers between devices, per_device(): lax.ppermute(rate_tables[0], ('bin', 'wave'), plan.table_moves(wave_total))  4.04 us
    pallas_call x1, Pallas kernels, per_device(): pl.pallas_call(functools.partial(pack_kernel, plan), out_shape=jax.ShapeD...  2.36 us
    pallas_call x1, Pallas kernels, per_device(): pl.pallas_call(window_kernel, out_shape=[jax.ShapeDtypeStruct(a, BF16) fo...  1.69 us
    ppermute x1, waiting for transfers between devices, per_device(): lax.ppermute(other, 'wave', [(i, i ^ 1) for i in range(wave_total)])  1.52 us
    ppermute x1, waiting for transfers between devices, per_device(): lax.ppermute(total, 'wave', [(i, i ^ step) for i in range(wave_total)])  1.17 us
  transfers between devices with their start and end apart: 4, of which 3 were waited for; matrix products, arithmetic and copies ran while one was open for 0% of the time, Pallas kernels for 12%

profile of v32, /device:TPU:0, one launch (start us, length us, event | category | flops | bytes accessed | tf_op | source)
XLA Modules:
  0.0 34.0 jit_solution(3939414260587831712)
XLA Ops:
  0.0 4.0 %collective-permute-start = (bf16[256,256]{1,0:T(8,128)(2,1)}, bf16[256,256]{1,0:T(8,128)(2,1)S(1)}, u32[]{:S(2)}, u32[]{:S(2)}) collective-permute-start(bf16[256,256]{1,0:T(8,128)(2,1)} %bitcast.11), channel_id=1, source_target_pairs={{0,16},{1,3},{2,18},{3,1},{4,20},{5,7},{6,22},{7,5},{8,24},{9,11},... | collective-permute-start | bytes 393224 | tf_op jit(solution)/shard_map/ppermute | solution.py:180
  4.0 2.4 %shard_map.64 = bf16[8,136,256]{2,1,0:T(8,128)(2,1)} custom-call(s32[1]{0:T(128)} %bitcast.1.me_ref, bf16[512,256]{1,0:T(8,128)(2,1)} %src_hbm.1, bf16[4,128]{1,0:T(4,128)(2,1)} %bitcast.10, s32[1,512]{1,0:T(1,128)} %bitcast.8, s32[1,512]{1,0:T(1,128)} %bitcast.9), custom_call_target="tpu_custom_call" | custom-call | tf_op jit(solution)/shard_map/pallas_call | solution.py:184
  6.4 4.7 %all-to-all-start = ((bf16[8,136,256]{2,1,0:T(8,128)(2,1)}), bf16[8,136,256]{2,1,0:T(8,128)(2,1)S(1)}, u32[]{:S(2)}, u32[]{:S(2)}) async-start(bf16[8,136,256]{2,1,0:T(8,128)(2,1)} %shard_map.64), calls=%async_computation | async-start | bytes 1114112 | tf_op jit(solution)/shard_map/all_to_all | solution.py:204
  11.2 0.0 collective-permute-done.arrived_ref
  11.2 1.7 %shard_map.65 = (bf16[256,512]{1,0:T(8,128)(2,1)S(1)}, bf16[256,512]{1,0:T(8,128)(2,1)S(1)}, bf16[256,4096]{1,0:T(8,128)(2,1)S(1)}) custom-call(bf16[256,256]{1,0:T(8,128)(2,1)S(1)} %collective-permute-done.arrived_ref, bf16[256,256]{1,0:T(8,128)(2,1)} %bitcast.12, bf16[256,4096]{1,0:T(8,128)(2,1)} %line_hbm.1), custom_call_target="tpu_custom_call" | custom-call | flops 10000000000 | bytes 262144 | tf_op jit(solution)/shard_map/pallas_call | solution.py:207
  12.9 0.1 collective-permute-start.1
  12.9 1.5 %collective-permute-done.1.passed_ref = bf16[256,512]{1,0:T(8,128)(2,1)S(1)} collective-permute-done((bf16[256,512]{1,0:T(8,128)(2,1)S(1)}, bf16[256,512]{1,0:T(8,128)(2,1)S(1)}, u32[]{:S(2)}, u32[]{:S(2)}) %collective-permute-start.1) | collective-permute-done | bytes 262176 | tf_op jit(solution)/shard_map/ppermute | solution.py:221
  14.5 4.5 %all-to-all-done.got_ref = bf16[8,136,256]{2,1,0:T(8,128)(2,1)S(1)} async-done(((bf16[8,136,256]{2,1,0:T(8,128)(2,1)}), bf16[8,136,256]{2,1,0:T(8,128)(2,1)S(1)}, u32[]{:S(2)}, u32[]{:S(2)}) %all-to-all-start) | async-done | bytes 557088 | tf_op jit(solution)/shard_map/all_to_all | solution.py:204
  19.0 1.0 %shard_map.66 = bf16[256,256]{1,0:T(8,128)(2,1)S(1)} custom-call(s32[1]{0:T(128)} %bitcast.core_ref, bf16[8,136,256]{2,1,0:T(8,128)(2,1)S(1)} %all-to-all-done.got_ref, bf16[256,512]{1,0:T(8,128)(2,1)S(1)} %get-tuple-element.8.own_ref, bf16[256,512]{1,0:T(8,128)(2,1)S(1)} %get-tuple-element.9.other_ref, bf16[256,512]{1,0:T(8,128)(2,1)S(1)} %collective-permute-done.1.passed_ref), custom_call_target="tpu_custom_call" | custom-call | tf_op jit(solution)/shard_map/pallas_call | solution.py:224
  19.9 11.6 %all_to_all.10 = bf16[16,16,256]{2,1,0:T(8,128)(2,1)S(1)} all-to-all(bf16[16,16,256]{2,1,0:T(8,128)(2,1)S(1)} %bitcast.7), channel_id=1, replica_groups=mesh['bin'=16,'wave'=2] {'bin'}, dimensions={0} | all-to-all | bytes 262144 | tf_op jit(solution)/shard_map/all_to_all | solution.py:231
  31.6 0.1 collective-permute-start.2
  31.7 1.2 %collective-permute-done.2.theirs_ref = f32[16,256]{1,0:T(8,128)S(1)} collective-permute-done((f32[16,256]{1,0:T(8,128)S(1)}, f32[16,256]{1,0:T(8,128)S(1)}, u32[]{:S(2)}, u32[]{:S(2)}) %collective-permute-start.2) | collective-permute-done | bytes 16416 | tf_op jit(solution)/shard_map/ppermute | solution.py:243
  32.8 1.1 %shard_map.67 = f32[16,4096]{1,0:T(8,128)} custom-call(f32[16,256]{1,0:T(8,128)S(1)} %convert_reduce_fusion.mine_ref, f32[16,256]{1,0:T(8,128)S(1)} %collective-permute-done.2.theirs_ref, bf16[256,4096]{1,0:T(8,128)(2,1)S(1)} %get-tuple-element.10.line_ref), custom_call_target="tpu_custom_call" | custom-call | tf_op jit(solution)/shard_map/pallas_call | solution.py:246
  (1 shorter events, 0.0 us)
Async XLA Ops:
  0.0 11.2 %collective-permute-start = (bf16[256,256]{1,0:T(8,128)(2,1)}, bf16[256,256]{1,0:T(8,128)(2,1)S(1)}, u32[]{:S(2)}, u32[]{:S(2)}) collective-permute-start(bf16[256,256]{1,0:T(8,128)(2,1)} %bitcast.11), channel_id=1, source_target_pairs={{0,16},{1,3},{2,18},{3,1},{4,20},{5,7},{6,22},{7,5},{8,24},{9,11},... | collective-permute-start | bytes 393224 | tf_op jit(solution)/shard_map/ppermute | solution.py:180
  6.4 12.6 %all-to-all-start = ((bf16[8,136,256]{2,1,0:T(8,128)(2,1)}), bf16[8,136,256]{2,1,0:T(8,128)(2,1)S(1)}, u32[]{:S(2)}, u32[]{:S(2)}) async-start(bf16[8,136,256]{2,1,0:T(8,128)(2,1)} %shard_map.64), calls=%async_computation | async-start | bytes 1114112 | tf_op jit(solution)/shard_map/all_to_all | solution.py:204
  12.9 1.6 %collective-permute-start.1 = (bf16[256,512]{1,0:T(8,128)(2,1)S(1)}, bf16[256,512]{1,0:T(8,128)(2,1)S(1)}, u32[]{:S(2)}, u32[]{:S(2)}) collective-permute-start(bf16[256,512]{1,0:T(8,128)(2,1)S(1)} %get-tuple-element.9.other_ref), channel_id=1, source_target_pairs={{0,1},{1,0},{2,3},{3,2},{4,5},{5,4},{6,7},{7,6},{8,9},{9,8},{10,11... | collective-permute-start | bytes 786440 | tf_op jit(solution)/shard_map/ppermute | solution.py:221
  31.6 1.2 %collective-permute-start.2 = (f32[16,256]{1,0:T(8,128)S(1)}, f32[16,256]{1,0:T(8,128)S(1)}, u32[]{:S(2)}, u32[]{:S(2)}) collective-permute-start(f32[16,256]{1,0:T(8,128)S(1)} %convert_reduce_fusion.mine_ref), channel_id=1, source_target_pairs={{0,1},{1,0},{2,3},{3,2},{4,5},{5,4},{6,7},{7,6},{8,9},{9,8},{10,11... | collective-permute-start | bytes 49160 | tf_op jit(solution)/shard_map/ppermute | solution.py:243

commit v33 on v32

--- a/solution.py
+++ b/solution.py
@@ -155,7 +155,7 @@
         moves = []
         for b in range(self.bins):
             for w in range(wave_total):
-                to = b ^ 1 if w % 2 else (b + self.targets) % self.bins
+                to = b ^ 2 if w % 2 else (b + self.targets) % self.bins
                 moves.append((b * wave_total + w, to * wave_total + w))
         return moves
 

time: 34.2 us -> 34.2 us (level)
  no operation moved by 1% of the time
where the time goes in v33:
time: 34.2 us; the launch traced here: 34 us
  blocking collectives  11.6 us (34%)
  starting transfers between devices  8.93 us (26%)
  waiting for transfers between devices  7.19 us (21%)
  Pallas kernels  6.14 us (18%)
    all_to_all x1, blocking collectives, per_device(): lax.all_to_all(partial_sums.reshape(bin_total, ray_rows, levels), 'bin',...  11.6 us
    all_to_all x1, starting transfers between devices, per_device(): lax.all_to_all(outgoing, 'bin', split_axis=0, concat_axis=0, tiled=True,...  4.75 us
    all_to_all x1, waiting for transfers between devices, per_device(): lax.all_to_all(outgoing, 'bin', split_axis=0, concat_axis=0, tiled=True,...  4.5 us
    ppermute x1, starting transfers between devices, per_device(): lax.ppermute(rate_tables[0], ('bin', 'wave'), plan.table_moves(wave_total))  4.04 us
    pallas_call x1, Pallas kernels, per_device(): pl.pallas_call(functools.partial(pack_kernel, plan), out_shape=jax.ShapeD...  2.36 us
    pallas_call x1, Pallas kernels, per_device(): pl.pallas_call(window_kernel, out_shape=[jax.ShapeDtypeStruct(a, BF16) fo...  1.69 us
    ppermute x1, waiting for transfers between devices, per_device(): lax.ppermute(other, 'wave', [(i, i ^ 1) for i in range(wave_total)])  1.52 us
    ppermute x1, waiting for transfers between devices, per_device(): lax.ppermute(total, 'wave', [(i, i ^ step) for i in range(wave_total)])  1.17 us
  transfers between devices with their start and end apart: 4, of which 3 were waited for; matrix products, arithmetic and copies ran while one was open for 0% of the time, Pallas kernels for 12%

profile of v33, /device:TPU:0, one launch (start us, length us, event | category | flops | bytes accessed | tf_op | source)
XLA Modules:
  0.0 34.0 jit_solution(12691576651473975550)
XLA Ops:
  0.0 4.0 %collective-permute-start = (bf16[256,256]{1,0:T(8,128)(2,1)}, bf16[256,256]{1,0:T(8,128)(2,1)S(1)}, u32[]{:S(2)}, u32[]{:S(2)}) collective-permute-start(bf16[256,256]{1,0:T(8,128)(2,1)} %bitcast.11), channel_id=1, source_target_pairs={{0,16},{1,5},{2,18},{3,7},{4,20},{5,1},{6,22},{7,3},{8,24},{9,13},... | collective-permute-start | bytes 393224 | tf_op jit(solution)/shard_map/ppermute | solution.py:180
  4.0 2.4 %shard_map.64 = bf16[8,136,256]{2,1,0:T(8,128)(2,1)} custom-call(s32[1]{0:T(128)} %bitcast.1.me_ref, bf16[512,256]{1,0:T(8,128)(2,1)} %src_hbm.1, bf16[4,128]{1,0:T(4,128)(2,1)} %bitcast.10, s32[1,512]{1,0:T(1,128)} %bitcast.8, s32[1,512]{1,0:T(1,128)} %bitcast.9), custom_call_target="tpu_custom_call" | custom-call | tf_op jit(solution)/shard_map/pallas_call | solution.py:184
  6.4 4.7 %all-to-all-start = ((bf16[8,136,256]{2,1,0:T(8,128)(2,1)}), bf16[8,136,256]{2,1,0:T(8,128)(2,1)S(1)}, u32[]{:S(2)}, u32[]{:S(2)}) async-start(bf16[8,136,256]{2,1,0:T(8,128)(2,1)} %shard_map.64), calls=%async_computation | async-start | bytes 1114112 | tf_op jit(solution)/shard_map/all_to_all | solution.py:204
  11.2 0.0 collective-permute-done.arrived_ref
  11.2 1.7 %shard_map.65 = (bf16[256,512]{1,0:T(8,128)(2,1)S(1)}, bf16[256,512]{1,0:T(8,128)(2,1)S(1)}, bf16[256,4096]{1,0:T(8,128)(2,1)S(1)}) custom-call(bf16[256,256]{1,0:T(8,128)(2,1)S(1)} %collective-permute-done.arrived_ref, bf16[256,256]{1,0:T(8,128)(2,1)} %bitcast.12, bf16[256,4096]{1,0:T(8,128)(2,1)} %line_hbm.1), custom_call_target="tpu_custom_call" | custom-call | flops 10000000000 | bytes 262144 | tf_op jit(solution)/shard_map/pallas_call | solution.py:207
  12.9 0.1 collective-permute-start.1
  12.9 1.5 %collective-permute-done.1.passed_ref = bf16[256,512]{1,0:T(8,128)(2,1)S(1)} collective-permute-done((bf16[256,512]{1,0:T(8,128)(2,1)S(1)}, bf16[256,512]{1,0:T(8,128)(2,1)S(1)}, u32[]{:S(2)}, u32[]{:S(2)}) %collective-permute-start.1) | collective-permute-done | bytes 262176 | tf_op jit(solution)/shard_map/ppermute | solution.py:221
  14.5 4.5 %all-to-all-done.got_ref = bf16[8,136,256]{2,1,0:T(8,128)(2,1)S(1)} async-done(((bf16[8,136,256]{2,1,0:T(8,128)(2,1)}), bf16[8,136,256]{2,1,0:T(8,128)(2,1)S(1)}, u32[]{:S(2)}, u32[]{:S(2)}) %all-to-all-start) | async-done | bytes 557088 | tf_op jit(solution)/shard_map/all_to_all | solution.py:204
  19.0 1.0 %shard_map.66 = bf16[256,256]{1,0:T(8,128)(2,1)S(1)} custom-call(s32[1]{0:T(128)} %bitcast.core_ref, bf16[8,136,256]{2,1,0:T(8,128)(2,1)S(1)} %all-to-all-done.got_ref, bf16[256,512]{1,0:T(8,128)(2,1)S(1)} %get-tuple-element.8.own_ref, bf16[256,512]{1,0:T(8,128)(2,1)S(1)} %get-tuple-element.9.other_ref, bf16[256,512]{1,0:T(8,128)(2,1)S(1)} %collective-permute-done.1.passed_ref), custom_call_target="tpu_custom_call" | custom-call | tf_op jit(solution)/shard_map/pallas_call | solution.py:224
  19.9 11.6 %all_to_all.10 = bf16[16,16,256]{2,1,0:T(8,128)(2,1)S(1)} all-to-all(bf16[16,16,256]{2,1,0:T(8,128)(2,1)S(1)} %bitcast.7), channel_id=1, replica_groups=mesh['bin'=16,'wave'=2] {'bin'}, dimensions={0} | all-to-all | bytes 262144 | tf_op jit(solution)/shard_map/all_to_all | solution.py:231
  31.6 0.1 collective-permute-start.2
  31.7 1.2 %collective-permute-done.2.theirs_ref = f32[16,256]{1,0:T(8,128)S(1)} collective-permute-done((f32[16,256]{1,0:T(8,128)S(1)}, f32[16,256]{1,0:T(8,128)S(1)}, u32[]{:S(2)}, u32[]{:S(2)}) %collective-permute-start.2) | collective-permute-done | bytes 16416 | tf_op jit(solution)/shard_map/ppermute | solution.py:243
  32.8 1.1 %shard_map.67 = f32[16,4096]{1,0:T(8,128)} custom-call(f32[16,256]{1,0:T(8,128)S(1)} %convert_reduce_fusion.mine_ref, f32[16,256]{1,0:T(8,128)S(1)} %collective-permute-done.2.theirs_ref, bf16[256,4096]{1,0:T(8,128)(2,1)S(1)} %get-tuple-element.10.line_ref), custom_call_target="tpu_custom_call" | custom-call | tf_op jit(solution)/shard_map/pallas_call | solution.py:246
  (1 shorter events, 0.0 us)
Async XLA Ops:
  0.0 11.2 %collective-permute-start = (bf16[256,256]{1,0:T(8,128)(2,1)}, bf16[256,256]{1,0:T(8,128)(2,1)S(1)}, u32[]{:S(2)}, u32[]{:S(2)}) collective-permute-start(bf16[256,256]{1,0:T(8,128)(2,1)} %bitcast.11), channel_id=1, source_target_pairs={{0,16},{1,5},{2,18},{3,7},{4,20},{5,1},{6,22},{7,3},{8,24},{9,13},... | collective-permute-start | bytes 393224 | tf_op jit(solution)/shard_map/ppermute | solution.py:180
  6.4 12.6 %all-to-all-start = ((bf16[8,136,256]{2,1,0:T(8,128)(2,1)}), bf16[8,136,256]{2,1,0:T(8,128)(2,1)S(1)}, u32[]{:S(2)}, u32[]{:S(2)}) async-start(bf16[8,136,256]{2,1,0:T(8,128)(2,1)} %shard_map.64), calls=%async_computation | async-start | bytes 1114112 | tf_op jit(solution)/shard_map/all_to_all | solution.py:204
  12.9 1.6 %collective-permute-start.1 = (bf16[256,512]{1,0:T(8,128)(2,1)S(1)}, bf16[256,512]{1,0:T(8,128)(2,1)S(1)}, u32[]{:S(2)}, u32[]{:S(2)}) collective-permute-start(bf16[256,512]{1,0:T(8,128)(2,1)S(1)} %get-tuple-element.9.other_ref), channel_id=1, source_target_pairs={{0,1},{1,0},{2,3},{3,2},{4,5},{5,4},{6,7},{7,6},{8,9},{9,8},{10,11... | collective-permute-start | bytes 786440 | tf_op jit(solution)/shard_map/ppermute | solution.py:221
  31.6 1.2 %collective-permute-start.2 = (f32[16,256]{1,0:T(8,128)S(1)}, f32[16,256]{1,0:T(8,128)S(1)}, u32[]{:S(2)}, u32[]{:S(2)}) collective-permute-start(f32[16,256]{1,0:T(8,128)S(1)} %convert_reduce_fusion.mine_ref), channel_id=1, source_target_pairs={{0,1},{1,0},{2,3},{3,2},{4,5},{5,4},{6,7},{7,6},{8,9},{9,8},{10,11... | collective-permute-start | bytes 49160 | tf_op jit(solution)/shard_map/ppermute | solution.py:243

commit v34 on v33

--- a/solution.py
+++ b/solution.py
@@ -11,7 +11,7 @@
 META_ROWS = 8
 RAY_BASE = 32
 LANES = 128
-LINE_CHUNKS = 4
+LINE_CHUNKS = 8
 OVERLAP_FLOPS = 10**10
 VMEM_LIMIT = 32 * 1024 * 1024
 F32 = jnp.float32

time: 34.2 us -> 34.3 us (level)
  no operation moved by 1% of the time
where the time goes in v34:
time: 34.3 us; the launch traced here: 34 us
  blocking collectives  11.6 us (34%)
  starting transfers between devices  8.93 us (26%)
  waiting for transfers between devices  7.19 us (21%)
  Pallas kernels  6.17 us (18%)
    all_to_all x1, blocking collectives, per_device(): lax.all_to_all(partial_sums.reshape(bin_total, ray_rows, levels), 'bin',...  11.6 us
    all_to_all x1, starting transfers between devices, per_device(): lax.all_to_all(outgoing, 'bin', split_axis=0, concat_axis=0, tiled=True,...  4.75 us
    all_to_all x1, waiting for transfers between devices, per_device(): lax.all_to_all(outgoing, 'bin', split_axis=0, concat_axis=0, tiled=True,...  4.5 us
    ppermute x1, starting transfers between devices, per_device(): lax.ppermute(rate_tables[0], ('bin', 'wave'), plan.table_moves(wave_total))  4.04 us
    pallas_call x1, Pallas kernels, per_device(): pl.pallas_call(functools.partial(pack_kernel, plan), out_shape=jax.ShapeD...  2.36 us
    pallas_call x1, Pallas kernels, per_device(): pl.pallas_call(window_kernel, out_shape=[jax.ShapeDtypeStruct(a, BF16) fo...  1.69 us
    ppermute x1, waiting for transfers between devices, per_device(): lax.ppermute(other, 'wave', [(i, i ^ 1) for i in range(wave_total)])  1.52 us
    ppermute x1, waiting for transfers between devices, per_device(): lax.ppermute(total, 'wave', [(i, i ^ step) for i in range(wave_total)])  1.17 us
  transfers between devices with their start and end apart: 4, of which 3 were waited for; matrix products, arithmetic and copies ran while one was open for 0% of the time, Pallas kernels for 12%

profile of v34, /device:TPU:0, one launch (start us, length us, event | category | flops | bytes accessed | tf_op | source)
XLA Modules:
  0.0 34.0 jit_solution(11879377442456926634)
XLA Ops:
  0.0 4.0 %collective-permute-start = (bf16[256,256]{1,0:T(8,128)(2,1)}, bf16[256,256]{1,0:T(8,128)(2,1)S(1)}, u32[]{:S(2)}, u32[]{:S(2)}) collective-permute-start(bf16[256,256]{1,0:T(8,128)(2,1)} %bitcast.11), channel_id=1, source_target_pairs={{0,16},{1,5},{2,18},{3,7},{4,20},{5,1},{6,22},{7,3},{8,24},{9,13},... | collective-permute-start | bytes 393224 | tf_op jit(solution)/shard_map/ppermute | solution.py:180
  4.0 2.4 %shard_map.64 = bf16[8,136,256]{2,1,0:T(8,128)(2,1)} custom-call(s32[1]{0:T(128)} %bitcast.1.me_ref, bf16[512,256]{1,0:T(8,128)(2,1)} %src_hbm.1, bf16[4,128]{1,0:T(4,128)(2,1)} %bitcast.10, s32[1,512]{1,0:T(1,128)} %bitcast.8, s32[1,512]{1,0:T(1,128)} %bitcast.9), custom_call_target="tpu_custom_call" | custom-call | tf_op jit(solution)/shard_map/pallas_call | solution.py:184
  6.4 4.7 %all-to-all-start = ((bf16[8,136,256]{2,1,0:T(8,128)(2,1)}), bf16[8,136,256]{2,1,0:T(8,128)(2,1)S(1)}, u32[]{:S(2)}, u32[]{:S(2)}) async-start(bf16[8,136,256]{2,1,0:T(8,128)(2,1)} %shard_map.64), calls=%async_computation | async-start | bytes 1114112 | tf_op jit(solution)/shard_map/all_to_all | solution.py:204
  11.2 0.0 collective-permute-done.arrived_ref
  11.2 1.7 %shard_map.65 = (bf16[256,512]{1,0:T(8,128)(2,1)S(1)}, bf16[256,512]{1,0:T(8,128)(2,1)S(1)}, bf16[256,4096]{1,0:T(8,128)(2,1)S(1)}) custom-call(bf16[256,256]{1,0:T(8,128)(2,1)S(1)} %collective-permute-done.arrived_ref, bf16[256,256]{1,0:T(8,128)(2,1)} %bitcast.12, bf16[256,4096]{1,0:T(8,128)(2,1)} %line_hbm.1), custom_call_target="tpu_custom_call" | custom-call | flops 10000000000 | bytes 262144 | tf_op jit(solution)/shard_map/pallas_call | solution.py:207
  12.9 0.1 collective-permute-start.1
  12.9 1.5 %collective-permute-done.1.passed_ref = bf16[256,512]{1,0:T(8,128)(2,1)S(1)} collective-permute-done((bf16[256,512]{1,0:T(8,128)(2,1)S(1)}, bf16[256,512]{1,0:T(8,128)(2,1)S(1)}, u32[]{:S(2)}, u32[]{:S(2)}) %collective-permute-start.1) | collective-permute-done | bytes 262176 | tf_op jit(solution)/shard_map/ppermute | solution.py:221
  14.5 4.5 %all-to-all-done.got_ref = bf16[8,136,256]{2,1,0:T(8,128)(2,1)S(1)} async-done(((bf16[8,136,256]{2,1,0:T(8,128)(2,1)}), bf16[8,136,256]{2,1,0:T(8,128)(2,1)S(1)}, u32[]{:S(2)}, u32[]{:S(2)}) %all-to-all-start) | async-done | bytes 557088 | tf_op jit(solution)/shard_map/all_to_all | solution.py:204
  19.0 1.0 %shard_map.66 = bf16[256,256]{1,0:T(8,128)(2,1)S(1)} custom-call(s32[1]{0:T(128)} %bitcast.core_ref, bf16[8,136,256]{2,1,0:T(8,128)(2,1)S(1)} %all-to-all-done.got_ref, bf16[256,512]{1,0:T(8,128)(2,1)S(1)} %get-tuple-element.8.own_ref, bf16[256,512]{1,0:T(8,128)(2,1)S(1)} %get-tuple-element.9.other_ref, bf16[256,512]{1,0:T(8,128)(2,1)S(1)} %collective-permute-done.1.passed_ref), custom_call_target="tpu_custom_call" | custom-call | tf_op jit(solution)/shard_map/pallas_call | solution.py:224
  19.9 11.6 %all_to_all.10 = bf16[16,16,256]{2,1,0:T(8,128)(2,1)S(1)} all-to-all(bf16[16,16,256]{2,1,0:T(8,128)(2,1)S(1)} %bitcast.7), channel_id=1, replica_groups=mesh['bin'=16,'wave'=2] {'bin'}, dimensions={0} | all-to-all | bytes 262144 | tf_op jit(solution)/shard_map/all_to_all | solution.py:231
  31.6 0.1 collective-permute-start.2
  31.7 1.2 %collective-permute-done.2.theirs_ref = f32[16,256]{1,0:T(8,128)S(1)} collective-permute-done((f32[16,256]{1,0:T(8,128)S(1)}, f32[16,256]{1,0:T(8,128)S(1)}, u32[]{:S(2)}, u32[]{:S(2)}) %collective-permute-start.2) | collective-permute-done | bytes 16416 | tf_op jit(solution)/shard_map/ppermute | solution.py:243
  32.8 1.1 %shard_map.67 = f32[16,4096]{1,0:T(8,128)} custom-call(f32[16,256]{1,0:T(8,128)S(1)} %convert_reduce_fusion.mine_ref, f32[16,256]{1,0:T(8,128)S(1)} %collective-permute-done.2.theirs_ref, bf16[256,4096]{1,0:T(8,128)(2,1)S(1)} %get-tuple-element.10.line_ref), custom_call_target="tpu_custom_call" | custom-call | tf_op jit(solution)/shard_map/pallas_call | solution.py:246
  (1 shorter events, 0.0 us)
Async XLA Ops:
  0.0 11.2 %collective-permute-start = (bf16[256,256]{1,0:T(8,128)(2,1)}, bf16[256,256]{1,0:T(8,128)(2,1)S(1)}, u32[]{:S(2)}, u32[]{:S(2)}) collective-permute-start(bf16[256,256]{1,0:T(8,128)(2,1)} %bitcast.11), channel_id=1, source_target_pairs={{0,16},{1,5},{2,18},{3,7},{4,20},{5,1},{6,22},{7,3},{8,24},{9,13},... | collective-permute-start | bytes 393224 | tf_op jit(solution)/shard_map/ppermute | solution.py:180
  6.4 12.6 %all-to-all-start = ((bf16[8,136,256]{2,1,0:T(8,128)(2,1)}), bf16[8,136,256]{2,1,0:T(8,128)(2,1)S(1)}, u32[]{:S(2)}, u32[]{:S(2)}) async-start(bf16[8,136,256]{2,1,0:T(8,128)(2,1)} %shard_map.64), calls=%async_computation | async-start | bytes 1114112 | tf_op jit(solution)/shard_map/all_to_all | solution.py:204
  12.9 1.6 %collective-permute-start.1 = (bf16[256,512]{1,0:T(8,128)(2,1)S(1)}, bf16[256,512]{1,0:T(8,128)(2,1)S(1)}, u32[]{:S(2)}, u32[]{:S(2)}) collective-permute-start(bf16[256,512]{1,0:T(8,128)(2,1)S(1)} %get-tuple-element.9.other_ref), channel_id=1, source_target_pairs={{0,1},{1,0},{2,3},{3,2},{4,5},{5,4},{6,7},{7,6},{8,9},{9,8},{10,11... | collective-permute-start | bytes 786440 | tf_op jit(solution)/shard_map/ppermute | solution.py:221
  31.6 1.2 %collective-permute-start.2 = (f32[16,256]{1,0:T(8,128)S(1)}, f32[16,256]{1,0:T(8,128)S(1)}, u32[]{:S(2)}, u32[]{:S(2)}) collective-permute-start(f32[16,256]{1,0:T(8,128)S(1)} %convert_reduce_fusion.mine_ref), channel_id=1, source_target_pairs={{0,1},{1,0},{2,3},{3,2},{4,5},{5,4},{6,7},{7,6},{8,9},{9,8},{10,11... | collective-permute-start | bytes 49160 | tf_op jit(solution)/shard_map/ppermute | solution.py:243

commit v35 on v33

--- a/solution.py
+++ b/solution.py
@@ -126,7 +126,7 @@
 
 
 def line_kernel(mine_ref, theirs_ref, line_ref, out_hbm, out_ref, sems):
-    sums = mine_ref[...] + theirs_ref[...]
+    sums = mine_ref[...] + theirs_ref[...].astype(F32)
     rows = sums.shape[0]
     high = sums.astype(BF16)
     low = (sums - high.astype(F32)).astype(BF16)
@@ -240,7 +240,7 @@
     step = 1
     while step < wave_total:
         total = total + theirs if step > 1 else total
-        theirs = lax.ppermute(total, "wave", [(i, i ^ step) for i in range(wave_total)])
+        theirs = lax.ppermute(total.astype(BF16), "wave", [(i, i ^ step) for i in range(wave_total)])
         step *= 2
     out_shape = (ray_rows, line_table.shape[1])
     return pl.pallas_call(

time: 34.2 us -> 34.2 us (level)
  no operation moved by 1% of the time
where the time goes in v35:
time: 34.2 us; the launch traced here: 34 us
  blocking collectives  11.6 us (34%)
  starting transfers between devices  8.93 us (26%)
  waiting for transfers between devices  7.18 us (21%)
  Pallas kernels  6.14 us (18%)
    all_to_all x1, blocking collectives, per_device(): lax.all_to_all(partial_sums.reshape(bin_total, ray_rows, levels), 'bin',...  11.6 us
    all_to_all x1, starting transfers between devices, per_device(): lax.all_to_all(outgoing, 'bin', split_axis=0, concat_axis=0, tiled=True,...  4.75 us
    all_to_all x1, waiting for transfers between devices, per_device(): lax.all_to_all(outgoing, 'bin', split_axis=0, concat_axis=0, tiled=True,...  4.5 us
    ppermute x1, starting transfers between devices, per_device(): lax.ppermute(rate_tables[0], ('bin', 'wave'), plan.table_moves(wave_total))  4.04 us
    pallas_call x1, Pallas kernels, per_device(): pl.pallas_call(functools.partial(pack_kernel, plan), out_shape=jax.ShapeD...  2.36 us
    pallas_call x1, Pallas kernels, per_device(): pl.pallas_call(window_kernel, out_shape=[jax.ShapeDtypeStruct(a, BF16) fo...  1.69 us
    ppermute x1, waiting for transfers between devices, per_device(): lax.ppermute(other, 'wave', [(i, i ^ 1) for i in range(wave_total)])  1.52 us
    ppermute x1, waiting for transfers between devices, per_device(): lax.ppermute(total.astype(BF16), 'wave', [(i, i ^ step) for i in range(wa...  1.16 us
  transfers between devices with their start and end apart: 4, of which 3 were waited for; matrix products, arithmetic and copies ran while one was open for 0% of the time, Pallas kernels for 12%

profile of v35, /device:TPU:0, one launch (start us, length us, event | category | flops | bytes accessed | tf_op | source)
XLA Modules:
  0.0 34.0 jit_solution(10195863553364775007)
XLA Ops:
  0.0 4.0 %collective-permute-start = (bf16[256,256]{1,0:T(8,128)(2,1)}, bf16[256,256]{1,0:T(8,128)(2,1)S(1)}, u32[]{:S(2)}, u32[]{:S(2)}) collective-permute-start(bf16[256,256]{1,0:T(8,128)(2,1)} %bitcast.11), channel_id=1, source_target_pairs={{0,16},{1,5},{2,18},{3,7},{4,20},{5,1},{6,22},{7,3},{8,24},{9,13},... | collective-permute-start | bytes 393224 | tf_op jit(solution)/shard_map/ppermute | solution.py:180
  4.0 2.4 %shard_map.64 = bf16[8,136,256]{2,1,0:T(8,128)(2,1)} custom-call(s32[1]{0:T(128)} %bitcast.1.me_ref, bf16[512,256]{1,0:T(8,128)(2,1)} %src_hbm.1, bf16[4,128]{1,0:T(4,128)(2,1)} %bitcast.10, s32[1,512]{1,0:T(1,128)} %bitcast.8, s32[1,512]{1,0:T(1,128)} %bitcast.9), custom_call_target="tpu_custom_call" | custom-call | tf_op jit(solution)/shard_map/pallas_call | solution.py:184
  6.4 4.7 %all-to-all-start = ((bf16[8,136,256]{2,1,0:T(8,128)(2,1)}), bf16[8,136,256]{2,1,0:T(8,128)(2,1)S(1)}, u32[]{:S(2)}, u32[]{:S(2)}) async-start(bf16[8,136,256]{2,1,0:T(8,128)(2,1)} %shard_map.64), calls=%async_computation | async-start | bytes 1114112 | tf_op jit(solution)/shard_map/all_to_all | solution.py:204
  11.2 0.0 collective-permute-done.arrived_ref
  11.2 1.7 %shard_map.65 = (bf16[256,512]{1,0:T(8,128)(2,1)S(1)}, bf16[256,512]{1,0:T(8,128)(2,1)S(1)}, bf16[256,4096]{1,0:T(8,128)(2,1)S(1)}) custom-call(bf16[256,256]{1,0:T(8,128)(2,1)S(1)} %collective-permute-done.arrived_ref, bf16[256,256]{1,0:T(8,128)(2,1)} %bitcast.12, bf16[256,4096]{1,0:T(8,128)(2,1)} %line_hbm.1), custom_call_target="tpu_custom_call" | custom-call | flops 10000000000 | bytes 262144 | tf_op jit(solution)/shard_map/pallas_call | solution.py:207
  12.9 0.1 collective-permute-start.1
  12.9 1.5 %collective-permute-done.1.passed_ref = bf16[256,512]{1,0:T(8,128)(2,1)S(1)} collective-permute-done((bf16[256,512]{1,0:T(8,128)(2,1)S(1)}, bf16[256,512]{1,0:T(8,128)(2,1)S(1)}, u32[]{:S(2)}, u32[]{:S(2)}) %collective-permute-start.1) | collective-permute-done | bytes 262176 | tf_op jit(solution)/shard_map/ppermute | solution.py:221
  14.5 4.5 %all-to-all-done.got_ref = bf16[8,136,256]{2,1,0:T(8,128)(2,1)S(1)} async-done(((bf16[8,136,256]{2,1,0:T(8,128)(2,1)}), bf16[8,136,256]{2,1,0:T(8,128)(2,1)S(1)}, u32[]{:S(2)}, u32[]{:S(2)}) %all-to-all-start) | async-done | bytes 557088 | tf_op jit(solution)/shard_map/all_to_all | solution.py:204
  19.0 1.0 %shard_map.66 = bf16[256,256]{1,0:T(8,128)(2,1)S(1)} custom-call(s32[1]{0:T(128)} %bitcast.core_ref, bf16[8,136,256]{2,1,0:T(8,128)(2,1)S(1)} %all-to-all-done.got_ref, bf16[256,512]{1,0:T(8,128)(2,1)S(1)} %get-tuple-element.8.own_ref, bf16[256,512]{1,0:T(8,128)(2,1)S(1)} %get-tuple-element.9.other_ref, bf16[256,512]{1,0:T(8,128)(2,1)S(1)} %collective-permute-done.1.passed_ref), custom_call_target="tpu_custom_call" | custom-call | tf_op jit(solution)/shard_map/pallas_call | solution.py:224
  19.9 11.6 %all_to_all.10 = bf16[16,16,256]{2,1,0:T(8,128)(2,1)S(1)} all-to-all(bf16[16,16,256]{2,1,0:T(8,128)(2,1)S(1)} %bitcast.7), channel_id=1, replica_groups=mesh['bin'=16,'wave'=2] {'bin'}, dimensions={0} | all-to-all | bytes 262144 | tf_op jit(solution)/shard_map/all_to_all | solution.py:231
  31.6 0.1 collective-permute-start.2
  31.7 1.2 %collective-permute-done.2.theirs_ref = bf16[16,256]{1,0:T(8,128)(2,1)S(1)} collective-permute-done((bf16[16,256]{1,0:T(8,128)(2,1)S(1)}, bf16[16,256]{1,0:T(8,128)(2,1)S(1)}, u32[]{:S(2)}, u32[]{:S(2)}) %collective-permute-start.2) | collective-permute-done | bytes 8224 | tf_op jit(solution)/shard_map/ppermute | solution.py:243
  32.8 1.1 %shard_map.67 = f32[16,4096]{1,0:T(8,128)} custom-call(f32[16,256]{1,0:T(8,128)S(1)} %convert_reduce_fusion.mine_ref, bf16[16,256]{1,0:T(8,128)(2,1)S(1)} %collective-permute-done.2.theirs_ref, bf16[256,4096]{1,0:T(8,128)(2,1)S(1)} %get-tuple-element.10.line_ref), custom_call_target="tpu_custom_call" | custom-call | tf_op jit(solution)/shard_map/pallas_call | solution.py:246
  (2 shorter events, 0.0 us)
Async XLA Ops:
  0.0 11.2 %collective-permute-start = (bf16[256,256]{1,0:T(8,128)(2,1)}, bf16[256,256]{1,0:T(8,128)(2,1)S(1)}, u32[]{:S(2)}, u32[]{:S(2)}) collective-permute-start(bf16[256,256]{1,0:T(8,128)(2,1)} %bitcast.11), channel_id=1, source_target_pairs={{0,16},{1,5},{2,18},{3,7},{4,20},{5,1},{6,22},{7,3},{8,24},{9,13},... | collective-permute-start | bytes 393224 | tf_op jit(solution)/shard_map/ppermute | solution.py:180
  6.4 12.6 %all-to-all-start = ((bf16[8,136,256]{2,1,0:T(8,128)(2,1)}), bf16[8,136,256]{2,1,0:T(8,128)(2,1)S(1)}, u32[]{:S(2)}, u32[]{:S(2)}) async-start(bf16[8,136,256]{2,1,0:T(8,128)(2,1)} %shard_map.64), calls=%async_computation | async-start | bytes 1114112 | tf_op jit(solution)/shard_map/all_to_all | solution.py:204
  12.9 1.6 %collective-permute-start.1 = (bf16[256,512]{1,0:T(8,128)(2,1)S(1)}, bf16[256,512]{1,0:T(8,128)(2,1)S(1)}, u32[]{:S(2)}, u32[]{:S(2)}) collective-permute-start(bf16[256,512]{1,0:T(8,128)(2,1)S(1)} %get-tuple-element.9.other_ref), channel_id=1, source_target_pairs={{0,1},{1,0},{2,3},{3,2},{4,5},{5,4},{6,7},{7,6},{8,9},{9,8},{10,11... | collective-permute-start | bytes 786440 | tf_op jit(solution)/shard_map/ppermute | solution.py:221
  31.6 1.2 %collective-permute-start.2 = (bf16[16,256]{1,0:T(8,128)(2,1)S(1)}, bf16[16,256]{1,0:T(8,128)(2,1)S(1)}, u32[]{:S(2)}, u32[]{:S(2)}) collective-permute-start(bf16[16,256]{1,0:T(8,128)(2,1)S(1)} %convert_element_type.7), channel_id=1, source_target_pairs={{0,1},{1,0},{2,3},{3,2},{4,5},{5,4},{6,7},{7,6},{8,9},{9,8},{10,11... | collective-permute-start | bytes 24584 | tf_op jit(solution)/shard_map/ppermute | solution.py:243
